TPU v7x, 128 devices: a whole 4x4x4 slice. The times are simulated.
128 devices in a mesh: strip: 4 (over x), tile: 32 (over z, y, core).
Axes of the slice: x: 4, y: 4, z: 4, core: 2. Of those that a mesh axis runs over, the one named last changes fastest.
Arguments:
- right_side: float32 [8, 4, 384, 32, 256], P('strip', None, 'tile'), may hold values from -1.2 to 1.2
- starting_iterate: float32 [8, 4, 384, 32, 256], P('strip', None, 'tile'), may hold values from -1.2 to 1.2
- inverse_diagonal_blocks: bfloat16 [8, 4, 384, 256, 256], P('strip', None, 'tile'), may hold values from -0.15 to 1, as said below
- couple: float32 [6, 8, 4, 384, 256], P(None, 'strip', None, 'tile'), may hold values from 0.02 to 2, as said below
- ice_mask: int32 [8, 4, 384], P('strip', None, 'tile'), may hold values 0 or 1
Outputs:
- solution_field: float32 [8, 4, 384, 32, 256], P('strip', None, 'tile')
Inputs may be any that keep to these rules, and one draw needn't show every extreme that they name: `inverse_diagonal_blocks`: each block is an inverse diagonal block of a diagonally dominant operator. `couple`: all couplings are positive.
All inputs are finite; a program needn't handle non-finite values. No bound on the sum of `ice_mask` on one device may be relied on, other than what follows from the above.
Results may differ from a plain program's by a relative error of at most 0.014.
Values sent between devices are 32-bit elements; how exact they have to be, the bound alone decides.
No kernel may reach another device: no remote copies, remote signals or barrier semaphores. Data moves between devices by JAX's collectives and lax.ppermute only.
A program may use at most 128 MiB of HBM per device.

v0:
```python
import jax
import jax.numpy as jnp
from jax import lax
from jax.sharding import PartitionSpec as P


def extended(cells, sides, width):
    for axis, dim in sides:
        count = lax.axis_size(axis)
        ends = count - 1
        head = lax.slice_in_dim(cells, 0, width, axis=dim)
        tail = lax.slice_in_dim(cells, cells.shape[dim] - width, cells.shape[dim], axis=dim)
        cells = jnp.concatenate(
            [
                lax.ppermute(tail, axis, [(i, (i + 1) % count) for i in range(ends)]),
                cells,
                lax.ppermute(head, axis, [((i + 1) % count, i) for i in range(ends)]),
            ],
            axis=dim,
        )
    return cells


def from_behind(value, axis, steps):
    count = lax.axis_size(axis)
    initial, last = (max(0, -steps), min(count, count - steps))
    return lax.ppermute(value, axis, [(source, source + steps) for source in range(initial, last)])


def lateral(field, couple):
    lane_count = field.shape[2]
    padded = extended(field, (("tile", 2),), 2)
    total = couple[2][:, :, :, None, :] * padded[:, :, 1 : lane_count + 1]
    total = total + couple[3][:, :, :, None, :] * padded[:, :, 3 : lane_count + 3]
    total = total + couple[4][:, :, :, None, :] * padded[:, :, 0:lane_count]
    total = total + couple[5][:, :, :, None, :] * padded[:, :, 4 : lane_count + 4]
    return total


def flatten(array):
    return array.reshape((array.shape[0] * array.shape[1],) + array.shape[2:])


def strip_rims(flat_field):
    return extended(flat_field, (("strip", 0),), 1)


def column_pass(source, lagged, inverse, up_coef, down_coef, weight, incoming, backward):
    column_count = source.shape[0]
    solved_list = [None] * column_count
    carried = incoming
    order = range(column_count - 1, -1, -1) if backward else range(column_count)
    for column_index in order:
        if backward:
            total = (
                source[column_index]
                + up_coef[column_index] * lagged[column_index]
                + down_coef[column_index] * carried
            )
        else:
            total = (
                source[column_index]
                + up_coef[column_index] * carried
                + down_coef[column_index] * lagged[column_index]
            )
        rounded = total.astype(jnp.bfloat16)
        solved = weight[column_index] * jnp.einsum(
            "lij,lrj->lri", inverse[column_index], rounded, preferred_element_type=jnp.float32
        )
        solved_list[column_index] = solved
        carried = solved
    return jnp.stack(solved_list, 0)


def send_edge(columns, backward):
    if backward:
        return from_behind(columns[0], "strip", -1)
    return from_behind(columns[-1], "strip", 1)


def sweep(source, lagged, inverse, up_coef, down_coef, weight, backward):
    strip_count = lax.axis_size("strip")
    incoming = jnp.zeros_like(source[0])
    columns = source
    for step_index in range(strip_count):
        columns = column_pass(
            source, lagged, inverse, up_coef, down_coef, weight, incoming, backward
        )
        if step_index + 1 < strip_count:
            incoming = send_edge(columns, backward)
    return columns


def on_device(right_side, starting_iterate, inverse_diagonal_blocks, couple, ice_mask):
    ice_weight = ice_mask.astype(jnp.float32)[:, :, :, None, None]
    initial = ice_weight * starting_iterate
    inverse = flatten(inverse_diagonal_blocks)
    weight = flatten(ice_weight)
    up_coef = flatten(couple[0])[:, :, None, :]
    down_coef = flatten(couple[1])[:, :, None, :]
    old_rims = strip_rims(flatten(initial))
    source = flatten(right_side + lateral(initial, couple))
    forward = sweep(source, old_rims[2:], inverse, up_coef, down_coef, weight, False)
    forward_rims = strip_rims(forward)
    source_back = flatten(right_side + lateral(forward.reshape(initial.shape), couple))
    backward = sweep(source_back, forward_rims[:-2], inverse, up_coef, down_coef, weight, True)
    return backward.reshape(initial.shape)


def solution(mesh):
    return jax.shard_map(
        on_device,
        mesh=mesh,
        in_specs=(
            P("strip", None, "tile", None, None),
            P("strip", None, "tile", None, None),
            P("strip", None, "tile", None, None),
            P(None, "strip", None, "tile", None),
            P("strip", None, "tile"),
        ),
        out_specs=P("strip", None, "tile", None, None),
        check_vma=False,
    )
```

profile of v0, /device:TPU:96, one launch (start us, length us, event | category | flops | bytes accessed | tf_op | source)
XLA Modules:
  0.0 240.3 jit_solution(3969799772627498257)
XLA Ops:
  0.7 2.2 broadcast_multiply_fusion
  3.0 2.2 collective-permute-start
  5.2 5.8 %collective-permute-start.1 = (f32[2,4,2,32,256]{4,3,2,1,0:T(8,128)S(1)}, f32[2,4,2,32,256]{4,3,2,1,0:T(8,128)S(1)}, u32[]{:S(2)}, u32[]{:S(2)}) collective-permute-start(f32[2,4,2,32,256]{4,3,2,1,0:T(8,128)S(1)} %get-tuple-element.16), channel_id=1, source_target_pairs={{1,0},{2,1},{3,2},{4,3},{5,4},{6,5},{7,6},{8,7},{9,8},{10,9},{11,1... | collective-permute-start | bytes 1572872 | tf_op jit(solution)/shard_map/ppermute | solution.py:17
  11.8 1.3 collective-permute-start.2
  19.8 3.5 %fusion.13 = f32[2,4,12,32,256]{4,3,2,1,0:T(8,128)} fusion(f32[2,4,12,32,256]{4,3,2,1,0:T(8,128)S(1)} %copy-done.1, f32[2,4,12,32,256]{4,3,2,1,0:T(8,128)S(1)} %broadcast_multiply_fusion, f32[2,4,2,32,256]{4,3,2,1,0:T(8,128)S(1)} %collective-permute-done.1, f32[2,4,2,32,256]{4,3,2,1,0:T(8,128)S(1)} %collective-permute-done, f32[2,4,12,256]{3,2,1,0:T(8,128)S(1)} %copy.13, ...), kind=kLoop, calls=%fused_computation.21 | loop fusion | flops 9437184 | bytes 10878976 | tf_op jit(solution)/shard_map/add | solution.py:102
  23.3 4.0 %fusion.147 = bf16[12,32,256]{2,1,0:T(8,128)(2,1)} fusion(f32[8,12,32,256]{3,2,1,0:T(8,128)} %bitcast.594, bf16[8,12,256,256]{3,2,1,0:T(8,128)(2,1)} %bitcast.537, f32[8,12,32,256]{3,2,1,0:T(8,128)S(1)} %bitcast.578, f32[12,256]{1,0:T(8,128)} %get-tuple-element.66, f32[12,256]{1,0:T(8,128)} %get-tuple-element.69, f32[12,256]{1,0:T(8,128)} %get-tuple-element.70, ...), kind=kOutput, calls=%fused_computation.232 | convolution fusion | flops 102236160 | bytes 5800960 | tf_op jit(solution)/shard_map/lij,lrj->lri/dot_general | solution.py:67
  27.4 3.9 %fusion.145 = bf16[12,32,256]{2,1,0:T(8,128)(2,1)} fusion(bf16[12,32,256]{2,1,0:T(8,128)(2,1)} %fusion.147, f32[8,12,32,256]{3,2,1,0:T(8,128)} %bitcast.595, bf16[8,12,256,256]{3,2,1,0:T(8,128)(2,1)} %bitcast.538, f32[8,12,32,256]{3,2,1,0:T(8,128)S(1)} %bitcast.579, f32[12,256]{1,0:T(8,128)} %get-tuple-element.67, f32[12,256]{1,0:T(8,128)} %get-tuple-element.68, ...), kind=kOutput, calls=%fused_computation.230 | convolution fusion | flops 101842944 | bytes 5178368 | tf_op jit(solution)/shard_map/lij,lrj->lri/dot_general | solution.py:67
  31.3 4.0 %fusion.143 = bf16[12,32,256]{2,1,0:T(8,128)(2,1)} fusion(bf16[12,32,256]{2,1,0:T(8,128)(2,1)} %fusion.145, f32[8,12,32,256]{3,2,1,0:T(8,128)} %bitcast.596, bf16[8,12,256,256]{3,2,1,0:T(8,128)(2,1)} %bitcast.539, f32[8,12,32,256]{3,2,1,0:T(8,128)S(1)} %bitcast.580, f32[12,256]{1,0:T(8,128)} %get-tuple-element.64, f32[12,256]{1,0:T(8,128)} %get-tuple-element.65, ...), kind=kOutput, calls=%fused_computation.228 | convolution fusion | flops 101842944 | bytes 5178368 | tf_op jit(solution)/shard_map/lij,lrj->lri/dot_general | solution.py:67
  35.3 3.8 %convolution_multiply_fusion.56 = f32[12,32,256]{2,1,0:T(8,128)} fusion(bf16[12,32,256]{2,1,0:T(8,128)(2,1)} %fusion.143, f32[1,12,32,256]{3,2,1,0:T(8,128)S(1)} %collective-permute-done.2, f32[8,12,32,256]{3,2,1,0:T(8,128)} %bitcast.597, bf16[8,12,256,256]{3,2,1,0:T(8,128)(2,1)} %bitcast.540, f32[12,256]{1,0:T(8,128)S(1)} %get-tuple-element.63, ...), kind=kOutput, calls=%fused_computation.170 | convolution fusion | flops 101351424 | bytes 4551680 | tf_op jit(solution)/shard_map/lij,lrj->lri/dot_general | solution.py:67
  39.1 5.3 %collective-permute-start.3 = (f32[12,32,256]{2,1,0:T(8,128)}, f32[12,32,256]{2,1,0:T(8,128)}, u32[]{:S(2)}, u32[]{:S(2)}) collective-permute-start(f32[12,32,256]{2,1,0:T(8,128)} %convolution_multiply_fusion.56), channel_id=1, source_target_pairs={{0,32},{32,64},{64,96},{1,33},{33,65},{65,97},{2,34},{34,66},{66,9... | collective-permute-start | bytes 1179656 | tf_op jit(solution)/shard_map/ppermute | solution.py:27
  44.4 1.3 copy.54
  45.7 4.3 %collective-permute-done.3 = f32[12,32,256]{2,1,0:T(8,128)} collective-permute-done((f32[12,32,256]{2,1,0:T(8,128)}, f32[12,32,256]{2,1,0:T(8,128)}, u32[]{:S(2)}, u32[]{:S(2)}) %collective-permute-start.3) | collective-permute-done | bytes 393248 | tf_op jit(solution)/shard_map/ppermute | solution.py:27
  50.0 4.1 %fusion.140 = bf16[12,32,256]{2,1,0:T(8,128)(2,1)} fusion(f32[8,12,32,256]{3,2,1,0:T(8,128)} %bitcast.598, bf16[8,12,256,256]{3,2,1,0:T(8,128)(2,1)} %bitcast.541, f32[8,12,32,256]{3,2,1,0:T(8,128)S(1)} %bitcast.581, f32[12,32,256]{2,1,0:T(8,128)} %collective-permute-done.3, f32[12,256]{1,0:T(8,128)} %get-tuple-element.66, ...), kind=kOutput, calls=%fused_computation.225 | convolution fusion | flops 102334464 | bytes 6194176 | tf_op jit(solution)/shard_map/lij,lrj->lri/dot_general | solution.py:67
  54.1 3.9 %fusion.138 = bf16[12,32,256]{2,1,0:T(8,128)(2,1)} fusion(bf16[12,32,256]{2,1,0:T(8,128)(2,1)} %fusion.140, f32[8,12,32,256]{3,2,1,0:T(8,128)} %bitcast.599, bf16[8,12,256,256]{3,2,1,0:T(8,128)(2,1)} %bitcast.542, f32[8,12,32,256]{3,2,1,0:T(8,128)S(1)} %bitcast.582, f32[12,256]{1,0:T(8,128)} %get-tuple-element.67, f32[12,256]{1,0:T(8,128)} %get-tuple-element.68, ...), kind=kOutput, calls=%fused_computation.223 | convolution fusion | flops 101842944 | bytes 5178368 | tf_op jit(solution)/shard_map/lij,lrj->lri/dot_general | solution.py:67
  58.1 4.0 %fusion.136 = bf16[12,32,256]{2,1,0:T(8,128)(2,1)} fusion(bf16[12,32,256]{2,1,0:T(8,128)(2,1)} %fusion.138, f32[8,12,32,256]{3,2,1,0:T(8,128)} %bitcast.600, bf16[8,12,256,256]{3,2,1,0:T(8,128)(2,1)} %bitcast.543, f32[8,12,32,256]{3,2,1,0:T(8,128)S(1)} %bitcast.583, f32[12,256]{1,0:T(8,128)} %get-tuple-element.64, f32[12,256]{1,0:T(8,128)} %get-tuple-element.65, ...), kind=kOutput, calls=%fused_computation.221 | convolution fusion | flops 101842944 | bytes 5178368 | tf_op jit(solution)/shard_map/lij,lrj->lri/dot_general | solution.py:67
  62.0 3.8 %convolution_multiply_fusion.48 = f32[12,32,256]{2,1,0:T(8,128)} fusion(bf16[12,32,256]{2,1,0:T(8,128)(2,1)} %fusion.136, f32[1,12,32,256]{3,2,1,0:T(8,128)S(1)} %collective-permute-done.2, f32[8,12,32,256]{3,2,1,0:T(8,128)} %bitcast.601, bf16[8,12,256,256]{3,2,1,0:T(8,128)(2,1)} %bitcast.544, f32[12,256]{1,0:T(8,128)S(1)} %get-tuple-element.63, ...), kind=kOutput, calls=%fused_computation.148 | convolution fusion | flops 101351424 | bytes 4551680 | tf_op jit(solution)/shard_map/lij,lrj->lri/dot_general | solution.py:67
  65.8 5.2 %collective-permute-start.4 = (f32[12,32,256]{2,1,0:T(8,128)}, f32[12,32,256]{2,1,0:T(8,128)}, u32[]{:S(2)}, u32[]{:S(2)}) collective-permute-start(f32[12,32,256]{2,1,0:T(8,128)} %convolution_multiply_fusion.48), channel_id=1, source_target_pairs={{0,32},{32,64},{64,96},{1,33},{33,65},{65,97},{2,34},{34,66},{66,9... | collective-permute-start | bytes 1179656 | tf_op jit(solution)/shard_map/ppermute | solution.py:27
  71.0 4.8 %collective-permute-done.4 = f32[12,32,256]{2,1,0:T(8,128)} collective-permute-done((f32[12,32,256]{2,1,0:T(8,128)}, f32[12,32,256]{2,1,0:T(8,128)}, u32[]{:S(2)}, u32[]{:S(2)}) %collective-permute-start.4) | collective-permute-done | bytes 393248 | tf_op jit(solution)/shard_map/ppermute | solution.py:27
  75.8 4.1 %fusion.133 = bf16[12,32,256]{2,1,0:T(8,128)(2,1)} fusion(f32[8,12,32,256]{3,2,1,0:T(8,128)} %bitcast.602, bf16[8,12,256,256]{3,2,1,0:T(8,128)(2,1)} %bitcast.545, f32[8,12,32,256]{3,2,1,0:T(8,128)S(1)} %bitcast.584, f32[12,32,256]{2,1,0:T(8,128)} %collective-permute-done.4, f32[12,256]{1,0:T(8,128)} %get-tuple-element.66, ...), kind=kOutput, calls=%fused_computation.218 | convolution fusion | flops 102334464 | bytes 6194176 | tf_op jit(solution)/shard_map/lij,lrj->lri/dot_general | solution.py:67
  79.9 3.9 %fusion.131 = bf16[12,32,256]{2,1,0:T(8,128)(2,1)} fusion(bf16[12,32,256]{2,1,0:T(8,128)(2,1)} %fusion.133, f32[8,12,32,256]{3,2,1,0:T(8,128)} %bitcast.603, bf16[8,12,256,256]{3,2,1,0:T(8,128)(2,1)} %bitcast.546, f32[8,12,32,256]{3,2,1,0:T(8,128)S(1)} %bitcast.585, f32[12,256]{1,0:T(8,128)} %get-tuple-element.67, f32[12,256]{1,0:T(8,128)} %get-tuple-element.68, ...), kind=kOutput, calls=%fused_computation.216 | convolution fusion | flops 101842944 | bytes 5178368 | tf_op jit(solution)/shard_map/lij,lrj->lri/dot_general | solution.py:67
  83.8 4.0 %fusion.129 = bf16[12,32,256]{2,1,0:T(8,128)(2,1)} fusion(bf16[12,32,256]{2,1,0:T(8,128)(2,1)} %fusion.131, f32[8,12,32,256]{3,2,1,0:T(8,128)} %bitcast.604, bf16[8,12,256,256]{3,2,1,0:T(8,128)(2,1)} %bitcast.547, f32[8,12,32,256]{3,2,1,0:T(8,128)S(1)} %bitcast.586, f32[12,256]{1,0:T(8,128)} %get-tuple-element.64, f32[12,256]{1,0:T(8,128)} %get-tuple-element.65, ...), kind=kOutput, calls=%fused_computation.214 | convolution fusion | flops 101842944 | bytes 5178368 | tf_op jit(solution)/shard_map/lij,lrj->lri/dot_general | solution.py:67
  87.8 3.8 %convolution_multiply_fusion.40 = f32[12,32,256]{2,1,0:T(8,128)} fusion(bf16[12,32,256]{2,1,0:T(8,128)(2,1)} %fusion.129, f32[1,12,32,256]{3,2,1,0:T(8,128)S(1)} %collective-permute-done.2, f32[8,12,32,256]{3,2,1,0:T(8,128)} %bitcast.605, bf16[8,12,256,256]{3,2,1,0:T(8,128)(2,1)} %bitcast.548, f32[12,256]{1,0:T(8,128)S(1)} %get-tuple-element.63, ...), kind=kOutput, calls=%fused_computation.126 | convolution fusion | flops 101351424 | bytes 4551680 | tf_op jit(solution)/shard_map/lij,lrj->lri/dot_general | solution.py:67
  91.6 4.9 %collective-permute-start.5 = (f32[12,32,256]{2,1,0:T(8,128)}, f32[12,32,256]{2,1,0:T(8,128)S(1)}, u32[]{:S(2)}, u32[]{:S(2)}) collective-permute-start(f32[12,32,256]{2,1,0:T(8,128)} %convolution_multiply_fusion.40), channel_id=1, source_target_pairs={{0,32},{32,64},{64,96},{1,33},{33,65},{65,97},{2,34},{34,66},{66,9... | collective-permute-start | bytes 1179656 | tf_op jit(solution)/shard_map/ppermute | solution.py:27
  96.5 5.4 %collective-permute-done.5 = f32[12,32,256]{2,1,0:T(8,128)S(1)} collective-permute-done((f32[12,32,256]{2,1,0:T(8,128)}, f32[12,32,256]{2,1,0:T(8,128)S(1)}, u32[]{:S(2)}, u32[]{:S(2)}) %collective-permute-start.5) | collective-permute-done | bytes 393248 | tf_op jit(solution)/shard_map/ppermute | solution.py:27
  101.9 2.1 bitcast_dynamic-update-slice_fusion.13
  104.0 2.1 bitcast_dynamic-update-slice_fusion.12
  106.2 2.0 bitcast_dynamic-update-slice_fusion.11
  108.3 2.0 bitcast_dynamic-update-slice_fusion.10
  110.3 2.0 bitcast_dynamic-update-slice_fusion.9
  112.4 2.0 bitcast_dynamic-update-slice_fusion.8
  114.4 2.0 bitcast_dynamic-update-slice_fusion.7
  116.5 2.9 %constant_dynamic-update-slice_fusion = (f32[8,12,32,256]{3,2,1,0:T(8,128)S(1)}, f32[1,12,32,256]{3,2,1,0:T(8,128)}) fusion(f32[8,12,32,256]{3,2,1,0:T(8,128)S(1)} %get-tuple-element.59, bf16[8,12,256,256]{3,2,1,0:T(8,128)(2,1)} %bitcast.556, f32[12,32,256]{2,1,0:T(8,128)S(1)} %get-tuple-element.60, f32[1,12,32,256]{3,2,1,0:T(8,128)S(1)} %collective-permute-done.2, ...), kind=kOutput, calls=%fused_computation.428 | convolution fusion | flops 50921472 | bytes 3572224 | tf_op jit(solution)/shard_map/lij,lrj->lri/dot_general | solution.py:67
  119.5 1.9 collective-permute-start.6
  121.4 7.5 %collective-permute-start.7 = (f32[2,4,2,32,256]{4,3,2,1,0:T(8,128)S(1)}, f32[2,4,2,32,256]{4,3,2,1,0:T(8,128)S(1)}, u32[]{:S(2)}, u32[]{:S(2)}) collective-permute-start(f32[2,4,2,32,256]{4,3,2,1,0:T(8,128)S(1)} %get-tuple-element.14), channel_id=1, source_target_pairs={{1,0},{2,1},{3,2},{4,3},{5,4},{6,5},{7,6},{8,7},{9,8},{10,9},{11,1... | collective-permute-start | bytes 1572872 | tf_op jit(solution)/shard_map/ppermute | solution.py:17
  129.5 5.1 %collective-permute-start.8 = (f32[1,12,32,256]{3,2,1,0:T(8,128)}, f32[1,12,32,256]{3,2,1,0:T(8,128)}, u32[]{:S(2)}, u32[]{:S(2)}) collective-permute-start(f32[1,12,32,256]{3,2,1,0:T(8,128)} %get-tuple-element.62), channel_id=1, source_target_pairs={{0,32},{32,64},{64,96},{1,33},{33,65},{65,97},{2,34},{34,66},{66,9... | collective-permute-start | bytes 1179656 | tf_op jit(solution)/shard_map/ppermute | solution.py:15
  135.6 2.6 %fusion.5 = f32[2,4,12,32,256]{4,3,2,1,0:T(8,128)S(1)} fusion(f32[2,4,12,32,256]{4,3,2,1,0:T(8,128)S(1)} %copy-done.2, f32[2,4,12,32,256]{4,3,2,1,0:T(8,128)S(1)} %bitcast.617, f32[2,4,2,32,256]{4,3,2,1,0:T(8,128)S(1)} %collective-permute-done.7, f32[2,4,2,32,256]{4,3,2,1,0:T(8,128)S(1)} %collective-permute-done.6, f32[2,4,12,256]{3,2,1,0:T(8,128)S(1)} %copy-done.18, ...), kind=kLoop, calls=%fused_computation.13 | loop fusion | flops 9437184 | bytes 10878976 | tf_op jit(solution)/shard_map/add | solution.py:105
  138.2 1.5 fusion.170
  139.7 4.0 %fusion.150 = bf16[12,32,256]{2,1,0:T(8,128)(2,1)} fusion(f32[12,32,256]{2,1,0:T(8,128)} %get-tuple-element.7, f32[12,32,256]{2,1,0:T(8,128)} %get-tuple-element.6, bf16[8,12,256,256]{3,2,1,0:T(8,128)(2,1)} %bitcast.557, f32[12,32,256]{2,1,0:T(8,128)} %get-tuple-element.5, f32[12,256]{1,0:T(8,128)} %broadcast_multiply_fusion.1, ...), kind=kOutput, calls=%fused_computation.235 | convolution fusion | flops 101646336 | bytes 4572160 | tf_op jit(solution)/shard_map/lij,lrj->lri/dot_general | solution.py:67
  143.7 3.9 %fusion.152 = bf16[12,32,256]{2,1,0:T(8,128)(2,1)} fusion(f32[12,32,256]{2,1,0:T(8,128)} %get-tuple-element.9, f32[12,32,256]{2,1,0:T(8,128)} %get-tuple-element.8, bf16[12,32,256]{2,1,0:T(8,128)(2,1)} %fusion.150, bf16[8,12,256,256]{3,2,1,0:T(8,128)(2,1)} %bitcast.558, f32[12,256]{1,0:T(8,128)} %get-tuple-element.67, f32[12,256]{1,0:T(8,128)} %get-tuple-element.68, ...), kind=kOutput, calls=%fused_computation.237 | convolution fusion | flops 101449728 | bytes 4359168 | tf_op jit(solution)/shard_map/lij,lrj->lri/dot_general | solution.py:67
  147.6 2.2 fusion.176
  149.8 3.1 %fusion.154 = bf16[12,32,256]{2,1,0:T(8,128)(2,1)S(1)} fusion(f32[12,32,256]{2,1,0:T(8,128)} %get-tuple-element.11, f32[12,32,256]{2,1,0:T(8,128)S(1)} %get-tuple-element.10, bf16[12,32,256]{2,1,0:T(8,128)(2,1)} %fusion.152, bf16[8,12,256,256]{3,2,1,0:T(8,128)(2,1)} %bitcast.559, f32[12,256]{1,0:T(8,128)} %get-tuple-element.66, ...), kind=kOutput, calls=%fused_computation.239 | convolution fusion | flops 101449728 | bytes 4359168 | tf_op jit(solution)/shard_map/lij,lrj->lri/dot_general | solution.py:67
  153.0 3.0 %convolution_multiply_fusion.24 = f32[12,32,256]{2,1,0:T(8,128)S(1)} fusion(f32[12,32,256]{2,1,0:T(8,128)S(1)} %copy-done.5, bf16[12,32,256]{2,1,0:T(8,128)(2,1)S(1)} %fusion.154, bf16[8,12,256,256]{3,2,1,0:T(8,128)(2,1)} %bitcast.560, f32[12,256]{1,0:T(8,128)S(1)} %copy-done.19, f32[12]{0:T(128)S(1)} %copy-done.57, f32[12]{0:T(128)S(1)} %copy-done.54), kind=kOutput, calls=%fused_computation.95 | convolution fusion | flops 101154816 | bytes 4141152 | tf_op jit(solution)/shard_map/lij,lrj->lri/dot_general | solution.py:67
  156.0 1.4 collective-permute-start.9
  157.5 12.2 %collective-permute-done.9 = f32[12,32,256]{2,1,0:T(8,128)} collective-permute-done((f32[12,32,256]{2,1,0:T(8,128)S(1)}, f32[12,32,256]{2,1,0:T(8,128)}, u32[]{:S(2)}, u32[]{:S(2)}) %collective-permute-start.9) | collective-permute-done | bytes 393248 | tf_op jit(solution)/shard_map/ppermute | solution.py:27
  169.7 3.0 %fusion.157 = bf16[12,32,256]{2,1,0:T(8,128)(2,1)S(1)} fusion(f32[12,32,256]{2,1,0:T(8,128)S(1)} %copy-done.7, f32[12,32,256]{2,1,0:T(8,128)S(1)} %copy-done.8, bf16[8,12,256,256]{3,2,1,0:T(8,128)(2,1)} %bitcast.561, f32[12,32,256]{2,1,0:T(8,128)S(1)} %copy-done.9, f32[12,32,256]{2,1,0:T(8,128)} %collective-permute-done.9, ...), kind=kOutput, calls=%fused_computation.242 | convolution fusion | flops 101744640 | bytes 4952160 | tf_op jit(solution)/shard_map/lij,lrj->lri/dot_general | solution.py:67
  172.8 3.0 %fusion.159 = bf16[12,32,256]{2,1,0:T(8,128)(2,1)S(1)} fusion(f32[12,32,256]{2,1,0:T(8,128)S(1)} %copy-done.3, f32[12,32,256]{2,1,0:T(8,128)S(1)} %copy-done.4, bf16[12,32,256]{2,1,0:T(8,128)(2,1)S(1)} %fusion.157, bf16[8,12,256,256]{3,2,1,0:T(8,128)(2,1)} %bitcast.562, f32[12,256]{1,0:T(8,128)} %get-tuple-element.67, f32[12,256]{1,0:T(8,128)} %get-tuple-element.68, ...), kind=kOutput, calls=%fused_computation.244 | convolution fusion | flops 101449728 | bytes 4359168 | tf_op jit(solution)/shard_map/lij,lrj->lri/dot_general | solution.py:67
  175.8 2.9 %fusion.161 = bf16[12,32,256]{2,1,0:T(8,128)(2,1)S(1)} fusion(f32[12,32,256]{2,1,0:T(8,128)S(1)} %copy-done.6, f32[12,32,256]{2,1,0:T(8,128)S(1)} %get-tuple-element.10, bf16[12,32,256]{2,1,0:T(8,128)(2,1)S(1)} %fusion.159, bf16[8,12,256,256]{3,2,1,0:T(8,128)(2,1)} %bitcast.563, f32[12,256]{1,0:T(8,128)} %get-tuple-element.66, ...), kind=kOutput, calls=%fused_computation.246 | convolution fusion | flops 101449728 | bytes 4359168 | tf_op jit(solution)/shard_map/lij,lrj->lri/dot_general | solution.py:67
  178.8 3.7 %convolution_multiply_fusion.16 = f32[12,32,256]{2,1,0:T(8,128)} fusion(f32[12,32,256]{2,1,0:T(8,128)S(1)} %copy-done.5, bf16[12,32,256]{2,1,0:T(8,128)(2,1)S(1)} %fusion.161, bf16[8,12,256,256]{3,2,1,0:T(8,128)(2,1)} %bitcast.564, f32[12,256]{1,0:T(8,128)} %get-tuple-element.70, f32[12]{0:T(128)} %get-tuple-element.40, f32[12]{0:T(128)} %get-tuple-element.46), kind=kOutput, calls=%fused_computation.73 | convolution fusion | flops 101154816 | bytes 4146176 | tf_op jit(solution)/shard_map/lij,lrj->lri/dot_general | solution.py:67
  183.8 12.9 %collective-permute-done.10 = f32[12,32,256]{2,1,0:T(8,128)} collective-permute-done((f32[12,32,256]{2,1,0:T(8,128)}, f32[12,32,256]{2,1,0:T(8,128)}, u32[]{:S(2)}, u32[]{:S(2)}) %collective-permute-start.10) | collective-permute-done | bytes 393248 | tf_op jit(solution)/shard_map/ppermute | solution.py:27
  196.7 3.0 %fusion.164 = bf16[12,32,256]{2,1,0:T(8,128)(2,1)S(1)} fusion(f32[12,32,256]{2,1,0:T(8,128)S(1)} %copy-done.7, f32[12,32,256]{2,1,0:T(8,128)S(1)} %copy-done.8, bf16[8,12,256,256]{3,2,1,0:T(8,128)(2,1)} %bitcast.565, f32[12,32,256]{2,1,0:T(8,128)S(1)} %copy-done.9, f32[12,32,256]{2,1,0:T(8,128)} %collective-permute-done.10, ...), kind=kOutput, calls=%fused_computation.249 | convolution fusion | flops 101744640 | bytes 4952160 | tf_op jit(solution)/shard_map/lij,lrj->lri/dot_general | solution.py:67
  199.7 2.9 %fusion.166 = bf16[12,32,256]{2,1,0:T(8,128)(2,1)S(1)} fusion(f32[12,32,256]{2,1,0:T(8,128)S(1)} %copy-done.3, f32[12,32,256]{2,1,0:T(8,128)S(1)} %copy-done.4, bf16[12,32,256]{2,1,0:T(8,128)(2,1)S(1)} %fusion.164, bf16[8,12,256,256]{3,2,1,0:T(8,128)(2,1)} %bitcast.566, f32[12,256]{1,0:T(8,128)} %get-tuple-element.67, f32[12,256]{1,0:T(8,128)} %get-tuple-element.68, ...), kind=kOutput, calls=%fused_computation.251 | convolution fusion | flops 101449728 | bytes 4359168 | tf_op jit(solution)/shard_map/lij,lrj->lri/dot_general | solution.py:67
  202.6 2.9 %fusion.168 = bf16[12,32,256]{2,1,0:T(8,128)(2,1)S(1)} fusion(f32[12,32,256]{2,1,0:T(8,128)S(1)} %copy-done.6, f32[12,32,256]{2,1,0:T(8,128)S(1)} %get-tuple-element.10, bf16[12,32,256]{2,1,0:T(8,128)(2,1)S(1)} %fusion.166, bf16[8,12,256,256]{3,2,1,0:T(8,128)(2,1)} %bitcast.567, f32[12,256]{1,0:T(8,128)} %get-tuple-element.66, ...), kind=kOutput, calls=%fused_computation.253 | convolution fusion | flops 101449728 | bytes 4359168 | tf_op jit(solution)/shard_map/lij,lrj->lri/dot_general | solution.py:67
  205.6 3.7 %convolution_multiply_fusion.8 = f32[12,32,256]{2,1,0:T(8,128)} fusion(f32[12,32,256]{2,1,0:T(8,128)S(1)} %copy-done.5, bf16[12,32,256]{2,1,0:T(8,128)(2,1)S(1)} %fusion.168, bf16[8,12,256,256]{3,2,1,0:T(8,128)(2,1)} %bitcast.568, f32[12,256]{1,0:T(8,128)} %get-tuple-element.70, f32[12]{0:T(128)} %get-tuple-element.40, f32[12]{0:T(128)} %get-tuple-element.46), kind=kOutput, calls=%fused_computation.51 | convolution fusion | flops 101154816 | bytes 4146176 | tf_op jit(solution)/shard_map/lij,lrj->lri/dot_general | solution.py:67
  209.3 1.6 collective-permute-start.11
  210.9 11.4 %collective-permute-done.11 = f32[12,32,256]{2,1,0:T(8,128)S(1)} collective-permute-done((f32[12,32,256]{2,1,0:T(8,128)}, f32[12,32,256]{2,1,0:T(8,128)S(1)}, u32[]{:S(2)}, u32[]{:S(2)}) %collective-permute-start.11) | collective-permute-done | bytes 393248 | tf_op jit(solution)/shard_map/ppermute | solution.py:27
  222.3 2.0 convolution_multiply_fusion.7
  224.3 2.0 convolution_multiply_fusion.6
  226.3 2.0 convolution_multiply_fusion.5
  228.3 2.0 convolution_multiply_fusion.4
  230.3 2.0 convolution_multiply_fusion.3
  232.4 2.0 convolution_multiply_fusion.2
  234.4 2.0 convolution_multiply_fusion.1
  236.4 2.0 fusion.21
  238.6 1.7 copy-done.47
  (171 shorter events, 11.7 us)
Async XLA Ops:
  0.7 12.4 %copy-start.37 = (f32[6,2,4,12,256]{4,2,3,1,0:T(4,128)S(1)}, f32[6,2,4,12,256]{4,2,3,1,0:T(4,128)}, u32[]{:S(2)}) copy-start(f32[6,2,4,12,256]{4,2,3,1,0:T(4,128)} %param.8) | copy-start | bytes 1769476
  2.9 16.9 %copy-start.1 = (f32[2,4,12,32,256]{4,3,2,1,0:T(8,128)S(1)}, f32[2,4,12,32,256]{4,3,2,1,0:T(8,128)}, u32[]{:S(2)}) copy-start(f32[2,4,12,32,256]{4,3,2,1,0:T(8,128)} %param.5) | copy-start | bytes 9437188
  3.0 16.7 %collective-permute-start = (f32[2,4,2,32,256]{4,3,2,1,0:T(8,128)S(1)}, f32[2,4,2,32,256]{4,3,2,1,0:T(8,128)S(1)}, u32[]{:S(2)}, u32[]{:S(2)}) collective-permute-start(f32[2,4,2,32,256]{4,3,2,1,0:T(8,128)S(1)} %get-tuple-element.15), channel_id=1, source_target_pairs={{0,1},{1,2},{2,3},{3,4},{4,5},{5,6},{6,7},{7,8},{8,9},{9,10},{10,1... | collective-permute-start | bytes 1572872 | tf_op jit(solution)/shard_map/ppermute | solution.py:15
  5.2 14.5 %collective-permute-start.1 = (f32[2,4,2,32,256]{4,3,2,1,0:T(8,128)S(1)}, f32[2,4,2,32,256]{4,3,2,1,0:T(8,128)S(1)}, u32[]{:S(2)}, u32[]{:S(2)}) collective-permute-start(f32[2,4,2,32,256]{4,3,2,1,0:T(8,128)S(1)} %get-tuple-element.16), channel_id=1, source_target_pairs={{1,0},{2,1},{3,2},{4,3},{5,4},{6,5},{7,6},{8,7},{9,8},{10,9},{11,1... | collective-permute-start | bytes 1572872 | tf_op jit(solution)/shard_map/ppermute | solution.py:17
  11.8 23.5 %collective-permute-start.2 = (f32[1,12,32,256]{3,2,1,0:T(8,128)}, f32[1,12,32,256]{3,2,1,0:T(8,128)S(1)}, u32[]{:S(2)}, u32[]{:S(2)}) collective-permute-start(f32[1,12,32,256]{3,2,1,0:T(8,128)} %slice.291), channel_id=1, source_target_pairs={{32,0},{64,32},{96,64},{33,1},{65,33},{97,65},{34,2},{66,34},{98,6... | collective-permute-start | bytes 1179656 | tf_op jit(solution)/shard_map/ppermute | solution.py:17
  13.3 6.5 %copy-start.44 = (f32[1,12,1,256]{3,2,1,0:T(1,128)}, f32[1,12,1,256]{3,2,1,0:T(1,128)S(1)}, u32[]{:S(2)}) copy-start(f32[1,12,1,256]{3,2,1,0:T(1,128)S(1)} %get-tuple-element.31) | copy-start | bytes 36868
  13.5 4.3 %copy-start.46 = (f32[1,12,1,256]{3,2,1,0:T(1,128)}, f32[1,12,1,256]{3,2,1,0:T(1,128)S(1)}, u32[]{:S(2)}) copy-start(f32[1,12,1,256]{3,2,1,0:T(1,128)S(1)} %get-tuple-element.30) | copy-start | bytes 36868
  17.8 5.5 %copy-start.11 = (f32[2,4,12,256]{3,2,1,0:T(8,128)}, f32[2,4,12,256]{3,2,1,0:T(8,128)S(1)}, u32[]{:S(2)}) copy-start(f32[2,4,12,256]{3,2,1,0:T(8,128)S(1)} %copy.10) | copy-start | bytes 294916
  17.8 5.5 %copy-start.13 = (f32[2,4,12,256]{3,2,1,0:T(8,128)}, f32[2,4,12,256]{3,2,1,0:T(8,128)S(1)}, u32[]{:S(2)}) copy-start(f32[2,4,12,256]{3,2,1,0:T(8,128)S(1)} %copy.11) | copy-start | bytes 294916
  17.8 5.5 %copy-start.15 = (f32[2,4,12,256]{3,2,1,0:T(8,128)}, f32[2,4,12,256]{3,2,1,0:T(8,128)S(1)}, u32[]{:S(2)}) copy-start(f32[2,4,12,256]{3,2,1,0:T(8,128)S(1)} %copy.12) | copy-start | bytes 294916
  17.9 5.4 %copy-start.17 = (f32[2,4,12,256]{3,2,1,0:T(8,128)}, f32[2,4,12,256]{3,2,1,0:T(8,128)S(1)}, u32[]{:S(2)}) copy-start(f32[2,4,12,256]{3,2,1,0:T(8,128)S(1)} %copy.13) | copy-start | bytes 294916
  39.1 10.9 %collective-permute-start.3 = (f32[12,32,256]{2,1,0:T(8,128)}, f32[12,32,256]{2,1,0:T(8,128)}, u32[]{:S(2)}, u32[]{:S(2)}) collective-permute-start(f32[12,32,256]{2,1,0:T(8,128)} %convolution_multiply_fusion.56), channel_id=1, source_target_pairs={{0,32},{32,64},{64,96},{1,33},{33,65},{65,97},{2,34},{34,66},{66,9... | collective-permute-start | bytes 1179656 | tf_op jit(solution)/shard_map/ppermute | solution.py:27
  65.8 10.0 %collective-permute-start.4 = (f32[12,32,256]{2,1,0:T(8,128)}, f32[12,32,256]{2,1,0:T(8,128)}, u32[]{:S(2)}, u32[]{:S(2)}) collective-permute-start(f32[12,32,256]{2,1,0:T(8,128)} %convolution_multiply_fusion.48), channel_id=1, source_target_pairs={{0,32},{32,64},{64,96},{1,33},{33,65},{65,97},{2,34},{34,66},{66,9... | collective-permute-start | bytes 1179656 | tf_op jit(solution)/shard_map/ppermute | solution.py:27
  91.6 12.4 %copy-start = (f32[2,4,12,32,256]{4,3,2,1,0:T(8,128)S(1)}, f32[2,4,12,32,256]{4,3,2,1,0:T(8,128)}, u32[]{:S(2)}) copy-start(f32[2,4,12,32,256]{4,3,2,1,0:T(8,128)} %fusion.13) | copy-start | bytes 9437188
  91.6 12.4 %copy-start.23 = (f32[12,256]{1,0:T(8,128)S(1)}, f32[12,256]{1,0:T(8,128)}, u32[]{:S(2)}) copy-start(f32[12,256]{1,0:T(8,128)} %get-tuple-element.69) | copy-start | bytes 36868
  91.6 12.4 %copy-start.38 = (f32[12,256]{1,0:T(8,128)S(1)}, f32[12,256]{1,0:T(8,128)}, u32[]{:S(2)}) copy-start(f32[12,256]{1,0:T(8,128)} %get-tuple-element.71) | copy-start | bytes 36868
  91.6 12.4 %copy-start.56 = (f32[12]{0:T(128)S(1)}, f32[12]{0:T(128)}, u32[]{:S(2)}) copy-start(f32[12]{0:T(128)} %get-tuple-element.40) | copy-start | bytes 148
  91.6 14.6 %copy-start.21 = (f32[12,256]{1,0:T(8,128)S(1)}, f32[12,256]{1,0:T(8,128)}, u32[]{:S(2)}) copy-start(f32[12,256]{1,0:T(8,128)} %get-tuple-element.66) | copy-start | bytes 36868
  91.6 14.6 %copy-start.39 = (f32[12,256]{1,0:T(8,128)S(1)}, f32[12,256]{1,0:T(8,128)}, u32[]{:S(2)}) copy-start(f32[12,256]{1,0:T(8,128)} %get-tuple-element.72) | copy-start | bytes 36868
  91.6 14.6 %copy-start.59 = (f32[12]{0:T(128)S(1)}, f32[12]{0:T(128)}, u32[]{:S(2)}) copy-start(f32[12]{0:T(128)} %get-tuple-element.41) | copy-start | bytes 148
  91.6 10.3 %collective-permute-start.5 = (f32[12,32,256]{2,1,0:T(8,128)}, f32[12,32,256]{2,1,0:T(8,128)S(1)}, u32[]{:S(2)}, u32[]{:S(2)}) collective-permute-start(f32[12,32,256]{2,1,0:T(8,128)} %convolution_multiply_fusion.40), channel_id=1, source_target_pairs={{0,32},{32,64},{64,96},{1,33},{33,65},{65,97},{2,34},{34,66},{66,9... | collective-permute-start | bytes 1179656 | tf_op jit(solution)/shard_map/ppermute | solution.py:27
  103.9 4.3 %copy-start.10 = (f32[12,32,256]{2,1,0:T(8,128)}, f32[12,32,256]{2,1,0:T(8,128)S(1)}, u32[]{:S(2)}) copy-start(f32[12,32,256]{2,1,0:T(8,128)S(1)} %get-tuple-element.48) | copy-start | bytes 1179652
  104.0 4.2 %copy-start.29 = (f32[12,256]{1,0:T(8,128)S(1)}, f32[12,256]{1,0:T(8,128)}, u32[]{:S(2)}) copy-start(f32[12,256]{1,0:T(8,128)} %get-tuple-element.68) | copy-start | bytes 36868
  104.0 4.2 %copy-start.40 = (f32[12,256]{1,0:T(8,128)S(1)}, f32[12,256]{1,0:T(8,128)}, u32[]{:S(2)}) copy-start(f32[12,256]{1,0:T(8,128)} %get-tuple-element.73) | copy-start | bytes 36868
  104.0 4.2 %copy-start.61 = (f32[12]{0:T(128)S(1)}, f32[12]{0:T(128)}, u32[]{:S(2)}) copy-start(f32[12]{0:T(128)} %get-tuple-element.42) | copy-start | bytes 148
  106.2 4.1 %copy-start.31 = (f32[12,256]{1,0:T(8,128)S(1)}, f32[12,256]{1,0:T(8,128)}, u32[]{:S(2)}) copy-start(f32[12,256]{1,0:T(8,128)} %get-tuple-element.67) | copy-start | bytes 36868
  106.2 4.1 %copy-start.41 = (f32[12,256]{1,0:T(8,128)S(1)}, f32[12,256]{1,0:T(8,128)}, u32[]{:S(2)}) copy-start(f32[12,256]{1,0:T(8,128)} %get-tuple-element.74) | copy-start | bytes 36868
  106.2 4.1 %copy-start.63 = (f32[12]{0:T(128)S(1)}, f32[12]{0:T(128)}, u32[]{:S(2)}) copy-start(f32[12]{0:T(128)} %get-tuple-element.43) | copy-start | bytes 148
  108.2 4.1 %copy-start.25 = (f32[12,256]{1,0:T(8,128)S(1)}, f32[12,256]{1,0:T(8,128)}, u32[]{:S(2)}) copy-start(f32[12,256]{1,0:T(8,128)} %get-tuple-element.65) | copy-start | bytes 36868
  108.3 4.1 %copy-start.42 = (f32[12,256]{1,0:T(8,128)S(1)}, f32[12,256]{1,0:T(8,128)}, u32[]{:S(2)}) copy-start(f32[12,256]{1,0:T(8,128)} %get-tuple-element.75) | copy-start | bytes 36868
  108.3 4.1 %copy-start.65 = (f32[12]{0:T(128)S(1)}, f32[12]{0:T(128)}, u32[]{:S(2)}) copy-start(f32[12]{0:T(128)} %get-tuple-element.44) | copy-start | bytes 148
  110.3 4.1 %copy-start.33 = (f32[12,256]{1,0:T(8,128)S(1)}, f32[12,256]{1,0:T(8,128)}, u32[]{:S(2)}) copy-start(f32[12,256]{1,0:T(8,128)} %get-tuple-element.64) | copy-start | bytes 36868
  110.3 4.1 %copy-start.43 = (f32[12,256]{1,0:T(8,128)S(1)}, f32[12,256]{1,0:T(8,128)}, u32[]{:S(2)}) copy-start(f32[12,256]{1,0:T(8,128)} %get-tuple-element.76) | copy-start | bytes 36868
  110.3 4.1 %copy-start.48 = (f32[12]{0:T(128)S(1)}, f32[12]{0:T(128)}, u32[]{:S(2)}) copy-start(f32[12]{0:T(128)} %get-tuple-element.45) | copy-start | bytes 148
  112.4 4.1 %copy-start.36 = (f32[1,12,1,256]{3,1,2,0:T(8,128)S(1)}, f32[1,12,1,256]{3,1,2,0:T(8,128)}, u32[]{:S(2)}) copy-start(f32[1,12,1,256]{3,1,2,0:T(8,128)} %copy.53) | copy-start | bytes 36868
  112.4 4.1 %copy-start.51 = (f32[12]{0:T(128)S(1)}, f32[12]{0:T(128)}, u32[]{:S(2)}) copy-start(f32[12]{0:T(128)} %get-tuple-element.39) | copy-start | bytes 148
  116.4 12.5 %copy-start.45 = (f32[1,12,1,256]{3,2,1,0:T(1,128)S(1)}, f32[1,12,1,256]{3,2,1,0:T(1,128)}, u32[]{:S(2)}) copy-start(f32[1,12,1,256]{3,2,1,0:T(1,128)} %copy-done.44) | copy-start | bytes 36868
  116.5 19.1 %copy-start.2 = (f32[2,4,12,32,256]{4,3,2,1,0:T(8,128)S(1)}, f32[2,4,12,32,256]{4,3,2,1,0:T(8,128)}, u32[]{:S(2)}) copy-start(f32[2,4,12,32,256]{4,3,2,1,0:T(8,128)} %param.5) | copy-start | bytes 9437188
  116.5 19.1 %copy-start.12 = (f32[2,4,12,256]{3,2,1,0:T(8,128)S(1)}, f32[2,4,12,256]{3,2,1,0:T(8,128)}, u32[]{:S(2)}) copy-start(f32[2,4,12,256]{3,2,1,0:T(8,128)} %copy-done.11) | copy-start | bytes 294916
  116.5 19.1 %copy-start.14 = (f32[2,4,12,256]{3,2,1,0:T(8,128)S(1)}, f32[2,4,12,256]{3,2,1,0:T(8,128)}, u32[]{:S(2)}) copy-start(f32[2,4,12,256]{3,2,1,0:T(8,128)} %copy-done.13) | copy-start | bytes 294916
  116.5 19.1 %copy-start.16 = (f32[2,4,12,256]{3,2,1,0:T(8,128)S(1)}, f32[2,4,12,256]{3,2,1,0:T(8,128)}, u32[]{:S(2)}) copy-start(f32[2,4,12,256]{3,2,1,0:T(8,128)} %copy-done.15) | copy-start | bytes 294916
  116.5 19.1 %copy-start.18 = (f32[2,4,12,256]{3,2,1,0:T(8,128)S(1)}, f32[2,4,12,256]{3,2,1,0:T(8,128)}, u32[]{:S(2)}) copy-start(f32[2,4,12,256]{3,2,1,0:T(8,128)} %copy-done.17) | copy-start | bytes 294916
  119.5 15.1 %collective-permute-start.6 = (f32[2,4,2,32,256]{4,3,2,1,0:T(8,128)S(1)}, f32[2,4,2,32,256]{4,3,2,1,0:T(8,128)S(1)}, u32[]{:S(2)}, u32[]{:S(2)}) collective-permute-start(f32[2,4,2,32,256]{4,3,2,1,0:T(8,128)S(1)} %get-tuple-element.13), channel_id=1, source_target_pairs={{0,1},{1,2},{2,3},{3,4},{4,5},{5,6},{6,7},{7,8},{8,9},{9,10},{10,1... | collective-permute-start | bytes 1572872 | tf_op jit(solution)/shard_map/ppermute | solution.py:15
  121.4 14.2 %collective-permute-start.7 = (f32[2,4,2,32,256]{4,3,2,1,0:T(8,128)S(1)}, f32[2,4,2,32,256]{4,3,2,1,0:T(8,128)S(1)}, u32[]{:S(2)}, u32[]{:S(2)}) collective-permute-start(f32[2,4,2,32,256]{4,3,2,1,0:T(8,128)S(1)} %get-tuple-element.14), channel_id=1, source_target_pairs={{1,0},{2,1},{3,2},{4,3},{5,4},{6,5},{7,6},{8,7},{9,8},{10,9},{11,1... | collective-permute-start | bytes 1572872 | tf_op jit(solution)/shard_map/ppermute | solution.py:17
  129.5 18.1 %collective-permute-start.8 = (f32[1,12,32,256]{3,2,1,0:T(8,128)}, f32[1,12,32,256]{3,2,1,0:T(8,128)}, u32[]{:S(2)}, u32[]{:S(2)}) collective-permute-start(f32[1,12,32,256]{3,2,1,0:T(8,128)} %get-tuple-element.62), channel_id=1, source_target_pairs={{0,32},{32,64},{64,96},{1,33},{33,65},{65,97},{2,34},{34,66},{66,9... | collective-permute-start | bytes 1179656 | tf_op jit(solution)/shard_map/ppermute | solution.py:15
  152.9 16.8 %copy-start.7 = (f32[12,32,256]{2,1,0:T(8,128)S(1)}, f32[12,32,256]{2,1,0:T(8,128)}, u32[]{:S(2)}) copy-start(f32[12,32,256]{2,1,0:T(8,128)} %get-tuple-element.7) | copy-start | bytes 1179652
  152.9 16.7 %copy-start.8 = (f32[12,32,256]{2,1,0:T(8,128)S(1)}, f32[12,32,256]{2,1,0:T(8,128)}, u32[]{:S(2)}) copy-start(f32[12,32,256]{2,1,0:T(8,128)} %get-tuple-element.6) | copy-start | bytes 1179652
  152.9 16.7 %copy-start.9 = (f32[12,32,256]{2,1,0:T(8,128)S(1)}, f32[12,32,256]{2,1,0:T(8,128)}, u32[]{:S(2)}) copy-start(f32[12,32,256]{2,1,0:T(8,128)} %get-tuple-element.5) | copy-start | bytes 1179652
  153.0 16.7 %copy-start.26 = (f32[12,256]{1,0:T(8,128)S(1)}, f32[12,256]{1,0:T(8,128)}, u32[]{:S(2)}) copy-start(f32[12,256]{1,0:T(8,128)} %get-tuple-element.65) | copy-start | bytes 36868
  153.0 16.7 %copy-start.34 = (f32[12,256]{1,0:T(8,128)S(1)}, f32[12,256]{1,0:T(8,128)}, u32[]{:S(2)}) copy-start(f32[12,256]{1,0:T(8,128)} %get-tuple-element.64) | copy-start | bytes 36868
  153.0 16.7 %copy-start.49 = (f32[12]{0:T(128)S(1)}, f32[12]{0:T(128)}, u32[]{:S(2)}) copy-start(f32[12]{0:T(128)} %get-tuple-element.45) | copy-start | bytes 148
  153.0 16.7 %copy-start.52 = (f32[12]{0:T(128)S(1)}, f32[12]{0:T(128)}, u32[]{:S(2)}) copy-start(f32[12]{0:T(128)} %get-tuple-element.39) | copy-start | bytes 148
  156.0 16.8 %copy-start.3 = (f32[12,32,256]{2,1,0:T(8,128)S(1)}, f32[12,32,256]{2,1,0:T(8,128)}, u32[]{:S(2)}) copy-start(f32[12,32,256]{2,1,0:T(8,128)} %get-tuple-element.9) | copy-start | bytes 1179652
  156.0 16.8 %copy-start.4 = (f32[12,32,256]{2,1,0:T(8,128)S(1)}, f32[12,32,256]{2,1,0:T(8,128)}, u32[]{:S(2)}) copy-start(f32[12,32,256]{2,1,0:T(8,128)} %get-tuple-element.8) | copy-start | bytes 1179652
  156.0 13.6 %collective-permute-start.9 = (f32[12,32,256]{2,1,0:T(8,128)S(1)}, f32[12,32,256]{2,1,0:T(8,128)}, u32[]{:S(2)}, u32[]{:S(2)}) collective-permute-start(f32[12,32,256]{2,1,0:T(8,128)S(1)} %convolution_multiply_fusion.24), channel_id=1, source_target_pairs={{32,0},{64,32},{96,64},{33,1},{65,33},{97,65},{34,2},{66,34},{98,6... | collective-permute-start | bytes 1179656 | tf_op jit(solution)/shard_map/ppermute | solution.py:27
  178.7 17.9 %copy-start.27 = (f32[12,256]{1,0:T(8,128)S(1)}, f32[12,256]{1,0:T(8,128)}, u32[]{:S(2)}) copy-start(f32[12,256]{1,0:T(8,128)} %get-tuple-element.65) | copy-start | bytes 36868
  178.8 17.9 %copy-start.35 = (f32[12,256]{1,0:T(8,128)S(1)}, f32[12,256]{1,0:T(8,128)}, u32[]{:S(2)}) copy-start(f32[12,256]{1,0:T(8,128)} %get-tuple-element.64) | copy-start | bytes 36868
  178.8 17.9 %copy-start.50 = (f32[12]{0:T(128)S(1)}, f32[12]{0:T(128)}, u32[]{:S(2)}) copy-start(f32[12]{0:T(128)} %get-tuple-element.45) | copy-start | bytes 148
  178.8 17.9 %copy-start.53 = (f32[12]{0:T(128)S(1)}, f32[12]{0:T(128)}, u32[]{:S(2)}) copy-start(f32[12]{0:T(128)} %get-tuple-element.39) | copy-start | bytes 148
  182.5 14.2 %collective-permute-start.10 = (f32[12,32,256]{2,1,0:T(8,128)}, f32[12,32,256]{2,1,0:T(8,128)}, u32[]{:S(2)}, u32[]{:S(2)}) collective-permute-start(f32[12,32,256]{2,1,0:T(8,128)} %convolution_multiply_fusion.16), channel_id=1, source_target_pairs={{32,0},{64,32},{96,64},{33,1},{65,33},{97,65},{34,2},{66,34},{98,6... | collective-permute-start | bytes 1179656 | tf_op jit(solution)/shard_map/ppermute | solution.py:27
  209.3 17.0 %copy-start.28 = (f32[12,256]{1,0:T(8,128)S(1)}, f32[12,256]{1,0:T(8,128)}, u32[]{:S(2)}) copy-start(f32[12,256]{1,0:T(8,128)} %get-tuple-element.65) | copy-start | bytes 36868
  209.3 17.0 %copy-start.66 = (f32[12]{0:T(128)S(1)}, f32[12]{0:T(128)}, u32[]{:S(2)}) copy-start(f32[12]{0:T(128)} %get-tuple-element.44) | copy-start | bytes 148
  209.3 13.0 %collective-permute-start.11 = (f32[12,32,256]{2,1,0:T(8,128)}, f32[12,32,256]{2,1,0:T(8,128)S(1)}, u32[]{:S(2)}, u32[]{:S(2)}) collective-permute-start(f32[12,32,256]{2,1,0:T(8,128)} %convolution_multiply_fusion.8), channel_id=1, source_target_pairs={{32,0},{64,32},{96,64},{33,1},{65,33},{97,65},{34,2},{66,34},{98,6... | collective-permute-start | bytes 1179656 | tf_op jit(solution)/shard_map/ppermute | solution.py:27
  224.3 4.0 %copy-start.32 = (f32[12,256]{1,0:T(8,128)S(1)}, f32[12,256]{1,0:T(8,128)}, u32[]{:S(2)}) copy-start(f32[12,256]{1,0:T(8,128)} %get-tuple-element.67) | copy-start | bytes 36868
  (15 other events, 53.9 us)
where the time goes:
time: 242 us; the launch traced here: 240 us
  matrix products  119 us (49%)
  waiting for transfers between devices  52 us (21%)
  starting transfers between devices  43.3 us (18%)
  other arithmetic  13.9 us (6%)
  local copies, waits for them, and re-layouts  10.4 us (4%)
    dot_general x40, matrix products, column_pass(): jnp.einsum('lij,lrj->lri', inverse[column_index], rounded, preferred_elem...  119 us
    ppermute x6, waiting for transfers between devices, from_behind(): lax.ppermute(value, axis, [(source, source + steps) for source in range(i...  51 us
    ppermute x6, starting transfers between devices, from_behind(): lax.ppermute(value, axis, [(source, source + steps) for source in range(i...  19.7 us
    ppermute x3, starting transfers between devices, extended(): lax.ppermute(head, axis, [((i + 1) % count, i) for i in range(ends)])  14.5 us
    ppermute x3, starting transfers between devices, extended(): lax.ppermute(tail, axis, [(i, (i + 1) % count) for i in range(ends)])  9.16 us
    unnamed x148, local copies, waits for them, and re-layouts  7.81 us
  transfers between devices with their start and end apart: 12, of which 7 were waited for; matrix products, arithmetic and copies ran while one was open for 15% of the time, Pallas kernels for 0%

commit v1 on v0

v1 whole, which is shorter than its diff:
```python
import functools

import jax
import jax.numpy as jnp
from jax import lax
from jax.experimental import pallas as pl
from jax.experimental.pallas import tpu as pltpu
from jax.sharding import PartitionSpec as P

COLS = 8
LANES = 12
R = 32
BS = 256
CHUNKS = ((2, 3, 4, 5), (6, 7, 8, 9), (0, 1, 10, 11))
EDGE = 2
STRIP = 4
NT = (((1,), (1,)), ((), ()))
VMEM = pltpu.VMEM
ANY = pl.ANY


def runs_of(lanes):
    runs = []
    for lane in lanes:
        if runs and runs[-1][0] + runs[-1][1] == lane:
            runs[-1][1] += 1
        else:
            runs.append([lane, 1])
    return [tuple(run) for run in runs]


def place_of(chunk, lane):
    if chunk == 0:
        return lane
    if chunk == 1:
        return lane - 4
    return lane + 2 if lane < 6 else lane - 2


def solve(xs, inverse, q, lanes):
    return [
        lax.dot_general(
            x.astype(jnp.bfloat16), inverse[q, lane], NT, preferred_element_type=jnp.float32
        )
        for x, lane in zip(xs, lanes)
    ]


def coef(ref, k, q, lane):
    return ref[k, q, pl.ds(lane, 1), :]


def weight(ref, q, lane):
    return ref[q, pl.ds(lane, 1), :]


def forward_chain(lanes, stage_edge, q, source, inverse, couple, mask, field, carry, left, right):
    xs = [source[q, lane] + coef(couple, 0, q, lane) * carry[j] for j, lane in enumerate(lanes)]
    ys = solve(xs, inverse, q, lanes)
    for j, lane in enumerate(lanes):
        value = weight(mask, q, lane) * ys[j]
        field[q + 1, lane] = value
        carry[j] = value
        if stage_edge:
            if lane < 2:
                left[q, lane] = value
            else:
                right[q, lane - (LANES - 2)] = value


def first_kernel(chunk, *refs):
    lanes = CHUNKS[chunk]
    edge = chunk == EDGE
    refs = list(refs)
    inv_hbm, rs_hbm, st_hbm, nxt, couple, mask = refs[:6]
    refs = refs[6:]
    if edge:
        halo_l, halo_r = refs[:2]
        refs = refs[2:]
    if chunk > 0:
        refs = refs[4:]
    inverse, rs, source, field = refs[:4]
    refs = refs[4:]
    if edge:
        left, right = refs[:2]
        refs = refs[2:]
    else:
        left = right = None
    sent, start, carry, sem_inv, sem_rs, sem_st = refs
    active = lax.axis_index("strip") == 0

    if edge:
        st_runs = [(0, 4, 2), (8, 4, 6)]
    else:
        st_runs = [(lanes[0] - 2, 8, 0)]

    def st_copies(q):
        return [
            pltpu.make_async_copy(
                st_hbm.at[q, pl.ds(a, n)], start.at[q, pl.ds(b, n)], sem_st.at[q]
            )
            for a, n, b in st_runs
        ] + (
            [
                pltpu.make_async_copy(halo_l.at[q], start.at[q, pl.ds(0, 2)], sem_st.at[q]),
                pltpu.make_async_copy(halo_r.at[q], start.at[q, pl.ds(10, 2)], sem_st.at[q]),
            ]
            if edge
            else []
        )

    def nxt_copies():
        at, copies = 0, []
        for a, n in runs_of(lanes):
            copies.append(
                pltpu.make_async_copy(
                    nxt.at[pl.ds(at, n)],
                    start.at[COLS, pl.ds(place_of(chunk, a), n)],
                    sem_st.at[COLS],
                )
            )
            at += n
        return copies

    def rs_copies(q):
        return [
            pltpu.make_async_copy(rs_hbm.at[q, pl.ds(a, n)], rs.at[q, pl.ds(a, n)], sem_rs.at[q])
            for a, n in runs_of(lanes)
        ]

    def inv_copies(q):
        return [
            pltpu.make_async_copy(
                inv_hbm.at[q, pl.ds(a, n)], inverse.at[q, pl.ds(a, n)], sem_inv.at[q]
            )
            for a, n in runs_of(lanes)
        ]

    for copy in st_copies(0) + st_copies(1) + rs_copies(0) + inv_copies(0):
        copy.start()

    def launch(q, _):
        for copy in st_copies(q + 1) + rs_copies(q) + inv_copies(q):
            copy.start()
        return 0

    lax.fori_loop(1, COLS - 1, launch, 0)
    for copy in nxt_copies() + rs_copies(COLS - 1) + inv_copies(COLS - 1):
        copy.start()

    def make_source(q):
        for lane in lanes:
            total = rs[q, lane]
            for k, step in ((2, -1), (3, 1), (4, -2), (5, 2)):
                other = lane + step
                factor = coef(couple, k, q, lane)
                if 0 <= other < LANES:
                    factor = factor * weight(mask, q, other)
                total = total + factor * start[q, place_of(chunk, other)]
            factor = coef(couple, 1, q, lane) * weight(mask, q + 1, lane)
            source[q, lane] = total + factor * start[q + 1, place_of(chunk, lane)]

    def wait_source(q):
        for copy in rs_copies(q):
            copy.wait()

        @pl.when(q < COLS - 1)
        def _():
            for copy in st_copies(q + 1):
                copy.wait()

        @pl.when(q == COLS - 1)
        def _():
            for copy in nxt_copies():
                copy.wait()

    for copy in st_copies(0):
        copy.wait()

    @pl.when(active)
    def _():
        for lane in lanes:
            field[0, lane] = jnp.zeros((R, BS), jnp.float32)
        carry[...] = jnp.zeros_like(carry)
        wait_source(0)
        make_source(0)

        def step(q, _):
            later = jnp.minimum(q + 1, COLS - 1)

            @pl.when(q < COLS - 1)
            def _():
                wait_source(later)

            for copy in inv_copies(q):
                copy.wait()
            forward_chain(
                lanes, edge, q, source, inverse, couple, mask, field, carry, left, right
            )
            make_source(later)
            return 0

        lax.fori_loop(0, COLS, step, 0)
        sent[...] = carry[...]

    @pl.when(jnp.logical_not(active))
    def _():
        def step(q, _):
            wait_source(q)
            make_source(q)
            return 0

        lax.fori_loop(0, COLS, step, 0)

        def drain(q, _):
            for copy in inv_copies(q):
                copy.wait()
            return 0

        lax.fori_loop(0, COLS, drain, 0)


def forward_kernel(chunk, stage, *refs):
    lanes = CHUNKS[chunk]
    edge = chunk == EDGE
    refs = list(refs)
    came, inverse, source, couple, mask = refs[:5]
    refs = refs[5:]
    if edge:
        _, _, _, field, left, right, sent = refs[:7]
        refs = refs[7:]
    else:
        _, field, sent = refs[:3]
        refs = refs[3:]
        left = right = None
    (carry,) = refs
    active = lax.axis_index("strip") == stage

    @pl.when(active)
    def _():
        for j, lane in enumerate(lanes):
            carry[j] = came[j]
            field[0, lane] = came[j]

        def step(q, _):
            forward_chain(
                lanes, edge, q, source, inverse, couple, mask, field, carry, left, right
            )
            return 0

        lax.fori_loop(0, COLS, step, 0)
        sent[...] = carry[...]


def backward_chain(lanes, q, source, inverse, couple, mask, carry, result):
    xs = [source[q, lane] + coef(couple, 1, q, lane) * carry[j] for j, lane in enumerate(lanes)]
    ys = solve(xs, inverse, q, lanes)
    for j, lane in enumerate(lanes):
        value = weight(mask, q, lane) * ys[j]
        result[q, j] = value
        carry[j] = value


def result_copies(lanes, q, result, out, sem):
    at, copies = 0, []
    for a, n in runs_of(lanes):
        copies.append(
            pltpu.make_async_copy(
                result.at[q, pl.ds(at, n)], out.at[q, pl.ds(a, n)], sem.at[q]
            )
        )
        at += n
    return copies


def last_kernel(chunk, *refs):
    lanes = CHUNKS[chunk]
    edge = chunk == EDGE
    refs = list(refs)
    inverse, rs, field, couple, mask = refs[:5]
    refs = refs[5:]
    if edge:
        halo_l, halo_r = refs[:2]
        refs = refs[2:]
    refs = refs[1:]
    if chunk > 0:
        refs = refs[1:]
    source, out, sent, carry, result, sem = refs
    active = lax.axis_index("strip") == STRIP - 1

    def near(q, lane):
        if lane < 0:
            return halo_l[q, lane + 2]
        if lane >= LANES:
            return halo_r[q, lane - LANES]
        return field[q + 1, lane]

    def make_source(q):
        for lane in lanes:
            total = rs[q, lane] + coef(couple, 0, q, lane) * field[q, lane]
            for k, step in ((2, -1), (3, 1), (4, -2), (5, 2)):
                total = total + coef(couple, k, q, lane) * near(q, lane + step)
            source[q, lane] = total

    @pl.when(active)
    def _():
        carry[...] = jnp.zeros_like(carry)
        make_source(COLS - 1)

        def step(i, _):
            q = COLS - 1 - i
            backward_chain(lanes, q, source, inverse, couple, mask, carry, result)
            for copy in result_copies(lanes, q, result, out, sem):
                copy.start()
            make_source(jnp.maximum(q - 1, 0))
            return 0

        lax.fori_loop(0, COLS, step, 0)
        sent[...] = carry[...]

        def drain(q, _):
            for copy in result_copies(lanes, q, result, out, sem):
                copy.wait()
            return 0

        lax.fori_loop(0, COLS, drain, 0)

    @pl.when(jnp.logical_not(active))
    def _():
        def step(q, _):
            make_source(q)
            return 0

        lax.fori_loop(0, COLS, step, 0)


def backward_kernel(chunk, stage, came, inverse, source, couple, mask, _, out, sent, carry, result, sem):
    lanes = CHUNKS[chunk]
    active = lax.axis_index("strip") == stage

    @pl.when(active)
    def _():
        carry[...] = came[...]

        def step(i, _):
            q = COLS - 1 - i
            backward_chain(lanes, q, source, inverse, couple, mask, carry, result)
            for copy in result_copies(lanes, q, result, out, sem):
                copy.start()
            return 0

        lax.fori_loop(0, COLS, step, 0)
        sent[...] = carry[...]

        def drain(q, _):
            for copy in result_copies(lanes, q, result, out, sem):
                copy.wait()
            return 0

        lax.fori_loop(0, COLS, drain, 0)


def vmem(shape, dtype=jnp.float32):
    return VMEM(shape, dtype)


def held(array):
    return pltpu.with_memory_space_constraint(array, VMEM)


def run(kernel, name, operands, outs, scratch, aliases):
    arrays = [held(a) if space is VMEM else a for a, space in operands]
    return pl.pallas_call(
        kernel,
        name=name,
        out_shape=[o for o, _ in outs],
        in_specs=[pl.BlockSpec(memory_space=space) for _, space in operands],
        out_specs=[pl.BlockSpec(memory_space=space) for _, space in outs],
        scratch_shapes=scratch,
        input_output_aliases=aliases,
        compiler_params=pltpu.CompilerParams(vmem_limit_bytes=16 * 2**20),
        cost_estimate=pl.CostEstimate(flops=2**27, bytes_accessed=2**22, transcendentals=0),
    )(*arrays)


FIELD = (COLS, LANES, R, BS)
FIELD_IN = (COLS + 1, LANES, R, BS)
PIECE = (4, R, BS)
SIDE = (COLS, 2, R, BS)


def on_device(right_side, starting_iterate, inverse_diagonal_blocks, couple, ice_mask):
    rs_hbm = right_side.reshape(FIELD)
    st_hbm = starting_iterate.reshape(FIELD)
    inv_hbm = inverse_diagonal_blocks.reshape((COLS, LANES, BS, BS))
    coefs = couple.reshape((6, COLS, LANES, BS))
    flat_mask = ice_mask.reshape((COLS, LANES)).astype(jnp.float32)
    mask = jnp.broadcast_to(
        jnp.concatenate([flat_mask, jnp.ones((1, LANES), jnp.float32)], 0)[:, :, None],
        (COLS + 1, LANES, BS),
    )
    weights = flat_mask[:, :, None, None]
    tiles = lax.axis_size("tile")
    to_right = [(i, i + 1) for i in range(tiles - 1)]
    to_left = [(i + 1, i) for i in range(tiles - 1)]
    to_back = [(i + 1, i) for i in range(STRIP - 1)]

    nxt = []
    for lanes in CHUNKS:
        first = jnp.concatenate(
            [weights[0, a : a + n] * st_hbm[0, a : a + n] for a, n in runs_of(lanes)], 0
        )
        nxt.append(lax.ppermute(first, "strip", to_back))
    start_l = lax.ppermute(weights[:, LANES - 2 :] * st_hbm[:, LANES - 2 :], "tile", to_right)
    start_r = lax.ppermute(weights[:, :2] * st_hbm[:, :2], "tile", to_left)

    dma = pltpu.SemaphoreType.DMA
    piece = vmem(PIECE)
    inverse = rs = source = field = left = right = None
    sents = []
    for chunk in range(3):
        operands = [
            (inv_hbm, ANY), (rs_hbm, ANY), (st_hbm, ANY), (nxt[chunk], ANY), (coefs, VMEM), (mask, VMEM),
        ]
        outs = [
            (vmem((COLS, LANES, BS, BS), jnp.bfloat16), VMEM),
            (vmem(FIELD), VMEM),
            (vmem(FIELD), VMEM),
            (vmem(FIELD_IN), VMEM),
        ]
        if chunk == EDGE:
            operands += [(start_l, ANY), (start_r, ANY)]
            outs += [(vmem(SIDE), VMEM), (vmem(SIDE), VMEM)]
        outs.append((vmem(PIECE), VMEM))
        aliases = {}
        if chunk > 0:
            base = len(operands)
            operands += [(inverse, VMEM), (rs, VMEM), (source, VMEM), (field, VMEM)]
            aliases = {base + i: i for i in range(4)}
        got = run(
            functools.partial(first_kernel, chunk),
            f"first_{chunk}",
            operands,
            outs,
            [
                vmem((COLS + 1, 12, R, BS)),
                piece,
                dma((COLS,)),
                dma((COLS,)),
                dma((COLS + 1,)),
            ],
            aliases,
        )
        inverse, rs, source, field = got[:4]
        if chunk == EDGE:
            left, right = got[4:6]
        sents.append(got[-1])

    for stage in range(1, STRIP):
        cames = [lax.ppermute(sent, "strip", [(stage - 1, stage)]) for sent in sents]
        sents = []
        for chunk in range(3):
            operands = [(cames[chunk], VMEM), (inverse, VMEM), (source, VMEM), (coefs, VMEM), (mask, VMEM)]
            outs = [(vmem(FIELD_IN), VMEM)]
            base = len(operands)
            operands += [(field, VMEM)]
            aliases = {base: 0}
            if chunk == EDGE:
                operands += [(left, VMEM), (right, VMEM)]
                outs += [(vmem(SIDE), VMEM), (vmem(SIDE), VMEM)]
                aliases |= {base + 1: 1, base + 2: 2}
            outs.append((vmem(PIECE), VMEM))
            got = run(
                functools.partial(forward_kernel, chunk, stage),
                f"forward_{stage}_{chunk}",
                operands,
                outs,
                [piece],
                aliases,
            )
            field = got[0]
            if chunk == EDGE:
                left, right = got[1:3]
            sents.append(got[-1])

    halo_l = lax.ppermute(right, "tile", to_right)
    halo_r = lax.ppermute(left, "tile", to_left)

    out_shape = jax.ShapeDtypeStruct(FIELD, jnp.float32)
    out_scratch = [piece, vmem((COLS,) + PIECE), dma((COLS,))]
    out = None
    sents = []
    for chunk in range(3):
        operands = [(inverse, VMEM), (rs, VMEM), (field, VMEM), (coefs, VMEM), (mask, VMEM)]
        if chunk == EDGE:
            operands += [(halo_l, VMEM), (halo_r, VMEM)]
        base = len(operands)
        operands += [(source, VMEM)]
        aliases = {base: 0}
        if chunk > 0:
            operands += [(out, ANY)]
            aliases[base + 1] = 1
        source, out, sent = run(
            functools.partial(last_kernel, chunk),
            f"last_{chunk}",
            operands,
            [(vmem(FIELD), VMEM), (out_shape, ANY), (vmem(PIECE), VMEM)],
            out_scratch,
            aliases,
        )
        sents.append(sent)

    for stage in range(STRIP - 2, -1, -1):
        cames = [lax.ppermute(sent, "strip", [(stage + 1, stage)]) for sent in sents]
        sents = []
        for chunk in range(3):
            operands = [
                (cames[chunk], VMEM), (inverse, VMEM), (source, VMEM), (coefs, VMEM), (mask, VMEM), (out, ANY),
            ]
            out, sent = run(
                functools.partial(backward_kernel, chunk, stage),
                f"backward_{stage}_{chunk}",
                operands,
                [(out_shape, ANY), (vmem(PIECE), VMEM)],
                out_scratch,
                {5: 0},
            )
            sents.append(sent)
    return out.reshape(right_side.shape)


def solution(mesh):
    return jax.shard_map(
        on_device,
        mesh=mesh,
        in_specs=(
            P("strip", None, "tile", None, None),
            P("strip", None, "tile", None, None),
            P("strip", None, "tile", None, None),
            P(None, "strip", None, "tile", None),
            P("strip", None, "tile"),
        ),
        out_specs=P("strip", None, "tile", None, None),
        check_vma=False,
    )
```

time: 242 us -> 110 us (0.45)
  matrix products: 119 us -> 0 us
  Pallas kernels: 0 us -> 31.7 us
  waiting for transfers between devices: 52 us -> 32.3 us
  other arithmetic: 13.9 us -> 4.23 us
  local copies, waits for them, and re-layouts: 10.4 us -> 3.38 us
  starting transfers between devices: 43.3 us -> 36.6 us
    dot_general x40 -> x0, matrix products: 119 us -> none  [column_pass(): jnp.einsum('lij,lrj->lri', inverse[column_index], rounded, preferred_elem...]
    pallas_call x0 -> x24, Pallas kernels: none -> 31.7 us  [run(): pl.pallas_call(kernel, name=name, out_shape=[o for o, _ in outs], in_spec...]
    ppermute x12 -> x25, waiting for transfers between devices: 52 us -> 32.3 us  [the longest x9 26.8 us: on_device(): lax.ppermute(sent, 'strip', [(stage + 1, stage)])]
    add x4 -> x0, other arithmetic: 9.8 us -> none  [the longest x2 3.7 us: column_pass(): source[column_index] + up_coef[column_index] * lagged[column_index]]
    ppermute x12 -> x25, starting transfers between devices: 43.3 us -> 36.6 us  [the longest x9 11 us: on_device(): lax.ppermute(sent, 'strip', [(stage - 1, stage)])]
    unnamed x148 -> x5, local copies, waits for them, and re-layouts: 7.81 us -> 3.07 us
  transfers between devices with their start and end apart: 12 -> 25, of which waited for: 7 -> 5; matrix products, arithmetic and copies ran while one was open for 15% -> 3% of each run, Pallas kernels for 0% -> 25%
where the time goes in v1:
time: 110 us; the launch traced here: 109 us
  starting transfers between devices  36.6 us (33%)
  waiting for transfers between devices  32.3 us (29%)
  Pallas kernels  31.7 us (29%)
  other arithmetic  4.23 us (4%)
  local copies, waits for them, and re-layouts  3.38 us (3%)
    pallas_call x24, Pallas kernels, run(): pl.pallas_call(kernel, name=name, out_shape=[o for o, _ in outs], in_spec...  31.7 us
    ppermute x9, waiting for transfers between devices, on_device(): lax.ppermute(sent, 'strip', [(stage + 1, stage)])  26.8 us
    ppermute x9, starting transfers between devices, on_device(): lax.ppermute(sent, 'strip', [(stage - 1, stage)])  11 us
    ppermute x9, starting transfers between devices, on_device(): lax.ppermute(sent, 'strip', [(stage + 1, stage)])  7.89 us
    ppermute x1, starting transfers between devices, on_device(): halo_r = lax.ppermute(left, 'tile', to_left)  5.75 us
    ppermute x1, starting transfers between devices, on_device(): start_r = lax.ppermute(weights[:, :2] * st_hbm[:, :2], 'tile', to_left)  4.2 us
    ppermute x3, starting transfers between devices, on_device(): nxt.append(lax.ppermute(first, 'strip', to_back))  3.88 us
    unnamed x5, local copies, waits for them, and re-layouts  3.07 us
  transfers between devices with their start and end apart: 25, of which 5 were waited for; matrix products, arithmetic and copies ran while one was open for 3% of the time, Pallas kernels for 25%

profile of v1, /device:TPU:96, one launch (start us, length us, event | category | flops | bytes accessed | tf_op | source)
XLA Modules:
  0.0 108.8 jit_solution(1214146903183434974)
XLA Ops:
  0.0 0.8 convert_element_type.16
  0.8 0.1 slice_bitcast_fusion.6
  0.9 1.1 %fusion = (f32[4,32,256]{2,1,0:T(8,128)S(1)}, f32[4,32,256]{2,1,0:T(8,128)S(1)}) fusion(f32[8,12,32,256]{3,2,1,0:T(8,128)} %bitcast.59, f32[4]{0:T(128)S(1)} %get-tuple-element.135, f32[4]{0:T(128)S(1)} %get-tuple-element.136), kind=kLoop, calls=%fused_computation.3 | loop fusion | flops 65536 | bytes 524320 | tf_op jit(solution)/shard_map/mul | solution.py:411
  2.0 1.3 %collective-permute-start.4 = (f32[4,32,256]{2,1,0:T(8,128)S(1)}, f32[4,32,256]{2,1,0:T(8,128)S(1)}, u32[]{:S(2)}, u32[]{:S(2)}) collective-permute-start(f32[4,32,256]{2,1,0:T(8,128)S(1)} %get-tuple-element.129), channel_id=1, source_target_pairs={{32,0},{64,32},{96,64},{33,1},{65,33},{97,65},{34,2},{66,34},{98,6... | collective-permute-start | bytes 393224 | tf_op jit(solution)/shard_map/ppermute | solution.py:413
  3.3 1.3 %collective-permute-start.3 = (f32[4,32,256]{2,1,0:T(8,128)S(1)}, f32[4,32,256]{2,1,0:T(8,128)S(1)}, u32[]{:S(2)}, u32[]{:S(2)}) collective-permute-start(f32[4,32,256]{2,1,0:T(8,128)S(1)} %get-tuple-element.130), channel_id=1, source_target_pairs={{32,0},{64,32},{96,64},{33,1},{65,33},{97,65},{34,2},{66,34},{98,6... | collective-permute-start | bytes 393224 | tf_op jit(solution)/shard_map/ppermute | solution.py:413
  4.6 0.1 slice_bitcast_fusion.4
  4.7 1.3 %slice_multiply_fusion = (f32[8,2,32,256]{3,2,1,0:T(8,128)S(1)}, f32[8,2,32,256]{3,2,1,0:T(8,128)S(1)}) fusion(f32[8,12,32,256]{3,2,1,0:T(8,128)} %bitcast.60, f32[8,2]{1,0:T(8,128)S(1)} %get-tuple-element.137, f32[8,2]{1,0:T(8,128)S(1)} %get-tuple-element.138), kind=kLoop, calls=%fused_computation | loop fusion | flops 262144 | bytes 2097280 | tf_op jit(solution)/shard_map/mul | solution.py:415
  6.0 4.2 %collective-permute-start.2 = (f32[8,2,32,256]{3,2,1,0:T(8,128)S(1)}, f32[8,2,32,256]{3,2,1,0:T(8,128)S(1)}, u32[]{:S(2)}, u32[]{:S(2)}) collective-permute-start(f32[8,2,32,256]{3,2,1,0:T(8,128)S(1)} %get-tuple-element.131), channel_id=1, source_target_pairs={{1,0},{2,1},{3,2},{4,3},{5,4},{6,5},{7,6},{8,7},{9,8},{10,9},{11,1... | collective-permute-start | bytes 1572872 | tf_op jit(solution)/shard_map/ppermute | solution.py:415
  10.2 1.9 %collective-permute-start.1 = (f32[8,2,32,256]{3,2,1,0:T(8,128)S(1)}, f32[8,2,32,256]{3,2,1,0:T(8,128)S(1)}, u32[]{:S(2)}, u32[]{:S(2)}) collective-permute-start(f32[8,2,32,256]{3,2,1,0:T(8,128)S(1)} %get-tuple-element.132), channel_id=1, source_target_pairs={{0,1},{1,2},{2,3},{3,4},{4,5},{5,6},{6,7},{7,8},{8,9},{9,10},{10,1... | collective-permute-start | bytes 1572872 | tf_op jit(solution)/shard_map/ppermute | solution.py:414
  12.2 0.1 slice_bitcast_fusion.9
  12.2 0.9 fusion.3
  13.2 1.3 %collective-permute-start = (f32[4,32,256]{2,1,0:T(8,128)S(1)}, f32[4,32,256]{2,1,0:T(8,128)S(1)}, u32[]{:S(2)}, u32[]{:S(2)}) collective-permute-start(f32[4,32,256]{2,1,0:T(8,128)S(1)} %pad_maximum_fusion), channel_id=1, source_target_pairs={{32,0},{64,32},{96,64},{33,1},{65,33},{97,65},{34,2},{66,34},{98,6... | collective-permute-start | bytes 393224 | tf_op jit(solution)/shard_map/ppermute | solution.py:413
  14.5 1.2 %copy.43 = f32[6,2,4,12,256]{4,3,2,1,0:T(8,128)S(1)} copy(f32[6,2,4,12,256]{4,2,3,1,0:T(4,128)} %param.8) | data formatting | bytes 1179648 | tf_op args[3]
  15.7 0.0 collective-permute-done.4.refs_3_
  15.7 0.1 broadcast_in_dim.2.refs_5_.refs_4_.mask
  15.8 0.0 copy-start.1
  15.8 1.9 %copy-done.1 = f32[2,4,12,32,256]{4,3,2,1,0:T(8,128)S(1)} copy-done((f32[2,4,12,32,256]{4,3,2,1,0:T(8,128)S(1)}, f32[2,4,12,32,256]{4,3,2,1,0:T(8,128)}, u32[]{:S(2)}) %copy-start.1) | copy-done | bytes 3145752
  17.7 4.2 %first_0.1 = (bf16[8,12,256,256]{3,2,1,0:T(8,128)(2,1)S(1)}, f32[8,12,32,256]{3,2,1,0:T(8,128)S(1)}, f32[8,12,32,256]{3,2,1,0:T(8,128)S(1)}, f32[9,12,32,256]{3,2,1,0:T(8,128)S(1)}, f32[4,32,256]{2,1,0:T(8,128)S(1)}) custom-call(bf16[8,12,256,256]{3,2,1,0:T(8,128)(2,1)} %bitcast.68, f32[8,12,32,256]{3,2,1,0:T(8,128)S(1)} %bitcast.65, ...), custom_call_target="tpu_custom_call" | custom-call | flops 134217728 | bytes 4194304 | tf_op jit(solution)/shard_map/first_0/pallas_call | solution.py:373
  22.0 4.4 %collective-permute-start.7 = (f32[4,32,256]{2,1,0:T(8,128)S(1)}, f32[4,32,256]{2,1,0:T(8,128)S(1)}, u32[]{:S(2)}, u32[]{:S(2)}) collective-permute-start(f32[4,32,256]{2,1,0:T(8,128)S(1)} %get-tuple-element.80), channel_id=1, source_target_pairs={{0,32},{1,33},{2,34},{3,35},{4,36},{5,37},{6,38},{7,39},{8,40},{9,... | collective-permute-start | bytes 393224 | tf_op jit(solution)/shard_map/ppermute | solution.py:460
  26.4 0.0 collective-permute-done.3.refs_3_
  26.4 4.3 %first_1.1 = (bf16[8,12,256,256]{3,2,1,0:T(8,128)(2,1)S(1)}, f32[8,12,32,256]{3,2,1,0:T(8,128)S(1)}, f32[8,12,32,256]{3,2,1,0:T(8,128)S(1)}, f32[9,12,32,256]{3,2,1,0:T(8,128)S(1)}, f32[4,32,256]{2,1,0:T(8,128)S(1)}) custom-call(bf16[8,12,256,256]{3,2,1,0:T(8,128)(2,1)} %bitcast.69, ...), custom_call_target="tpu_custom_call", output_to_operand_aliasing={{0}: (6, {}), {1}: (7, {}), {2}: (8, {}), {3}: (9, {})} | custom-call | flops 134217728 | bytes 4194304 | tf_op jit(solution)/shard_map/first_1/pallas_call | solution.py:373
  30.7 1.3 %collective-permute-start.6 = (f32[4,32,256]{2,1,0:T(8,128)S(1)}, f32[4,32,256]{2,1,0:T(8,128)S(1)}, u32[]{:S(2)}, u32[]{:S(2)}) collective-permute-start(f32[4,32,256]{2,1,0:T(8,128)S(1)} %get-tuple-element.79), channel_id=1, source_target_pairs={{0,32},{1,33},{2,34},{3,35},{4,36},{5,37},{6,38},{7,39},{8,40},{9,... | collective-permute-start | bytes 393224 | tf_op jit(solution)/shard_map/ppermute | solution.py:460
  32.0 0.0 collective-permute-done.2.refs_7_
  32.0 0.0 collective-permute-done.1.refs_6_
  32.0 8.4 %first_2.1 = (bf16[8,12,256,256]{3,2,1,0:T(8,128)(2,1)S(1)}, f32[8,12,32,256]{3,2,1,0:T(8,128)S(1)}, f32[8,12,32,256]{3,2,1,0:T(8,128)S(1)}, f32[9,12,32,256]{3,...) custom-call(bf16[8,12,256,256]{3,2,1,0:T(8,128)(2,1)} %bitcast.70, ...), custom_call_target="tpu_custom_call", output_to_operand_aliasing={{0}: (8, {}), {1}: (9, {}), {2}: (10, {}), {3}: (11, {})} | custom-call | flops 134217728 | bytes 4194304 | tf_op jit(solution)/shard_map/first_2/pallas_call | solution.py:373
  40.5 1.3 %collective-permute-start.5 = (f32[4,32,256]{2,1,0:T(8,128)S(1)}, f32[4,32,256]{2,1,0:T(8,128)S(1)}, u32[]{:S(2)}, u32[]{:S(2)}) collective-permute-start(f32[4,32,256]{2,1,0:T(8,128)S(1)} %get-tuple-element.77), channel_id=1, source_target_pairs={{0,32},{1,33},{2,34},{3,35},{4,36},{5,37},{6,38},{7,39},{8,40},{9,... | collective-permute-start | bytes 393224 | tf_op jit(solution)/shard_map/ppermute | solution.py:460
  41.8 0.0 collective-permute-done.7.refs_0_
  41.8 0.7 collective-permute-start.10
  42.5 0.7 collective-permute-start.9
  43.2 1.1 %collective-permute-done.5.refs_0_ = f32[4,32,256]{2,1,0:T(8,128)S(1)} collective-permute-done((f32[4,32,256]{2,1,0:T(8,128)S(1)}, f32[4,32,256]{2,1,0:T(8,128)S(1)}, u32[]{:S(2)}, u32[]{:S(2)}) %collective-permute-start.5) | collective-permute-done | bytes 131104 | tf_op jit(solution)/shard_map/ppermute | solution.py:460
  44.4 0.7 collective-permute-start.8
  45.1 0.7 collective-permute-start.13
  45.8 0.7 collective-permute-start.12
  46.5 0.7 collective-permute-start.11
  47.2 0.7 forward_3_0.1
  47.9 0.7 forward_3_1.1
  48.5 0.7 forward_3_2.1
  49.2 1.9 %collective-permute-start.14 = (f32[8,2,32,256]{3,2,1,0:T(8,128)S(1)}, f32[8,2,32,256]{3,2,1,0:T(8,128)S(1)}, u32[]{:S(2)}, u32[]{:S(2)}) collective-permute-start(f32[8,2,32,256]{3,2,1,0:T(8,128)S(1)} %get-tuple-element.103), channel_id=1, source_target_pairs={{0,1},{1,2},{2,3},{3,4},{4,5},{5,6},{6,7},{7,8},{8,9},{9,10},{10,1... | collective-permute-start | bytes 1572872 | tf_op jit(solution)/shard_map/ppermute | solution.py:486
  51.1 5.8 %collective-permute-start.15 = (f32[8,2,32,256]{3,2,1,0:T(8,128)S(1)}, f32[8,2,32,256]{3,2,1,0:T(8,128)S(1)}, u32[]{:S(2)}, u32[]{:S(2)}) collective-permute-start(f32[8,2,32,256]{3,2,1,0:T(8,128)S(1)} %get-tuple-element.104), channel_id=1, source_target_pairs={{1,0},{2,1},{3,2},{4,3},{5,4},{6,5},{7,6},{8,7},{9,8},{10,9},{11,1... | collective-permute-start | bytes 1572872 | tf_op jit(solution)/shard_map/ppermute | solution.py:487
  56.8 0.5 last_0.1
  57.3 0.7 collective-permute-start.18
  58.0 0.5 last_1.1
  58.5 0.7 collective-permute-start.17
  59.2 2.6 %collective-permute-done.14.refs_5_ = f32[8,2,32,256]{3,2,1,0:T(8,128)S(1)} collective-permute-done((f32[8,2,32,256]{3,2,1,0:T(8,128)S(1)}, f32[8,2,32,256]{3,2,1,0:T(8,128)S(1)}, u32[]{:S(2)}, u32[]{:S(2)}) %collective-permute-start.14) | collective-permute-done | bytes 524320 | tf_op jit(solution)/shard_map/ppermute | solution.py:486
  61.8 1.8 %collective-permute-done.15.refs_6_ = f32[8,2,32,256]{3,2,1,0:T(8,128)S(1)} collective-permute-done((f32[8,2,32,256]{3,2,1,0:T(8,128)S(1)}, f32[8,2,32,256]{3,2,1,0:T(8,128)S(1)}, u32[]{:S(2)}, u32[]{:S(2)}) %collective-permute-start.15) | collective-permute-done | bytes 524320 | tf_op jit(solution)/shard_map/ppermute | solution.py:487
  63.5 0.5 last_2.1
  64.0 0.7 collective-permute-start.16
  64.7 0.1 backward_2_0.1
  64.8 0.7 collective-permute-start.21
  65.5 0.1 backward_2_1.1
  65.6 0.7 collective-permute-start.20
  66.3 0.1 backward_2_2.1
  66.4 0.7 collective-permute-start.19
  67.0 0.1 backward_1_0.1
  67.1 1.3 %collective-permute-start.24 = (f32[4,32,256]{2,1,0:T(8,128)S(1)}, f32[4,32,256]{2,1,0:T(8,128)S(1)}, u32[]{:S(2)}, u32[]{:S(2)}) collective-permute-start(f32[4,32,256]{2,1,0:T(8,128)S(1)} %get-tuple-element.124), channel_id=1, source_target_pairs={{32,0},{33,1},{34,2},{35,3},{36,4},{37,5},{38,6},{39,7},{40,8},{41... | collective-permute-start | bytes 393224 | tf_op jit(solution)/shard_map/ppermute | solution.py:514
  68.5 0.1 backward_1_1.1
  68.6 1.3 %collective-permute-start.23 = (f32[4,32,256]{2,1,0:T(8,128)S(1)}, f32[4,32,256]{2,1,0:T(8,128)S(1)}, u32[]{:S(2)}, u32[]{:S(2)}) collective-permute-start(f32[4,32,256]{2,1,0:T(8,128)S(1)} %get-tuple-element.123), channel_id=1, source_target_pairs={{32,0},{33,1},{34,2},{35,3},{36,4},{37,5},{38,6},{39,7},{40,8},{41... | collective-permute-start | bytes 393224 | tf_op jit(solution)/shard_map/ppermute | solution.py:514
  69.9 0.1 backward_1_2.1
  70.0 1.3 %collective-permute-start.22 = (f32[4,32,256]{2,1,0:T(8,128)S(1)}, f32[4,32,256]{2,1,0:T(8,128)S(1)}, u32[]{:S(2)}, u32[]{:S(2)}) collective-permute-start(f32[4,32,256]{2,1,0:T(8,128)S(1)} %get-tuple-element.122), channel_id=1, source_target_pairs={{32,0},{33,1},{34,2},{35,3},{36,4},{37,5},{38,6},{39,7},{40,8},{41... | collective-permute-start | bytes 393224 | tf_op jit(solution)/shard_map/ppermute | solution.py:514
  71.3 25.6 %collective-permute-done.24.came = f32[4,32,256]{2,1,0:T(8,128)S(1)} collective-permute-done((f32[4,32,256]{2,1,0:T(8,128)S(1)}, f32[4,32,256]{2,1,0:T(8,128)S(1)}, u32[]{:S(2)}, u32[]{:S(2)}) %collective-permute-start.24) | collective-permute-done | bytes 131104 | tf_op jit(solution)/shard_map/ppermute | solution.py:514
  96.8 3.6 %backward_0_0.1 = (f32[8,12,32,256]{3,2,1,0:T(8,128)}, f32[4,32,256]{2,1,0:T(8,128)}) custom-call(f32[4,32,256]{2,1,0:T(8,128)S(1)} %collective-permute-done.24.came, bf16[8,12,256,256]{3,2,1,0:T(8,128)(2,1)S(1)} %get-tuple-element.75.refs_1_.refs_0_.inverse, f32[8,12,32,256]{3,2,1,0:T(8,128)S(1)} %get-tuple-element.110.source, ...), custom_call_target="tpu_custom_call", output_to_operand_aliasing={{0}: (5, {})} | custom-call | flops 134217728 | bytes 4194304 | tf_op jit(solution)/shard_map/backward_0_0/pallas_call | solution.py:373
  100.4 1.2 %collective-permute-done.23.came = f32[4,32,256]{2,1,0:T(8,128)S(1)} collective-permute-done((f32[4,32,256]{2,1,0:T(8,128)S(1)}, f32[4,32,256]{2,1,0:T(8,128)S(1)}, u32[]{:S(2)}, u32[]{:S(2)}) %collective-permute-start.23) | collective-permute-done | bytes 131104 | tf_op jit(solution)/shard_map/ppermute | solution.py:514
  101.7 3.6 %backward_0_1.1 = (f32[8,12,32,256]{3,2,1,0:T(8,128)}, f32[4,32,256]{2,1,0:T(8,128)}) custom-call(f32[4,32,256]{2,1,0:T(8,128)S(1)} %collective-permute-done.23.came, bf16[8,12,256,256]{3,2,1,0:T(8,128)(2,1)S(1)} %get-tuple-element.75.refs_1_.refs_0_.inverse, f32[8,12,32,256]{3,2,1,0:T(8,128)S(1)} %get-tuple-element.110.source, ...), custom_call_target="tpu_custom_call", output_to_operand_aliasing={{0}: (5, {})} | custom-call | flops 134217728 | bytes 4194304 | tf_op jit(solution)/shard_map/backward_0_1/pallas_call | solution.py:373
  105.2 3.6 %backward_0_2.1 = (f32[8,12,32,256]{3,2,1,0:T(8,128)}, f32[4,32,256]{2,1,0:T(8,128)}) custom-call(f32[4,32,256]{2,1,0:T(8,128)S(1)} %collective-permute-done.22.came, bf16[8,12,256,256]{3,2,1,0:T(8,128)(2,1)S(1)} %get-tuple-element.75.refs_1_.refs_0_.inverse, f32[8,12,32,256]{3,2,1,0:T(8,128)S(1)} %get-tuple-element.110.source, ...), custom_call_target="tpu_custom_call", output_to_operand_aliasing={{0}: (5, {})} | custom-call | flops 134217728 | bytes 4194304 | tf_op jit(solution)/shard_map/backward_0_2/pallas_call | solution.py:373
  (25 shorter events, 0.2 us)
Async XLA Ops:
  0.0 15.8 %copy-start = (f32[2,4,12,32,256]{4,3,2,1,0:T(8,128)S(1)}, f32[2,4,12,32,256]{4,3,2,1,0:T(8,128)}, u32[]{:S(2)}) copy-start(f32[2,4,12,32,256]{4,3,2,1,0:T(8,128)} %param.6) | copy-start | bytes 9437188
  2.0 13.7 %collective-permute-start.4 = (f32[4,32,256]{2,1,0:T(8,128)S(1)}, f32[4,32,256]{2,1,0:T(8,128)S(1)}, u32[]{:S(2)}, u32[]{:S(2)}) collective-permute-start(f32[4,32,256]{2,1,0:T(8,128)S(1)} %get-tuple-element.129), channel_id=1, source_target_pairs={{32,0},{64,32},{96,64},{33,1},{65,33},{97,65},{34,2},{66,34},{98,6... | collective-permute-start | bytes 393224 | tf_op jit(solution)/shard_map/ppermute | solution.py:413
  3.3 23.1 %collective-permute-start.3 = (f32[4,32,256]{2,1,0:T(8,128)S(1)}, f32[4,32,256]{2,1,0:T(8,128)S(1)}, u32[]{:S(2)}, u32[]{:S(2)}) collective-permute-start(f32[4,32,256]{2,1,0:T(8,128)S(1)} %get-tuple-element.130), channel_id=1, source_target_pairs={{32,0},{64,32},{96,64},{33,1},{65,33},{97,65},{34,2},{66,34},{98,6... | collective-permute-start | bytes 393224 | tf_op jit(solution)/shard_map/ppermute | solution.py:413
  6.0 26.0 %collective-permute-start.2 = (f32[8,2,32,256]{3,2,1,0:T(8,128)S(1)}, f32[8,2,32,256]{3,2,1,0:T(8,128)S(1)}, u32[]{:S(2)}, u32[]{:S(2)}) collective-permute-start(f32[8,2,32,256]{3,2,1,0:T(8,128)S(1)} %get-tuple-element.131), channel_id=1, source_target_pairs={{1,0},{2,1},{3,2},{4,3},{5,4},{6,5},{7,6},{8,7},{9,8},{10,9},{11,1... | collective-permute-start | bytes 1572872 | tf_op jit(solution)/shard_map/ppermute | solution.py:415
  10.2 21.8 %collective-permute-start.1 = (f32[8,2,32,256]{3,2,1,0:T(8,128)S(1)}, f32[8,2,32,256]{3,2,1,0:T(8,128)S(1)}, u32[]{:S(2)}, u32[]{:S(2)}) collective-permute-start(f32[8,2,32,256]{3,2,1,0:T(8,128)S(1)} %get-tuple-element.132), channel_id=1, source_target_pairs={{0,1},{1,2},{2,3},{3,4},{4,5},{5,6},{6,7},{7,8},{8,9},{9,10},{10,1... | collective-permute-start | bytes 1572872 | tf_op jit(solution)/shard_map/ppermute | solution.py:414
  13.2 18.8 %collective-permute-start = (f32[4,32,256]{2,1,0:T(8,128)S(1)}, f32[4,32,256]{2,1,0:T(8,128)S(1)}, u32[]{:S(2)}, u32[]{:S(2)}) collective-permute-start(f32[4,32,256]{2,1,0:T(8,128)S(1)} %pad_maximum_fusion), channel_id=1, source_target_pairs={{32,0},{64,32},{96,64},{33,1},{65,33},{97,65},{34,2},{66,34},{98,6... | collective-permute-start | bytes 393224 | tf_op jit(solution)/shard_map/ppermute | solution.py:413
  15.8 1.9 %copy-start.1 = (f32[2,4,12,32,256]{4,3,2,1,0:T(8,128)S(1)}, f32[2,4,12,32,256]{4,3,2,1,0:T(8,128)}, u32[]{:S(2)}) copy-start(f32[2,4,12,32,256]{4,3,2,1,0:T(8,128)} %param.5) | copy-start | bytes 9437188
  22.0 19.8 %collective-permute-start.7 = (f32[4,32,256]{2,1,0:T(8,128)S(1)}, f32[4,32,256]{2,1,0:T(8,128)S(1)}, u32[]{:S(2)}, u32[]{:S(2)}) collective-permute-start(f32[4,32,256]{2,1,0:T(8,128)S(1)} %get-tuple-element.80), channel_id=1, source_target_pairs={{0,32},{1,33},{2,34},{3,35},{4,36},{5,37},{6,38},{7,39},{8,40},{9,... | collective-permute-start | bytes 393224 | tf_op jit(solution)/shard_map/ppermute | solution.py:460
  30.7 11.8 %collective-permute-start.6 = (f32[4,32,256]{2,1,0:T(8,128)S(1)}, f32[4,32,256]{2,1,0:T(8,128)S(1)}, u32[]{:S(2)}, u32[]{:S(2)}) collective-permute-start(f32[4,32,256]{2,1,0:T(8,128)S(1)} %get-tuple-element.79), channel_id=1, source_target_pairs={{0,32},{1,33},{2,34},{3,35},{4,36},{5,37},{6,38},{7,39},{8,40},{9,... | collective-permute-start | bytes 393224 | tf_op jit(solution)/shard_map/ppermute | solution.py:460
  40.5 3.9 %collective-permute-start.5 = (f32[4,32,256]{2,1,0:T(8,128)S(1)}, f32[4,32,256]{2,1,0:T(8,128)S(1)}, u32[]{:S(2)}, u32[]{:S(2)}) collective-permute-start(f32[4,32,256]{2,1,0:T(8,128)S(1)} %get-tuple-element.77), channel_id=1, source_target_pairs={{0,32},{1,33},{2,34},{3,35},{4,36},{5,37},{6,38},{7,39},{8,40},{9,... | collective-permute-start | bytes 393224 | tf_op jit(solution)/shard_map/ppermute | solution.py:460
  41.8 3.2 %collective-permute-start.10 = (f32[4,32,256]{2,1,0:T(8,128)S(1)}, f32[4,32,256]{2,1,0:T(8,128)S(1)}, u32[]{:S(2)}, u32[]{:S(2)}) collective-permute-start(f32[4,32,256]{2,1,0:T(8,128)S(1)} %get-tuple-element.88), channel_id=1, source_target_pairs={{32,64},{33,65},{34,66},{35,67},{36,68},{37,69},{38,70},{39,71},{4... | collective-permute-start | bytes 393224 | tf_op jit(solution)/shard_map/ppermute | solution.py:460
  42.5 3.2 %collective-permute-start.9 = (f32[4,32,256]{2,1,0:T(8,128)S(1)}, f32[4,32,256]{2,1,0:T(8,128)S(1)}, u32[]{:S(2)}, u32[]{:S(2)}) collective-permute-start(f32[4,32,256]{2,1,0:T(8,128)S(1)} %get-tuple-element.87), channel_id=1, source_target_pairs={{32,64},{33,65},{34,66},{35,67},{36,68},{37,69},{38,70},{39,71},{4... | collective-permute-start | bytes 393224 | tf_op jit(solution)/shard_map/ppermute | solution.py:460
  44.4 2.1 %collective-permute-start.8 = (f32[4,32,256]{2,1,0:T(8,128)S(1)}, f32[4,32,256]{2,1,0:T(8,128)S(1)}, u32[]{:S(2)}, u32[]{:S(2)}) collective-permute-start(f32[4,32,256]{2,1,0:T(8,128)S(1)} %get-tuple-element.86), channel_id=1, source_target_pairs={{32,64},{33,65},{34,66},{35,67},{36,68},{37,69},{38,70},{39,71},{4... | collective-permute-start | bytes 393224 | tf_op jit(solution)/shard_map/ppermute | solution.py:460
  45.1 2.1 %collective-permute-start.13 = (f32[4,32,256]{2,1,0:T(8,128)S(1)}, f32[4,32,256]{2,1,0:T(8,128)S(1)}, u32[]{:S(2)}, u32[]{:S(2)}) collective-permute-start(f32[4,32,256]{2,1,0:T(8,128)S(1)} %get-tuple-element.96), channel_id=1, source_target_pairs={{64,96},{65,97},{66,98},{67,99},{68,100},{69,101},{70,102},{71,103... | collective-permute-start | bytes 393224 | tf_op jit(solution)/shard_map/ppermute | solution.py:460
  45.8 2.1 %collective-permute-start.12 = (f32[4,32,256]{2,1,0:T(8,128)S(1)}, f32[4,32,256]{2,1,0:T(8,128)S(1)}, u32[]{:S(2)}, u32[]{:S(2)}) collective-permute-start(f32[4,32,256]{2,1,0:T(8,128)S(1)} %get-tuple-element.95), channel_id=1, source_target_pairs={{64,96},{65,97},{66,98},{67,99},{68,100},{69,101},{70,102},{71,103... | collective-permute-start | bytes 393224 | tf_op jit(solution)/shard_map/ppermute | solution.py:460
  46.5 2.0 %collective-permute-start.11 = (f32[4,32,256]{2,1,0:T(8,128)S(1)}, f32[4,32,256]{2,1,0:T(8,128)S(1)}, u32[]{:S(2)}, u32[]{:S(2)}) collective-permute-start(f32[4,32,256]{2,1,0:T(8,128)S(1)} %get-tuple-element.94), channel_id=1, source_target_pairs={{64,96},{65,97},{66,98},{67,99},{68,100},{69,101},{70,102},{71,103... | collective-permute-start | bytes 393224 | tf_op jit(solution)/shard_map/ppermute | solution.py:460
  49.2 12.6 %collective-permute-start.14 = (f32[8,2,32,256]{3,2,1,0:T(8,128)S(1)}, f32[8,2,32,256]{3,2,1,0:T(8,128)S(1)}, u32[]{:S(2)}, u32[]{:S(2)}) collective-permute-start(f32[8,2,32,256]{3,2,1,0:T(8,128)S(1)} %get-tuple-element.103), channel_id=1, source_target_pairs={{0,1},{1,2},{2,3},{3,4},{4,5},{5,6},{6,7},{7,8},{8,9},{9,10},{10,1... | collective-permute-start | bytes 1572872 | tf_op jit(solution)/shard_map/ppermute | solution.py:486
  51.1 12.4 %collective-permute-start.15 = (f32[8,2,32,256]{3,2,1,0:T(8,128)S(1)}, f32[8,2,32,256]{3,2,1,0:T(8,128)S(1)}, u32[]{:S(2)}, u32[]{:S(2)}) collective-permute-start(f32[8,2,32,256]{3,2,1,0:T(8,128)S(1)} %get-tuple-element.104), channel_id=1, source_target_pairs={{1,0},{2,1},{3,2},{4,3},{5,4},{6,5},{7,6},{8,7},{9,8},{10,9},{11,1... | collective-permute-start | bytes 1572872 | tf_op jit(solution)/shard_map/ppermute | solution.py:487
  57.3 7.3 %collective-permute-start.18 = (f32[4,32,256]{2,1,0:T(8,128)S(1)}, f32[4,32,256]{2,1,0:T(8,128)S(1)}, u32[]{:S(2)}, u32[]{:S(2)}) collective-permute-start(f32[4,32,256]{2,1,0:T(8,128)S(1)} %get-tuple-element.112), channel_id=1, source_target_pairs={{96,64},{97,65},{98,66},{99,67},{100,68},{101,69},{102,70},{103,71... | collective-permute-start | bytes 393224 | tf_op jit(solution)/shard_map/ppermute | solution.py:514
  58.5 6.9 %collective-permute-start.17 = (f32[4,32,256]{2,1,0:T(8,128)S(1)}, f32[4,32,256]{2,1,0:T(8,128)S(1)}, u32[]{:S(2)}, u32[]{:S(2)}) collective-permute-start(f32[4,32,256]{2,1,0:T(8,128)S(1)} %get-tuple-element.111), channel_id=1, source_target_pairs={{96,64},{97,65},{98,66},{99,67},{100,68},{101,69},{102,70},{103,71... | collective-permute-start | bytes 393224 | tf_op jit(solution)/shard_map/ppermute | solution.py:514
  64.0 2.3 %collective-permute-start.16 = (f32[4,32,256]{2,1,0:T(8,128)S(1)}, f32[4,32,256]{2,1,0:T(8,128)S(1)}, u32[]{:S(2)}, u32[]{:S(2)}) collective-permute-start(f32[4,32,256]{2,1,0:T(8,128)S(1)} %get-tuple-element.109), channel_id=1, source_target_pairs={{96,64},{97,65},{98,66},{99,67},{100,68},{101,69},{102,70},{103,71... | collective-permute-start | bytes 393224 | tf_op jit(solution)/shard_map/ppermute | solution.py:514
  64.8 2.3 %collective-permute-start.21 = (f32[4,32,256]{2,1,0:T(8,128)S(1)}, f32[4,32,256]{2,1,0:T(8,128)S(1)}, u32[]{:S(2)}, u32[]{:S(2)}) collective-permute-start(f32[4,32,256]{2,1,0:T(8,128)S(1)} %get-tuple-element.118), channel_id=1, source_target_pairs={{64,32},{65,33},{66,34},{67,35},{68,36},{69,37},{70,38},{71,39},{7... | collective-permute-start | bytes 393224 | tf_op jit(solution)/shard_map/ppermute | solution.py:514
  65.6 2.9 %collective-permute-start.20 = (f32[4,32,256]{2,1,0:T(8,128)S(1)}, f32[4,32,256]{2,1,0:T(8,128)S(1)}, u32[]{:S(2)}, u32[]{:S(2)}) collective-permute-start(f32[4,32,256]{2,1,0:T(8,128)S(1)} %get-tuple-element.117), channel_id=1, source_target_pairs={{64,32},{65,33},{66,34},{67,35},{68,36},{69,37},{70,38},{71,39},{7... | collective-permute-start | bytes 393224 | tf_op jit(solution)/shard_map/ppermute | solution.py:514
  66.4 3.5 %collective-permute-start.19 = (f32[4,32,256]{2,1,0:T(8,128)S(1)}, f32[4,32,256]{2,1,0:T(8,128)S(1)}, u32[]{:S(2)}, u32[]{:S(2)}) collective-permute-start(f32[4,32,256]{2,1,0:T(8,128)S(1)} %get-tuple-element.116), channel_id=1, source_target_pairs={{64,32},{65,33},{66,34},{67,35},{68,36},{69,37},{70,38},{71,39},{7... | collective-permute-start | bytes 393224 | tf_op jit(solution)/shard_map/ppermute | solution.py:514
  67.1 29.7 %collective-permute-start.24 = (f32[4,32,256]{2,1,0:T(8,128)S(1)}, f32[4,32,256]{2,1,0:T(8,128)S(1)}, u32[]{:S(2)}, u32[]{:S(2)}) collective-permute-start(f32[4,32,256]{2,1,0:T(8,128)S(1)} %get-tuple-element.124), channel_id=1, source_target_pairs={{32,0},{33,1},{34,2},{35,3},{36,4},{37,5},{38,6},{39,7},{40,8},{41... | collective-permute-start | bytes 393224 | tf_op jit(solution)/shard_map/ppermute | solution.py:514
  68.6 33.1 %collective-permute-start.23 = (f32[4,32,256]{2,1,0:T(8,128)S(1)}, f32[4,32,256]{2,1,0:T(8,128)S(1)}, u32[]{:S(2)}, u32[]{:S(2)}) collective-permute-start(f32[4,32,256]{2,1,0:T(8,128)S(1)} %get-tuple-element.123), channel_id=1, source_target_pairs={{32,0},{33,1},{34,2},{35,3},{36,4},{37,5},{38,6},{39,7},{40,8},{41... | collective-permute-start | bytes 393224 | tf_op jit(solution)/shard_map/ppermute | solution.py:514
  70.0 35.3 %collective-permute-start.22 = (f32[4,32,256]{2,1,0:T(8,128)S(1)}, f32[4,32,256]{2,1,0:T(8,128)S(1)}, u32[]{:S(2)}, u32[]{:S(2)}) collective-permute-start(f32[4,32,256]{2,1,0:T(8,128)S(1)} %get-tuple-element.122), channel_id=1, source_target_pairs={{32,0},{33,1},{34,2},{35,3},{36,4},{37,5},{38,6},{39,7},{40,8},{41... | collective-permute-start | bytes 393224 | tf_op jit(solution)/shard_map/ppermute | solution.py:514

commit v2 on v0

v2 whole, which is shorter than its diff:
```python
import functools

import jax
import jax.numpy as jnp
from jax import lax
from jax.experimental import pallas as pl
from jax.experimental.pallas import tpu as pltpu
from jax.sharding import PartitionSpec as P

COLS = 8
LANES = 12
R = 32
BS = 256
FORWARD = ((2, 3, 4, 5), (6, 7, 8, 9), (0, 1, 10, 11))
BACKWARD = ((2, 3, 4, 5), (6, 7, 8, 9), (0, 1, 10, 11))
STRIP = 4
SIDES = ((2, -1), (3, 1), (4, -2), (5, 2))
NT = (((1,), (1,)), ((), ()))
VMEM = pltpu.VMEM
ANY = pl.ANY
HBM = pltpu.HBM

FIELD = (COLS, LANES, R, BS)
FIELD_MORE = (COLS + 1, LANES, R, BS)
EDGE = (COLS, 2, R, BS)
BLOCKS = (COLS, LANES, BS, BS)
PER = 4
COEFS = (6, COLS // PER, LANES, PER, BS)
WEIGHTS = (COLS + 1, LANES, BS)


def runs_of(lanes):
    runs = []
    for lane in lanes:
        if runs and runs[-1][0] + runs[-1][1] == lane:
            runs[-1][1] += 1
        else:
            runs.append([lane, 1])
    return [tuple(run) for run in runs]


def coef(ref, k, q, lane):
    return ref[k, q // PER, lane, pl.ds(q % PER, 1), :]


def weight(ref, q, lane):
    return ref[q, pl.ds(lane, 1), :]


def solve(xs, inverse, q, lanes):
    return [
        lax.dot_general(
            x.astype(jnp.bfloat16), inverse[q, lane], NT, preferred_element_type=jnp.float32
        )
        for x, lane in zip(xs, lanes)
    ]


def lane_copies(src, dst, q, lanes, sem):
    return [
        pltpu.make_async_copy(src.at[q, pl.ds(a, n)], dst.at[q, pl.ds(a, n)], sem.at[q])
        for a, n in runs_of(lanes)
    ]


def prep_kernel(ice, st_hbm, couple_hbm, first, edge_l, edge_r, couple, mask, sem):
    copies = [
        pltpu.make_async_copy(st_hbm.at[0], first, sem.at[0]),
        pltpu.make_async_copy(st_hbm.at[:, pl.ds(0, 2)], edge_l, sem.at[1]),
        pltpu.make_async_copy(st_hbm.at[:, pl.ds(LANES - 2, 2)], edge_r, sem.at[2]),
        pltpu.make_async_copy(couple_hbm, couple, sem.at[3]),
    ]
    for copy in copies:
        copy.start()

    def ice_weight(q, lane):
        return ice[q // PER, q % PER, lane].astype(jnp.float32)

    for q in range(COLS):
        for lane in range(LANES):
            mask[q, pl.ds(lane, 1), :] = jnp.full((1, BS), ice_weight(q, lane), jnp.float32)
    mask[COLS] = jnp.ones((LANES, BS), jnp.float32)
    copies[0].wait()
    for lane in range(LANES):
        first[lane] = weight(mask, 0, lane) * first[lane]
    copies[1].wait()
    copies[2].wait()

    def scale(q, _):
        for j in range(2):
            edge_l[q, j] = weight(mask, q, j) * edge_l[q, j]
            edge_r[q, j] = weight(mask, q, LANES - 2 + j) * edge_r[q, j]
        return 0

    lax.fori_loop(0, COLS, scale, 0)
    copies[3].wait()


def make_source(lanes, q, rs, start, couple, mask, source, halo_l=None, halo_r=None):
    for lane in lanes:
        total = rs[q, lane]
        for k, step in SIDES:
            other = lane + step
            if 0 <= other < LANES:
                factor = coef(couple, k, q, lane) * weight(mask, q, other)
                total = total + factor * start[q, other]
            elif other < 0 and halo_l is not None:
                total = total + coef(couple, k, q, lane) * halo_l[q, other + 2]
            elif other >= LANES and halo_r is not None:
                total = total + coef(couple, k, q, lane) * halo_r[q, other - LANES]
        factor = coef(couple, 1, q, lane) * weight(mask, q + 1, lane)
        source[q, lane] = total + factor * start[q + 1, lane]


def forward_chain(lanes, q, source, inverse, couple, mask, field, sent, left=None, right=None):
    xs = [source[q, lane] + coef(couple, 0, q, lane) * sent[j] for j, lane in enumerate(lanes)]
    ys = solve(xs, inverse, q, lanes)
    for j, lane in enumerate(lanes):
        value = weight(mask, q, lane) * ys[j]
        field[q + 1, lane] = value
        sent[j] = value
        if left is not None and lane < 2:
            left[q, lane] = value
        if right is not None and lane >= LANES - 2:
            right[q, lane - (LANES - 2)] = value


def first_kernel(
    inv_hbm, rs_hbm, st_hbm, couple, mask, inverse, rs, start, source, field, sent, sem_a, sem_b, sem_st
):
    lanes, later_lanes = FORWARD[0], FORWARD[1]

    def column(q):
        return lane_copies(inv_hbm, inverse, q, lanes, sem_a) + lane_copies(
            rs_hbm, rs, q, lanes, sem_a
        )

    def column_later(q):
        return lane_copies(inv_hbm, inverse, q, later_lanes, sem_b) + lane_copies(
            rs_hbm, rs, q, later_lanes, sem_b
        )

    def column_start(q):
        return lane_copies(st_hbm, start, q, range(LANES), sem_st)

    def launch(q, _):
        for copy in column(q):
            copy.start()

        @pl.when(q < COLS - 1)
        def _():
            for copy in column_start(q + 1):
                copy.start()

        return 0

    def launch_later(q, _):
        for copy in column_later(q):
            copy.start()
        return 0

    def wait_for(copies):
        for copy in copies:
            copy.wait()

    @pl.when(lax.axis_index("strip") == 0)
    def _():
        for copy in column_start(0):
            copy.start()
        lax.fori_loop(0, COLS, launch, 0)
        lax.fori_loop(0, COLS, launch_later, 0)
        for j, lane in enumerate(lanes):
            sent[j] = jnp.zeros((R, BS), jnp.float32)
        field[0] = jnp.zeros((LANES, R, BS), jnp.float32)
        wait_for(column_start(0) + column_start(1) + column(0))
        make_source(lanes, 0, rs, start, couple, mask, source)

        def step(q, _):
            later = jnp.minimum(q + 1, COLS - 2)

            @pl.when(q < COLS - 2)
            def _():
                wait_for(column_start(later + 1) + column(later))

            forward_chain(lanes, q, source, inverse, couple, mask, field, sent)
            make_source(lanes, later, rs, start, couple, mask, source)
            return 0

        lax.fori_loop(0, COLS - 1, step, 0)
        wait_for(column(COLS - 1))

        def drain(q, _):
            wait_for(column_later(q))
            return 0

        lax.fori_loop(0, COLS, drain, 0)


def tail_kernel(nxt, rs, couple, mask, inverse, *refs):
    start, source, field, sent = refs[4:]
    lanes = FORWARD[0]
    start[COLS] = nxt[...]

    @pl.when(lax.axis_index("strip") == 0)
    def _():
        make_source(lanes, COLS - 1, rs, start, couple, mask, source)
        forward_chain(lanes, COLS - 1, source, inverse, couple, mask, field, sent)


def load_kernel(inv_hbm, rs_hbm, st_hbm, couple, mask, *refs):
    inverse, rs, start, source, field, sent, sem_inv, sem_rs, sem_st = refs[5:]
    first = lax.axis_index("strip") == 0
    lanes, last_lanes = FORWARD[1], FORWARD[2]
    every = range(LANES)

    def wait_for(copies):
        for copy in copies:
            copy.wait()

    @pl.when(first)
    def _():
        def column(q):
            return lane_copies(inv_hbm, inverse, q, last_lanes, sem_inv) + lane_copies(
                rs_hbm, rs, q, last_lanes, sem_rs
            )

        def launch(q, _):
            for copy in column(q):
                copy.start()
            return 0

        lax.fori_loop(0, COLS, launch, 0)
        for j, lane in enumerate(lanes):
            sent[j] = jnp.zeros((R, BS), jnp.float32)
        make_source(lanes, 0, rs, start, couple, mask, source)

        def step(q, _):
            forward_chain(lanes, q, source, inverse, couple, mask, field, sent)
            make_source(
                lanes, jnp.minimum(q + 1, COLS - 1), rs, start, couple, mask, source
            )
            return 0

        lax.fori_loop(0, COLS, step, 0)

        def drain(q, _):
            wait_for(column(q))
            return 0

        lax.fori_loop(0, COLS, drain, 0)

    @pl.when(jnp.logical_not(first))
    def _():
        def launch(q, _):
            for copy in (
                lane_copies(st_hbm, start, q, every, sem_st)
                + lane_copies(rs_hbm, rs, q, every, sem_rs)
                + lane_copies(inv_hbm, inverse, q, every, sem_inv)
            ):
                copy.start()
            return 0

        lax.fori_loop(0, COLS, launch, 0)
        wait_for(lane_copies(st_hbm, start, 0, every, sem_st))

        def step(q, _):
            wait_for(lane_copies(rs_hbm, rs, q, every, sem_rs))

            @pl.when(q < COLS - 1)
            def _():
                wait_for(lane_copies(st_hbm, start, q + 1, every, sem_st))

            make_source(every, q, rs, start, couple, mask, source)
            return 0

        lax.fori_loop(0, COLS, step, 0)

        def drain(q, _):
            wait_for(lane_copies(inv_hbm, inverse, q, every, sem_inv))
            return 0

        lax.fori_loop(0, COLS, drain, 0)


def edge_kernel(halo_l, halo_r, inverse, rs, start, couple, mask, *refs):
    source, field, left, right, sent = refs[2:]
    lanes = FORWARD[2]
    first = lax.axis_index("strip") == 0

    @pl.when(first)
    def _():
        for j in range(len(lanes)):
            sent[j] = jnp.zeros((R, BS), jnp.float32)

        def source_of(q):
            make_source(lanes, q, rs, start, couple, mask, source, halo_l, halo_r)

        source_of(0)

        def step(q, _):
            forward_chain(lanes, q, source, inverse, couple, mask, field, sent, left, right)
            source_of(jnp.minimum(q + 1, COLS - 1))
            return 0

        lax.fori_loop(0, COLS, step, 0)

    @pl.when(jnp.logical_not(first))
    def _():
        def step(q, _):
            for lane in lanes:
                total = source[q, lane]
                for k, move in SIDES:
                    other = lane + move
                    if other < 0:
                        total = total + coef(couple, k, q, lane) * halo_l[q, other + 2]
                    elif other >= LANES:
                        total = total + coef(couple, k, q, lane) * halo_r[q, other - LANES]
                source[q, lane] = total
            return 0

        lax.fori_loop(0, COLS, step, 0)


def forward_kernel(chunk, stage, came, inverse, source, couple, mask, *refs):
    lanes = FORWARD[chunk]
    left = right = None
    if chunk == 2:
        field, left, right, sent = refs[3:]
    else:
        field, sent = refs[1:]

    @pl.when(lax.axis_index("strip") == stage)
    def _():
        for j, lane in enumerate(lanes):
            sent[j] = came[j]
            field[0, lane] = came[j]

        def step(q, _):
            forward_chain(lanes, q, source, inverse, couple, mask, field, sent, left, right)
            return 0

        lax.fori_loop(0, COLS, step, 0)


def backward_chain(lanes, q, source, inverse, couple, mask, result, sent):
    xs = [source[q, lane] + coef(couple, 1, q, lane) * sent[j] for j, lane in enumerate(lanes)]
    ys = solve(xs, inverse, q, lanes)
    for j, lane in enumerate(lanes):
        value = weight(mask, q, lane) * ys[j]
        result[q, lane] = value
        sent[j] = value


def backward_sweep(chunk, inverse, source, couple, mask, result, out, sent, sem, sem_own, beside):
    lanes = BACKWARD[chunk]
    last = chunk == len(BACKWARD) - 1

    def before(q):
        return lane_copies(result, out, q, BACKWARD[chunk - 1], sem) if chunk > 0 else []

    def own(q):
        return lane_copies(result, out, q, lanes, sem_own) if last else []

    def launch(q, _):
        for copy in before(q):
            copy.start()
        return 0

    lax.fori_loop(0, COLS, launch, 0)

    def step(i, _):
        q = COLS - 1 - i
        backward_chain(lanes, q, source, inverse, couple, mask, result, sent)
        for copy in own(q):
            copy.start()
        if beside is not None:
            beside(jnp.maximum(q - 1, 0))
        return 0

    lax.fori_loop(0, COLS, step, 0)

    def drain(q, _):
        for copy in before(q) + own(q):
            copy.wait()
        return 0

    lax.fori_loop(0, COLS, drain, 0)


def last_kernel(chunk, inverse, rs, field, couple, mask, halo_l, halo_r, *refs):
    lanes = BACKWARD[chunk]
    source, result, out, sent, sem, sem_own = refs[-6:]
    active = lax.axis_index("strip") == STRIP - 1

    def near(q, lane):
        if lane < 0:
            return halo_l[q, lane + 2]
        if lane >= LANES:
            return halo_r[q, lane - LANES]
        return field[q + 1, lane]

    def source_of(q):
        for lane in lanes:
            total = rs[q, lane] + coef(couple, 0, q, lane) * field[q, lane]
            for k, step in SIDES:
                total = total + coef(couple, k, q, lane) * near(q, lane + step)
            source[q, lane] = total

    @pl.when(active)
    def _():
        for j in range(len(lanes)):
            sent[j] = jnp.zeros((R, BS), jnp.float32)
        source_of(COLS - 1)
        backward_sweep(
            chunk, inverse, source, couple, mask, result, out, sent, sem, sem_own, source_of
        )

    @pl.when(jnp.logical_not(active))
    def _():
        def step(q, _):
            source_of(q)
            return 0

        lax.fori_loop(0, COLS, step, 0)


def backward_kernel(chunk, stage, came, inverse, source, couple, mask, *refs):
    result, out, sent, sem, sem_own = refs[2:]

    @pl.when(lax.axis_index("strip") == stage)
    def _():
        sent[...] = came[...]
        backward_sweep(
            chunk, inverse, source, couple, mask, result, out, sent, sem, sem_own, None
        )


def vmem(shape, dtype=jnp.float32):
    return VMEM(shape, dtype)


def run(kernel, name, operands, outs, scratch, aliases=None):
    arrays = [
        pltpu.with_memory_space_constraint(a, space) if space in (VMEM, HBM) else a
        for a, space in operands
    ]
    return pl.pallas_call(
        kernel,
        name=name,
        out_shape=[o for o, _ in outs],
        in_specs=[pl.BlockSpec(memory_space=space) for _, space in operands],
        out_specs=[pl.BlockSpec(memory_space=space) for _, space in outs],
        scratch_shapes=scratch,
        input_output_aliases=aliases or {},
        compiler_params=pltpu.CompilerParams(vmem_limit_bytes=8 * 2**20),
        cost_estimate=pl.CostEstimate(flops=2**26, bytes_accessed=2**21, transcendentals=0),
    )(*arrays)


def on_device(right_side, starting_iterate, inverse_diagonal_blocks, couple, ice_mask):
    rs_hbm = right_side.reshape(FIELD)
    st_hbm = starting_iterate.reshape(FIELD)
    inv_hbm = inverse_diagonal_blocks.reshape(BLOCKS)
    tiles = lax.axis_size("tile")
    to_right = [(i, i + 1) for i in range(tiles - 1)]
    to_left = [(i + 1, i) for i in range(tiles - 1)]
    to_back = [(i + 1, i) for i in range(STRIP - 1)]
    dma = pltpu.SemaphoreType.DMA

    def inside(*arrays):
        return [(a, VMEM) for a in arrays]

    def made(*shapes):
        return [(vmem(shape), VMEM) for shape in shapes]

    def piece(lanes):
        return (len(lanes), R, BS)

    first, edge_l, edge_r, coefs, mask = run(
        prep_kernel,
        "prep",
        [(ice_mask, pltpu.SMEM), (st_hbm, HBM), (couple.transpose(0, 1, 3, 2, 4), HBM)],
        made((LANES, R, BS), EDGE, EDGE, COEFS, WEIGHTS),
        [dma((4,))],
    )
    nxt = lax.ppermute(first, "strip", to_back)
    start_l = lax.ppermute(edge_r, "tile", to_right)
    start_r = lax.ppermute(edge_l, "tile", to_left)

    inverse, rs, start, source, field, sent = run(
        first_kernel,
        "first",
        [(inv_hbm, HBM), (rs_hbm, HBM), (st_hbm, HBM)] + inside(coefs, mask),
        [(vmem(BLOCKS, jnp.bfloat16), VMEM)]
        + made(FIELD, FIELD_MORE, FIELD, FIELD_MORE, piece(FORWARD[0])),
        [dma((COLS,)), dma((COLS,)), dma((COLS,))],
    )
    start, source, field, sent = run(
        tail_kernel,
        "tail",
        inside(nxt, rs, coefs, mask, inverse, start, source, field, sent),
        made(FIELD_MORE, FIELD, FIELD_MORE, piece(FORWARD[0])),
        [],
        {5: 0, 6: 1, 7: 2, 8: 3},
    )
    sents = {(0, 0): sent}
    inverse, rs, start, source, field, sents[0, 1] = run(
        load_kernel,
        "load",
        [(inv_hbm, HBM), (rs_hbm, HBM), (st_hbm, HBM)]
        + inside(coefs, mask, inverse, rs, start, source, field),
        [(vmem(BLOCKS, jnp.bfloat16), VMEM)]
        + made(FIELD, FIELD_MORE, FIELD, FIELD_MORE, piece(FORWARD[1])),
        [dma((COLS,)), dma((COLS,)), dma((COLS,))],
        {5: 0, 6: 1, 7: 2, 8: 3, 9: 4},
    )
    source, field, left, right, sents[0, 2] = run(
        edge_kernel,
        "edge",
        inside(start_l, start_r, inverse, rs, start, coefs, mask, source, field),
        made(FIELD, FIELD_MORE, EDGE, EDGE, piece(FORWARD[2])),
        [],
        {7: 0, 8: 1},
    )

    for stage in range(1, STRIP):
        for chunk, lanes in enumerate(FORWARD):
            came = lax.ppermute(sents[stage - 1, chunk], "strip", [(stage - 1, stage)])
            sending = stage + 1 < STRIP
            operands = inside(came, inverse, source, coefs, mask, field)
            outs = made(FIELD_MORE)
            aliases = {5: 0}
            if chunk == 2:
                operands += inside(left, right)
                outs += made(EDGE, EDGE)
                aliases |= {6: 1, 7: 2}
            got = run(
                functools.partial(forward_kernel, chunk, stage),
                f"forward_{stage}_{chunk}",
                operands,
                outs + (made(piece(lanes)) if sending else []),
                [] if sending else [vmem(piece(lanes))],
                aliases,
            )
            field = got[0]
            if chunk == 2:
                left, right = got[1:3]
            if sending:
                sents[stage, chunk] = got[-1]

    halo_l = lax.ppermute(right, "tile", to_right)
    halo_r = lax.ppermute(left, "tile", to_left)

    out_shape = [(jax.ShapeDtypeStruct(FIELD, jnp.float32), HBM)]
    sems = [dma((COLS,)), dma((COLS,))]
    result = out = None
    for chunk, lanes in enumerate(BACKWARD):
        sides = inside(halo_l, halo_r) if min(lanes) < 2 or max(lanes) >= LANES - 2 else []
        operands = inside(inverse, rs, field, coefs, mask) + sides + inside(source)
        base = len(operands) - 1
        aliases = {base: 0}
        kernel = functools.partial(last_kernel, chunk)
        if not sides:
            kernel = functools.partial(without_halos, kernel)
        if chunk > 0:
            operands += inside(result) + [(out, HBM)]
            aliases |= {base + 1: 1, base + 2: 2}
        source, result, out, sents[STRIP - 1, chunk] = run(
            kernel,
            f"last_{chunk}",
            operands,
            made(FIELD, FIELD) + out_shape + made(piece(lanes)),
            sems,
            aliases,
        )

    for stage in range(STRIP - 2, -1, -1):
        for chunk, lanes in enumerate(BACKWARD):
            came = lax.ppermute(sents[stage + 1, chunk], "strip", [(stage + 1, stage)])
            sending = stage > 0
            got = run(
                functools.partial(backward_kernel, chunk, stage),
                f"backward_{stage}_{chunk}",
                inside(came, inverse, source, coefs, mask, result) + [(out, HBM)],
                made(FIELD) + out_shape + (made(piece(lanes)) if sending else []),
                ([] if sending else [vmem(piece(lanes))]) + sems,
                {5: 0, 6: 1},
            )
            result, out = got[:2]
            if sending:
                sents[stage, chunk] = got[2]
    return out.reshape(right_side.shape)


def without_halos(kernel, inverse, rs, field, couple, mask, *refs):
    kernel(inverse, rs, field, couple, mask, None, None, *refs)


def solution(mesh):
    return jax.shard_map(
        on_device,
        mesh=mesh,
        in_specs=(
            P("strip", None, "tile", None, None),
            P("strip", None, "tile", None, None),
            P("strip", None, "tile", None, None),
            P(None, "strip", None, "tile", None),
            P("strip", None, "tile"),
        ),
        out_specs=P("strip", None, "tile", None, None),
        check_vma=False,
    )
```

time: 242 us -> 104 us (0.43)
  matrix products: 119 us -> 0 us
  Pallas kernels: 0 us -> 23.2 us
  other arithmetic: 13.9 us -> 0 us
  waiting for transfers between devices: 52 us -> 40.6 us
  local copies, waits for them, and re-layouts: 10.4 us -> 0.69 us
  starting transfers between devices: 43.3 us -> 38.3 us
    dot_general x40 -> x0, matrix products: 119 us -> none  [column_pass(): jnp.einsum('lij,lrj->lri', inverse[column_index], rounded, preferred_elem...]
    pallas_call x0 -> x26, Pallas kernels: none -> 23.2 us  [run(): pl.pallas_call(kernel, name=name, out_shape=[o for o, _ in outs], in_spec...]
    ppermute x12 -> x23, waiting for transfers between devices: 52 us -> 40.6 us  [the longest x9 31.1 us: on_device(): came = lax.ppermute(sents[stage + 1, chunk], 'strip', [(stage + 1, stage)])]
    add x4 -> x0, other arithmetic: 9.8 us -> none  [the longest x2 3.7 us: column_pass(): source[column_index] + up_coef[column_index] * lagged[column_index]]
    unnamed x148 -> x2, local copies, waits for them, and re-layouts: 7.81 us -> 0.69 us
    ppermute x12 -> x23, starting transfers between devices: 43.3 us -> 38.3 us  [the longest x9 13.7 us: on_device(): came = lax.ppermute(sents[stage - 1, chunk], 'strip', [(stage - 1, stage)])]
    mul x3 -> x0, other arithmetic: 3.42 us -> none  [the longest x1 2.22 us: on_device(): initial = ice_weight * starting_iterate]
  transfers between devices with their start and end apart: 12 -> 23, of which waited for: 7 -> 7; matrix products, arithmetic and copies ran while one was open for 15% -> 0% of each run, Pallas kernels for 0% -> 17%
where the time goes in v2:
time: 104 us; the launch traced here: 103 us
  waiting for transfers between devices  40.6 us (39%)
  starting transfers between devices  38.3 us (37%)
  Pallas kernels  23.2 us (22%)
    ppermute x9, waiting for transfers between devices, on_device(): came = lax.ppermute(sents[stage + 1, chunk], 'strip', [(stage + 1, stage)])  31.1 us
    pallas_call x26, Pallas kernels, run(): pl.pallas_call(kernel, name=name, out_shape=[o for o, _ in outs], in_spec...  23.2 us
    ppermute x9, starting transfers between devices, on_device(): came = lax.ppermute(sents[stage - 1, chunk], 'strip', [(stage - 1, stage)])  13.7 us
    ppermute x9, starting transfers between devices, on_device(): came = lax.ppermute(sents[stage + 1, chunk], 'strip', [(stage + 1, stage)])  7.89 us
    ppermute x1, starting transfers between devices, on_device(): start_r = lax.ppermute(edge_l, 'tile', to_left)  5.75 us
    ppermute x1, starting transfers between devices, on_device(): halo_r = lax.ppermute(left, 'tile', to_left)  5.75 us
    ppermute x1, waiting for transfers between devices, on_device(): nxt = lax.ppermute(first, 'strip', to_back)  4.36 us
    ppermute x1, waiting for transfers between devices, on_device(): halo_l = lax.ppermute(right, 'tile', to_right)  2.33 us
  transfers between devices with their start and end apart: 23, of which 7 were waited for; matrix products, arithmetic and copies ran while one was open for 0% of the time, Pallas kernels for 17%

profile of v2, /device:TPU:96, one launch (start us, length us, event | category | flops | bytes accessed | tf_op | source)
XLA Modules:
  0.0 103.2 jit_solution(13208148089415363238)
XLA Ops:
  0.0 0.7 copy-done
  0.7 2.1 %prep.1 = (f32[12,32,256]{2,1,0:T(8,128)S(1)}, f32[8,2,32,256]{3,2,1,0:T(8,128)S(1)}, f32[8,2,32,256]{3,2,1,0:T(8,128)S(1)}, f32[6,2,12,4,256]{4,3,2,1,0:T(4,128)S(1)}, f32[9,12,256]{2,1,0:T(8,128)S(1)}) custom-call(s32[2,4,12]{2,1,0:T(4,128)S(1)} %copy-done, f32[8,12,32,256]{3,2,1,0:T(8,128)} %bitcast.7, f32[6,2,12,4,256]{4,3,2,1,0:T(4,128)} %bitcast.12), custom_call_target="tpu_custom_call" | custom-call | flops 67108864 | bytes 2097152 | tf_op jit(solution)/shard_map/prep/pallas_call | solution.py:447
  2.8 1.9 %collective-permute-start.1 = (f32[8,2,32,256]{3,2,1,0:T(8,128)S(1)}, f32[8,2,32,256]{3,2,1,0:T(8,128)S(1)}, u32[]{:S(2)}, u32[]{:S(2)}) collective-permute-start(f32[8,2,32,256]{3,2,1,0:T(8,128)S(1)} %get-tuple-element.99), channel_id=1, source_target_pairs={{0,1},{1,2},{2,3},{3,4},{4,5},{5,6},{6,7},{7,8},{8,9},{9,10},{10,1... | collective-permute-start | bytes 1572872 | tf_op jit(solution)/shard_map/ppermute | solution.py:487
  4.8 5.8 %collective-permute-start.2 = (f32[8,2,32,256]{3,2,1,0:T(8,128)S(1)}, f32[8,2,32,256]{3,2,1,0:T(8,128)S(1)}, u32[]{:S(2)}, u32[]{:S(2)}) collective-permute-start(f32[8,2,32,256]{3,2,1,0:T(8,128)S(1)} %get-tuple-element.100), channel_id=1, source_target_pairs={{1,0},{2,1},{3,2},{4,3},{5,4},{6,5},{7,6},{8,7},{9,8},{10,9},{11,1... | collective-permute-start | bytes 1572872 | tf_op jit(solution)/shard_map/ppermute | solution.py:488
  10.5 1.3 %collective-permute-start = (f32[12,32,256]{2,1,0:T(8,128)S(1)}, f32[12,32,256]{2,1,0:T(8,128)S(1)}, u32[]{:S(2)}, u32[]{:S(2)}) collective-permute-start(f32[12,32,256]{2,1,0:T(8,128)S(1)} %get-tuple-element.89), channel_id=1, source_target_pairs={{32,0},{64,32},{96,64},{33,1},{65,33},{97,65},{34,2},{66,34},{98,6... | collective-permute-start | bytes 1179656 | tf_op jit(solution)/shard_map/ppermute | solution.py:486
  11.8 5.1 %first.1 = (bf16[8,12,256,256]{3,2,1,0:T(8,128)(2,1)S(1)}, f32[8,12,32,256]{3,2,1,0:T(8,128)S(1)}, f32[9,12,32,256]{3,2,1,0:T(8,128)S(1)}, f32[8,12,32,256]{3,2,...) custom-call(bf16[8,12,256,256]{3,2,1,0:T(8,128)(2,1)} %bitcast.5, ...), custom_call_target="tpu_custom_call" | custom-call | flops 67108864 | bytes 2097152 | tf_op jit(solution)/shard_map/first/pallas_call | solution.py:447
  16.9 4.4 %collective-permute-done.nxt = f32[12,32,256]{2,1,0:T(8,128)S(1)} collective-permute-done((f32[12,32,256]{2,1,0:T(8,128)S(1)}, f32[12,32,256]{2,1,0:T(8,128)S(1)}, u32[]{:S(2)}, u32[]{:S(2)}) %collective-permute-start) | collective-permute-done | bytes 393248 | tf_op jit(solution)/shard_map/ppermute | solution.py:486
  21.3 0.3 tail.1
  21.6 3.1 %collective-permute-start.5 = (f32[4,32,256]{2,1,0:T(8,128)S(1)}, f32[4,32,256]{2,1,0:T(8,128)S(1)}, u32[]{:S(2)}, u32[]{:S(2)}) collective-permute-start(f32[4,32,256]{2,1,0:T(8,128)S(1)} %get-tuple-element.107), channel_id=1, source_target_pairs={{0,32},{1,33},{2,34},{3,35},{4,36},{5,37},{6,38},{7,39},{8,40},{9,... | collective-permute-start | bytes 393224 | tf_op jit(solution)/shard_map/ppermute | solution.py:528
  24.7 2.7 %load.1 = (bf16[8,12,256,256]{3,2,1,0:T(8,128)(2,1)S(1)}, f32[8,12,32,256]{3,2,1,0:T(8,128)S(1)}, f32[9,12,32,256]{3,2,1,0:T(8,128)S(1)}, f32[8,12,32,256]{3,2,1...) custom-call(bf16[8,12,256,256]{3,2,1,0:T(8,128)(2,1)} %bitcast.6, ...), custom_call_target="tpu_custom_call", output_to_operand_aliasing={{0}: (5, {}), {1}: (6, {}), {2}: (7, {}), {3}: (8, {}), {4}... | custom-call | flops 67108864 | bytes 2097152 | tf_op jit(solution)/shard_map/load/pallas_call | solution.py:447
  27.4 5.3 %collective-permute-start.4 = (f32[4,32,256]{2,1,0:T(8,128)S(1)}, f32[4,32,256]{2,1,0:T(8,128)S(1)}, u32[]{:S(2)}, u32[]{:S(2)}) collective-permute-start(f32[4,32,256]{2,1,0:T(8,128)S(1)} %get-tuple-element.106), channel_id=1, source_target_pairs={{0,32},{1,33},{2,34},{3,35},{4,36},{5,37},{6,38},{7,39},{8,40},{9,... | collective-permute-start | bytes 393224 | tf_op jit(solution)/shard_map/ppermute | solution.py:528
  32.7 0.0 collective-permute-done.1.halo_l
  32.7 0.0 collective-permute-done.2.halo_r
  32.7 2.3 %edge.1 = (f32[8,12,32,256]{3,2,1,0:T(8,128)S(1)}, f32[9,12,32,256]{3,2,1,0:T(8,128)S(1)}, f32[8,2,32,256]{3,2,1,0:T(8,128)S(1)}, f32[8,2,32,256]{3,2,1,0:T(8,128)S(1)}, f32[4,32,256]{2,1,0:T(8,128)S(1)}) custom-call(f32[8,2,32,256]{3,2,1,0:T(8,128)S(1)} %collective-permute-done.1.halo_l, ...), custom_call_target="tpu_custom_call", output_to_operand_aliasing={{0}: (7, {}), {1}: (8, {})} | custom-call | flops 67108864 | bytes 2097152 | tf_op jit(solution)/shard_map/edge/pallas_call | solution.py:447
  35.0 1.3 %collective-permute-start.3 = (f32[4,32,256]{2,1,0:T(8,128)S(1)}, f32[4,32,256]{2,1,0:T(8,128)S(1)}, u32[]{:S(2)}, u32[]{:S(2)}) collective-permute-start(f32[4,32,256]{2,1,0:T(8,128)S(1)} %get-tuple-element.104), channel_id=1, source_target_pairs={{0,32},{1,33},{2,34},{3,35},{4,36},{5,37},{6,38},{7,39},{8,40},{9,... | collective-permute-start | bytes 393224 | tf_op jit(solution)/shard_map/ppermute | solution.py:528
  36.3 0.0 collective-permute-done.5.came
  36.4 0.7 collective-permute-start.8
  37.1 0.0 collective-permute-done.4.came
  37.1 0.7 collective-permute-start.7
  37.8 1.1 %collective-permute-done.3.came = f32[4,32,256]{2,1,0:T(8,128)S(1)} collective-permute-done((f32[4,32,256]{2,1,0:T(8,128)S(1)}, f32[4,32,256]{2,1,0:T(8,128)S(1)}, u32[]{:S(2)}, u32[]{:S(2)}) %collective-permute-start.3) | collective-permute-done | bytes 131104 | tf_op jit(solution)/shard_map/ppermute | solution.py:528
  38.8 0.7 collective-permute-start.6
  39.5 0.0 collective-permute-done.8.came
  39.5 0.7 collective-permute-start.11
  40.2 0.0 collective-permute-done.7.came
  40.3 0.7 collective-permute-start.10
  40.9 0.0 collective-permute-done.6.came
  41.0 0.7 collective-permute-start.9
  41.7 0.0 collective-permute-done.11.came
  41.7 0.0 collective-permute-done.10.came
  41.7 0.0 collective-permute-done.9.came
  41.8 1.9 %collective-permute-start.12 = (f32[8,2,32,256]{3,2,1,0:T(8,128)S(1)}, f32[8,2,32,256]{3,2,1,0:T(8,128)S(1)}, u32[]{:S(2)}, u32[]{:S(2)}) collective-permute-start(f32[8,2,32,256]{3,2,1,0:T(8,128)S(1)} %get-tuple-element.128), channel_id=1, source_target_pairs={{0,1},{1,2},{2,3},{3,4},{4,5},{5,6},{6,7},{7,8},{8,9},{9,10},{10,1... | collective-permute-start | bytes 1572872 | tf_op jit(solution)/shard_map/ppermute | solution.py:551
  43.7 5.8 %collective-permute-start.13 = (f32[8,2,32,256]{3,2,1,0:T(8,128)S(1)}, f32[8,2,32,256]{3,2,1,0:T(8,128)S(1)}, u32[]{:S(2)}, u32[]{:S(2)}) collective-permute-start(f32[8,2,32,256]{3,2,1,0:T(8,128)S(1)} %get-tuple-element.129), channel_id=1, source_target_pairs={{1,0},{2,1},{3,2},{4,3},{5,4},{6,5},{7,6},{8,7},{9,8},{10,9},{11,1... | collective-permute-start | bytes 1572872 | tf_op jit(solution)/shard_map/ppermute | solution.py:552
  49.4 0.6 last_0.1
  50.1 0.7 collective-permute-start.16
  50.7 0.6 last_1.1
  51.4 0.7 collective-permute-start.15
  52.0 2.3 %collective-permute-done.12.halo_l = f32[8,2,32,256]{3,2,1,0:T(8,128)S(1)} collective-permute-done((f32[8,2,32,256]{3,2,1,0:T(8,128)S(1)}, f32[8,2,32,256]{3,2,1,0:T(8,128)S(1)}, u32[]{:S(2)}, u32[]{:S(2)}) %collective-permute-start.12) | collective-permute-done | bytes 524320 | tf_op jit(solution)/shard_map/ppermute | solution.py:551
  54.4 1.8 %collective-permute-done.13.halo_r = f32[8,2,32,256]{3,2,1,0:T(8,128)S(1)} collective-permute-done((f32[8,2,32,256]{3,2,1,0:T(8,128)S(1)}, f32[8,2,32,256]{3,2,1,0:T(8,128)S(1)}, u32[]{:S(2)}, u32[]{:S(2)}) %collective-permute-start.13) | collective-permute-done | bytes 524320 | tf_op jit(solution)/shard_map/ppermute | solution.py:552
  56.1 0.6 last_2.1
  56.7 0.7 collective-permute-start.14
  57.4 0.0 collective-permute-done.16.came
  57.4 0.2 backward_2_0.1
  57.6 0.7 collective-permute-start.19
  58.3 0.0 collective-permute-done.15.came
  58.3 0.2 backward_2_1.1
  58.4 0.7 collective-permute-start.18
  59.1 0.0 collective-permute-done.14.came
  59.1 0.2 backward_2_2.1
  59.3 0.7 collective-permute-start.17
  60.0 0.0 collective-permute-done.19.came
  60.0 0.2 backward_1_0.1
  60.2 1.3 %collective-permute-start.22 = (f32[4,32,256]{2,1,0:T(8,128)S(1)}, f32[4,32,256]{2,1,0:T(8,128)S(1)}, u32[]{:S(2)}, u32[]{:S(2)}) collective-permute-start(f32[4,32,256]{2,1,0:T(8,128)S(1)} %get-tuple-element.157), channel_id=1, source_target_pairs={{32,0},{33,1},{34,2},{35,3},{36,4},{37,5},{38,6},{39,7},{40,8},{41... | collective-permute-start | bytes 393224 | tf_op jit(solution)/shard_map/ppermute | solution.py:579
  61.5 0.0 collective-permute-done.18.came
  61.5 0.2 backward_1_1.1
  61.6 1.3 %collective-permute-start.21 = (f32[4,32,256]{2,1,0:T(8,128)S(1)}, f32[4,32,256]{2,1,0:T(8,128)S(1)}, u32[]{:S(2)}, u32[]{:S(2)}) collective-permute-start(f32[4,32,256]{2,1,0:T(8,128)S(1)} %get-tuple-element.156), channel_id=1, source_target_pairs={{32,0},{33,1},{34,2},{35,3},{36,4},{37,5},{38,6},{39,7},{40,8},{41... | collective-permute-start | bytes 393224 | tf_op jit(solution)/shard_map/ppermute | solution.py:579
  62.9 0.0 collective-permute-done.17.came
  62.9 0.2 backward_1_2.1
  63.1 1.3 %collective-permute-start.20 = (f32[4,32,256]{2,1,0:T(8,128)S(1)}, f32[4,32,256]{2,1,0:T(8,128)S(1)}, u32[]{:S(2)}, u32[]{:S(2)}) collective-permute-start(f32[4,32,256]{2,1,0:T(8,128)S(1)} %get-tuple-element.155), channel_id=1, source_target_pairs={{32,0},{33,1},{34,2},{35,3},{36,4},{37,5},{38,6},{39,7},{40,8},{41... | collective-permute-start | bytes 393224 | tf_op jit(solution)/shard_map/ppermute | solution.py:579
  64.4 27.7 %collective-permute-done.22.came = f32[4,32,256]{2,1,0:T(8,128)S(1)} collective-permute-done((f32[4,32,256]{2,1,0:T(8,128)S(1)}, f32[4,32,256]{2,1,0:T(8,128)S(1)}, u32[]{:S(2)}, u32[]{:S(2)}) %collective-permute-start.22) | collective-permute-done | bytes 131104 | tf_op jit(solution)/shard_map/ppermute | solution.py:579
  92.1 2.3 %backward_0_0.1 = (f32[8,12,32,256]{3,2,1,0:T(8,128)S(1)}, f32[8,12,32,256]{3,2,1,0:T(8,128)}) custom-call(f32[4,32,256]{2,1,0:T(8,128)S(1)} %collective-permute-done.22.came, bf16[8,12,256,256]{3,2,1,0:T(8,128)(2,1)S(1)} %get-tuple-element.97.inverse, ...), custom_call_target="tpu_custom_call", output_to_operand_aliasing={{0}: (5, {}), {1}: (6, {})} | custom-call | flops 67108864 | bytes 2097152 | tf_op jit(solution)/shard_map/backward_0_0/pallas_call | solution.py:447
  94.4 2.7 %collective-permute-done.21.came = f32[4,32,256]{2,1,0:T(8,128)S(1)} collective-permute-done((f32[4,32,256]{2,1,0:T(8,128)S(1)}, f32[4,32,256]{2,1,0:T(8,128)S(1)}, u32[]{:S(2)}, u32[]{:S(2)}) %collective-permute-start.21) | collective-permute-done | bytes 131104 | tf_op jit(solution)/shard_map/ppermute | solution.py:579
  97.1 2.4 %backward_0_1.1 = (f32[8,12,32,256]{3,2,1,0:T(8,128)S(1)}, f32[8,12,32,256]{3,2,1,0:T(8,128)}) custom-call(f32[4,32,256]{2,1,0:T(8,128)S(1)} %collective-permute-done.21.came, bf16[8,12,256,256]{3,2,1,0:T(8,128)(2,1)S(1)} %get-tuple-element.97.inverse, ...), custom_call_target="tpu_custom_call", output_to_operand_aliasing={{0}: (5, {}), {1}: (6, {})} | custom-call | flops 67108864 | bytes 2097152 | tf_op jit(solution)/shard_map/backward_0_1/pallas_call | solution.py:447
  99.5 0.6 collective-permute-done.20.came
  100.2 3.0 %backward_0_2.1 = (f32[8,12,32,256]{3,2,1,0:T(8,128)S(1)}, f32[8,12,32,256]{3,2,1,0:T(8,128)}) custom-call(f32[4,32,256]{2,1,0:T(8,128)S(1)} %collective-permute-done.20.came, bf16[8,12,256,256]{3,2,1,0:T(8,128)(2,1)S(1)} %get-tuple-element.97.inverse, ...), custom_call_target="tpu_custom_call", output_to_operand_aliasing={{0}: (5, {}), {1}: (6, {})} | custom-call | flops 67108864 | bytes 2097152 | tf_op jit(solution)/shard_map/backward_0_2/pallas_call | solution.py:447
  (10 shorter events, 0.1 us)
Async XLA Ops:
  0.0 0.7 copy-start
  2.8 29.9 %collective-permute-start.1 = (f32[8,2,32,256]{3,2,1,0:T(8,128)S(1)}, f32[8,2,32,256]{3,2,1,0:T(8,128)S(1)}, u32[]{:S(2)}, u32[]{:S(2)}) collective-permute-start(f32[8,2,32,256]{3,2,1,0:T(8,128)S(1)} %get-tuple-element.99), channel_id=1, source_target_pairs={{0,1},{1,2},{2,3},{3,4},{4,5},{5,6},{6,7},{7,8},{8,9},{9,10},{10,1... | collective-permute-start | bytes 1572872 | tf_op jit(solution)/shard_map/ppermute | solution.py:487
  4.8 28.0 %collective-permute-start.2 = (f32[8,2,32,256]{3,2,1,0:T(8,128)S(1)}, f32[8,2,32,256]{3,2,1,0:T(8,128)S(1)}, u32[]{:S(2)}, u32[]{:S(2)}) collective-permute-start(f32[8,2,32,256]{3,2,1,0:T(8,128)S(1)} %get-tuple-element.100), channel_id=1, source_target_pairs={{1,0},{2,1},{3,2},{4,3},{5,4},{6,5},{7,6},{8,7},{9,8},{10,9},{11,1... | collective-permute-start | bytes 1572872 | tf_op jit(solution)/shard_map/ppermute | solution.py:488
  10.5 10.8 %collective-permute-start = (f32[12,32,256]{2,1,0:T(8,128)S(1)}, f32[12,32,256]{2,1,0:T(8,128)S(1)}, u32[]{:S(2)}, u32[]{:S(2)}) collective-permute-start(f32[12,32,256]{2,1,0:T(8,128)S(1)} %get-tuple-element.89), channel_id=1, source_target_pairs={{32,0},{64,32},{96,64},{33,1},{65,33},{97,65},{34,2},{66,34},{98,6... | collective-permute-start | bytes 1179656 | tf_op jit(solution)/shard_map/ppermute | solution.py:486
  21.6 14.8 %collective-permute-start.5 = (f32[4,32,256]{2,1,0:T(8,128)S(1)}, f32[4,32,256]{2,1,0:T(8,128)S(1)}, u32[]{:S(2)}, u32[]{:S(2)}) collective-permute-start(f32[4,32,256]{2,1,0:T(8,128)S(1)} %get-tuple-element.107), channel_id=1, source_target_pairs={{0,32},{1,33},{2,34},{3,35},{4,36},{5,37},{6,38},{7,39},{8,40},{9,... | collective-permute-start | bytes 393224 | tf_op jit(solution)/shard_map/ppermute | solution.py:528
  27.4 9.6 %collective-permute-start.4 = (f32[4,32,256]{2,1,0:T(8,128)S(1)}, f32[4,32,256]{2,1,0:T(8,128)S(1)}, u32[]{:S(2)}, u32[]{:S(2)}) collective-permute-start(f32[4,32,256]{2,1,0:T(8,128)S(1)} %get-tuple-element.106), channel_id=1, source_target_pairs={{0,32},{1,33},{2,34},{3,35},{4,36},{5,37},{6,38},{7,39},{8,40},{9,... | collective-permute-start | bytes 393224 | tf_op jit(solution)/shard_map/ppermute | solution.py:528
  35.0 3.8 %collective-permute-start.3 = (f32[4,32,256]{2,1,0:T(8,128)S(1)}, f32[4,32,256]{2,1,0:T(8,128)S(1)}, u32[]{:S(2)}, u32[]{:S(2)}) collective-permute-start(f32[4,32,256]{2,1,0:T(8,128)S(1)} %get-tuple-element.104), channel_id=1, source_target_pairs={{0,32},{1,33},{2,34},{3,35},{4,36},{5,37},{6,38},{7,39},{8,40},{9,... | collective-permute-start | bytes 393224 | tf_op jit(solution)/shard_map/ppermute | solution.py:528
  36.4 3.1 %collective-permute-start.8 = (f32[4,32,256]{2,1,0:T(8,128)S(1)}, f32[4,32,256]{2,1,0:T(8,128)S(1)}, u32[]{:S(2)}, u32[]{:S(2)}) collective-permute-start(f32[4,32,256]{2,1,0:T(8,128)S(1)} %get-tuple-element.115), channel_id=1, source_target_pairs={{32,64},{33,65},{34,66},{35,67},{36,68},{37,69},{38,70},{39,71},{4... | collective-permute-start | bytes 393224 | tf_op jit(solution)/shard_map/ppermute | solution.py:528
  37.1 3.1 %collective-permute-start.7 = (f32[4,32,256]{2,1,0:T(8,128)S(1)}, f32[4,32,256]{2,1,0:T(8,128)S(1)}, u32[]{:S(2)}, u32[]{:S(2)}) collective-permute-start(f32[4,32,256]{2,1,0:T(8,128)S(1)} %get-tuple-element.114), channel_id=1, source_target_pairs={{32,64},{33,65},{34,66},{35,67},{36,68},{37,69},{38,70},{39,71},{4... | collective-permute-start | bytes 393224 | tf_op jit(solution)/shard_map/ppermute | solution.py:528
  38.8 2.1 %collective-permute-start.6 = (f32[4,32,256]{2,1,0:T(8,128)S(1)}, f32[4,32,256]{2,1,0:T(8,128)S(1)}, u32[]{:S(2)}, u32[]{:S(2)}) collective-permute-start(f32[4,32,256]{2,1,0:T(8,128)S(1)} %get-tuple-element.113), channel_id=1, source_target_pairs={{32,64},{33,65},{34,66},{35,67},{36,68},{37,69},{38,70},{39,71},{4... | collective-permute-start | bytes 393224 | tf_op jit(solution)/shard_map/ppermute | solution.py:528
  39.5 2.1 %collective-permute-start.11 = (f32[4,32,256]{2,1,0:T(8,128)S(1)}, f32[4,32,256]{2,1,0:T(8,128)S(1)}, u32[]{:S(2)}, u32[]{:S(2)}) collective-permute-start(f32[4,32,256]{2,1,0:T(8,128)S(1)} %get-tuple-element.123), channel_id=1, source_target_pairs={{64,96},{65,97},{66,98},{67,99},{68,100},{69,101},{70,102},{71,103... | collective-permute-start | bytes 393224 | tf_op jit(solution)/shard_map/ppermute | solution.py:528
  40.3 1.4 %collective-permute-start.10 = (f32[4,32,256]{2,1,0:T(8,128)S(1)}, f32[4,32,256]{2,1,0:T(8,128)S(1)}, u32[]{:S(2)}, u32[]{:S(2)}) collective-permute-start(f32[4,32,256]{2,1,0:T(8,128)S(1)} %get-tuple-element.122), channel_id=1, source_target_pairs={{64,96},{65,97},{66,98},{67,99},{68,100},{69,101},{70,102},{71,103... | collective-permute-start | bytes 393224 | tf_op jit(solution)/shard_map/ppermute | solution.py:528
  41.0 0.8 collective-permute-start.9
  41.8 12.6 %collective-permute-start.12 = (f32[8,2,32,256]{3,2,1,0:T(8,128)S(1)}, f32[8,2,32,256]{3,2,1,0:T(8,128)S(1)}, u32[]{:S(2)}, u32[]{:S(2)}) collective-permute-start(f32[8,2,32,256]{3,2,1,0:T(8,128)S(1)} %get-tuple-element.128), channel_id=1, source_target_pairs={{0,1},{1,2},{2,3},{3,4},{4,5},{5,6},{6,7},{7,8},{8,9},{9,10},{10,1... | collective-permute-start | bytes 1572872 | tf_op jit(solution)/shard_map/ppermute | solution.py:551
  43.7 12.4 %collective-permute-start.13 = (f32[8,2,32,256]{3,2,1,0:T(8,128)S(1)}, f32[8,2,32,256]{3,2,1,0:T(8,128)S(1)}, u32[]{:S(2)}, u32[]{:S(2)}) collective-permute-start(f32[8,2,32,256]{3,2,1,0:T(8,128)S(1)} %get-tuple-element.129), channel_id=1, source_target_pairs={{1,0},{2,1},{3,2},{4,3},{5,4},{6,5},{7,6},{8,7},{9,8},{10,9},{11,1... | collective-permute-start | bytes 1572872 | tf_op jit(solution)/shard_map/ppermute | solution.py:552
  50.1 7.3 %collective-permute-start.16 = (f32[4,32,256]{2,1,0:T(8,128)S(1)}, f32[4,32,256]{2,1,0:T(8,128)S(1)}, u32[]{:S(2)}, u32[]{:S(2)}) collective-permute-start(f32[4,32,256]{2,1,0:T(8,128)S(1)} %get-tuple-element.139), channel_id=1, source_target_pairs={{96,64},{97,65},{98,66},{99,67},{100,68},{101,69},{102,70},{103,71... | collective-permute-start | bytes 393224 | tf_op jit(solution)/shard_map/ppermute | solution.py:579
  51.4 6.9 %collective-permute-start.15 = (f32[4,32,256]{2,1,0:T(8,128)S(1)}, f32[4,32,256]{2,1,0:T(8,128)S(1)}, u32[]{:S(2)}, u32[]{:S(2)}) collective-permute-start(f32[4,32,256]{2,1,0:T(8,128)S(1)} %get-tuple-element.138), channel_id=1, source_target_pairs={{96,64},{97,65},{98,66},{99,67},{100,68},{101,69},{102,70},{103,71... | collective-permute-start | bytes 393224 | tf_op jit(solution)/shard_map/ppermute | solution.py:579
  56.7 2.4 %collective-permute-start.14 = (f32[4,32,256]{2,1,0:T(8,128)S(1)}, f32[4,32,256]{2,1,0:T(8,128)S(1)}, u32[]{:S(2)}, u32[]{:S(2)}) collective-permute-start(f32[4,32,256]{2,1,0:T(8,128)S(1)} %get-tuple-element.136), channel_id=1, source_target_pairs={{96,64},{97,65},{98,66},{99,67},{100,68},{101,69},{102,70},{103,71... | collective-permute-start | bytes 393224 | tf_op jit(solution)/shard_map/ppermute | solution.py:579
  57.6 2.4 %collective-permute-start.19 = (f32[4,32,256]{2,1,0:T(8,128)S(1)}, f32[4,32,256]{2,1,0:T(8,128)S(1)}, u32[]{:S(2)}, u32[]{:S(2)}) collective-permute-start(f32[4,32,256]{2,1,0:T(8,128)S(1)} %get-tuple-element.148), channel_id=1, source_target_pairs={{64,32},{65,33},{66,34},{67,35},{68,36},{69,37},{70,38},{71,39},{7... | collective-permute-start | bytes 393224 | tf_op jit(solution)/shard_map/ppermute | solution.py:579
  58.4 3.0 %collective-permute-start.18 = (f32[4,32,256]{2,1,0:T(8,128)S(1)}, f32[4,32,256]{2,1,0:T(8,128)S(1)}, u32[]{:S(2)}, u32[]{:S(2)}) collective-permute-start(f32[4,32,256]{2,1,0:T(8,128)S(1)} %get-tuple-element.147), channel_id=1, source_target_pairs={{64,32},{65,33},{66,34},{67,35},{68,36},{69,37},{70,38},{71,39},{7... | collective-permute-start | bytes 393224 | tf_op jit(solution)/shard_map/ppermute | solution.py:579
  59.3 3.6 %collective-permute-start.17 = (f32[4,32,256]{2,1,0:T(8,128)S(1)}, f32[4,32,256]{2,1,0:T(8,128)S(1)}, u32[]{:S(2)}, u32[]{:S(2)}) collective-permute-start(f32[4,32,256]{2,1,0:T(8,128)S(1)} %get-tuple-element.146), channel_id=1, source_target_pairs={{64,32},{65,33},{66,34},{67,35},{68,36},{69,37},{70,38},{71,39},{7... | collective-permute-start | bytes 393224 | tf_op jit(solution)/shard_map/ppermute | solution.py:579
  60.2 32.0 %collective-permute-start.22 = (f32[4,32,256]{2,1,0:T(8,128)S(1)}, f32[4,32,256]{2,1,0:T(8,128)S(1)}, u32[]{:S(2)}, u32[]{:S(2)}) collective-permute-start(f32[4,32,256]{2,1,0:T(8,128)S(1)} %get-tuple-element.157), channel_id=1, source_target_pairs={{32,0},{33,1},{34,2},{35,3},{36,4},{37,5},{38,6},{39,7},{40,8},{41... | collective-permute-start | bytes 393224 | tf_op jit(solution)/shard_map/ppermute | solution.py:579
  61.6 35.5 %collective-permute-start.21 = (f32[4,32,256]{2,1,0:T(8,128)S(1)}, f32[4,32,256]{2,1,0:T(8,128)S(1)}, u32[]{:S(2)}, u32[]{:S(2)}) collective-permute-start(f32[4,32,256]{2,1,0:T(8,128)S(1)} %get-tuple-element.156), channel_id=1, source_target_pairs={{32,0},{33,1},{34,2},{35,3},{36,4},{37,5},{38,6},{39,7},{40,8},{41... | collective-permute-start | bytes 393224 | tf_op jit(solution)/shard_map/ppermute | solution.py:579
  63.1 37.0 %collective-permute-start.20 = (f32[4,32,256]{2,1,0:T(8,128)S(1)}, f32[4,32,256]{2,1,0:T(8,128)S(1)}, u32[]{:S(2)}, u32[]{:S(2)}) collective-permute-start(f32[4,32,256]{2,1,0:T(8,128)S(1)} %get-tuple-element.155), channel_id=1, source_target_pairs={{32,0},{33,1},{34,2},{35,3},{36,4},{37,5},{38,6},{39,7},{40,8},{41... | collective-permute-start | bytes 393224 | tf_op jit(solution)/shard_map/ppermute | solution.py:579

commit v3 on v2

v3 whole, which is shorter than its diff:
```python
import functools

import jax
import jax.numpy as jnp
from jax import lax
from jax.experimental import pallas as pl
from jax.experimental.pallas import tpu as pltpu
from jax.sharding import PartitionSpec as P

COLS = 8
LANES = 12
R = 32
BS = 256
FORWARD = ((2, 3, 4, 5), (6, 7, 8, 9), (0, 1, 10, 11))
BACKWARD = ((2, 3, 4, 5), (6, 7, 8, 9), (0, 1, 10, 11))
OUTER = 2
STRIP = 4
SIDES = ((2, -1), (3, 1), (4, -2), (5, 2))
NT = (((1,), (1,)), ((), ()))
VMEM = pltpu.VMEM
ANY = pl.ANY
HBM = pltpu.HBM

FIELD = (COLS, LANES, R, BS)
LATER = (LANES - 4, R, BS)
FIELD_MORE = (COLS + 1, LANES, R, BS)
EDGE = (COLS, 2, R, BS)
BLOCKS = (COLS, LANES, BS, BS)
PER = 4
COEFS = (6, COLS // PER, LANES, PER, BS)
WEIGHTS = (COLS + 1, LANES, BS)


def runs_of(lanes):
    runs = []
    for lane in lanes:
        if runs and runs[-1][0] + runs[-1][1] == lane:
            runs[-1][1] += 1
        else:
            runs.append([lane, 1])
    return [tuple(run) for run in runs]


def coef(ref, k, q, lane):
    return ref[k, q // PER, lane, pl.ds(q % PER, 1), :]


def weight(ref, q, lane):
    return ref[q, pl.ds(lane, 1), :]


def solve(xs, inverse, q, lanes):
    return [
        lax.dot_general(
            x.astype(jnp.bfloat16), inverse[q, lane], NT, preferred_element_type=jnp.float32
        )
        for x, lane in zip(xs, lanes)
    ]


def lane_copies(src, dst, q, lanes, sem):
    return [
        pltpu.make_async_copy(src.at[q, pl.ds(a, n)], dst.at[q, pl.ds(a, n)], sem.at[q])
        for a, n in runs_of(lanes)
    ]


def is_even():
    return lax.axis_index("tile") % 2 == 0


def ice_copy(ice_hbm, ice, sem):
    return pltpu.make_async_copy(ice_hbm, ice, sem)


def ice_weight(ice, q, lane):
    return ice[q // PER, q % PER, lane].astype(jnp.float32)


def near_prep_kernel(ice_hbm, st_hbm, now, later, ice, sem):
    at = 0
    copies = [ice_copy(ice_hbm, ice, sem.at[0])]
    for lanes in FORWARD:
        for a, n in runs_of(lanes):
            if lanes == FORWARD[0]:
                target = now.at[pl.ds(0, n)]
            else:
                target = later.at[pl.ds(at, n)]
                at += n
            copies.append(
                pltpu.make_async_copy(st_hbm.at[0, pl.ds(a, n)], target, sem.at[len(copies)])
            )
    for copy in copies:
        copy.start()
    for copy in copies:
        copy.wait()
    for j, lane in enumerate(FORWARD[0]):
        now[j] = ice_weight(ice, 0, lane) * now[j]
    for j, lane in enumerate(FORWARD[1] + FORWARD[2]):
        later[j] = ice_weight(ice, 0, lane) * later[j]


def prep_kernel(_, ice_hbm, st_hbm, couple_hbm, edge_in, edge_out, couple, mask, ice, sem):
    even = is_even()
    lane_in = jnp.where(even, LANES - 2, 0)
    lane_out = jnp.where(even, 0, LANES - 2)
    copies = [
        ice_copy(ice_hbm, ice, sem.at[0]),
        pltpu.make_async_copy(st_hbm.at[:, pl.ds(lane_out, 2)], edge_out, sem.at[1]),
        pltpu.make_async_copy(st_hbm.at[:, pl.ds(lane_in, 2)], edge_in, sem.at[2]),
        pltpu.make_async_copy(couple_hbm, couple, sem.at[3]),
    ]
    for copy in copies:
        copy.start()
    copies[0].wait()
    for q in range(COLS):
        for lane in range(LANES):
            mask[q, pl.ds(lane, 1), :] = jnp.full((1, BS), ice_weight(ice, q, lane), jnp.float32)
    copies[1].wait()
    copies[2].wait()
    for q in range(COLS):
        for j in range(2):
            edge_out[q, j] = ice_weight(ice, q, lane_out + j) * edge_out[q, j]
            edge_in[q, j] = ice_weight(ice, q, lane_in + j) * edge_in[q, j]
    copies[3].wait()


def halo_of(even, halo_in, halo_out, q, lane):
    if lane < 0:
        return jnp.where(even, halo_out[q, lane + 2], halo_in[q, lane + 2])
    return jnp.where(even, halo_in[q, lane - LANES], halo_out[q, lane - LANES])


def make_source(lanes, q, rs, start, couple, mask, source, halo=None, later=None):
    for j, lane in enumerate(lanes):
        total = rs[q, lane]
        for k, step in SIDES:
            other = lane + step
            if 0 <= other < LANES:
                factor = coef(couple, k, q, lane) * weight(mask, q, other)
                total = total + factor * start[q, other]
            elif halo is not None:
                total = total + coef(couple, k, q, lane) * halo(q, other)
        if later is None:
            factor = coef(couple, 1, q, lane) * weight(mask, q + 1, lane)
            total = total + factor * start[q + 1, lane]
        else:
            total = total + coef(couple, 1, q, lane) * later[j]
        source[q, lane] = total


def forward_chain(lanes, q, source, inverse, couple, mask, field, sent, edges=None):
    xs = [source[q, lane] + coef(couple, 0, q, lane) * sent[j] for j, lane in enumerate(lanes)]
    ys = solve(xs, inverse, q, lanes)
    values = [weight(mask, q, lane) * y for y, lane in zip(ys, lanes)]
    for j, lane in enumerate(lanes):
        field[q + 1, lane] = values[j]
        sent[j] = values[j]
    if edges is not None:
        even, edge_in, edge_out = edges
        for j in range(2):
            edge_in[q, j] = jnp.where(even, values[2 + j], values[j])
            edge_out[q, j] = jnp.where(even, values[j], values[2 + j])


def start_all(copies):
    def step(q, _):
        for copy in copies(q):
            copy.start()
        return 0

    lax.fori_loop(0, COLS, step, 0)


def wait_all(copies):
    def step(q, _):
        for copy in copies(q):
            copy.wait()
        return 0

    lax.fori_loop(0, COLS, step, 0)


def sweep_first(
    lanes, rs, start, source, inverse, couple, mask, field, sent, columns, halo, edges, arriving=None
):
    for j in range(len(lanes)):
        sent[j] = jnp.zeros((R, BS), jnp.float32)
    make_source(lanes, 0, rs, start, couple, mask, source, halo)

    def step(q, _):
        if arriving is not None:
            for copy in arriving(q):
                copy.wait()
        forward_chain(lanes, q, source, inverse, couple, mask, field, sent, edges)
        make_source(
            lanes, jnp.minimum(q + 1, columns - 1), rs, start, couple, mask, source, halo
        )
        return 0

    lax.fori_loop(0, columns, step, 0)


def first_kernel(inv_hbm, rs, start, couple, mask, inverse, source, field, sent, sem, sem_next):
    first = lax.axis_index("strip") == 0

    @pl.when(first)
    def _():
        def own(q):
            return lane_copies(inv_hbm, inverse, q, FORWARD[0], sem)

        def following(q):
            return lane_copies(inv_hbm, inverse, q, FORWARD[1], sem_next)

        start_all(own)
        start_all(following)
        field[0] = jnp.zeros((LANES, R, BS), jnp.float32)
        sweep_first(
            FORWARD[0],
            rs,
            start,
            source,
            inverse,
            couple,
            mask,
            field,
            sent,
            COLS - 1,
            None,
            None,
            own,
        )
        for copy in own(COLS - 1):
            copy.wait()
        wait_all(following)

    @pl.when(jnp.logical_not(first))
    def _():
        def every(q):
            return lane_copies(inv_hbm, inverse, q, range(LANES), sem)

        start_all(every)

        def step(q, _):
            make_source(range(LANES), q, rs, start, couple, mask, source)
            return 0

        lax.fori_loop(0, COLS - 1, step, 0)
        wait_all(every)


def tail_kernel(now, inverse, rs, start, couple, mask, *refs):
    source, field, sent = refs[3:]
    lanes, q = FORWARD[0], COLS - 1

    @pl.when(lax.axis_index("strip") == 0)
    def _():
        make_source(lanes, q, rs, start, couple, mask, source, None, now)
        forward_chain(lanes, q, source, inverse, couple, mask, field, sent)


def outer_kernel(now, later, halo_in, halo_out, inverse, rs, start, couple, mask, *refs):
    source, field, edge_in, edge_out, sent = refs[2:]
    lanes, q_last = FORWARD[OUTER], COLS - 1
    first = lax.axis_index("strip") == 0
    even = is_even()
    edges = (even, edge_in, edge_out)
    halo = functools.partial(halo_of, even, halo_in, halo_out)

    @pl.when(first)
    def _():
        own = later.at[pl.ds(len(FORWARD[1]), len(lanes))]
        sweep_first(
            lanes, rs, start, source, inverse, couple, mask, field, sent, COLS - 1, halo, edges
        )
        make_source(lanes, q_last, rs, start, couple, mask, source, halo, own)
        forward_chain(lanes, q_last, source, inverse, couple, mask, field, sent, edges)

    @pl.when(jnp.logical_not(first))
    def _():
        make_source(FORWARD[0], q_last, rs, start, couple, mask, source, None, now)
        make_source(
            FORWARD[1] + FORWARD[2], q_last, rs, start, couple, mask, source, None, later
        )

        def step(q, _):
            for lane in lanes:
                total = source[q, lane]
                for k, move in SIDES:
                    if not 0 <= lane + move < LANES:
                        total = total + coef(couple, k, q, lane) * halo(q, lane + move)
                source[q, lane] = total
            return 0

        lax.fori_loop(0, COLS, step, 0)


def inner_kernel(later, inv_hbm, rs, start, couple, mask, *refs):
    inverse, source, field, sent, sem = refs[3:]
    lanes, q = FORWARD[1], COLS - 1

    @pl.when(lax.axis_index("strip") == 0)
    def _():
        def following(q):
            return lane_copies(inv_hbm, inverse, q, FORWARD[2], sem)

        start_all(following)
        sweep_first(
            lanes, rs, start, source, inverse, couple, mask, field, sent, COLS - 1, None, None
        )
        make_source(lanes, q, rs, start, couple, mask, source, None, later)
        forward_chain(lanes, q, source, inverse, couple, mask, field, sent)
        wait_all(following)


def forward_kernel(chunk, stage, came, inverse, source, couple, mask, *refs):
    lanes = FORWARD[chunk]
    edges = None
    if chunk == OUTER:
        field, edge_in, edge_out, sent = refs[3:]
        edges = (is_even(), edge_in, edge_out)
    else:
        field, sent = refs[1:]

    @pl.when(lax.axis_index("strip") == stage)
    def _():
        for j, lane in enumerate(lanes):
            sent[j] = came[j]
            field[0, lane] = came[j]

        def step(q, _):
            forward_chain(lanes, q, source, inverse, couple, mask, field, sent, edges)
            return 0

        lax.fori_loop(0, COLS, step, 0)


def backward_chain(lanes, q, source, inverse, couple, mask, result, sent):
    xs = [source[q, lane] + coef(couple, 1, q, lane) * sent[j] for j, lane in enumerate(lanes)]
    ys = solve(xs, inverse, q, lanes)
    for j, lane in enumerate(lanes):
        value = weight(mask, q, lane) * ys[j]
        result[q, lane] = value
        sent[j] = value


def backward_sweep(
    chunk, final, inverse, source, couple, mask, result, out, sent, sem, sem_own, beside
):
    lanes = BACKWARD[chunk]
    last = final and chunk == len(BACKWARD) - 1

    def before(q):
        return lane_copies(result, out, q, BACKWARD[chunk - 1], sem) if chunk > 0 else []

    def own(q):
        return lane_copies(result, out, q, lanes, sem_own) if last else []

    def launch(q, _):
        for copy in before(q):
            copy.start()
        return 0

    lax.fori_loop(0, COLS, launch, 0)

    def step(i, _):
        q = COLS - 1 - i
        backward_chain(lanes, q, source, inverse, couple, mask, result, sent)
        for copy in own(q):
            copy.start()
        if beside is not None:
            beside(jnp.maximum(q - 1, 0))
        return 0

    lax.fori_loop(0, COLS, step, 0)

    def drain(q, _):
        for copy in before(q) + own(q):
            copy.wait()
        return 0

    lax.fori_loop(0, COLS, drain, 0)


def last_kernel(chunk, inverse, rs, field, couple, mask, halo_in, halo_out, *refs):
    lanes = BACKWARD[chunk]
    source, result, out, sent, sem, sem_own = refs[-6:]
    active = lax.axis_index("strip") == STRIP - 1
    even = is_even()

    def near(q, lane):
        if 0 <= lane < LANES:
            return field[q + 1, lane]
        return halo_of(even, halo_in, halo_out, q, lane)

    def source_of(q):
        for lane in lanes:
            total = rs[q, lane] + coef(couple, 0, q, lane) * field[q, lane]
            for k, step in SIDES:
                total = total + coef(couple, k, q, lane) * near(q, lane + step)
            source[q, lane] = total

    @pl.when(active)
    def _():
        for j in range(len(lanes)):
            sent[j] = jnp.zeros((R, BS), jnp.float32)
        source_of(COLS - 1)
        backward_sweep(
            chunk, False, inverse, source, couple, mask, result, out, sent, sem, sem_own, source_of
        )

    @pl.when(jnp.logical_not(active))
    def _():
        def step(q, _):
            source_of(q)
            return 0

        lax.fori_loop(0, COLS, step, 0)


def backward_kernel(chunk, stage, came, inverse, source, couple, mask, *refs):
    result, out, sent, sem, sem_own = refs[2:]
    strip = lax.axis_index("strip")

    @pl.when(strip == stage)
    def _():
        sent[...] = came[...]
        backward_sweep(
            chunk, stage == 0, inverse, source, couple, mask, result, out, sent, sem, sem_own, None
        )

    if chunk == 0:

        @pl.when(strip == stage + 1)
        def _():
            copies = [
                pltpu.make_async_copy(
                    result.at[:, pl.ds(a, n)], out.at[:, pl.ds(a, n)], sem_own.at[i]
                )
                for i, (a, n) in enumerate(runs_of(BACKWARD[-1]))
            ]
            for copy in copies:
                copy.start()
            for copy in copies:
                copy.wait()


def vmem(shape, dtype=jnp.float32):
    return VMEM(shape, dtype)


def run(kernel, name, operands, outs, scratch, aliases=None):
    arrays = [
        pltpu.with_memory_space_constraint(a, space) if space in (VMEM, HBM) else a
        for a, space in operands
    ]
    return pl.pallas_call(
        kernel,
        name=name,
        out_shape=[o for o, _ in outs],
        in_specs=[pl.BlockSpec(memory_space=space) for _, space in operands],
        out_specs=[pl.BlockSpec(memory_space=space) for _, space in outs],
        scratch_shapes=scratch,
        input_output_aliases=aliases or {},
        compiler_params=pltpu.CompilerParams(vmem_limit_bytes=8 * 2**20),
        cost_estimate=pl.CostEstimate(
            flops=2**26, bytes_accessed=2**21, transcendentals=0
        ),
    )(*arrays)


def on_device(right_side, starting_iterate, inverse_diagonal_blocks, couple, ice_mask):
    rs = right_side.reshape(FIELD)
    start = starting_iterate.reshape(FIELD)
    inverse = inverse_diagonal_blocks.reshape(BLOCKS)
    tiles = lax.axis_size("tile")
    pairs_in = [(i, i + 1) for i in range(0, tiles - 1, 2)]
    pairs_out = [(i, i + 1) for i in range(1, tiles - 1, 2)]
    to_back = [(i + 1, i) for i in range(STRIP - 1)]
    dma = pltpu.SemaphoreType.DMA

    def swapped(value, pairs):
        return lax.ppermute(value, "tile", pairs + [(b, a) for a, b in pairs])

    def inside(*arrays):
        return [(a, VMEM) for a in arrays]

    def made(*shapes):
        return [(vmem(shape), VMEM) for shape in shapes]

    def piece(lanes):
        return (len(lanes), R, BS)

    ice = pltpu.SMEM(ice_mask.shape, jnp.int32)
    now, later = run(
        near_prep_kernel,
        "near_prep",
        [(ice_mask, HBM), (start, HBM)],
        made(piece(FORWARD[0]), LATER),
        [ice, dma((6,))],
    )
    now_sent = now
    now = lax.ppermute(now, "strip", to_back)
    edge_in, edge_out, coefs, mask = run(
        prep_kernel,
        "prep",
        inside(now_sent)
        + [(ice_mask, HBM), (start, HBM), (couple.transpose(0, 1, 3, 2, 4), HBM)],
        made(EDGE, EDGE, COEFS, WEIGHTS),
        [ice, dma((4,))],
    )
    halo_out = swapped(edge_out, pairs_out)
    halo_in = swapped(edge_in, pairs_in)
    later = lax.ppermute(later, "strip", to_back)

    sents = {}
    blocks = [(vmem(BLOCKS, jnp.bfloat16), VMEM)]
    inv_hbm = [(inverse, HBM)]
    rest = inside(rs, start, coefs, mask)
    inverse, source, field, sent = run(
        first_kernel,
        "first",
        inv_hbm + rest,
        blocks + made(FIELD, FIELD_MORE, piece(FORWARD[0])),
        [dma((COLS,)), dma((COLS,))],
    )
    source, field, sents[0, 0] = run(
        tail_kernel,
        "tail",
        inside(now, inverse) + rest + inside(source, field, sent),
        made(FIELD, FIELD_MORE, piece(FORWARD[0])),
        [],
        {6: 0, 7: 1, 8: 2},
    )
    inverse, source, field, sents[0, 1] = run(
        inner_kernel,
        "inner",
        inside(later) + inv_hbm + rest + inside(inverse, source, field),
        blocks + made(FIELD, FIELD_MORE, piece(FORWARD[1])),
        [dma((COLS,))],
        {6: 0, 7: 1, 8: 2},
    )
    source, field, edge_in, edge_out, sents[0, 2] = run(
        outer_kernel,
        "outer",
        inside(now, later, halo_in, halo_out, inverse) + rest + inside(source, field),
        made(FIELD, FIELD_MORE, EDGE, EDGE, piece(FORWARD[2])),
        [],
        {9: 0, 10: 1},
    )

    for stage in range(1, STRIP):
        for chunk, lanes in enumerate(FORWARD):
            came = lax.ppermute(sents[stage - 1, chunk], "strip", [(stage - 1, stage)])
            sending = stage + 1 < STRIP
            operands = inside(came, inverse, source, coefs, mask, field)
            outs = made(FIELD_MORE)
            aliases = {5: 0}
            if chunk == OUTER:
                operands += inside(edge_in, edge_out)
                outs += made(EDGE, EDGE)
                aliases |= {6: 1, 7: 2}
            got = run(
                functools.partial(forward_kernel, chunk, stage),
                f"forward_{stage}_{chunk}",
                operands,
                outs + (made(piece(lanes)) if sending else []),
                [] if sending else [vmem(piece(lanes))],
                aliases,
            )
            field = got[0]
            if chunk == OUTER:
                edge_in, edge_out = got[1:3]
            if sending:
                sents[stage, chunk] = got[-1]

    halo_out = swapped(edge_out, pairs_out)
    halo_in = swapped(edge_in, pairs_in)

    out_shape = [(jax.ShapeDtypeStruct(FIELD, jnp.float32), HBM)]
    sems = [dma((COLS,)), dma((COLS,))]
    result = out = None
    for chunk, lanes in enumerate(BACKWARD):
        sides = inside(halo_in, halo_out) if min(lanes) < 2 or max(lanes) >= LANES - 2 else []
        operands = inside(inverse, rs, field, coefs, mask) + sides + inside(source)
        base = len(operands) - 1
        aliases = {base: 0}
        kernel = functools.partial(last_kernel, chunk)
        if not sides:
            kernel = functools.partial(without_halos, kernel)
        if chunk > 0:
            operands += inside(result) + [(out, HBM)]
            aliases |= {base + 1: 1, base + 2: 2}
        source, result, out, sents[STRIP - 1, chunk] = run(
            kernel,
            f"last_{chunk}",
            operands,
            made(FIELD, FIELD) + out_shape + made(piece(lanes)),
            sems,
            aliases,
        )

    for stage in range(STRIP - 2, -1, -1):
        for chunk, lanes in enumerate(BACKWARD):
            came = lax.ppermute(sents[stage + 1, chunk], "strip", [(stage + 1, stage)])
            sending = stage > 0
            got = run(
                functools.partial(backward_kernel, chunk, stage),
                f"backward_{stage}_{chunk}",
                inside(came, inverse, source, coefs, mask, result) + [(out, HBM)],
                made(FIELD) + out_shape + (made(piece(lanes)) if sending else []),
                ([] if sending else [vmem(piece(lanes))]) + sems,
                {5: 0, 6: 1},
            )
            result, out = got[:2]
            if sending:
                sents[stage, chunk] = got[2]
    return out.reshape(right_side.shape)


def without_halos(kernel, inverse, rs, field, couple, mask, *refs):
    kernel(inverse, rs, field, couple, mask, None, None, *refs)


def solution(mesh):
    return jax.shard_map(
        on_device,
        mesh=mesh,
        in_specs=(
            P("strip", None, "tile", None, None),
            P("strip", None, "tile", None, None),
            P("strip", None, "tile", None, None),
            P(None, "strip", None, "tile", None),
            P("strip", None, "tile"),
        ),
        out_specs=P("strip", None, "tile", None, None),
        check_vma=False,
    )
```

time: 104 us -> 92.9 us (0.89)
  starting transfers between devices: 38.3 us -> 30 us
  waiting for transfers between devices: 40.6 us -> 39.3 us
    ppermute x5 -> x6, starting transfers between devices: 16.6 us -> 12.4 us  [the longest x4 9.78 us: swapped(): return lax.ppermute(value, 'tile', pairs + [(b, a) for a, b in pairs])]
    ppermute x9, starting transfers between devices: 13.7 us -> 9.72 us  [on_device(): came = lax.ppermute(sents[stage - 1, chunk], 'strip', [(stage - 1, stage)])]
    ppermute x9, waiting for transfers between devices: 31.1 us -> 27.5 us  [on_device(): came = lax.ppermute(sents[stage + 1, chunk], 'strip', [(stage + 1, stage)])]
    ppermute x5 -> x6, waiting for transfers between devices: 8.45 us -> 10.7 us  [the longest x1 5.48 us: on_device(): now = lax.ppermute(now, 'strip', to_back)]
    pallas_call x26 -> x27, Pallas kernels: 23.2 us -> 22.6 us  [run(): pl.pallas_call(kernel, name=name, out_shape=[o for o, _ in outs], in_spec...]
  transfers between devices with their start and end apart: 23 -> 24, of which waited for: 7 -> 6; matrix products, arithmetic and copies ran while one was open for 0% -> 0% of each run, Pallas kernels for 17% -> 17%
where the time goes in v3:
time: 92.9 us; the launch traced here: 92.4 us
  waiting for transfers between devices  39.3 us (42%)
  starting transfers between devices  30 us (32%)
  Pallas kernels  22.6 us (24%)
    ppermute x9, waiting for transfers between devices, on_device(): came = lax.ppermute(sents[stage + 1, chunk], 'strip', [(stage + 1, stage)])  27.5 us
    pallas_call x27, Pallas kernels, run(): pl.pallas_call(kernel, name=name, out_shape=[o for o, _ in outs], in_spec...  22.6 us
    ppermute x4, starting transfers between devices, swapped(): return lax.ppermute(value, 'tile', pairs + [(b, a) for a, b in pairs])  9.78 us
    ppermute x9, starting transfers between devices, on_device(): came = lax.ppermute(sents[stage - 1, chunk], 'strip', [(stage - 1, stage)])  9.72 us
    ppermute x9, starting transfers between devices, on_device(): came = lax.ppermute(sents[stage + 1, chunk], 'strip', [(stage + 1, stage)])  7.89 us
    ppermute x1, waiting for transfers between devices, on_device(): now = lax.ppermute(now, 'strip', to_back)  5.48 us
    ppermute x4, waiting for transfers between devices, swapped(): return lax.ppermute(value, 'tile', pairs + [(b, a) for a, b in pairs])  5.25 us
  transfers between devices with their start and end apart: 24, of which 6 were waited for; matrix products, arithmetic and copies ran while one was open for 0% of the time, Pallas kernels for 17%

profile of v3, /device:TPU:96, one launch (start us, length us, event | category | flops | bytes accessed | tf_op | source)
XLA Modules:
  0.0 92.4 jit_solution(10583373224166185704)
XLA Ops:
  0.0 1.2 %near_prep.1 = (f32[4,32,256]{2,1,0:T(8,128)S(1)}, f32[8,32,256]{2,1,0:T(8,128)S(1)}) custom-call(s32[2,4,12]{2,1,0:T(4,128)} %ice_hbm.3, f32[8,12,32,256]{3,2,1,0:T(8,128)} %bitcast.12), custom_call_target="tpu_custom_call" | custom-call | flops 67108864 | bytes 2097152 | tf_op jit(solution)/shard_map/near_prep/pallas_call | solution.py:457
  1.2 2.2 %prep.1 = (f32[8,2,32,256]{3,2,1,0:T(8,128)S(1)}, f32[8,2,32,256]{3,2,1,0:T(8,128)S(1)}, f32[6,2,12,4,256]{4,3,2,1,0:T(4,128)S(1)}, f32[9,12,256]{2,1,0:T(8,128)S(1)}) custom-call(f32[4,32,256]{2,1,0:T(8,128)S(1)} %get-tuple-element.82._, s32[2,4,12]{2,1,0:T(4,128)} %ice_hbm.3, f32[8,12,32,256]{3,2,1,0:T(8,128)} %bitcast.13, f32[6,2,12,4,256]{4,3,2,1,0:T(4,128)} %bitcast.20), custom_call_target="tpu_custom_call" | custom-call | flops 67108864 | bytes 2097152 | tf_op jit(solution)/shard_map/prep/pallas_call | solution.py:457
  3.4 0.1 collective-permute-start.2
  3.5 4.9 %collective-permute-start.3 = (f32[8,2,32,256]{3,2,1,0:T(8,128)S(1)}, f32[8,2,32,256]{3,2,1,0:T(8,128)S(1)}, u32[]{:S(2)}, u32[]{:S(2)}) collective-permute-start(f32[8,2,32,256]{3,2,1,0:T(8,128)S(1)} %get-tuple-element.93), channel_id=1, source_target_pairs={{1,2},{3,4},{5,6},{7,8},{9,10},{11,12},{13,14},{15,16},{17,18},{19... | collective-permute-start | bytes 1572872 | tf_op jit(solution)/shard_map/ppermute | solution.py:483
  8.4 1.3 %collective-permute-start = (f32[8,32,256]{2,1,0:T(8,128)S(1)}, f32[8,32,256]{2,1,0:T(8,128)S(1)}, u32[]{:S(2)}, u32[]{:S(2)}) collective-permute-start(f32[8,32,256]{2,1,0:T(8,128)S(1)} %get-tuple-element.81), channel_id=1, source_target_pairs={{32,0},{64,32},{96,64},{33,1},{65,33},{97,65},{34,2},{66,34},{98,6... | collective-permute-start | bytes 786440 | tf_op jit(solution)/shard_map/ppermute | solution.py:514
  9.7 1.3 %collective-permute-start.1 = (f32[4,32,256]{2,1,0:T(8,128)S(1)}, f32[4,32,256]{2,1,0:T(8,128)S(1)}, u32[]{:S(2)}, u32[]{:S(2)}) collective-permute-start(f32[4,32,256]{2,1,0:T(8,128)S(1)} %get-tuple-element.82._), channel_id=1, source_target_pairs={{32,0},{64,32},{96,64},{33,1},{65,33},{97,65},{34,2},{66,34},{98,6... | collective-permute-start | bytes 393224 | tf_op jit(solution)/shard_map/ppermute | solution.py:503
  11.0 3.6 %first.1 = (bf16[8,12,256,256]{3,2,1,0:T(8,128)(2,1)S(1)}, f32[8,12,32,256]{3,2,1,0:T(8,128)S(1)}, f32[9,12,32,256]{3,2,1,0:T(8,128)S(1)}, f32[4,32,256]{2,1,0:T(8,128)S(1)}) custom-call(bf16[8,12,256,256]{3,2,1,0:T(8,128)(2,1)} %bitcast.18, f32[8,12,32,256]{3,2,1,0:T(8,128)S(1)} %bitcast.5, f32[8,12,32,256]{3,2,1,0:T(8,128)S(1)} %bitcast.14, ...), custom_call_target="tpu_custom_call" | custom-call | flops 67108864 | bytes 2097152 | tf_op jit(solution)/shard_map/first/pallas_call | solution.py:457
  14.6 5.5 %collective-permute-done.1.now = f32[4,32,256]{2,1,0:T(8,128)S(1)} collective-permute-done((f32[4,32,256]{2,1,0:T(8,128)S(1)}, f32[4,32,256]{2,1,0:T(8,128)S(1)}, u32[]{:S(2)}, u32[]{:S(2)}) %collective-permute-start.1) | collective-permute-done | bytes 131104 | tf_op jit(solution)/shard_map/ppermute | solution.py:503
  20.1 0.3 tail.1
  20.3 3.1 %collective-permute-start.6 = (f32[4,32,256]{2,1,0:T(8,128)S(1)}, f32[4,32,256]{2,1,0:T(8,128)S(1)}, u32[]{:S(2)}, u32[]{:S(2)}) collective-permute-start(f32[4,32,256]{2,1,0:T(8,128)S(1)} %get-tuple-element.99), channel_id=1, source_target_pairs={{0,32},{1,33},{2,34},{3,35},{4,36},{5,37},{6,38},{7,39},{8,40},{9,... | collective-permute-start | bytes 393224 | tf_op jit(solution)/shard_map/ppermute | solution.py:554
  23.5 0.0 collective-permute-done.later
  23.5 2.4 %inner.1 = (bf16[8,12,256,256]{3,2,1,0:T(8,128)(2,1)S(1)}, f32[8,12,32,256]{3,2,1,0:T(8,128)S(1)}, f32[9,12,32,256]{3,2,1,0:T(8,128)S(1)}, f32[4,32,256]{2,1,0:T(8,128)S(1)}) custom-call(f32[8,32,256]{2,1,0:T(8,128)S(1)} %collective-permute-done.later, ...), custom_call_target="tpu_custom_call", output_to_operand_aliasing={{0}: (6, {}), {1}: (7, {}), {2}: (8, {})} | custom-call | flops 67108864 | bytes 2097152 | tf_op jit(solution)/shard_map/inner/pallas_call | solution.py:457
  25.9 1.3 %collective-permute-start.5 = (f32[4,32,256]{2,1,0:T(8,128)S(1)}, f32[4,32,256]{2,1,0:T(8,128)S(1)}, u32[]{:S(2)}, u32[]{:S(2)}) collective-permute-start(f32[4,32,256]{2,1,0:T(8,128)S(1)} %get-tuple-element.98), channel_id=1, source_target_pairs={{0,32},{1,33},{2,34},{3,35},{4,36},{5,37},{6,38},{7,39},{8,40},{9,... | collective-permute-start | bytes 393224 | tf_op jit(solution)/shard_map/ppermute | solution.py:554
  27.2 0.0 collective-permute-done.2.halo_in
  27.2 0.0 collective-permute-done.3.halo_out
  27.2 2.3 %outer.1 = (f32[8,12,32,256]{3,2,1,0:T(8,128)S(1)}, f32[9,12,32,256]{3,2,1,0:T(8,128)S(1)}, f32[8,2,32,256]{3,2,1,0:T(8,128)S(1)}, f32[8,2,32,256]{3,2,1,0:T(8,128)S(1)}, f32[4,32,256]{2,1,0:T(8,128)S(1)}) custom-call(f32[4,32,256]{2,1,0:T(8,128)S(1)} %collective-permute-done.1.now, ...), custom_call_target="tpu_custom_call", output_to_operand_aliasing={{0}: (9, {}), {1}: (10, {})} | custom-call | flops 67108864 | bytes 2097152 | tf_op jit(solution)/shard_map/outer/pallas_call | solution.py:457
  29.5 1.3 %collective-permute-start.4 = (f32[4,32,256]{2,1,0:T(8,128)S(1)}, f32[4,32,256]{2,1,0:T(8,128)S(1)}, u32[]{:S(2)}, u32[]{:S(2)}) collective-permute-start(f32[4,32,256]{2,1,0:T(8,128)S(1)} %get-tuple-element.96), channel_id=1, source_target_pairs={{0,32},{1,33},{2,34},{3,35},{4,36},{5,37},{6,38},{7,39},{8,40},{9,... | collective-permute-start | bytes 393224 | tf_op jit(solution)/shard_map/ppermute | solution.py:554
  30.8 0.0 collective-permute-done.6.came
  30.8 0.7 collective-permute-start.9
  31.5 0.0 collective-permute-done.5.came
  31.5 0.7 collective-permute-start.8
  32.2 1.1 %collective-permute-done.4.came = f32[4,32,256]{2,1,0:T(8,128)S(1)} collective-permute-done((f32[4,32,256]{2,1,0:T(8,128)S(1)}, f32[4,32,256]{2,1,0:T(8,128)S(1)}, u32[]{:S(2)}, u32[]{:S(2)}) %collective-permute-start.4) | collective-permute-done | bytes 131104 | tf_op jit(solution)/shard_map/ppermute | solution.py:554
  33.3 0.7 collective-permute-start.7
  34.0 0.0 collective-permute-done.9.came
  34.0 0.7 collective-permute-start.12
  34.7 0.0 collective-permute-done.8.came
  34.7 0.7 collective-permute-start.11
  35.4 0.0 collective-permute-done.7.came
  35.4 0.7 collective-permute-start.10
  36.1 0.0 collective-permute-done.12.came
  36.1 0.0 collective-permute-done.11.came
  36.2 0.0 collective-permute-done.10.came
  36.2 0.1 collective-permute-start.13
  36.3 4.8 %collective-permute-start.14 = (f32[8,2,32,256]{3,2,1,0:T(8,128)S(1)}, f32[8,2,32,256]{3,2,1,0:T(8,128)S(1)}, u32[]{:S(2)}, u32[]{:S(2)}) collective-permute-start(f32[8,2,32,256]{3,2,1,0:T(8,128)S(1)} %get-tuple-element.121), channel_id=1, source_target_pairs={{1,2},{3,4},{5,6},{7,8},{9,10},{11,12},{13,14},{15,16},{17,18},{19... | collective-permute-start | bytes 1572872 | tf_op jit(solution)/shard_map/ppermute | solution.py:483
  41.1 0.6 last_0.1
  41.7 0.7 collective-permute-start.17
  42.4 0.6 last_1.1
  43.0 0.7 collective-permute-start.16
  43.7 0.0 collective-permute-done.13.halo_in
  43.7 5.2 %collective-permute-done.14.halo_out = f32[8,2,32,256]{3,2,1,0:T(8,128)S(1)} collective-permute-done((f32[8,2,32,256]{3,2,1,0:T(8,128)S(1)}, f32[8,2,32,256]{3,2,1,0:T(8,128)S(1)}, u32[]{:S(2)}, u32[]{:S(2)}) %collective-permute-start.14) | collective-permute-done | bytes 524320 | tf_op jit(solution)/shard_map/ppermute | solution.py:483
  48.9 0.6 last_2.1
  49.5 0.7 collective-permute-start.15
  50.2 0.0 collective-permute-done.17.came
  50.2 0.2 backward_2_0.1
  50.4 0.7 collective-permute-start.20
  51.1 0.0 collective-permute-done.16.came
  51.1 0.2 backward_2_1.1
  51.3 0.7 collective-permute-start.19
  51.9 0.0 collective-permute-done.15.came
  52.0 0.2 backward_2_2.1
  52.1 0.7 collective-permute-start.18
  52.8 0.0 collective-permute-done.20.came
  52.8 0.2 backward_1_0.1
  53.0 1.3 %collective-permute-start.23 = (f32[4,32,256]{2,1,0:T(8,128)S(1)}, f32[4,32,256]{2,1,0:T(8,128)S(1)}, u32[]{:S(2)}, u32[]{:S(2)}) collective-permute-start(f32[4,32,256]{2,1,0:T(8,128)S(1)} %get-tuple-element.149), channel_id=1, source_target_pairs={{32,0},{33,1},{34,2},{35,3},{36,4},{37,5},{38,6},{39,7},{40,8},{41... | collective-permute-start | bytes 393224 | tf_op jit(solution)/shard_map/ppermute | solution.py:605
  54.3 0.2 backward_1_1.1
  54.5 1.3 %collective-permute-start.22 = (f32[4,32,256]{2,1,0:T(8,128)S(1)}, f32[4,32,256]{2,1,0:T(8,128)S(1)}, u32[]{:S(2)}, u32[]{:S(2)}) collective-permute-start(f32[4,32,256]{2,1,0:T(8,128)S(1)} %get-tuple-element.148), channel_id=1, source_target_pairs={{32,0},{33,1},{34,2},{35,3},{36,4},{37,5},{38,6},{39,7},{40,8},{41... | collective-permute-start | bytes 393224 | tf_op jit(solution)/shard_map/ppermute | solution.py:605
  55.8 0.2 backward_1_2.1
  56.0 1.3 %collective-permute-start.21 = (f32[4,32,256]{2,1,0:T(8,128)S(1)}, f32[4,32,256]{2,1,0:T(8,128)S(1)}, u32[]{:S(2)}, u32[]{:S(2)}) collective-permute-start(f32[4,32,256]{2,1,0:T(8,128)S(1)} %get-tuple-element.147), channel_id=1, source_target_pairs={{32,0},{33,1},{34,2},{35,3},{36,4},{37,5},{38,6},{39,7},{40,8},{41... | collective-permute-start | bytes 393224 | tf_op jit(solution)/shard_map/ppermute | solution.py:605
  57.3 22.6 %collective-permute-done.23.came = f32[4,32,256]{2,1,0:T(8,128)S(1)} collective-permute-done((f32[4,32,256]{2,1,0:T(8,128)S(1)}, f32[4,32,256]{2,1,0:T(8,128)S(1)}, u32[]{:S(2)}, u32[]{:S(2)}) %collective-permute-start.23) | collective-permute-done | bytes 131104 | tf_op jit(solution)/shard_map/ppermute | solution.py:605
  79.9 2.3 %backward_0_0.1 = (f32[8,12,32,256]{3,2,1,0:T(8,128)S(1)}, f32[8,12,32,256]{3,2,1,0:T(8,128)}) custom-call(f32[4,32,256]{2,1,0:T(8,128)S(1)} %collective-permute-done.23.came, bf16[8,12,256,256]{3,2,1,0:T(8,128)(2,1)S(1)} %get-tuple-element.91.inverse, ...), custom_call_target="tpu_custom_call", output_to_operand_aliasing={{0}: (5, {}), {1}: (6, {})} | custom-call | flops 67108864 | bytes 2097152 | tf_op jit(solution)/shard_map/backward_0_0/pallas_call | solution.py:457
  82.2 1.9 %collective-permute-done.22.came = f32[4,32,256]{2,1,0:T(8,128)S(1)} collective-permute-done((f32[4,32,256]{2,1,0:T(8,128)S(1)}, f32[4,32,256]{2,1,0:T(8,128)S(1)}, u32[]{:S(2)}, u32[]{:S(2)}) %collective-permute-start.22) | collective-permute-done | bytes 131104 | tf_op jit(solution)/shard_map/ppermute | solution.py:605
  84.1 2.4 %backward_0_1.1 = (f32[8,12,32,256]{3,2,1,0:T(8,128)S(1)}, f32[8,12,32,256]{3,2,1,0:T(8,128)}) custom-call(f32[4,32,256]{2,1,0:T(8,128)S(1)} %collective-permute-done.22.came, bf16[8,12,256,256]{3,2,1,0:T(8,128)(2,1)S(1)} %get-tuple-element.91.inverse, ...), custom_call_target="tpu_custom_call", output_to_operand_aliasing={{0}: (5, {}), {1}: (6, {})} | custom-call | flops 67108864 | bytes 2097152 | tf_op jit(solution)/shard_map/backward_0_1/pallas_call | solution.py:457
  86.5 3.0 %collective-permute-done.21.came = f32[4,32,256]{2,1,0:T(8,128)S(1)} collective-permute-done((f32[4,32,256]{2,1,0:T(8,128)S(1)}, f32[4,32,256]{2,1,0:T(8,128)S(1)}, u32[]{:S(2)}, u32[]{:S(2)}) %collective-permute-start.21) | collective-permute-done | bytes 131104 | tf_op jit(solution)/shard_map/ppermute | solution.py:605
  89.4 3.0 %backward_0_2.1 = (f32[8,12,32,256]{3,2,1,0:T(8,128)S(1)}, f32[8,12,32,256]{3,2,1,0:T(8,128)}) custom-call(f32[4,32,256]{2,1,0:T(8,128)S(1)} %collective-permute-done.21.came, bf16[8,12,256,256]{3,2,1,0:T(8,128)(2,1)S(1)} %get-tuple-element.91.inverse, ...), custom_call_target="tpu_custom_call", output_to_operand_aliasing={{0}: (5, {}), {1}: (6, {})} | custom-call | flops 67108864 | bytes 2097152 | tf_op jit(solution)/shard_map/backward_0_2/pallas_call | solution.py:457
  (15 shorter events, 0.2 us)
Async XLA Ops:
  0.0 11.0 %copy-start = (f32[2,4,12,32,256]{4,3,2,1,0:T(8,128)S(1)}, f32[2,4,12,32,256]{4,3,2,1,0:T(8,128)}, u32[]{:S(2)}) copy-start(f32[2,4,12,32,256]{4,3,2,1,0:T(8,128)} %param.5) | copy-start | bytes 9437188
  0.0 11.0 %copy-start.1 = (f32[2,4,12,32,256]{4,3,2,1,0:T(8,128)S(1)}, f32[2,4,12,32,256]{4,3,2,1,0:T(8,128)}, u32[]{:S(2)}) copy-start(f32[2,4,12,32,256]{4,3,2,1,0:T(8,128)} %param.6) | copy-start | bytes 9437188
  3.4 23.7 %collective-permute-start.2 = (f32[8,2,32,256]{3,2,1,0:T(8,128)S(1)}, f32[8,2,32,256]{3,2,1,0:T(8,128)S(1)}, u32[]{:S(2)}, u32[]{:S(2)}) collective-permute-start(f32[8,2,32,256]{3,2,1,0:T(8,128)S(1)} %get-tuple-element.92), channel_id=1, source_target_pairs={{0,1},{2,3},{4,5},{6,7},{8,9},{10,11},{12,13},{14,15},{16,17},{18,... | collective-permute-start | bytes 1572872 | tf_op jit(solution)/shard_map/ppermute | solution.py:483
  3.5 23.6 %collective-permute-start.3 = (f32[8,2,32,256]{3,2,1,0:T(8,128)S(1)}, f32[8,2,32,256]{3,2,1,0:T(8,128)S(1)}, u32[]{:S(2)}, u32[]{:S(2)}) collective-permute-start(f32[8,2,32,256]{3,2,1,0:T(8,128)S(1)} %get-tuple-element.93), channel_id=1, source_target_pairs={{1,2},{3,4},{5,6},{7,8},{9,10},{11,12},{13,14},{15,16},{17,18},{19... | collective-permute-start | bytes 1572872 | tf_op jit(solution)/shard_map/ppermute | solution.py:483
  8.4 15.1 %collective-permute-start = (f32[8,32,256]{2,1,0:T(8,128)S(1)}, f32[8,32,256]{2,1,0:T(8,128)S(1)}, u32[]{:S(2)}, u32[]{:S(2)}) collective-permute-start(f32[8,32,256]{2,1,0:T(8,128)S(1)} %get-tuple-element.81), channel_id=1, source_target_pairs={{32,0},{64,32},{96,64},{33,1},{65,33},{97,65},{34,2},{66,34},{98,6... | collective-permute-start | bytes 786440 | tf_op jit(solution)/shard_map/ppermute | solution.py:514
  9.7 10.4 %collective-permute-start.1 = (f32[4,32,256]{2,1,0:T(8,128)S(1)}, f32[4,32,256]{2,1,0:T(8,128)S(1)}, u32[]{:S(2)}, u32[]{:S(2)}) collective-permute-start(f32[4,32,256]{2,1,0:T(8,128)S(1)} %get-tuple-element.82._), channel_id=1, source_target_pairs={{32,0},{64,32},{96,64},{33,1},{65,33},{97,65},{34,2},{66,34},{98,6... | collective-permute-start | bytes 393224 | tf_op jit(solution)/shard_map/ppermute | solution.py:503
  20.3 10.5 %collective-permute-start.6 = (f32[4,32,256]{2,1,0:T(8,128)S(1)}, f32[4,32,256]{2,1,0:T(8,128)S(1)}, u32[]{:S(2)}, u32[]{:S(2)}) collective-permute-start(f32[4,32,256]{2,1,0:T(8,128)S(1)} %get-tuple-element.99), channel_id=1, source_target_pairs={{0,32},{1,33},{2,34},{3,35},{4,36},{5,37},{6,38},{7,39},{8,40},{9,... | collective-permute-start | bytes 393224 | tf_op jit(solution)/shard_map/ppermute | solution.py:554
  25.9 5.7 %collective-permute-start.5 = (f32[4,32,256]{2,1,0:T(8,128)S(1)}, f32[4,32,256]{2,1,0:T(8,128)S(1)}, u32[]{:S(2)}, u32[]{:S(2)}) collective-permute-start(f32[4,32,256]{2,1,0:T(8,128)S(1)} %get-tuple-element.98), channel_id=1, source_target_pairs={{0,32},{1,33},{2,34},{3,35},{4,36},{5,37},{6,38},{7,39},{8,40},{9,... | collective-permute-start | bytes 393224 | tf_op jit(solution)/shard_map/ppermute | solution.py:554
  29.5 3.8 %collective-permute-start.4 = (f32[4,32,256]{2,1,0:T(8,128)S(1)}, f32[4,32,256]{2,1,0:T(8,128)S(1)}, u32[]{:S(2)}, u32[]{:S(2)}) collective-permute-start(f32[4,32,256]{2,1,0:T(8,128)S(1)} %get-tuple-element.96), channel_id=1, source_target_pairs={{0,32},{1,33},{2,34},{3,35},{4,36},{5,37},{6,38},{7,39},{8,40},{9,... | collective-permute-start | bytes 393224 | tf_op jit(solution)/shard_map/ppermute | solution.py:554
  30.8 3.1 %collective-permute-start.9 = (f32[4,32,256]{2,1,0:T(8,128)S(1)}, f32[4,32,256]{2,1,0:T(8,128)S(1)}, u32[]{:S(2)}, u32[]{:S(2)}) collective-permute-start(f32[4,32,256]{2,1,0:T(8,128)S(1)} %get-tuple-element.107), channel_id=1, source_target_pairs={{32,64},{33,65},{34,66},{35,67},{36,68},{37,69},{38,70},{39,71},{4... | collective-permute-start | bytes 393224 | tf_op jit(solution)/shard_map/ppermute | solution.py:554
  31.5 3.1 %collective-permute-start.8 = (f32[4,32,256]{2,1,0:T(8,128)S(1)}, f32[4,32,256]{2,1,0:T(8,128)S(1)}, u32[]{:S(2)}, u32[]{:S(2)}) collective-permute-start(f32[4,32,256]{2,1,0:T(8,128)S(1)} %get-tuple-element.106), channel_id=1, source_target_pairs={{32,64},{33,65},{34,66},{35,67},{36,68},{37,69},{38,70},{39,71},{4... | collective-permute-start | bytes 393224 | tf_op jit(solution)/shard_map/ppermute | solution.py:554
  33.3 2.1 %collective-permute-start.7 = (f32[4,32,256]{2,1,0:T(8,128)S(1)}, f32[4,32,256]{2,1,0:T(8,128)S(1)}, u32[]{:S(2)}, u32[]{:S(2)}) collective-permute-start(f32[4,32,256]{2,1,0:T(8,128)S(1)} %get-tuple-element.105), channel_id=1, source_target_pairs={{32,64},{33,65},{34,66},{35,67},{36,68},{37,69},{38,70},{39,71},{4... | collective-permute-start | bytes 393224 | tf_op jit(solution)/shard_map/ppermute | solution.py:554
  34.0 2.1 %collective-permute-start.12 = (f32[4,32,256]{2,1,0:T(8,128)S(1)}, f32[4,32,256]{2,1,0:T(8,128)S(1)}, u32[]{:S(2)}, u32[]{:S(2)}) collective-permute-start(f32[4,32,256]{2,1,0:T(8,128)S(1)} %get-tuple-element.115), channel_id=1, source_target_pairs={{64,96},{65,97},{66,98},{67,99},{68,100},{69,101},{70,102},{71,103... | collective-permute-start | bytes 393224 | tf_op jit(solution)/shard_map/ppermute | solution.py:554
  34.7 1.4 %collective-permute-start.11 = (f32[4,32,256]{2,1,0:T(8,128)S(1)}, f32[4,32,256]{2,1,0:T(8,128)S(1)}, u32[]{:S(2)}, u32[]{:S(2)}) collective-permute-start(f32[4,32,256]{2,1,0:T(8,128)S(1)} %get-tuple-element.114), channel_id=1, source_target_pairs={{64,96},{65,97},{66,98},{67,99},{68,100},{69,101},{70,102},{71,103... | collective-permute-start | bytes 393224 | tf_op jit(solution)/shard_map/ppermute | solution.py:554
  35.4 0.8 collective-permute-start.10
  36.2 7.5 %collective-permute-start.13 = (f32[8,2,32,256]{3,2,1,0:T(8,128)S(1)}, f32[8,2,32,256]{3,2,1,0:T(8,128)S(1)}, u32[]{:S(2)}, u32[]{:S(2)}) collective-permute-start(f32[8,2,32,256]{3,2,1,0:T(8,128)S(1)} %get-tuple-element.120), channel_id=1, source_target_pairs={{0,1},{2,3},{4,5},{6,7},{8,9},{10,11},{12,13},{14,15},{16,17},{18,... | collective-permute-start | bytes 1572872 | tf_op jit(solution)/shard_map/ppermute | solution.py:483
  36.3 12.6 %collective-permute-start.14 = (f32[8,2,32,256]{3,2,1,0:T(8,128)S(1)}, f32[8,2,32,256]{3,2,1,0:T(8,128)S(1)}, u32[]{:S(2)}, u32[]{:S(2)}) collective-permute-start(f32[8,2,32,256]{3,2,1,0:T(8,128)S(1)} %get-tuple-element.121), channel_id=1, source_target_pairs={{1,2},{3,4},{5,6},{7,8},{9,10},{11,12},{13,14},{15,16},{17,18},{19... | collective-permute-start | bytes 1572872 | tf_op jit(solution)/shard_map/ppermute | solution.py:483
  41.7 8.5 %collective-permute-start.17 = (f32[4,32,256]{2,1,0:T(8,128)S(1)}, f32[4,32,256]{2,1,0:T(8,128)S(1)}, u32[]{:S(2)}, u32[]{:S(2)}) collective-permute-start(f32[4,32,256]{2,1,0:T(8,128)S(1)} %get-tuple-element.131), channel_id=1, source_target_pairs={{96,64},{97,65},{98,66},{99,67},{100,68},{101,69},{102,70},{103,71... | collective-permute-start | bytes 393224 | tf_op jit(solution)/shard_map/ppermute | solution.py:605
  43.0 8.1 %collective-permute-start.16 = (f32[4,32,256]{2,1,0:T(8,128)S(1)}, f32[4,32,256]{2,1,0:T(8,128)S(1)}, u32[]{:S(2)}, u32[]{:S(2)}) collective-permute-start(f32[4,32,256]{2,1,0:T(8,128)S(1)} %get-tuple-element.130), channel_id=1, source_target_pairs={{96,64},{97,65},{98,66},{99,67},{100,68},{101,69},{102,70},{103,71... | collective-permute-start | bytes 393224 | tf_op jit(solution)/shard_map/ppermute | solution.py:605
  49.5 2.4 %collective-permute-start.15 = (f32[4,32,256]{2,1,0:T(8,128)S(1)}, f32[4,32,256]{2,1,0:T(8,128)S(1)}, u32[]{:S(2)}, u32[]{:S(2)}) collective-permute-start(f32[4,32,256]{2,1,0:T(8,128)S(1)} %get-tuple-element.128), channel_id=1, source_target_pairs={{96,64},{97,65},{98,66},{99,67},{100,68},{101,69},{102,70},{103,71... | collective-permute-start | bytes 393224 | tf_op jit(solution)/shard_map/ppermute | solution.py:605
  50.4 2.4 %collective-permute-start.20 = (f32[4,32,256]{2,1,0:T(8,128)S(1)}, f32[4,32,256]{2,1,0:T(8,128)S(1)}, u32[]{:S(2)}, u32[]{:S(2)}) collective-permute-start(f32[4,32,256]{2,1,0:T(8,128)S(1)} %get-tuple-element.140), channel_id=1, source_target_pairs={{64,32},{65,33},{66,34},{67,35},{68,36},{69,37},{70,38},{71,39},{7... | collective-permute-start | bytes 393224 | tf_op jit(solution)/shard_map/ppermute | solution.py:605
  51.3 3.0 %collective-permute-start.19 = (f32[4,32,256]{2,1,0:T(8,128)S(1)}, f32[4,32,256]{2,1,0:T(8,128)S(1)}, u32[]{:S(2)}, u32[]{:S(2)}) collective-permute-start(f32[4,32,256]{2,1,0:T(8,128)S(1)} %get-tuple-element.139), channel_id=1, source_target_pairs={{64,32},{65,33},{66,34},{67,35},{68,36},{69,37},{70,38},{71,39},{7... | collective-permute-start | bytes 393224 | tf_op jit(solution)/shard_map/ppermute | solution.py:605
  52.1 3.6 %collective-permute-start.18 = (f32[4,32,256]{2,1,0:T(8,128)S(1)}, f32[4,32,256]{2,1,0:T(8,128)S(1)}, u32[]{:S(2)}, u32[]{:S(2)}) collective-permute-start(f32[4,32,256]{2,1,0:T(8,128)S(1)} %get-tuple-element.138), channel_id=1, source_target_pairs={{64,32},{65,33},{66,34},{67,35},{68,36},{69,37},{70,38},{71,39},{7... | collective-permute-start | bytes 393224 | tf_op jit(solution)/shard_map/ppermute | solution.py:605
  53.0 26.9 %collective-permute-start.23 = (f32[4,32,256]{2,1,0:T(8,128)S(1)}, f32[4,32,256]{2,1,0:T(8,128)S(1)}, u32[]{:S(2)}, u32[]{:S(2)}) collective-permute-start(f32[4,32,256]{2,1,0:T(8,128)S(1)} %get-tuple-element.149), channel_id=1, source_target_pairs={{32,0},{33,1},{34,2},{35,3},{36,4},{37,5},{38,6},{39,7},{40,8},{41... | collective-permute-start | bytes 393224 | tf_op jit(solution)/shard_map/ppermute | solution.py:605
  54.5 29.6 %collective-permute-start.22 = (f32[4,32,256]{2,1,0:T(8,128)S(1)}, f32[4,32,256]{2,1,0:T(8,128)S(1)}, u32[]{:S(2)}, u32[]{:S(2)}) collective-permute-start(f32[4,32,256]{2,1,0:T(8,128)S(1)} %get-tuple-element.148), channel_id=1, source_target_pairs={{32,0},{33,1},{34,2},{35,3},{36,4},{37,5},{38,6},{39,7},{40,8},{41... | collective-permute-start | bytes 393224 | tf_op jit(solution)/shard_map/ppermute | solution.py:605
  56.0 33.5 %collective-permute-start.21 = (f32[4,32,256]{2,1,0:T(8,128)S(1)}, f32[4,32,256]{2,1,0:T(8,128)S(1)}, u32[]{:S(2)}, u32[]{:S(2)}) collective-permute-start(f32[4,32,256]{2,1,0:T(8,128)S(1)} %get-tuple-element.147), channel_id=1, source_target_pairs={{32,0},{33,1},{34,2},{35,3},{36,4},{37,5},{38,6},{39,7},{40,8},{41... | collective-permute-start | bytes 393224 | tf_op jit(solution)/shard_map/ppermute | solution.py:605

commit v4 on v3

--- a/solution.py
+++ b/solution.py
@@ -77,9 +77,19 @@
     return ice[q // PER, q % PER, lane].astype(jnp.float32)
 
 
-def near_prep_kernel(ice_hbm, st_hbm, now, later, ice, sem):
+def prep_kernel(
+    ice_hbm, st_hbm, couple_hbm, inv_hbm, now, later, edge_in, edge_out, couple, mask, inverse, ice, sem, sem_inv
+):
+    even = is_even()
+    lane_in = jnp.where(even, LANES - 2, 0)
+    lane_out = jnp.where(even, 0, LANES - 2)
+    copies = [
+        pltpu.make_async_copy(ice_hbm, ice, sem.at[0]),
+        pltpu.make_async_copy(couple_hbm, couple, sem.at[1]),
+        pltpu.make_async_copy(st_hbm.at[:, pl.ds(lane_out, 2)], edge_out, sem.at[2]),
+        pltpu.make_async_copy(st_hbm.at[:, pl.ds(lane_in, 2)], edge_in, sem.at[3]),
+    ]
     at = 0
-    copies = [ice_copy(ice_hbm, ice, sem.at[0])]
     for lanes in FORWARD:
         for a, n in runs_of(lanes):
             if lanes == FORWARD[0]:
@@ -90,39 +100,32 @@
             copies.append(
                 pltpu.make_async_copy(st_hbm.at[0, pl.ds(a, n)], target, sem.at[len(copies)])
             )
+
+    def own(q):
+        return lane_copies(inv_hbm, inverse, q, FORWARD[0], sem_inv)
+
     for copy in copies:
         copy.start()
-    for copy in copies:
-        copy.wait()
-    for j, lane in enumerate(FORWARD[0]):
-        now[j] = ice_weight(ice, 0, lane) * now[j]
-    for j, lane in enumerate(FORWARD[1] + FORWARD[2]):
-        later[j] = ice_weight(ice, 0, lane) * later[j]
-
-
-def prep_kernel(_, ice_hbm, st_hbm, couple_hbm, edge_in, edge_out, couple, mask, ice, sem):
-    even = is_even()
-    lane_in = jnp.where(even, LANES - 2, 0)
-    lane_out = jnp.where(even, 0, LANES - 2)
-    copies = [
-        ice_copy(ice_hbm, ice, sem.at[0]),
-        pltpu.make_async_copy(st_hbm.at[:, pl.ds(lane_out, 2)], edge_out, sem.at[1]),
-        pltpu.make_async_copy(st_hbm.at[:, pl.ds(lane_in, 2)], edge_in, sem.at[2]),
-        pltpu.make_async_copy(couple_hbm, couple, sem.at[3]),
-    ]
-    for copy in copies:
-        copy.start()
+    start_all(own)
+
+    def ice_weight(q, lane):
+        return ice[q // PER, q % PER, lane].astype(jnp.float32)
+
     copies[0].wait()
     for q in range(COLS):
         for lane in range(LANES):
-            mask[q, pl.ds(lane, 1), :] = jnp.full((1, BS), ice_weight(ice, q, lane), jnp.float32)
-    copies[1].wait()
-    copies[2].wait()
+            mask[q, pl.ds(lane, 1), :] = jnp.full((1, BS), ice_weight(q, lane), jnp.float32)
+    for copy in copies[1:]:
+        copy.wait()
     for q in range(COLS):
         for j in range(2):
-            edge_out[q, j] = ice_weight(ice, q, lane_out + j) * edge_out[q, j]
-            edge_in[q, j] = ice_weight(ice, q, lane_in + j) * edge_in[q, j]
-    copies[3].wait()
+            edge_out[q, j] = ice_weight(q, lane_out + j) * edge_out[q, j]
+            edge_in[q, j] = ice_weight(q, lane_in + j) * edge_in[q, j]
+    for j, lane in enumerate(FORWARD[0]):
+        now[j] = weight(mask, 0, lane) * now[j]
+    for j, lane in enumerate(FORWARD[1] + FORWARD[2]):
+        later[j] = weight(mask, 0, lane) * later[j]
+    wait_all(own)
 
 
 def halo_of(even, halo_in, halo_out, q, lane):
@@ -182,16 +185,13 @@
 
 
 def sweep_first(
-    lanes, rs, start, source, inverse, couple, mask, field, sent, columns, halo, edges, arriving=None
+    lanes, rs, start, source, inverse, couple, mask, field, sent, columns, halo, edges
 ):
     for j in range(len(lanes)):
         sent[j] = jnp.zeros((R, BS), jnp.float32)
     make_source(lanes, 0, rs, start, couple, mask, source, halo)
 
     def step(q, _):
-        if arriving is not None:
-            for copy in arriving(q):
-                copy.wait()
         forward_chain(lanes, q, source, inverse, couple, mask, field, sent, edges)
         make_source(
             lanes, jnp.minimum(q + 1, columns - 1), rs, start, couple, mask, source, halo
@@ -201,52 +201,18 @@
     lax.fori_loop(0, columns, step, 0)
 
 
-def first_kernel(inv_hbm, rs, start, couple, mask, inverse, source, field, sent, sem, sem_next):
-    first = lax.axis_index("strip") == 0
-
-    @pl.when(first)
-    def _():
-        def own(q):
-            return lane_copies(inv_hbm, inverse, q, FORWARD[0], sem)
-
+def first_kernel(inv_hbm, rs, start, couple, mask, _, inverse, source, field, sent, sem):
+    @pl.when(lax.axis_index("strip") == 0)
+    def _():
         def following(q):
-            return lane_copies(inv_hbm, inverse, q, FORWARD[1], sem_next)
-
-        start_all(own)
+            return lane_copies(inv_hbm, inverse, q, FORWARD[1], sem)
+
         start_all(following)
         field[0] = jnp.zeros((LANES, R, BS), jnp.float32)
         sweep_first(
-            FORWARD[0],
-            rs,
-            start,
-            source,
-            inverse,
-            couple,
-            mask,
-            field,
-            sent,
-            COLS - 1,
-            None,
-            None,
-            own,
-        )
-        for copy in own(COLS - 1):
-            copy.wait()
+            FORWARD[0], rs, start, source, inverse, couple, mask, field, sent, COLS - 1, None, None
+        )
         wait_all(following)
-
-    @pl.when(jnp.logical_not(first))
-    def _():
-        def every(q):
-            return lane_copies(inv_hbm, inverse, q, range(LANES), sem)
-
-        start_all(every)
-
-        def step(q, _):
-            make_source(range(LANES), q, rs, start, couple, mask, source)
-            return 0
-
-        lax.fori_loop(0, COLS - 1, step, 0)
-        wait_all(every)
 
 
 def tail_kernel(now, inverse, rs, start, couple, mask, *refs):
@@ -296,20 +262,37 @@
 
 
 def inner_kernel(later, inv_hbm, rs, start, couple, mask, *refs):
-    inverse, source, field, sent, sem = refs[3:]
-    lanes, q = FORWARD[1], COLS - 1
-
-    @pl.when(lax.axis_index("strip") == 0)
-    def _():
-        def following(q):
-            return lane_copies(inv_hbm, inverse, q, FORWARD[2], sem)
-
+    inverse, source, field, sent, sem, sem_next = refs[3:]
+    lanes, q_last = FORWARD[1], COLS - 1
+    first = lax.axis_index("strip") == 0
+
+    def following(q):
+        return lane_copies(inv_hbm, inverse, q, FORWARD[2], sem)
+
+    def own(q):
+        return lane_copies(inv_hbm, inverse, q, lanes, sem_next)
+
+    @pl.when(first)
+    def _():
         start_all(following)
         sweep_first(
             lanes, rs, start, source, inverse, couple, mask, field, sent, COLS - 1, None, None
         )
-        make_source(lanes, q, rs, start, couple, mask, source, None, later)
-        forward_chain(lanes, q, source, inverse, couple, mask, field, sent)
+        make_source(lanes, q_last, rs, start, couple, mask, source, None, later)
+        forward_chain(lanes, q_last, source, inverse, couple, mask, field, sent)
+        wait_all(following)
+
+    @pl.when(jnp.logical_not(first))
+    def _():
+        start_all(own)
+        start_all(following)
+
+        def step(q, _):
+            make_source(range(LANES), q, rs, start, couple, mask, source)
+            return 0
+
+        lax.fori_loop(0, COLS - 1, step, 0)
+        wait_all(own)
         wait_all(following)
 
 
@@ -449,7 +432,7 @@
     return VMEM(shape, dtype)
 
 
-def run(kernel, name, operands, outs, scratch, aliases=None):
+def run(kernel, name, operands, outs, scratch, aliases=None, cost=0):
     arrays = [
         pltpu.with_memory_space_constraint(a, space) if space in (VMEM, HBM) else a
         for a, space in operands
@@ -464,7 +447,7 @@
         input_output_aliases=aliases or {},
         compiler_params=pltpu.CompilerParams(vmem_limit_bytes=8 * 2**20),
         cost_estimate=pl.CostEstimate(
-            flops=2**26, bytes_accessed=2**21, transcendentals=0
+            flops=2 ** (26 + cost), bytes_accessed=2 ** (21 + cost), transcendentals=0
         ),
     )(*arrays)
 
@@ -491,38 +474,30 @@
     def piece(lanes):
         return (len(lanes), R, BS)
 
-    ice = pltpu.SMEM(ice_mask.shape, jnp.int32)
-    now, later = run(
-        near_prep_kernel,
-        "near_prep",
-        [(ice_mask, HBM), (start, HBM)],
-        made(piece(FORWARD[0]), LATER),
-        [ice, dma((6,))],
-    )
-    now_sent = now
-    now = lax.ppermute(now, "strip", to_back)
-    edge_in, edge_out, coefs, mask = run(
+    blocks = [(vmem(BLOCKS, jnp.bfloat16), VMEM)]
+    inv_hbm = [(inverse, HBM)]
+    now, later, edge_in, edge_out, coefs, mask, inverse = run(
         prep_kernel,
         "prep",
-        inside(now_sent)
-        + [(ice_mask, HBM), (start, HBM), (couple.transpose(0, 1, 3, 2, 4), HBM)],
-        made(EDGE, EDGE, COEFS, WEIGHTS),
-        [ice, dma((4,))],
+        [(ice_mask, HBM), (start, HBM), (couple.transpose(0, 1, 3, 2, 4), HBM)] + inv_hbm,
+        made(piece(FORWARD[0]), LATER, EDGE, EDGE, COEFS, WEIGHTS) + blocks,
+        [pltpu.SMEM(ice_mask.shape, jnp.int32), dma((9,)), dma((COLS,))],
     )
+    now = lax.ppermute(now, "strip", to_back)
+    later = lax.ppermute(later, "strip", to_back)
     halo_out = swapped(edge_out, pairs_out)
     halo_in = swapped(edge_in, pairs_in)
-    later = lax.ppermute(later, "strip", to_back)
 
     sents = {}
-    blocks = [(vmem(BLOCKS, jnp.bfloat16), VMEM)]
-    inv_hbm = [(inverse, HBM)]
     rest = inside(rs, start, coefs, mask)
     inverse, source, field, sent = run(
         first_kernel,
         "first",
-        inv_hbm + rest,
+        inv_hbm + rest + inside(inverse),
         blocks + made(FIELD, FIELD_MORE, piece(FORWARD[0])),
-        [dma((COLS,)), dma((COLS,))],
+        [dma((COLS,))],
+        {5: 0},
+        cost=-10,
     )
     source, field, sents[0, 0] = run(
         tail_kernel,
@@ -531,13 +506,14 @@
         made(FIELD, FIELD_MORE, piece(FORWARD[0])),
         [],
         {6: 0, 7: 1, 8: 2},
+        cost=8,
     )
     inverse, source, field, sents[0, 1] = run(
         inner_kernel,
         "inner",
         inside(later) + inv_hbm + rest + inside(inverse, source, field),
         blocks + made(FIELD, FIELD_MORE, piece(FORWARD[1])),
-        [dma((COLS,))],
+        [dma((COLS,)), dma((COLS,))],
         {6: 0, 7: 1, 8: 2},
     )
     source, field, edge_in, edge_out, sents[0, 2] = run(

time: 92.9 us -> 88.2 us (0.949)
  waiting for transfers between devices: 39.3 us -> 33.1 us
  starting transfers between devices: 30 us -> 32.8 us
  Pallas kernels: 22.6 us -> 21 us
    ppermute x1, waiting for transfers between devices: 5.48 us -> 0.01 us  [on_device(): now = lax.ppermute(now, 'strip', to_back)]
    ppermute x9, starting transfers between devices: 9.72 us -> 12.3 us  [on_device(): came = lax.ppermute(sents[stage - 1, chunk], 'strip', [(stage - 1, stage)])]
    pallas_call x27 -> x26, Pallas kernels: 22.6 us -> 21 us  [run(): pl.pallas_call(kernel, name=name, out_shape=[o for o, _ in outs], in_spec...]
  transfers between devices with their start and end apart: 24 -> 24, of which waited for: 6 -> 5; matrix products, arithmetic and copies ran while one was open for 0% -> 0% of each run, Pallas kernels for 17% -> 17%
where the time goes in v4:
time: 88.2 us; the launch traced here: 87.5 us
  waiting for transfers between devices  33.1 us (38%)
  starting transfers between devices  32.8 us (37%)
  Pallas kernels  21 us (24%)
    ppermute x9, waiting for transfers between devices, on_device(): came = lax.ppermute(sents[stage + 1, chunk], 'strip', [(stage + 1, stage)])  26.9 us
    pallas_call x26, Pallas kernels, run(): pl.pallas_call(kernel, name=name, out_shape=[o for o, _ in outs], in_spec...  21 us
    ppermute x9, starting transfers between devices, on_device(): came = lax.ppermute(sents[stage - 1, chunk], 'strip', [(stage - 1, stage)])  12.3 us
    ppermute x4, starting transfers between devices, swapped(): return lax.ppermute(value, 'tile', pairs + [(b, a) for a, b in pairs])  9.87 us
    ppermute x9, starting transfers between devices, on_device(): came = lax.ppermute(sents[stage + 1, chunk], 'strip', [(stage + 1, stage)])  7.89 us
    ppermute x4, waiting for transfers between devices, swapped(): return lax.ppermute(value, 'tile', pairs + [(b, a) for a, b in pairs])  5.16 us
  transfers between devices with their start and end apart: 24, of which 5 were waited for; matrix products, arithmetic and copies ran while one was open for 0% of the time, Pallas kernels for 17%

profile of v4, /device:TPU:96, one launch (start us, length us, event | category | flops | bytes accessed | tf_op | source)
XLA Modules:
  0.0 87.5 jit_solution(13276908055392460798)
XLA Ops:
  0.0 3.0 %prep.1 = (f32[4,32,256]{2,1,0:T(8,128)S(1)}, f32[8,32,256]{2,1,0:T(8,128)S(1)}, f32[8,2,32,256]{3,2,1,0:T(8,128)S(1)}, f32[8,2,32,256]{3,2,1,0:T(8,128)S(1)}, f...) custom-call(s32[2,4,12]{2,1,0:T(4,128)} %ice_hbm.1, ...), custom_call_target="tpu_custom_call" | custom-call | flops 67108864 | bytes 2097152 | tf_op jit(solution)/shard_map/prep/pallas_call | solution.py:440
  3.1 1.4 %collective-permute-start.1 = (f32[4,32,256]{2,1,0:T(8,128)S(1)}, f32[4,32,256]{2,1,0:T(8,128)S(1)}, u32[]{:S(2)}, u32[]{:S(2)}) collective-permute-start(f32[4,32,256]{2,1,0:T(8,128)S(1)} %get-tuple-element.87), channel_id=1, source_target_pairs={{32,0},{64,32},{96,64},{33,1},{65,33},{97,65},{34,2},{66,34},{98,6... | collective-permute-start | bytes 393224 | tf_op jit(solution)/shard_map/ppermute | solution.py:486
  4.5 1.3 %collective-permute-start = (f32[8,32,256]{2,1,0:T(8,128)S(1)}, f32[8,32,256]{2,1,0:T(8,128)S(1)}, u32[]{:S(2)}, u32[]{:S(2)}) collective-permute-start(f32[8,32,256]{2,1,0:T(8,128)S(1)} %get-tuple-element.82), channel_id=1, source_target_pairs={{32,0},{64,32},{96,64},{33,1},{65,33},{97,65},{34,2},{66,34},{98,6... | collective-permute-start | bytes 786440 | tf_op jit(solution)/shard_map/ppermute | solution.py:487
  5.8 0.1 collective-permute-start.2
  5.9 4.9 %collective-permute-start.3 = (f32[8,2,32,256]{3,2,1,0:T(8,128)S(1)}, f32[8,2,32,256]{3,2,1,0:T(8,128)S(1)}, u32[]{:S(2)}, u32[]{:S(2)}) collective-permute-start(f32[8,2,32,256]{3,2,1,0:T(8,128)S(1)} %get-tuple-element.95), channel_id=1, source_target_pairs={{1,2},{3,4},{5,6},{7,8},{9,10},{11,12},{13,14},{15,16},{17,18},{19... | collective-permute-start | bytes 1572872 | tf_op jit(solution)/shard_map/ppermute | solution.py:466
  10.8 2.2 %first.1 = (bf16[8,12,256,256]{3,2,1,0:T(8,128)(2,1)S(1)}, f32[8,12,32,256]{3,2,1,0:T(8,128)S(1)}, f32[9,12,32,256]{3,2,1,0:T(8,128)S(1)}, f32[4,32,256]{2,1,0:T(8,128)S(1)}) custom-call(bf16[8,12,256,256]{3,2,1,0:T(8,128)(2,1)} %bitcast.18, f32[8,12,32,256]{3,2,1,0:T(8,128)S(1)} %bitcast.5, ...), custom_call_target="tpu_custom_call", output_to_operand_aliasing={{0}: (5, {})} | custom-call | flops 65536 | bytes 2048 | tf_op jit(solution)/shard_map/first/pallas_call | solution.py:440
  13.0 0.0 collective-permute-done.1.now
  13.0 0.3 tail.1
  13.3 2.8 %collective-permute-start.6 = (f32[4,32,256]{2,1,0:T(8,128)S(1)}, f32[4,32,256]{2,1,0:T(8,128)S(1)}, u32[]{:S(2)}, u32[]{:S(2)}) collective-permute-start(f32[4,32,256]{2,1,0:T(8,128)S(1)} %get-tuple-element.101), channel_id=1, source_target_pairs={{0,32},{1,33},{2,34},{3,35},{4,36},{5,37},{6,38},{7,39},{8,40},{9,... | collective-permute-start | bytes 393224 | tf_op jit(solution)/shard_map/ppermute | solution.py:530
  16.1 0.0 collective-permute-done.later
  16.1 2.5 %inner.1 = (bf16[8,12,256,256]{3,2,1,0:T(8,128)(2,1)S(1)}, f32[8,12,32,256]{3,2,1,0:T(8,128)S(1)}, f32[9,12,32,256]{3,2,1,0:T(8,128)S(1)}, f32[4,32,256]{2,1,0:T(8,128)S(1)}) custom-call(f32[8,32,256]{2,1,0:T(8,128)S(1)} %collective-permute-done.later, ...), custom_call_target="tpu_custom_call", output_to_operand_aliasing={{0}: (6, {}), {1}: (7, {}), {2}: (8, {})} | custom-call | flops 67108864 | bytes 2097152 | tf_op jit(solution)/shard_map/inner/pallas_call | solution.py:440
  18.6 4.3 %collective-permute-start.5 = (f32[4,32,256]{2,1,0:T(8,128)S(1)}, f32[4,32,256]{2,1,0:T(8,128)S(1)}, u32[]{:S(2)}, u32[]{:S(2)}) collective-permute-start(f32[4,32,256]{2,1,0:T(8,128)S(1)} %get-tuple-element.100), channel_id=1, source_target_pairs={{0,32},{1,33},{2,34},{3,35},{4,36},{5,37},{6,38},{7,39},{8,40},{9,... | collective-permute-start | bytes 393224 | tf_op jit(solution)/shard_map/ppermute | solution.py:530
  22.9 0.0 collective-permute-done.2.halo_in
  22.9 0.0 collective-permute-done.3.halo_out
  22.9 2.3 %outer.1 = (f32[8,12,32,256]{3,2,1,0:T(8,128)S(1)}, f32[9,12,32,256]{3,2,1,0:T(8,128)S(1)}, f32[8,2,32,256]{3,2,1,0:T(8,128)S(1)}, f32[8,2,32,256]{3,2,1,0:T(8,128)S(1)}, f32[4,32,256]{2,1,0:T(8,128)S(1)}) custom-call(f32[4,32,256]{2,1,0:T(8,128)S(1)} %collective-permute-done.1.now, ...), custom_call_target="tpu_custom_call", output_to_operand_aliasing={{0}: (9, {}), {1}: (10, {})} | custom-call | flops 67108864 | bytes 2097152 | tf_op jit(solution)/shard_map/outer/pallas_call | solution.py:440
  25.2 1.3 %collective-permute-start.4 = (f32[4,32,256]{2,1,0:T(8,128)S(1)}, f32[4,32,256]{2,1,0:T(8,128)S(1)}, u32[]{:S(2)}, u32[]{:S(2)}) collective-permute-start(f32[4,32,256]{2,1,0:T(8,128)S(1)} %get-tuple-element.98), channel_id=1, source_target_pairs={{0,32},{1,33},{2,34},{3,35},{4,36},{5,37},{6,38},{7,39},{8,40},{9,... | collective-permute-start | bytes 393224 | tf_op jit(solution)/shard_map/ppermute | solution.py:530
  26.5 0.0 collective-permute-done.6.came
  26.5 0.7 collective-permute-start.9
  27.2 0.0 collective-permute-done.5.came
  27.2 0.7 collective-permute-start.8
  27.9 1.1 %collective-permute-done.4.came = f32[4,32,256]{2,1,0:T(8,128)S(1)} collective-permute-done((f32[4,32,256]{2,1,0:T(8,128)S(1)}, f32[4,32,256]{2,1,0:T(8,128)S(1)}, u32[]{:S(2)}, u32[]{:S(2)}) %collective-permute-start.4) | collective-permute-done | bytes 131104 | tf_op jit(solution)/shard_map/ppermute | solution.py:530
  29.0 0.7 collective-permute-start.7
  29.6 0.0 collective-permute-done.9.came
  29.7 0.7 collective-permute-start.12
  30.4 0.0 collective-permute-done.8.came
  30.4 0.7 collective-permute-start.11
  31.1 0.0 collective-permute-done.7.came
  31.1 0.7 collective-permute-start.10
  31.8 0.0 collective-permute-done.12.came
  31.8 0.0 collective-permute-done.11.came
  31.9 0.0 collective-permute-done.10.came
  31.9 0.1 collective-permute-start.13
  32.0 4.8 %collective-permute-start.14 = (f32[8,2,32,256]{3,2,1,0:T(8,128)S(1)}, f32[8,2,32,256]{3,2,1,0:T(8,128)S(1)}, u32[]{:S(2)}, u32[]{:S(2)}) collective-permute-start(f32[8,2,32,256]{3,2,1,0:T(8,128)S(1)} %get-tuple-element.123), channel_id=1, source_target_pairs={{1,2},{3,4},{5,6},{7,8},{9,10},{11,12},{13,14},{15,16},{17,18},{19... | collective-permute-start | bytes 1572872 | tf_op jit(solution)/shard_map/ppermute | solution.py:466
  36.9 0.6 last_0.1
  37.5 0.7 collective-permute-start.17
  38.1 0.6 last_1.1
  38.8 0.7 collective-permute-start.16
  39.4 0.0 collective-permute-done.13.halo_in
  39.5 5.2 %collective-permute-done.14.halo_out = f32[8,2,32,256]{3,2,1,0:T(8,128)S(1)} collective-permute-done((f32[8,2,32,256]{3,2,1,0:T(8,128)S(1)}, f32[8,2,32,256]{3,2,1,0:T(8,128)S(1)}, u32[]{:S(2)}, u32[]{:S(2)}) %collective-permute-start.14) | collective-permute-done | bytes 524320 | tf_op jit(solution)/shard_map/ppermute | solution.py:466
  44.6 0.6 last_2.1
  45.2 0.7 collective-permute-start.15
  45.9 0.0 collective-permute-done.17.came
  45.9 0.2 backward_2_0.1
  46.1 0.7 collective-permute-start.20
  46.8 0.0 collective-permute-done.16.came
  46.8 0.2 backward_2_1.1
  47.0 0.7 collective-permute-start.19
  47.6 0.0 collective-permute-done.15.came
  47.6 0.2 backward_2_2.1
  47.8 0.7 collective-permute-start.18
  48.5 0.0 collective-permute-done.20.came
  48.5 0.2 backward_1_0.1
  48.7 1.3 %collective-permute-start.23 = (f32[4,32,256]{2,1,0:T(8,128)S(1)}, f32[4,32,256]{2,1,0:T(8,128)S(1)}, u32[]{:S(2)}, u32[]{:S(2)}) collective-permute-start(f32[4,32,256]{2,1,0:T(8,128)S(1)} %get-tuple-element.151), channel_id=1, source_target_pairs={{32,0},{33,1},{34,2},{35,3},{36,4},{37,5},{38,6},{39,7},{40,8},{41... | collective-permute-start | bytes 393224 | tf_op jit(solution)/shard_map/ppermute | solution.py:581
  50.0 0.2 backward_1_1.1
  50.2 1.3 %collective-permute-start.22 = (f32[4,32,256]{2,1,0:T(8,128)S(1)}, f32[4,32,256]{2,1,0:T(8,128)S(1)}, u32[]{:S(2)}, u32[]{:S(2)}) collective-permute-start(f32[4,32,256]{2,1,0:T(8,128)S(1)} %get-tuple-element.150), channel_id=1, source_target_pairs={{32,0},{33,1},{34,2},{35,3},{36,4},{37,5},{38,6},{39,7},{40,8},{41... | collective-permute-start | bytes 393224 | tf_op jit(solution)/shard_map/ppermute | solution.py:581
  51.5 0.0 collective-permute-done.18.came
  51.5 0.2 backward_1_2.1
  51.6 1.3 %collective-permute-start.21 = (f32[4,32,256]{2,1,0:T(8,128)S(1)}, f32[4,32,256]{2,1,0:T(8,128)S(1)}, u32[]{:S(2)}, u32[]{:S(2)}) collective-permute-start(f32[4,32,256]{2,1,0:T(8,128)S(1)} %get-tuple-element.149), channel_id=1, source_target_pairs={{32,0},{33,1},{34,2},{35,3},{36,4},{37,5},{38,6},{39,7},{40,8},{41... | collective-permute-start | bytes 393224 | tf_op jit(solution)/shard_map/ppermute | solution.py:581
  52.9 24.6 %collective-permute-done.23.came = f32[4,32,256]{2,1,0:T(8,128)S(1)} collective-permute-done((f32[4,32,256]{2,1,0:T(8,128)S(1)}, f32[4,32,256]{2,1,0:T(8,128)S(1)}, u32[]{:S(2)}, u32[]{:S(2)}) %collective-permute-start.23) | collective-permute-done | bytes 131104 | tf_op jit(solution)/shard_map/ppermute | solution.py:581
  77.5 2.3 %backward_0_0.1 = (f32[8,12,32,256]{3,2,1,0:T(8,128)S(1)}, f32[8,12,32,256]{3,2,1,0:T(8,128)}) custom-call(f32[4,32,256]{2,1,0:T(8,128)S(1)} %collective-permute-done.23.came, bf16[8,12,256,256]{3,2,1,0:T(8,128)(2,1)S(1)} %get-tuple-element.93.inverse, ...), custom_call_target="tpu_custom_call", output_to_operand_aliasing={{0}: (5, {}), {1}: (6, {})} | custom-call | flops 67108864 | bytes 2097152 | tf_op jit(solution)/shard_map/backward_0_0/pallas_call | solution.py:440
  79.8 2.1 %collective-permute-done.22.came = f32[4,32,256]{2,1,0:T(8,128)S(1)} collective-permute-done((f32[4,32,256]{2,1,0:T(8,128)S(1)}, f32[4,32,256]{2,1,0:T(8,128)S(1)}, u32[]{:S(2)}, u32[]{:S(2)}) %collective-permute-start.22) | collective-permute-done | bytes 131104 | tf_op jit(solution)/shard_map/ppermute | solution.py:581
  81.9 2.4 %backward_0_1.1 = (f32[8,12,32,256]{3,2,1,0:T(8,128)S(1)}, f32[8,12,32,256]{3,2,1,0:T(8,128)}) custom-call(f32[4,32,256]{2,1,0:T(8,128)S(1)} %collective-permute-done.22.came, bf16[8,12,256,256]{3,2,1,0:T(8,128)(2,1)S(1)} %get-tuple-element.93.inverse, ...), custom_call_target="tpu_custom_call", output_to_operand_aliasing={{0}: (5, {}), {1}: (6, {})} | custom-call | flops 67108864 | bytes 2097152 | tf_op jit(solution)/shard_map/backward_0_1/pallas_call | solution.py:440
  84.3 0.2 collective-permute-done.21.came
  84.5 3.0 %backward_0_2.1 = (f32[8,12,32,256]{3,2,1,0:T(8,128)S(1)}, f32[8,12,32,256]{3,2,1,0:T(8,128)}) custom-call(f32[4,32,256]{2,1,0:T(8,128)S(1)} %collective-permute-done.21.came, bf16[8,12,256,256]{3,2,1,0:T(8,128)(2,1)S(1)} %get-tuple-element.93.inverse, ...), custom_call_target="tpu_custom_call", output_to_operand_aliasing={{0}: (5, {}), {1}: (6, {})} | custom-call | flops 67108864 | bytes 2097152 | tf_op jit(solution)/shard_map/backward_0_2/pallas_call | solution.py:440
  (14 shorter events, 0.2 us)
Async XLA Ops:
  0.0 10.7 %copy-start = (f32[2,4,12,32,256]{4,3,2,1,0:T(8,128)S(1)}, f32[2,4,12,32,256]{4,3,2,1,0:T(8,128)}, u32[]{:S(2)}) copy-start(f32[2,4,12,32,256]{4,3,2,1,0:T(8,128)} %param.5) | copy-start | bytes 9437188
  0.0 10.8 %copy-start.1 = (f32[2,4,12,32,256]{4,3,2,1,0:T(8,128)S(1)}, f32[2,4,12,32,256]{4,3,2,1,0:T(8,128)}, u32[]{:S(2)}) copy-start(f32[2,4,12,32,256]{4,3,2,1,0:T(8,128)} %param.6) | copy-start | bytes 9437188
  3.1 10.0 %collective-permute-start.1 = (f32[4,32,256]{2,1,0:T(8,128)S(1)}, f32[4,32,256]{2,1,0:T(8,128)S(1)}, u32[]{:S(2)}, u32[]{:S(2)}) collective-permute-start(f32[4,32,256]{2,1,0:T(8,128)S(1)} %get-tuple-element.87), channel_id=1, source_target_pairs={{32,0},{64,32},{96,64},{33,1},{65,33},{97,65},{34,2},{66,34},{98,6... | collective-permute-start | bytes 393224 | tf_op jit(solution)/shard_map/ppermute | solution.py:486
  4.5 11.6 %collective-permute-start = (f32[8,32,256]{2,1,0:T(8,128)S(1)}, f32[8,32,256]{2,1,0:T(8,128)S(1)}, u32[]{:S(2)}, u32[]{:S(2)}) collective-permute-start(f32[8,32,256]{2,1,0:T(8,128)S(1)} %get-tuple-element.82), channel_id=1, source_target_pairs={{32,0},{64,32},{96,64},{33,1},{65,33},{97,65},{34,2},{66,34},{98,6... | collective-permute-start | bytes 786440 | tf_op jit(solution)/shard_map/ppermute | solution.py:487
  5.8 17.1 %collective-permute-start.2 = (f32[8,2,32,256]{3,2,1,0:T(8,128)S(1)}, f32[8,2,32,256]{3,2,1,0:T(8,128)S(1)}, u32[]{:S(2)}, u32[]{:S(2)}) collective-permute-start(f32[8,2,32,256]{3,2,1,0:T(8,128)S(1)} %get-tuple-element.94), channel_id=1, source_target_pairs={{0,1},{2,3},{4,5},{6,7},{8,9},{10,11},{12,13},{14,15},{16,17},{18,... | collective-permute-start | bytes 1572872 | tf_op jit(solution)/shard_map/ppermute | solution.py:466
  5.9 17.0 %collective-permute-start.3 = (f32[8,2,32,256]{3,2,1,0:T(8,128)S(1)}, f32[8,2,32,256]{3,2,1,0:T(8,128)S(1)}, u32[]{:S(2)}, u32[]{:S(2)}) collective-permute-start(f32[8,2,32,256]{3,2,1,0:T(8,128)S(1)} %get-tuple-element.95), channel_id=1, source_target_pairs={{1,2},{3,4},{5,6},{7,8},{9,10},{11,12},{13,14},{15,16},{17,18},{19... | collective-permute-start | bytes 1572872 | tf_op jit(solution)/shard_map/ppermute | solution.py:466
  13.3 13.2 %collective-permute-start.6 = (f32[4,32,256]{2,1,0:T(8,128)S(1)}, f32[4,32,256]{2,1,0:T(8,128)S(1)}, u32[]{:S(2)}, u32[]{:S(2)}) collective-permute-start(f32[4,32,256]{2,1,0:T(8,128)S(1)} %get-tuple-element.101), channel_id=1, source_target_pairs={{0,32},{1,33},{2,34},{3,35},{4,36},{5,37},{6,38},{7,39},{8,40},{9,... | collective-permute-start | bytes 393224 | tf_op jit(solution)/shard_map/ppermute | solution.py:530
  18.6 8.6 %collective-permute-start.5 = (f32[4,32,256]{2,1,0:T(8,128)S(1)}, f32[4,32,256]{2,1,0:T(8,128)S(1)}, u32[]{:S(2)}, u32[]{:S(2)}) collective-permute-start(f32[4,32,256]{2,1,0:T(8,128)S(1)} %get-tuple-element.100), channel_id=1, source_target_pairs={{0,32},{1,33},{2,34},{3,35},{4,36},{5,37},{6,38},{7,39},{8,40},{9,... | collective-permute-start | bytes 393224 | tf_op jit(solution)/shard_map/ppermute | solution.py:530
  25.2 3.8 %collective-permute-start.4 = (f32[4,32,256]{2,1,0:T(8,128)S(1)}, f32[4,32,256]{2,1,0:T(8,128)S(1)}, u32[]{:S(2)}, u32[]{:S(2)}) collective-permute-start(f32[4,32,256]{2,1,0:T(8,128)S(1)} %get-tuple-element.98), channel_id=1, source_target_pairs={{0,32},{1,33},{2,34},{3,35},{4,36},{5,37},{6,38},{7,39},{8,40},{9,... | collective-permute-start | bytes 393224 | tf_op jit(solution)/shard_map/ppermute | solution.py:530
  26.5 3.1 %collective-permute-start.9 = (f32[4,32,256]{2,1,0:T(8,128)S(1)}, f32[4,32,256]{2,1,0:T(8,128)S(1)}, u32[]{:S(2)}, u32[]{:S(2)}) collective-permute-start(f32[4,32,256]{2,1,0:T(8,128)S(1)} %get-tuple-element.109), channel_id=1, source_target_pairs={{32,64},{33,65},{34,66},{35,67},{36,68},{37,69},{38,70},{39,71},{4... | collective-permute-start | bytes 393224 | tf_op jit(solution)/shard_map/ppermute | solution.py:530
  27.2 3.1 %collective-permute-start.8 = (f32[4,32,256]{2,1,0:T(8,128)S(1)}, f32[4,32,256]{2,1,0:T(8,128)S(1)}, u32[]{:S(2)}, u32[]{:S(2)}) collective-permute-start(f32[4,32,256]{2,1,0:T(8,128)S(1)} %get-tuple-element.108), channel_id=1, source_target_pairs={{32,64},{33,65},{34,66},{35,67},{36,68},{37,69},{38,70},{39,71},{4... | collective-permute-start | bytes 393224 | tf_op jit(solution)/shard_map/ppermute | solution.py:530
  29.0 2.1 %collective-permute-start.7 = (f32[4,32,256]{2,1,0:T(8,128)S(1)}, f32[4,32,256]{2,1,0:T(8,128)S(1)}, u32[]{:S(2)}, u32[]{:S(2)}) collective-permute-start(f32[4,32,256]{2,1,0:T(8,128)S(1)} %get-tuple-element.107), channel_id=1, source_target_pairs={{32,64},{33,65},{34,66},{35,67},{36,68},{37,69},{38,70},{39,71},{4... | collective-permute-start | bytes 393224 | tf_op jit(solution)/shard_map/ppermute | solution.py:530
  29.7 2.1 %collective-permute-start.12 = (f32[4,32,256]{2,1,0:T(8,128)S(1)}, f32[4,32,256]{2,1,0:T(8,128)S(1)}, u32[]{:S(2)}, u32[]{:S(2)}) collective-permute-start(f32[4,32,256]{2,1,0:T(8,128)S(1)} %get-tuple-element.117), channel_id=1, source_target_pairs={{64,96},{65,97},{66,98},{67,99},{68,100},{69,101},{70,102},{71,103... | collective-permute-start | bytes 393224 | tf_op jit(solution)/shard_map/ppermute | solution.py:530
  30.4 1.4 %collective-permute-start.11 = (f32[4,32,256]{2,1,0:T(8,128)S(1)}, f32[4,32,256]{2,1,0:T(8,128)S(1)}, u32[]{:S(2)}, u32[]{:S(2)}) collective-permute-start(f32[4,32,256]{2,1,0:T(8,128)S(1)} %get-tuple-element.116), channel_id=1, source_target_pairs={{64,96},{65,97},{66,98},{67,99},{68,100},{69,101},{70,102},{71,103... | collective-permute-start | bytes 393224 | tf_op jit(solution)/shard_map/ppermute | solution.py:530
  31.1 0.8 collective-permute-start.10
  31.9 7.5 %collective-permute-start.13 = (f32[8,2,32,256]{3,2,1,0:T(8,128)S(1)}, f32[8,2,32,256]{3,2,1,0:T(8,128)S(1)}, u32[]{:S(2)}, u32[]{:S(2)}) collective-permute-start(f32[8,2,32,256]{3,2,1,0:T(8,128)S(1)} %get-tuple-element.122), channel_id=1, source_target_pairs={{0,1},{2,3},{4,5},{6,7},{8,9},{10,11},{12,13},{14,15},{16,17},{18,... | collective-permute-start | bytes 1572872 | tf_op jit(solution)/shard_map/ppermute | solution.py:466
  32.0 12.6 %collective-permute-start.14 = (f32[8,2,32,256]{3,2,1,0:T(8,128)S(1)}, f32[8,2,32,256]{3,2,1,0:T(8,128)S(1)}, u32[]{:S(2)}, u32[]{:S(2)}) collective-permute-start(f32[8,2,32,256]{3,2,1,0:T(8,128)S(1)} %get-tuple-element.123), channel_id=1, source_target_pairs={{1,2},{3,4},{5,6},{7,8},{9,10},{11,12},{13,14},{15,16},{17,18},{19... | collective-permute-start | bytes 1572872 | tf_op jit(solution)/shard_map/ppermute | solution.py:466
  37.5 8.4 %collective-permute-start.17 = (f32[4,32,256]{2,1,0:T(8,128)S(1)}, f32[4,32,256]{2,1,0:T(8,128)S(1)}, u32[]{:S(2)}, u32[]{:S(2)}) collective-permute-start(f32[4,32,256]{2,1,0:T(8,128)S(1)} %get-tuple-element.133), channel_id=1, source_target_pairs={{96,64},{97,65},{98,66},{99,67},{100,68},{101,69},{102,70},{103,71... | collective-permute-start | bytes 393224 | tf_op jit(solution)/shard_map/ppermute | solution.py:581
  38.8 8.0 %collective-permute-start.16 = (f32[4,32,256]{2,1,0:T(8,128)S(1)}, f32[4,32,256]{2,1,0:T(8,128)S(1)}, u32[]{:S(2)}, u32[]{:S(2)}) collective-permute-start(f32[4,32,256]{2,1,0:T(8,128)S(1)} %get-tuple-element.132), channel_id=1, source_target_pairs={{96,64},{97,65},{98,66},{99,67},{100,68},{101,69},{102,70},{103,71... | collective-permute-start | bytes 393224 | tf_op jit(solution)/shard_map/ppermute | solution.py:581
  45.2 2.4 %collective-permute-start.15 = (f32[4,32,256]{2,1,0:T(8,128)S(1)}, f32[4,32,256]{2,1,0:T(8,128)S(1)}, u32[]{:S(2)}, u32[]{:S(2)}) collective-permute-start(f32[4,32,256]{2,1,0:T(8,128)S(1)} %get-tuple-element.130), channel_id=1, source_target_pairs={{96,64},{97,65},{98,66},{99,67},{100,68},{101,69},{102,70},{103,71... | collective-permute-start | bytes 393224 | tf_op jit(solution)/shard_map/ppermute | solution.py:581
  46.1 2.4 %collective-permute-start.20 = (f32[4,32,256]{2,1,0:T(8,128)S(1)}, f32[4,32,256]{2,1,0:T(8,128)S(1)}, u32[]{:S(2)}, u32[]{:S(2)}) collective-permute-start(f32[4,32,256]{2,1,0:T(8,128)S(1)} %get-tuple-element.142), channel_id=1, source_target_pairs={{64,32},{65,33},{66,34},{67,35},{68,36},{69,37},{70,38},{71,39},{7... | collective-permute-start | bytes 393224 | tf_op jit(solution)/shard_map/ppermute | solution.py:581
  47.0 3.0 %collective-permute-start.19 = (f32[4,32,256]{2,1,0:T(8,128)S(1)}, f32[4,32,256]{2,1,0:T(8,128)S(1)}, u32[]{:S(2)}, u32[]{:S(2)}) collective-permute-start(f32[4,32,256]{2,1,0:T(8,128)S(1)} %get-tuple-element.141), channel_id=1, source_target_pairs={{64,32},{65,33},{66,34},{67,35},{68,36},{69,37},{70,38},{71,39},{7... | collective-permute-start | bytes 393224 | tf_op jit(solution)/shard_map/ppermute | solution.py:581
  47.8 3.6 %collective-permute-start.18 = (f32[4,32,256]{2,1,0:T(8,128)S(1)}, f32[4,32,256]{2,1,0:T(8,128)S(1)}, u32[]{:S(2)}, u32[]{:S(2)}) collective-permute-start(f32[4,32,256]{2,1,0:T(8,128)S(1)} %get-tuple-element.140), channel_id=1, source_target_pairs={{64,32},{65,33},{66,34},{67,35},{68,36},{69,37},{70,38},{71,39},{7... | collective-permute-start | bytes 393224 | tf_op jit(solution)/shard_map/ppermute | solution.py:581
  48.7 28.8 %collective-permute-start.23 = (f32[4,32,256]{2,1,0:T(8,128)S(1)}, f32[4,32,256]{2,1,0:T(8,128)S(1)}, u32[]{:S(2)}, u32[]{:S(2)}) collective-permute-start(f32[4,32,256]{2,1,0:T(8,128)S(1)} %get-tuple-element.151), channel_id=1, source_target_pairs={{32,0},{33,1},{34,2},{35,3},{36,4},{37,5},{38,6},{39,7},{40,8},{41... | collective-permute-start | bytes 393224 | tf_op jit(solution)/shard_map/ppermute | solution.py:581
  50.2 31.8 %collective-permute-start.22 = (f32[4,32,256]{2,1,0:T(8,128)S(1)}, f32[4,32,256]{2,1,0:T(8,128)S(1)}, u32[]{:S(2)}, u32[]{:S(2)}) collective-permute-start(f32[4,32,256]{2,1,0:T(8,128)S(1)} %get-tuple-element.150), channel_id=1, source_target_pairs={{32,0},{33,1},{34,2},{35,3},{36,4},{37,5},{38,6},{39,7},{40,8},{41... | collective-permute-start | bytes 393224 | tf_op jit(solution)/shard_map/ppermute | solution.py:581
  51.6 32.8 %collective-permute-start.21 = (f32[4,32,256]{2,1,0:T(8,128)S(1)}, f32[4,32,256]{2,1,0:T(8,128)S(1)}, u32[]{:S(2)}, u32[]{:S(2)}) collective-permute-start(f32[4,32,256]{2,1,0:T(8,128)S(1)} %get-tuple-element.149), channel_id=1, source_target_pairs={{32,0},{33,1},{34,2},{35,3},{36,4},{37,5},{38,6},{39,7},{40,8},{41... | collective-permute-start | bytes 393224 | tf_op jit(solution)/shard_map/ppermute | solution.py:581

commit v5 on v4

--- a/solution.py
+++ b/solution.py
@@ -11,21 +11,25 @@
 LANES = 12
 R = 32
 BS = 256
-FORWARD = ((2, 3, 4, 5), (6, 7, 8, 9), (0, 1, 10, 11))
+FORWARD = ((2, 3, 4, 5), (0, 1, 10, 11), (6, 7, 8, 9))
 BACKWARD = ((2, 3, 4, 5), (6, 7, 8, 9), (0, 1, 10, 11))
-OUTER = 2
+OUTER = 1
 STRIP = 4
+DOWN = tuple(range(COLS - 1, -1, -1))
 SIDES = ((2, -1), (3, 1), (4, -2), (5, 2))
+COST_TURN = 7
+COST_LAST = -3
 NT = (((1,), (1,)), ((), ()))
 VMEM = pltpu.VMEM
 ANY = pl.ANY
 HBM = pltpu.HBM
 
 FIELD = (COLS, LANES, R, BS)
-LATER = (LANES - 4, R, BS)
+FIRST = (LANES, R, BS)
 FIELD_MORE = (COLS + 1, LANES, R, BS)
 EDGE = (COLS, 2, R, BS)
 BLOCKS = (COLS, LANES, BS, BS)
+OWN_BLOCKS = (COLS, 4, BS, BS)
 PER = 4
 COEFS = (6, COLS // PER, LANES, PER, BS)
 WEIGHTS = (COLS + 1, LANES, BS)
@@ -50,11 +54,15 @@
 
 
 def solve(xs, inverse, q, lanes):
+    alone = inverse.shape[1] < LANES
     return [
         lax.dot_general(
-            x.astype(jnp.bfloat16), inverse[q, lane], NT, preferred_element_type=jnp.float32
+            x.astype(jnp.bfloat16),
+            inverse[q, j if alone else lane],
+            NT,
+            preferred_element_type=jnp.float32,
         )
-        for x, lane in zip(xs, lanes)
+        for j, (x, lane) in enumerate(zip(xs, lanes))
     ]
 
 
@@ -78,35 +86,22 @@
 
 
 def prep_kernel(
-    ice_hbm, st_hbm, couple_hbm, inv_hbm, now, later, edge_in, edge_out, couple, mask, inverse, ice, sem, sem_inv
+    ice_hbm, st_hbm, couple_hbm, inv_hbm, nxt, edge_in, edge_out, couple, mask, own, ice, sem
 ):
     even = is_even()
     lane_in = jnp.where(even, LANES - 2, 0)
     lane_out = jnp.where(even, 0, LANES - 2)
+    a, n = runs_of(FORWARD[0])[0]
     copies = [
         pltpu.make_async_copy(ice_hbm, ice, sem.at[0]),
         pltpu.make_async_copy(couple_hbm, couple, sem.at[1]),
-        pltpu.make_async_copy(st_hbm.at[:, pl.ds(lane_out, 2)], edge_out, sem.at[2]),
-        pltpu.make_async_copy(st_hbm.at[:, pl.ds(lane_in, 2)], edge_in, sem.at[3]),
+        pltpu.make_async_copy(st_hbm.at[0], nxt, sem.at[2]),
+        pltpu.make_async_copy(st_hbm.at[:, pl.ds(lane_out, 2)], edge_out, sem.at[3]),
+        pltpu.make_async_copy(st_hbm.at[:, pl.ds(lane_in, 2)], edge_in, sem.at[4]),
+        pltpu.make_async_copy(inv_hbm.at[:, pl.ds(a, n)], own, sem.at[5]),
     ]
-    at = 0
-    for lanes in FORWARD:
-        for a, n in runs_of(lanes):
-            if lanes == FORWARD[0]:
-                target = now.at[pl.ds(0, n)]
-            else:
-                target = later.at[pl.ds(at, n)]
-                at += n
-            copies.append(
-                pltpu.make_async_copy(st_hbm.at[0, pl.ds(a, n)], target, sem.at[len(copies)])
-            )
-
-    def own(q):
-        return lane_copies(inv_hbm, inverse, q, FORWARD[0], sem_inv)
-
     for copy in copies:
         copy.start()
-    start_all(own)
 
     def ice_weight(q, lane):
         return ice[q // PER, q % PER, lane].astype(jnp.float32)
@@ -115,17 +110,15 @@
     for q in range(COLS):
         for lane in range(LANES):
             mask[q, pl.ds(lane, 1), :] = jnp.full((1, BS), ice_weight(q, lane), jnp.float32)
-    for copy in copies[1:]:
+    for copy in copies[1:5]:
         copy.wait()
+    for lane in range(LANES):
+        nxt[lane] = weight(mask, 0, lane) * nxt[lane]
     for q in range(COLS):
         for j in range(2):
             edge_out[q, j] = ice_weight(q, lane_out + j) * edge_out[q, j]
             edge_in[q, j] = ice_weight(q, lane_in + j) * edge_in[q, j]
-    for j, lane in enumerate(FORWARD[0]):
-        now[j] = weight(mask, 0, lane) * now[j]
-    for j, lane in enumerate(FORWARD[1] + FORWARD[2]):
-        later[j] = weight(mask, 0, lane) * later[j]
-    wait_all(own)
+    copies[5].wait()
 
 
 def halo_of(even, halo_in, halo_out, q, lane):
@@ -134,8 +127,8 @@
     return jnp.where(even, halo_in[q, lane - LANES], halo_out[q, lane - LANES])
 
 
-def make_source(lanes, q, rs, start, couple, mask, source, halo=None, later=None):
-    for j, lane in enumerate(lanes):
+def make_source(lanes, q, rs, start, couple, mask, source, halo=None, nxt=None):
+    for lane in lanes:
         total = rs[q, lane]
         for k, step in SIDES:
             other = lane + step
@@ -144,11 +137,11 @@
                 total = total + factor * start[q, other]
             elif halo is not None:
                 total = total + coef(couple, k, q, lane) * halo(q, other)
-        if later is None:
+        if nxt is None:
             factor = coef(couple, 1, q, lane) * weight(mask, q + 1, lane)
             total = total + factor * start[q + 1, lane]
         else:
-            total = total + coef(couple, 1, q, lane) * later[j]
+            total = total + coef(couple, 1, q, lane) * nxt[lane]
         source[q, lane] = total
 
 
@@ -185,72 +178,98 @@
 
 
 def sweep_first(
-    lanes, rs, start, source, inverse, couple, mask, field, sent, columns, halo, edges
+    lanes, rs, start, source, inverse, couple, mask, field, sent, halo, edges, arriving=None
 ):
     for j in range(len(lanes)):
         sent[j] = jnp.zeros((R, BS), jnp.float32)
     make_source(lanes, 0, rs, start, couple, mask, source, halo)
-
-    def step(q, _):
+    for q in range(COLS - 1):
+        if arriving is not None:
+            arriving(q).wait()
         forward_chain(lanes, q, source, inverse, couple, mask, field, sent, edges)
-        make_source(
-            lanes, jnp.minimum(q + 1, columns - 1), rs, start, couple, mask, source, halo
-        )
-        return 0
-
-    lax.fori_loop(0, columns, step, 0)
-
-
-def first_kernel(inv_hbm, rs, start, couple, mask, _, inverse, source, field, sent, sem):
-    @pl.when(lax.axis_index("strip") == 0)
-    def _():
-        def following(q):
-            return lane_copies(inv_hbm, inverse, q, FORWARD[1], sem)
-
-        start_all(following)
+        if q + 2 < COLS:
+            make_source(lanes, q + 1, rs, start, couple, mask, source, halo)
+
+
+def first_kernel(
+    own, inv_hbm, rs, start, couple, mask, source, field, sent, sent_last, own_last, own_outer, sem, sem_outer
+):
+    first = lax.axis_index("strip") == 0
+    a, n = runs_of(FORWARD[2])[0]
+
+    @pl.when(first)
+    def _():
+        def arriving(q):
+            return pltpu.make_async_copy(inv_hbm.at[q, pl.ds(a, n)], own_last.at[q], sem.at[q])
+
+        for q in range(COLS):
+            arriving(q).start()
+        outer = [
+            pltpu.make_async_copy(
+                inv_hbm.at[:, pl.ds(b, 2)], own_outer.at[:, pl.ds(2 * i, 2)], sem_outer.at[i]
+            )
+            for i, (b, _) in enumerate(runs_of(FORWARD[OUTER]))
+        ]
+        for copy in outer:
+            copy.start()
         field[0] = jnp.zeros((LANES, R, BS), jnp.float32)
         sweep_first(
-            FORWARD[0], rs, start, source, inverse, couple, mask, field, sent, COLS - 1, None, None
+            FORWARD[0], rs, start, source, own, couple, mask, field, sent, None, None
         )
-        wait_all(following)
-
-
-def tail_kernel(now, inverse, rs, start, couple, mask, *refs):
+        sweep_first(
+            FORWARD[2], rs, start, source, own_last, couple, mask, field, sent_last, None, None, arriving
+        )
+        arriving(COLS - 1).wait()
+        for copy in outer:
+            copy.wait()
+
+    @pl.when(jnp.logical_not(first))
+    def _():
+        def step(q, _):
+            make_source(range(LANES), q, rs, start, couple, mask, source)
+            return 0
+
+        lax.fori_loop(0, COLS - 1, step, 0)
+
+
+def tail_kernel(chunk, nxt, own, rs, start, couple, mask, *refs):
     source, field, sent = refs[3:]
-    lanes, q = FORWARD[0], COLS - 1
-
-    @pl.when(lax.axis_index("strip") == 0)
-    def _():
-        make_source(lanes, q, rs, start, couple, mask, source, None, now)
-        forward_chain(lanes, q, source, inverse, couple, mask, field, sent)
-
-
-def outer_kernel(now, later, halo_in, halo_out, inverse, rs, start, couple, mask, *refs):
+    lanes, q = FORWARD[chunk], COLS - 1
+    first = lax.axis_index("strip") == 0
+
+    @pl.when(first)
+    def _():
+        make_source(lanes, q, rs, start, couple, mask, source, None, nxt)
+        forward_chain(lanes, q, source, own, couple, mask, field, sent)
+
+    if chunk == 0:
+
+        @pl.when(jnp.logical_not(first))
+        def _():
+            make_source(range(LANES), q, rs, start, couple, mask, source, None, nxt)
+
+
+def outer_kernel(nxt, halo_in, halo_out, own, rs, start, couple, mask, *refs):
     source, field, edge_in, edge_out, sent = refs[2:]
-    lanes, q_last = FORWARD[OUTER], COLS - 1
-    first = lax.axis_index("strip") == 0
+    lanes, q = FORWARD[OUTER], COLS - 1
     even = is_even()
     edges = (even, edge_in, edge_out)
     halo = functools.partial(halo_of, even, halo_in, halo_out)
 
-    @pl.when(first)
-    def _():
-        own = later.at[pl.ds(len(FORWARD[1]), len(lanes))]
-        sweep_first(
-            lanes, rs, start, source, inverse, couple, mask, field, sent, COLS - 1, halo, edges
-        )
-        make_source(lanes, q_last, rs, start, couple, mask, source, halo, own)
-        forward_chain(lanes, q_last, source, inverse, couple, mask, field, sent, edges)
-
-    @pl.when(jnp.logical_not(first))
-    def _():
-        make_source(FORWARD[0], q_last, rs, start, couple, mask, source, None, now)
-        make_source(
-            FORWARD[1] + FORWARD[2], q_last, rs, start, couple, mask, source, None, later
-        )
-
+    @pl.when(lax.axis_index("strip") == 0)
+    def _():
+        sweep_first(lanes, rs, start, source, own, couple, mask, field, sent, halo, edges)
+        make_source(lanes, q, rs, start, couple, mask, source, halo, nxt)
+        forward_chain(lanes, q, source, own, couple, mask, field, sent, edges)
+
+
+def halo_kernel(halo_in, halo_out, couple, _, source):
+    halo = functools.partial(halo_of, is_even(), halo_in, halo_out)
+
+    @pl.when(lax.axis_index("strip") != 0)
+    def _():
         def step(q, _):
-            for lane in lanes:
+            for lane in FORWARD[OUTER]:
                 total = source[q, lane]
                 for k, move in SIDES:
                     if not 0 <= lane + move < LANES:
@@ -259,41 +278,6 @@
             return 0
 
         lax.fori_loop(0, COLS, step, 0)
-
-
-def inner_kernel(later, inv_hbm, rs, start, couple, mask, *refs):
-    inverse, source, field, sent, sem, sem_next = refs[3:]
-    lanes, q_last = FORWARD[1], COLS - 1
-    first = lax.axis_index("strip") == 0
-
-    def following(q):
-        return lane_copies(inv_hbm, inverse, q, FORWARD[2], sem)
-
-    def own(q):
-        return lane_copies(inv_hbm, inverse, q, lanes, sem_next)
-
-    @pl.when(first)
-    def _():
-        start_all(following)
-        sweep_first(
-            lanes, rs, start, source, inverse, couple, mask, field, sent, COLS - 1, None, None
-        )
-        make_source(lanes, q_last, rs, start, couple, mask, source, None, later)
-        forward_chain(lanes, q_last, source, inverse, couple, mask, field, sent)
-        wait_all(following)
-
-    @pl.when(jnp.logical_not(first))
-    def _():
-        start_all(own)
-        start_all(following)
-
-        def step(q, _):
-            make_source(range(LANES), q, rs, start, couple, mask, source)
-            return 0
-
-        lax.fori_loop(0, COLS - 1, step, 0)
-        wait_all(own)
-        wait_all(following)
 
 
 def forward_kernel(chunk, stage, came, inverse, source, couple, mask, *refs):
@@ -311,11 +295,8 @@
             sent[j] = came[j]
             field[0, lane] = came[j]
 
-        def step(q, _):
+        for q in range(COLS):
             forward_chain(lanes, q, source, inverse, couple, mask, field, sent, edges)
-            return 0
-
-        lax.fori_loop(0, COLS, step, 0)
 
 
 def backward_chain(lanes, q, source, inverse, couple, mask, result, sent):
@@ -339,30 +320,16 @@
     def own(q):
         return lane_copies(result, out, q, lanes, sem_own) if last else []
 
-    def launch(q, _):
-        for copy in before(q):
-            copy.start()
-        return 0
-
-    lax.fori_loop(0, COLS, launch, 0)
-
-    def step(i, _):
-        q = COLS - 1 - i
+    start_all(before)
+    for q in DOWN:
         backward_chain(lanes, q, source, inverse, couple, mask, result, sent)
         for copy in own(q):
             copy.start()
-        if beside is not None:
-            beside(jnp.maximum(q - 1, 0))
-        return 0
-
-    lax.fori_loop(0, COLS, step, 0)
-
-    def drain(q, _):
-        for copy in before(q) + own(q):
-            copy.wait()
-        return 0
-
-    lax.fori_loop(0, COLS, drain, 0)
+        if beside is not None and q > 0:
+            beside(q - 1)
+    wait_all(before)
+    if last:
+        wait_all(own)
 
 
 def last_kernel(chunk, inverse, rs, field, couple, mask, halo_in, halo_out, *refs):
@@ -474,55 +441,56 @@
     def piece(lanes):
         return (len(lanes), R, BS)
 
-    blocks = [(vmem(BLOCKS, jnp.bfloat16), VMEM)]
-    inv_hbm = [(inverse, HBM)]
-    now, later, edge_in, edge_out, coefs, mask, inverse = run(
+    own_blocks = [(vmem(OWN_BLOCKS, jnp.bfloat16), VMEM)]
+    nxt, edge_in, edge_out, coefs, mask, own = run(
         prep_kernel,
         "prep",
-        [(ice_mask, HBM), (start, HBM), (couple.transpose(0, 1, 3, 2, 4), HBM)] + inv_hbm,
-        made(piece(FORWARD[0]), LATER, EDGE, EDGE, COEFS, WEIGHTS) + blocks,
-        [pltpu.SMEM(ice_mask.shape, jnp.int32), dma((9,)), dma((COLS,))],
-    )
-    now = lax.ppermute(now, "strip", to_back)
-    later = lax.ppermute(later, "strip", to_back)
+        [(ice_mask, HBM), (start, HBM), (couple.transpose(0, 1, 3, 2, 4), HBM), (inverse, HBM)],
+        made(FIRST, EDGE, EDGE, COEFS, WEIGHTS) + own_blocks,
+        [pltpu.SMEM(ice_mask.shape, jnp.int32), dma((6,))],
+    )
+    nxt = lax.ppermute(nxt, "strip", to_back)
     halo_out = swapped(edge_out, pairs_out)
     halo_in = swapped(edge_in, pairs_in)
 
     sents = {}
     rest = inside(rs, start, coefs, mask)
-    inverse, source, field, sent = run(
+    ends = [piece(FORWARD[0]), piece(FORWARD[2])]
+    source, field, sent, sent_last, own_last, own_outer = run(
         first_kernel,
         "first",
-        inv_hbm + rest + inside(inverse),
-        blocks + made(FIELD, FIELD_MORE, piece(FORWARD[0])),
-        [dma((COLS,))],
-        {5: 0},
+        inside(own) + [(inverse, HBM)] + rest,
+        made(FIELD, FIELD_MORE, *ends) + own_blocks * 2,
+        [dma((COLS,)), dma((2,))],
         cost=-10,
     )
     source, field, sents[0, 0] = run(
-        tail_kernel,
-        "tail",
-        inside(now, inverse) + rest + inside(source, field, sent),
-        made(FIELD, FIELD_MORE, piece(FORWARD[0])),
+        functools.partial(tail_kernel, 0),
+        "tail_0",
+        inside(nxt, own) + rest + inside(source, field, sent),
+        made(FIELD, FIELD_MORE, ends[0]),
         [],
         {6: 0, 7: 1, 8: 2},
         cost=8,
     )
-    inverse, source, field, sents[0, 1] = run(
-        inner_kernel,
-        "inner",
-        inside(later) + inv_hbm + rest + inside(inverse, source, field),
-        blocks + made(FIELD, FIELD_MORE, piece(FORWARD[1])),
-        [dma((COLS,)), dma((COLS,))],
-        {6: 0, 7: 1, 8: 2},
-    )
-    source, field, edge_in, edge_out, sents[0, 2] = run(
+    source, field, edge_in, edge_out, sents[0, 1] = run(
         outer_kernel,
         "outer",
-        inside(now, later, halo_in, halo_out, inverse) + rest + inside(source, field),
-        made(FIELD, FIELD_MORE, EDGE, EDGE, piece(FORWARD[2])),
+        inside(nxt, halo_in, halo_out, own_outer) + rest + inside(source, field),
+        made(FIELD, FIELD_MORE, EDGE, EDGE, piece(FORWARD[OUTER])),
         [],
-        {9: 0, 10: 1},
+        {8: 0, 9: 1},
+    )
+    source, field, sents[0, 2] = run(
+        functools.partial(tail_kernel, 2),
+        "tail_2",
+        inside(nxt, own_last) + rest + inside(source, field, sent_last),
+        made(FIELD, FIELD_MORE, ends[1]),
+        [],
+        {6: 0, 7: 1, 8: 2},
+    )
+    (source,) = run(
+        halo_kernel, "halo", inside(halo_in, halo_out, coefs, source), made(FIELD), [], {3: 0}
     )
 
     for stage in range(1, STRIP):
@@ -543,6 +511,7 @@
                 outs + (made(piece(lanes)) if sending else []),
                 [] if sending else [vmem(piece(lanes))],
                 aliases,
+                cost=COST_TURN if not sending and chunk > OUTER else 0,
             )
             field = got[0]
             if chunk == OUTER:
@@ -557,7 +526,7 @@
     sems = [dma((COLS,)), dma((COLS,))]
     result = out = None
     for chunk, lanes in enumerate(BACKWARD):
-        sides = inside(halo_in, halo_out) if min(lanes) < 2 or max(lanes) >= LANES - 2 else []
+        sides = inside(halo_in, halo_out) if chunk == len(BACKWARD) - 1 else []
         operands = inside(inverse, rs, field, coefs, mask) + sides + inside(source)
         base = len(operands) - 1
         aliases = {base: 0}
@@ -574,6 +543,7 @@
             made(FIELD, FIELD) + out_shape + made(piece(lanes)),
             sems,
             aliases,
+            cost=COST_LAST,
         )
 
     for stage in range(STRIP - 2, -1, -1):

time: 88.2 us -> 79.9 us (0.906)
  Pallas kernels: 21 us -> 17 us
  starting transfers between devices: 32.8 us -> 30.1 us
  waiting for transfers between devices: 33.1 us -> 31.4 us
    ppermute x9, waiting for transfers between devices: 26.9 us -> 22.6 us  [on_device(): came = lax.ppermute(sents[stage + 1, chunk], 'strip', [(stage + 1, stage)])]
    pallas_call x26 -> x27, Pallas kernels: 21 us -> 17 us  [run(): pl.pallas_call(kernel, name=name, out_shape=[o for o, _ in outs], in_spec...]
    ppermute x2 -> x1, waiting for transfers between devices: 0.01 us -> 2.86 us  [on_device(): nxt = lax.ppermute(nxt, 'strip', to_back)]
    ppermute x9, starting transfers between devices: 12.3 us -> 10.4 us  [on_device(): came = lax.ppermute(sents[stage - 1, chunk], 'strip', [(stage - 1, stage)])]
    ppermute x2 -> x1, starting transfers between devices: 2.72 us -> 1.42 us  [on_device(): nxt = lax.ppermute(nxt, 'strip', to_back)]
  transfers between devices with their start and end apart: 24 -> 23, of which waited for: 5 -> 7; matrix products, arithmetic and copies ran while one was open for 0% -> 0% of each run, Pallas kernels for 17% -> 15%
where the time goes in v5:
time: 79.9 us; the launch traced here: 79.5 us
  waiting for transfers between devices  31.4 us (39%)
  starting transfers between devices  30.1 us (38%)
  Pallas kernels  17 us (21%)
    ppermute x9, waiting for transfers between devices, on_device(): came = lax.ppermute(sents[stage + 1, chunk], 'strip', [(stage + 1, stage)])  22.6 us
    pallas_call x27, Pallas kernels, run(): pl.pallas_call(kernel, name=name, out_shape=[o for o, _ in outs], in_spec...  17 us
    ppermute x4, starting transfers between devices, swapped(): return lax.ppermute(value, 'tile', pairs + [(b, a) for a, b in pairs])  10.4 us
    ppermute x9, starting transfers between devices, on_device(): came = lax.ppermute(sents[stage - 1, chunk], 'strip', [(stage - 1, stage)])  10.4 us
    ppermute x9, starting transfers between devices, on_device(): came = lax.ppermute(sents[stage + 1, chunk], 'strip', [(stage + 1, stage)])  7.89 us
    ppermute x4, waiting for transfers between devices, swapped(): return lax.ppermute(value, 'tile', pairs + [(b, a) for a, b in pairs])  4.41 us
    ppermute x1, waiting for transfers between devices, on_device(): nxt = lax.ppermute(nxt, 'strip', to_back)  2.86 us
  transfers between devices with their start and end apart: 23, of which 7 were waited for; matrix products, arithmetic and copies ran while one was open for 0% of the time, Pallas kernels for 15%

profile of v5, /device:TPU:96, one launch (start us, length us, event | category | flops | bytes accessed | tf_op | source)
XLA Modules:
  0.0 79.5 jit_solution(11741378570753682486)
XLA Ops:
  0.0 3.0 %prep.1 = (f32[12,32,256]{2,1,0:T(8,128)S(1)}, f32[8,2,32,256]{3,2,1,0:T(8,128)S(1)}, f32[8,2,32,256]{3,2,1,0:T(8,128)S(1)}, f32[6,2,12,4,256]{4,3,2,1,0:T(4,128...) custom-call(s32[2,4,12]{2,1,0:T(4,128)} %ice_hbm.1, f32[8,12,32,256]{3,2,1,0:T(8,128)} %bitcast.37, ...), custom_call_target="tpu_custom_call" | custom-call | flops 67108864 | bytes 2097152 | tf_op jit(solution)/shard_map/prep/pallas_call | solution.py:407
  3.0 1.4 %collective-permute-start = (f32[12,32,256]{2,1,0:T(8,128)S(1)}, f32[12,32,256]{2,1,0:T(8,128)S(1)}, u32[]{:S(2)}, u32[]{:S(2)}) collective-permute-start(f32[12,32,256]{2,1,0:T(8,128)S(1)} %get-tuple-element.82), channel_id=1, source_target_pairs={{32,0},{64,32},{96,64},{33,1},{65,33},{97,65},{34,2},{66,34},{98,6... | collective-permute-start | bytes 1179656 | tf_op jit(solution)/shard_map/ppermute | solution.py:452
  4.4 0.1 collective-permute-start.1
  4.5 4.9 %collective-permute-start.2 = (f32[8,2,32,256]{3,2,1,0:T(8,128)S(1)}, f32[8,2,32,256]{3,2,1,0:T(8,128)S(1)}, u32[]{:S(2)}, u32[]{:S(2)}) collective-permute-start(f32[8,2,32,256]{3,2,1,0:T(8,128)S(1)} %get-tuple-element.88), channel_id=1, source_target_pairs={{1,2},{3,4},{5,6},{7,8},{9,10},{11,12},{13,14},{15,16},{17,18},{19... | collective-permute-start | bytes 1572872 | tf_op jit(solution)/shard_map/ppermute | solution.py:433
  9.4 3.6 %first.1 = (f32[8,12,32,256]{3,2,1,0:T(8,128)S(1)}, f32[9,12,32,256]{3,2,1,0:T(8,128)S(1)}, f32[4,32,256]{2,1,0:T(8,128)S(1)}, f32[4,32,256]{2,1,0:T(8,128)S(1)}...) custom-call(bf16[8,4,256,256]{3,2,1,0:T(8,128)(2,1)S(1)} %get-tuple-element.83.own, ...), custom_call_target="tpu_custom_call" | custom-call | flops 65536 | bytes 2048 | tf_op jit(solution)/shard_map/first/pallas_call | solution.py:407
  13.0 2.9 %collective-permute-done.nxt = f32[12,32,256]{2,1,0:T(8,128)S(1)} collective-permute-done((f32[12,32,256]{2,1,0:T(8,128)S(1)}, f32[12,32,256]{2,1,0:T(8,128)S(1)}, u32[]{:S(2)}, u32[]{:S(2)}) %collective-permute-start) | collective-permute-done | bytes 393248 | tf_op jit(solution)/shard_map/ppermute | solution.py:452
  15.9 0.3 tail_0.1
  16.2 3.3 %collective-permute-start.5 = (f32[4,32,256]{2,1,0:T(8,128)S(1)}, f32[4,32,256]{2,1,0:T(8,128)S(1)}, u32[]{:S(2)}, u32[]{:S(2)}) collective-permute-start(f32[4,32,256]{2,1,0:T(8,128)S(1)} %get-tuple-element.101), channel_id=1, source_target_pairs={{0,32},{1,33},{2,34},{3,35},{4,36},{5,37},{6,38},{7,39},{8,40},{9,... | collective-permute-start | bytes 393224 | tf_op jit(solution)/shard_map/ppermute | solution.py:498
  19.4 0.0 collective-permute-done.1.halo_in
  19.5 0.0 collective-permute-done.2.halo_out
  19.5 0.0 slice-start
  19.5 0.0 slice-start.1
  19.5 1.4 %outer.1 = (f32[8,12,32,256]{3,2,1,0:T(8,128)S(1)}, f32[9,12,32,256]{3,2,1,0:T(8,128)S(1)}, f32[8,2,32,256]{3,2,1,0:T(8,128)S(1)}, f32[8,2,32,256]{3,2,1,0:T(8,128)S(1)}, f32[4,32,256]{2,1,0:T(8,128)S(1)}) custom-call(f32[12,32,256]{2,1,0:T(8,128)S(1)} %collective-permute-done.nxt, ...), custom_call_target="tpu_custom_call", output_to_operand_aliasing={{0}: (8, {}), {1}: (9, {})} | custom-call | flops 67108864 | bytes 2097152 | tf_op jit(solution)/shard_map/outer/pallas_call | solution.py:407
  20.9 1.6 %collective-permute-start.4 = (f32[4,32,256]{2,1,0:T(8,128)S(1)}, f32[4,32,256]{2,1,0:T(8,128)S(1)}, u32[]{:S(2)}, u32[]{:S(2)}) collective-permute-start(f32[4,32,256]{2,1,0:T(8,128)S(1)} %get-tuple-element.100), channel_id=1, source_target_pairs={{0,32},{1,33},{2,34},{3,35},{4,36},{5,37},{6,38},{7,39},{8,40},{9,... | collective-permute-start | bytes 393224 | tf_op jit(solution)/shard_map/ppermute | solution.py:498
  22.5 0.0 slice-start.2
  22.5 0.3 tail_2.1
  22.8 1.6 %collective-permute-start.3 = (f32[4,32,256]{2,1,0:T(8,128)S(1)}, f32[4,32,256]{2,1,0:T(8,128)S(1)}, u32[]{:S(2)}, u32[]{:S(2)}) collective-permute-start(f32[4,32,256]{2,1,0:T(8,128)S(1)} %get-tuple-element.98), channel_id=1, source_target_pairs={{0,32},{1,33},{2,34},{3,35},{4,36},{5,37},{6,38},{7,39},{8,40},{9,... | collective-permute-start | bytes 393224 | tf_op jit(solution)/shard_map/ppermute | solution.py:498
  24.4 0.0 collective-permute-done.5.came
  24.4 0.4 slice-done.2
  24.8 0.7 collective-permute-start.8
  25.5 0.8 collective-permute-done.4.came
  26.2 0.7 collective-permute-start.7
  26.9 0.7 collective-permute-done.3.came
  27.6 0.7 collective-permute-start.6
  28.3 0.0 collective-permute-done.8.came
  28.3 0.7 collective-permute-start.11
  29.0 0.0 collective-permute-done.7.came
  29.0 0.7 collective-permute-start.10
  29.7 0.0 collective-permute-done.6.came
  29.8 0.7 collective-permute-start.9
  30.4 0.0 collective-permute-done.11.came
  30.5 0.0 collective-permute-done.10.came
  30.5 0.1 collective-permute-start.12
  30.6 5.4 %collective-permute-start.13 = (f32[8,2,32,256]{3,2,1,0:T(8,128)S(1)}, f32[8,2,32,256]{3,2,1,0:T(8,128)S(1)}, u32[]{:S(2)}, u32[]{:S(2)}) collective-permute-start(f32[8,2,32,256]{3,2,1,0:T(8,128)S(1)} %get-tuple-element.123), channel_id=1, source_target_pairs={{1,2},{3,4},{5,6},{7,8},{9,10},{11,12},{13,14},{15,16},{17,18},{19... | collective-permute-start | bytes 1572872 | tf_op jit(solution)/shard_map/ppermute | solution.py:433
  36.0 0.8 last_0.1
  36.8 0.7 collective-permute-start.16
  37.5 0.6 last_1.1
  38.1 0.7 collective-permute-start.15
  38.8 0.0 collective-permute-done.12.halo_in
  38.8 4.4 %collective-permute-done.13.halo_out = f32[8,2,32,256]{3,2,1,0:T(8,128)S(1)} collective-permute-done((f32[8,2,32,256]{3,2,1,0:T(8,128)S(1)}, f32[8,2,32,256]{3,2,1,0:T(8,128)S(1)}, u32[]{:S(2)}, u32[]{:S(2)}) %collective-permute-start.13) | collective-permute-done | bytes 524320 | tf_op jit(solution)/shard_map/ppermute | solution.py:433
  43.2 0.6 last_2.1
  43.8 0.7 collective-permute-start.14
  44.5 0.2 backward_2_0.1
  44.7 0.7 collective-permute-start.19
  45.4 0.0 collective-permute-done.15.came
  45.4 0.2 backward_2_1.1
  45.6 0.7 collective-permute-start.18
  46.2 0.0 collective-permute-done.14.came
  46.3 0.2 backward_2_2.1
  46.4 0.7 collective-permute-start.17
  47.1 0.2 backward_1_0.1
  47.3 1.3 %collective-permute-start.22 = (f32[4,32,256]{2,1,0:T(8,128)S(1)}, f32[4,32,256]{2,1,0:T(8,128)S(1)}, u32[]{:S(2)}, u32[]{:S(2)}) collective-permute-start(f32[4,32,256]{2,1,0:T(8,128)S(1)} %get-tuple-element.151), channel_id=1, source_target_pairs={{32,0},{33,1},{34,2},{35,3},{36,4},{37,5},{38,6},{39,7},{40,8},{41... | collective-permute-start | bytes 393224 | tf_op jit(solution)/shard_map/ppermute | solution.py:551
  48.6 0.0 collective-permute-done.18.came
  48.6 0.2 backward_1_1.1
  48.8 1.3 %collective-permute-start.21 = (f32[4,32,256]{2,1,0:T(8,128)S(1)}, f32[4,32,256]{2,1,0:T(8,128)S(1)}, u32[]{:S(2)}, u32[]{:S(2)}) collective-permute-start(f32[4,32,256]{2,1,0:T(8,128)S(1)} %get-tuple-element.150), channel_id=1, source_target_pairs={{32,0},{33,1},{34,2},{35,3},{36,4},{37,5},{38,6},{39,7},{40,8},{41... | collective-permute-start | bytes 393224 | tf_op jit(solution)/shard_map/ppermute | solution.py:551
  50.1 0.0 collective-permute-done.17.came
  50.1 0.2 backward_1_2.1
  50.2 1.3 %collective-permute-start.20 = (f32[4,32,256]{2,1,0:T(8,128)S(1)}, f32[4,32,256]{2,1,0:T(8,128)S(1)}, u32[]{:S(2)}, u32[]{:S(2)}) collective-permute-start(f32[4,32,256]{2,1,0:T(8,128)S(1)} %get-tuple-element.149), channel_id=1, source_target_pairs={{32,0},{33,1},{34,2},{35,3},{36,4},{37,5},{38,6},{39,7},{40,8},{41... | collective-permute-start | bytes 393224 | tf_op jit(solution)/shard_map/ppermute | solution.py:551
  51.5 20.0 %collective-permute-done.22.came = f32[4,32,256]{2,1,0:T(8,128)S(1)} collective-permute-done((f32[4,32,256]{2,1,0:T(8,128)S(1)}, f32[4,32,256]{2,1,0:T(8,128)S(1)}, u32[]{:S(2)}, u32[]{:S(2)}) %collective-permute-start.22) | collective-permute-done | bytes 131104 | tf_op jit(solution)/shard_map/ppermute | solution.py:551
  71.6 1.5 %backward_0_0.1 = (f32[8,12,32,256]{3,2,1,0:T(8,128)S(1)}, f32[8,12,32,256]{3,2,1,0:T(8,128)}) custom-call(f32[4,32,256]{2,1,0:T(8,128)S(1)} %collective-permute-done.22.came, bf16[8,12,256,256]{3,2,1,0:T(8,128)(2,1)S(1)} %bitcast.27, f32[8,12,32,256]{3,2,1,0:T(8,128)S(1)} %get-tuple-element.131.source, ...), custom_call_target="tpu_custom_call", output_to_operand_aliasing={{0}: (5, {}), {1}: (6, {})} | custom-call | flops 67108864 | bytes 2097152 | tf_op jit(solution)/shard_map/backward_0_0/pallas_call | solution.py:407
  73.1 1.1 %collective-permute-done.21.came = f32[4,32,256]{2,1,0:T(8,128)S(1)} collective-permute-done((f32[4,32,256]{2,1,0:T(8,128)S(1)}, f32[4,32,256]{2,1,0:T(8,128)S(1)}, u32[]{:S(2)}, u32[]{:S(2)}) %collective-permute-start.21) | collective-permute-done | bytes 131104 | tf_op jit(solution)/shard_map/ppermute | solution.py:551
  74.2 1.6 %backward_0_1.1 = (f32[8,12,32,256]{3,2,1,0:T(8,128)S(1)}, f32[8,12,32,256]{3,2,1,0:T(8,128)}) custom-call(f32[4,32,256]{2,1,0:T(8,128)S(1)} %collective-permute-done.21.came, bf16[8,12,256,256]{3,2,1,0:T(8,128)(2,1)S(1)} %bitcast.28, f32[8,12,32,256]{3,2,1,0:T(8,128)S(1)} %get-tuple-element.131.source, ...), custom_call_target="tpu_custom_call", output_to_operand_aliasing={{0}: (5, {}), {1}: (6, {})} | custom-call | flops 67108864 | bytes 2097152 | tf_op jit(solution)/shard_map/backward_0_1/pallas_call | solution.py:407
  75.8 1.4 %collective-permute-done.20.came = f32[4,32,256]{2,1,0:T(8,128)S(1)} collective-permute-done((f32[4,32,256]{2,1,0:T(8,128)S(1)}, f32[4,32,256]{2,1,0:T(8,128)S(1)}, u32[]{:S(2)}, u32[]{:S(2)}) %collective-permute-start.20) | collective-permute-done | bytes 131104 | tf_op jit(solution)/shard_map/ppermute | solution.py:551
  77.2 2.2 %backward_0_2.1 = (f32[8,12,32,256]{3,2,1,0:T(8,128)S(1)}, f32[8,12,32,256]{3,2,1,0:T(8,128)}) custom-call(f32[4,32,256]{2,1,0:T(8,128)S(1)} %collective-permute-done.20.came, bf16[8,12,256,256]{3,2,1,0:T(8,128)(2,1)S(1)} %bitcast.29, f32[8,12,32,256]{3,2,1,0:T(8,128)S(1)} %get-tuple-element.131.source, ...), custom_call_target="tpu_custom_call", output_to_operand_aliasing={{0}: (5, {}), {1}: (6, {})} | custom-call | flops 67108864 | bytes 2097152 | tf_op jit(solution)/shard_map/backward_0_2/pallas_call | solution.py:407
  (20 shorter events, 0.1 us)
Async XLA Ops:
  0.0 9.4 %copy-start = (f32[2,4,12,32,256]{4,3,2,1,0:T(8,128)S(1)}, f32[2,4,12,32,256]{4,3,2,1,0:T(8,128)}, u32[]{:S(2)}) copy-start(f32[2,4,12,32,256]{4,3,2,1,0:T(8,128)} %param.5) | copy-start | bytes 9437188
  0.0 9.4 %copy-start.1 = (f32[2,4,12,32,256]{4,3,2,1,0:T(8,128)S(1)}, f32[2,4,12,32,256]{4,3,2,1,0:T(8,128)}, u32[]{:S(2)}) copy-start(f32[2,4,12,32,256]{4,3,2,1,0:T(8,128)} %param.6) | copy-start | bytes 9437188
  3.0 12.9 %collective-permute-start = (f32[12,32,256]{2,1,0:T(8,128)S(1)}, f32[12,32,256]{2,1,0:T(8,128)S(1)}, u32[]{:S(2)}, u32[]{:S(2)}) collective-permute-start(f32[12,32,256]{2,1,0:T(8,128)S(1)} %get-tuple-element.82), channel_id=1, source_target_pairs={{32,0},{64,32},{96,64},{33,1},{65,33},{97,65},{34,2},{66,34},{98,6... | collective-permute-start | bytes 1179656 | tf_op jit(solution)/shard_map/ppermute | solution.py:452
  4.4 15.0 %collective-permute-start.1 = (f32[8,2,32,256]{3,2,1,0:T(8,128)S(1)}, f32[8,2,32,256]{3,2,1,0:T(8,128)S(1)}, u32[]{:S(2)}, u32[]{:S(2)}) collective-permute-start(f32[8,2,32,256]{3,2,1,0:T(8,128)S(1)} %get-tuple-element.87), channel_id=1, source_target_pairs={{0,1},{2,3},{4,5},{6,7},{8,9},{10,11},{12,13},{14,15},{16,17},{18,... | collective-permute-start | bytes 1572872 | tf_op jit(solution)/shard_map/ppermute | solution.py:433
  4.5 14.9 %collective-permute-start.2 = (f32[8,2,32,256]{3,2,1,0:T(8,128)S(1)}, f32[8,2,32,256]{3,2,1,0:T(8,128)S(1)}, u32[]{:S(2)}, u32[]{:S(2)}) collective-permute-start(f32[8,2,32,256]{3,2,1,0:T(8,128)S(1)} %get-tuple-element.88), channel_id=1, source_target_pairs={{1,2},{3,4},{5,6},{7,8},{9,10},{11,12},{13,14},{15,16},{17,18},{19... | collective-permute-start | bytes 1572872 | tf_op jit(solution)/shard_map/ppermute | solution.py:433
  16.2 8.2 %collective-permute-start.5 = (f32[4,32,256]{2,1,0:T(8,128)S(1)}, f32[4,32,256]{2,1,0:T(8,128)S(1)}, u32[]{:S(2)}, u32[]{:S(2)}) collective-permute-start(f32[4,32,256]{2,1,0:T(8,128)S(1)} %get-tuple-element.101), channel_id=1, source_target_pairs={{0,32},{1,33},{2,34},{3,35},{4,36},{5,37},{6,38},{7,39},{8,40},{9,... | collective-permute-start | bytes 393224 | tf_op jit(solution)/shard_map/ppermute | solution.py:498
  19.5 4.9 %slice-start = ((s8[12582912]{0:T(1024)(128)(4,1)}), s8[4194304]{0:T(1024)(128)(4,1)S(1)}, s32[]{:S(2)}) async-start(s8[12582912]{0:T(1024)(128)(4,1)} %bitcast.7), calls=%async_computation | async-start | bytes 8388608
  19.5 4.9 %slice-start.1 = ((s8[12582912]{0:T(1024)(128)(4,1)}), s8[4194304]{0:T(1024)(128)(4,1)S(1)}, s32[]{:S(2)}) async-start(s8[12582912]{0:T(1024)(128)(4,1)} %bitcast.7), calls=%async_computation.1 | async-start | bytes 8388608
  20.9 5.3 %collective-permute-start.4 = (f32[4,32,256]{2,1,0:T(8,128)S(1)}, f32[4,32,256]{2,1,0:T(8,128)S(1)}, u32[]{:S(2)}, u32[]{:S(2)}) collective-permute-start(f32[4,32,256]{2,1,0:T(8,128)S(1)} %get-tuple-element.100), channel_id=1, source_target_pairs={{0,32},{1,33},{2,34},{3,35},{4,36},{5,37},{6,38},{7,39},{8,40},{9,... | collective-permute-start | bytes 393224 | tf_op jit(solution)/shard_map/ppermute | solution.py:498
  22.5 2.3 %slice-start.2 = ((s8[12582912]{0:T(1024)(128)(4,1)}), s8[4194304]{0:T(1024)(128)(4,1)S(1)}, s32[]{:S(2)}) async-start(s8[12582912]{0:T(1024)(128)(4,1)} %bitcast.7), calls=%async_computation.2 | async-start | bytes 8388608
  22.8 4.8 %collective-permute-start.3 = (f32[4,32,256]{2,1,0:T(8,128)S(1)}, f32[4,32,256]{2,1,0:T(8,128)S(1)}, u32[]{:S(2)}, u32[]{:S(2)}) collective-permute-start(f32[4,32,256]{2,1,0:T(8,128)S(1)} %get-tuple-element.98), channel_id=1, source_target_pairs={{0,32},{1,33},{2,34},{3,35},{4,36},{5,37},{6,38},{7,39},{8,40},{9,... | collective-permute-start | bytes 393224 | tf_op jit(solution)/shard_map/ppermute | solution.py:498
  24.8 3.5 %collective-permute-start.8 = (f32[4,32,256]{2,1,0:T(8,128)S(1)}, f32[4,32,256]{2,1,0:T(8,128)S(1)}, u32[]{:S(2)}, u32[]{:S(2)}) collective-permute-start(f32[4,32,256]{2,1,0:T(8,128)S(1)} %get-tuple-element.109), channel_id=1, source_target_pairs={{32,64},{33,65},{34,66},{35,67},{36,68},{37,69},{38,70},{39,71},{4... | collective-permute-start | bytes 393224 | tf_op jit(solution)/shard_map/ppermute | solution.py:498
  26.2 2.8 %collective-permute-start.7 = (f32[4,32,256]{2,1,0:T(8,128)S(1)}, f32[4,32,256]{2,1,0:T(8,128)S(1)}, u32[]{:S(2)}, u32[]{:S(2)}) collective-permute-start(f32[4,32,256]{2,1,0:T(8,128)S(1)} %get-tuple-element.108), channel_id=1, source_target_pairs={{32,64},{33,65},{34,66},{35,67},{36,68},{37,69},{38,70},{39,71},{4... | collective-permute-start | bytes 393224 | tf_op jit(solution)/shard_map/ppermute | solution.py:498
  27.6 2.1 %collective-permute-start.6 = (f32[4,32,256]{2,1,0:T(8,128)S(1)}, f32[4,32,256]{2,1,0:T(8,128)S(1)}, u32[]{:S(2)}, u32[]{:S(2)}) collective-permute-start(f32[4,32,256]{2,1,0:T(8,128)S(1)} %get-tuple-element.107), channel_id=1, source_target_pairs={{32,64},{33,65},{34,66},{35,67},{36,68},{37,69},{38,70},{39,71},{4... | collective-permute-start | bytes 393224 | tf_op jit(solution)/shard_map/ppermute | solution.py:498
  28.3 2.1 %collective-permute-start.11 = (f32[4,32,256]{2,1,0:T(8,128)S(1)}, f32[4,32,256]{2,1,0:T(8,128)S(1)}, u32[]{:S(2)}, u32[]{:S(2)}) collective-permute-start(f32[4,32,256]{2,1,0:T(8,128)S(1)} %get-tuple-element.117), channel_id=1, source_target_pairs={{64,96},{65,97},{66,98},{67,99},{68,100},{69,101},{70,102},{71,103... | collective-permute-start | bytes 393224 | tf_op jit(solution)/shard_map/ppermute | solution.py:498
  29.0 1.4 %collective-permute-start.10 = (f32[4,32,256]{2,1,0:T(8,128)S(1)}, f32[4,32,256]{2,1,0:T(8,128)S(1)}, u32[]{:S(2)}, u32[]{:S(2)}) collective-permute-start(f32[4,32,256]{2,1,0:T(8,128)S(1)} %get-tuple-element.116), channel_id=1, source_target_pairs={{64,96},{65,97},{66,98},{67,99},{68,100},{69,101},{70,102},{71,103... | collective-permute-start | bytes 393224 | tf_op jit(solution)/shard_map/ppermute | solution.py:498
  29.8 6.2 %collective-permute-start.9 = (f32[4,32,256]{2,1,0:T(8,128)S(1)}, f32[4,32,256]{2,1,0:T(8,128)S(1)}, u32[]{:S(2)}, u32[]{:S(2)}) collective-permute-start(f32[4,32,256]{2,1,0:T(8,128)S(1)} %get-tuple-element.115), channel_id=1, source_target_pairs={{64,96},{65,97},{66,98},{67,99},{68,100},{69,101},{70,102},{71,103... | collective-permute-start | bytes 393224 | tf_op jit(solution)/shard_map/ppermute | solution.py:498
  30.5 8.3 %collective-permute-start.12 = (f32[8,2,32,256]{3,2,1,0:T(8,128)S(1)}, f32[8,2,32,256]{3,2,1,0:T(8,128)S(1)}, u32[]{:S(2)}, u32[]{:S(2)}) collective-permute-start(f32[8,2,32,256]{3,2,1,0:T(8,128)S(1)} %get-tuple-element.122), channel_id=1, source_target_pairs={{0,1},{2,3},{4,5},{6,7},{8,9},{10,11},{12,13},{14,15},{16,17},{18,... | collective-permute-start | bytes 1572872 | tf_op jit(solution)/shard_map/ppermute | solution.py:433
  30.6 12.6 %collective-permute-start.13 = (f32[8,2,32,256]{3,2,1,0:T(8,128)S(1)}, f32[8,2,32,256]{3,2,1,0:T(8,128)S(1)}, u32[]{:S(2)}, u32[]{:S(2)}) collective-permute-start(f32[8,2,32,256]{3,2,1,0:T(8,128)S(1)} %get-tuple-element.123), channel_id=1, source_target_pairs={{1,2},{3,4},{5,6},{7,8},{9,10},{11,12},{13,14},{15,16},{17,18},{19... | collective-permute-start | bytes 1572872 | tf_op jit(solution)/shard_map/ppermute | solution.py:433
  36.8 7.7 %collective-permute-start.16 = (f32[4,32,256]{2,1,0:T(8,128)S(1)}, f32[4,32,256]{2,1,0:T(8,128)S(1)}, u32[]{:S(2)}, u32[]{:S(2)}) collective-permute-start(f32[4,32,256]{2,1,0:T(8,128)S(1)} %get-tuple-element.133), channel_id=1, source_target_pairs={{96,64},{97,65},{98,66},{99,67},{100,68},{101,69},{102,70},{103,71... | collective-permute-start | bytes 393224 | tf_op jit(solution)/shard_map/ppermute | solution.py:551
  38.1 7.3 %collective-permute-start.15 = (f32[4,32,256]{2,1,0:T(8,128)S(1)}, f32[4,32,256]{2,1,0:T(8,128)S(1)}, u32[]{:S(2)}, u32[]{:S(2)}) collective-permute-start(f32[4,32,256]{2,1,0:T(8,128)S(1)} %get-tuple-element.132), channel_id=1, source_target_pairs={{96,64},{97,65},{98,66},{99,67},{100,68},{101,69},{102,70},{103,71... | collective-permute-start | bytes 393224 | tf_op jit(solution)/shard_map/ppermute | solution.py:551
  43.8 2.4 %collective-permute-start.14 = (f32[4,32,256]{2,1,0:T(8,128)S(1)}, f32[4,32,256]{2,1,0:T(8,128)S(1)}, u32[]{:S(2)}, u32[]{:S(2)}) collective-permute-start(f32[4,32,256]{2,1,0:T(8,128)S(1)} %get-tuple-element.130), channel_id=1, source_target_pairs={{96,64},{97,65},{98,66},{99,67},{100,68},{101,69},{102,70},{103,71... | collective-permute-start | bytes 393224 | tf_op jit(solution)/shard_map/ppermute | solution.py:551
  44.7 2.4 %collective-permute-start.19 = (f32[4,32,256]{2,1,0:T(8,128)S(1)}, f32[4,32,256]{2,1,0:T(8,128)S(1)}, u32[]{:S(2)}, u32[]{:S(2)}) collective-permute-start(f32[4,32,256]{2,1,0:T(8,128)S(1)} %get-tuple-element.142), channel_id=1, source_target_pairs={{64,32},{65,33},{66,34},{67,35},{68,36},{69,37},{70,38},{71,39},{7... | collective-permute-start | bytes 393224 | tf_op jit(solution)/shard_map/ppermute | solution.py:551
  45.6 3.0 %collective-permute-start.18 = (f32[4,32,256]{2,1,0:T(8,128)S(1)}, f32[4,32,256]{2,1,0:T(8,128)S(1)}, u32[]{:S(2)}, u32[]{:S(2)}) collective-permute-start(f32[4,32,256]{2,1,0:T(8,128)S(1)} %get-tuple-element.141), channel_id=1, source_target_pairs={{64,32},{65,33},{66,34},{67,35},{68,36},{69,37},{70,38},{71,39},{7... | collective-permute-start | bytes 393224 | tf_op jit(solution)/shard_map/ppermute | solution.py:551
  46.4 3.6 %collective-permute-start.17 = (f32[4,32,256]{2,1,0:T(8,128)S(1)}, f32[4,32,256]{2,1,0:T(8,128)S(1)}, u32[]{:S(2)}, u32[]{:S(2)}) collective-permute-start(f32[4,32,256]{2,1,0:T(8,128)S(1)} %get-tuple-element.140), channel_id=1, source_target_pairs={{64,32},{65,33},{66,34},{67,35},{68,36},{69,37},{70,38},{71,39},{7... | collective-permute-start | bytes 393224 | tf_op jit(solution)/shard_map/ppermute | solution.py:551
  47.3 24.3 %collective-permute-start.22 = (f32[4,32,256]{2,1,0:T(8,128)S(1)}, f32[4,32,256]{2,1,0:T(8,128)S(1)}, u32[]{:S(2)}, u32[]{:S(2)}) collective-permute-start(f32[4,32,256]{2,1,0:T(8,128)S(1)} %get-tuple-element.151), channel_id=1, source_target_pairs={{32,0},{33,1},{34,2},{35,3},{36,4},{37,5},{38,6},{39,7},{40,8},{41... | collective-permute-start | bytes 393224 | tf_op jit(solution)/shard_map/ppermute | solution.py:551
  48.8 25.4 %collective-permute-start.21 = (f32[4,32,256]{2,1,0:T(8,128)S(1)}, f32[4,32,256]{2,1,0:T(8,128)S(1)}, u32[]{:S(2)}, u32[]{:S(2)}) collective-permute-start(f32[4,32,256]{2,1,0:T(8,128)S(1)} %get-tuple-element.150), channel_id=1, source_target_pairs={{32,0},{33,1},{34,2},{35,3},{36,4},{37,5},{38,6},{39,7},{40,8},{41... | collective-permute-start | bytes 393224 | tf_op jit(solution)/shard_map/ppermute | solution.py:551
  50.2 26.9 %collective-permute-start.20 = (f32[4,32,256]{2,1,0:T(8,128)S(1)}, f32[4,32,256]{2,1,0:T(8,128)S(1)}, u32[]{:S(2)}, u32[]{:S(2)}) collective-permute-start(f32[4,32,256]{2,1,0:T(8,128)S(1)} %get-tuple-element.149), channel_id=1, source_target_pairs={{32,0},{33,1},{34,2},{35,3},{36,4},{37,5},{38,6},{39,7},{40,8},{41... | collective-permute-start | bytes 393224 | tf_op jit(solution)/shard_map/ppermute | solution.py:551

commit v6 on v5

--- a/solution.py
+++ b/solution.py
@@ -12,13 +12,15 @@
 R = 32
 BS = 256
 FORWARD = ((2, 3, 4, 5), (0, 1, 10, 11), (6, 7, 8, 9))
-BACKWARD = ((2, 3, 4, 5), (6, 7, 8, 9), (0, 1, 10, 11))
+LEFT, RIGHT = (0, 1), (10, 11)
+NEAR, FAR = 2, 3
 OUTER = 1
 STRIP = 4
 DOWN = tuple(range(COLS - 1, -1, -1))
 SIDES = ((2, -1), (3, 1), (4, -2), (5, 2))
 COST_TURN = 7
-COST_LAST = -3
+COST_LAST = (-3, -3, -3, -3)
+COST_BACK = (0, 0, 0, 3)
 NT = (((1,), (1,)), ((), ()))
 VMEM = pltpu.VMEM
 ANY = pl.ANY
@@ -29,7 +31,6 @@
 FIELD_MORE = (COLS + 1, LANES, R, BS)
 EDGE = (COLS, 2, R, BS)
 BLOCKS = (COLS, LANES, BS, BS)
-OWN_BLOCKS = (COLS, 4, BS, BS)
 PER = 4
 COEFS = (6, COLS // PER, LANES, PER, BS)
 WEIGHTS = (COLS + 1, LANES, BS)
@@ -54,15 +55,11 @@
 
 
 def solve(xs, inverse, q, lanes):
-    alone = inverse.shape[1] < LANES
     return [
         lax.dot_general(
-            x.astype(jnp.bfloat16),
-            inverse[q, j if alone else lane],
-            NT,
-            preferred_element_type=jnp.float32,
+            x.astype(jnp.bfloat16), inverse[q, lane], NT, preferred_element_type=jnp.float32
         )
-        for j, (x, lane) in enumerate(zip(xs, lanes))
+        for x, lane in zip(xs, lanes)
     ]
 
 
@@ -85,20 +82,15 @@
     return ice[q // PER, q % PER, lane].astype(jnp.float32)
 
 
-def prep_kernel(
-    ice_hbm, st_hbm, couple_hbm, inv_hbm, nxt, edge_in, edge_out, couple, mask, own, ice, sem
-):
+def prep_kernel(ice_hbm, st_hbm, nxt, edge_in, edge_out, mask, ice, sem):
     even = is_even()
     lane_in = jnp.where(even, LANES - 2, 0)
     lane_out = jnp.where(even, 0, LANES - 2)
-    a, n = runs_of(FORWARD[0])[0]
     copies = [
         pltpu.make_async_copy(ice_hbm, ice, sem.at[0]),
-        pltpu.make_async_copy(couple_hbm, couple, sem.at[1]),
-        pltpu.make_async_copy(st_hbm.at[0], nxt, sem.at[2]),
-        pltpu.make_async_copy(st_hbm.at[:, pl.ds(lane_out, 2)], edge_out, sem.at[3]),
-        pltpu.make_async_copy(st_hbm.at[:, pl.ds(lane_in, 2)], edge_in, sem.at[4]),
-        pltpu.make_async_copy(inv_hbm.at[:, pl.ds(a, n)], own, sem.at[5]),
+        pltpu.make_async_copy(st_hbm.at[0], nxt, sem.at[1]),
+        pltpu.make_async_copy(st_hbm.at[:, pl.ds(lane_out, 2)], edge_out, sem.at[2]),
+        pltpu.make_async_copy(st_hbm.at[:, pl.ds(lane_in, 2)], edge_in, sem.at[3]),
     ]
     for copy in copies:
         copy.start()
@@ -110,7 +102,7 @@
     for q in range(COLS):
         for lane in range(LANES):
             mask[q, pl.ds(lane, 1), :] = jnp.full((1, BS), ice_weight(q, lane), jnp.float32)
-    for copy in copies[1:5]:
+    for copy in copies[1:]:
         copy.wait()
     for lane in range(LANES):
         nxt[lane] = weight(mask, 0, lane) * nxt[lane]
@@ -118,7 +110,6 @@
         for j in range(2):
             edge_out[q, j] = ice_weight(q, lane_out + j) * edge_out[q, j]
             edge_in[q, j] = ice_weight(q, lane_in + j) * edge_in[q, j]
-    copies[5].wait()
 
 
 def halo_of(even, halo_in, halo_out, q, lane):
@@ -185,51 +176,53 @@
     make_source(lanes, 0, rs, start, couple, mask, source, halo)
     for q in range(COLS - 1):
         if arriving is not None:
-            arriving(q).wait()
+            for copy in arriving(q):
+                copy.wait()
         forward_chain(lanes, q, source, inverse, couple, mask, field, sent, edges)
         if q + 2 < COLS:
             make_source(lanes, q + 1, rs, start, couple, mask, source, halo)
 
 
 def first_kernel(
-    own, inv_hbm, rs, start, couple, mask, source, field, sent, sent_last, own_last, own_outer, sem, sem_outer
+    inv_hbm, couple_hbm, rs, start, mask, inverse, couple, source, field, sent, sent_last, sems, sem
 ):
     first = lax.axis_index("strip") == 0
-    a, n = runs_of(FORWARD[2])[0]
+    couplings = pltpu.make_async_copy(couple_hbm, couple, sem.at[0])
+
+    def coming(lanes, at):
+        return lambda q: lane_copies(inv_hbm, inverse, q, lanes, sems.at[at])
 
     @pl.when(first)
     def _():
-        def arriving(q):
-            return pltpu.make_async_copy(inv_hbm.at[q, pl.ds(a, n)], own_last.at[q], sem.at[q])
-
-        for q in range(COLS):
-            arriving(q).start()
-        outer = [
-            pltpu.make_async_copy(
-                inv_hbm.at[:, pl.ds(b, 2)], own_outer.at[:, pl.ds(2 * i, 2)], sem_outer.at[i]
-            )
-            for i, (b, _) in enumerate(runs_of(FORWARD[OUTER]))
-        ]
-        for copy in outer:
-            copy.start()
+        parts = [coming(FORWARD[chunk], chunk) for chunk in (0, 2, OUTER)]
+        couplings.start()
+        for part in parts:
+            start_all(part)
         field[0] = jnp.zeros((LANES, R, BS), jnp.float32)
+        couplings.wait()
         sweep_first(
-            FORWARD[0], rs, start, source, own, couple, mask, field, sent, None, None
+            FORWARD[0], rs, start, source, inverse, couple, mask, field, sent, None, None, parts[0]
         )
         sweep_first(
-            FORWARD[2], rs, start, source, own_last, couple, mask, field, sent_last, None, None, arriving
+            FORWARD[2], rs, start, source, inverse, couple, mask, field, sent_last, None, None, parts[1]
         )
-        arriving(COLS - 1).wait()
-        for copy in outer:
+        for copy in parts[0](COLS - 1) + parts[1](COLS - 1):
             copy.wait()
+        wait_all(parts[2])
 
     @pl.when(jnp.logical_not(first))
     def _():
+        every = coming(range(LANES), 0)
+        couplings.start()
+        start_all(every)
+        couplings.wait()
+
         def step(q, _):
             make_source(range(LANES), q, rs, start, couple, mask, source)
             return 0
 
         lax.fori_loop(0, COLS - 1, step, 0)
+        wait_all(every)
 
 
 def tail_kernel(chunk, nxt, own, rs, start, couple, mask, *refs):
@@ -308,32 +301,52 @@
         sent[j] = value
 
 
+def by_parity(active, even, chunk, body):
+    chunks = {
+        True: FORWARD[::2] + (RIGHT, LEFT),
+        False: FORWARD[::2] + (LEFT, RIGHT),
+    }
+    if chunk < NEAR:
+
+        @pl.when(active)
+        def _():
+            body(chunks[True][chunk], chunks[True][chunk - 1])
+
+    else:
+
+        @pl.when(jnp.logical_and(active, even))
+        def _():
+            body(chunks[True][chunk], chunks[True][chunk - 1])
+
+        @pl.when(jnp.logical_and(active, jnp.logical_not(even)))
+        def _():
+            body(chunks[False][chunk], chunks[False][chunk - 1])
+
+
 def backward_sweep(
-    chunk, final, inverse, source, couple, mask, result, out, sent, sem, sem_own, beside
+    lanes, before, last, inverse, source, couple, mask, result, out, sent, sem, sem_own, beside
 ):
-    lanes = BACKWARD[chunk]
-    last = final and chunk == len(BACKWARD) - 1
-
-    def before(q):
-        return lane_copies(result, out, q, BACKWARD[chunk - 1], sem) if chunk > 0 else []
+    def earlier(q):
+        return lane_copies(result, out, q, before, sem)
 
     def own(q):
         return lane_copies(result, out, q, lanes, sem_own) if last else []
 
-    start_all(before)
+    if before:
+        start_all(earlier)
     for q in DOWN:
         backward_chain(lanes, q, source, inverse, couple, mask, result, sent)
         for copy in own(q):
             copy.start()
         if beside is not None and q > 0:
             beside(q - 1)
-    wait_all(before)
+    if before:
+        wait_all(earlier)
     if last:
         wait_all(own)
 
 
-def last_kernel(chunk, inverse, rs, field, couple, mask, halo_in, halo_out, *refs):
-    lanes = BACKWARD[chunk]
+def last_kernel(chunk, inverse, rs, field, couple, mask, halo, *refs):
     source, result, out, sent, sem, sem_own = refs[-6:]
     active = lax.axis_index("strip") == STRIP - 1
     even = is_even()
@@ -341,58 +354,79 @@
     def near(q, lane):
         if 0 <= lane < LANES:
             return field[q + 1, lane]
-        return halo_of(even, halo_in, halo_out, q, lane)
-
-    def source_of(q):
+        return halo[q, lane + 2 if lane < 0 else lane - LANES]
+
+    def source_of(lanes, q):
         for lane in lanes:
             total = rs[q, lane] + coef(couple, 0, q, lane) * field[q, lane]
             for k, step in SIDES:
                 total = total + coef(couple, k, q, lane) * near(q, lane + step)
             source[q, lane] = total
 
-    @pl.when(active)
-    def _():
+    def sweep(lanes, before):
         for j in range(len(lanes)):
             sent[j] = jnp.zeros((R, BS), jnp.float32)
-        source_of(COLS - 1)
+        source_of(lanes, COLS - 1)
         backward_sweep(
-            chunk, False, inverse, source, couple, mask, result, out, sent, sem, sem_own, source_of
+            lanes,
+            before if chunk > 0 else None,
+            False,
+            inverse,
+            source,
+            couple,
+            mask,
+            result,
+            out,
+            sent,
+            sem,
+            sem_own,
+            functools.partial(source_of, lanes),
         )
 
-    @pl.when(jnp.logical_not(active))
-    def _():
+    def prepare(lanes, _):
         def step(q, _):
-            source_of(q)
+            source_of(lanes, q)
             return 0
 
         lax.fori_loop(0, COLS, step, 0)
+
+    by_parity(active, even, chunk, sweep)
+    by_parity(jnp.logical_not(active), even, chunk, prepare)
 
 
 def backward_kernel(chunk, stage, came, inverse, source, couple, mask, *refs):
     result, out, sent, sem, sem_own = refs[2:]
     strip = lax.axis_index("strip")
-
-    @pl.when(strip == stage)
-    def _():
+    even = is_even()
+
+    def sweep(lanes, before):
         sent[...] = came[...]
         backward_sweep(
-            chunk, stage == 0, inverse, source, couple, mask, result, out, sent, sem, sem_own, None
+            lanes,
+            before if chunk > 0 else None,
+            stage == 0 and chunk == FAR,
+            inverse,
+            source,
+            couple,
+            mask,
+            result,
+            out,
+            sent,
+            sem,
+            sem_own,
+            None,
         )
 
+    def flush(lanes, _):
+        copy = pltpu.make_async_copy(
+            result.at[:, pl.ds(lanes[0], 2)], out.at[:, pl.ds(lanes[0], 2)], sem_own.at[0]
+        )
+        copy.start()
+        copy.wait()
+
+    by_parity(strip == stage, even, chunk, sweep)
     if chunk == 0:
-
-        @pl.when(strip == stage + 1)
-        def _():
-            copies = [
-                pltpu.make_async_copy(
-                    result.at[:, pl.ds(a, n)], out.at[:, pl.ds(a, n)], sem_own.at[i]
-                )
-                for i, (a, n) in enumerate(runs_of(BACKWARD[-1]))
-            ]
-            for copy in copies:
-                copy.start()
-            for copy in copies:
-                copy.wait()
+        by_parity(strip == stage + 1, even, FAR, flush)
 
 
 def vmem(shape, dtype=jnp.float32):
@@ -441,33 +475,33 @@
     def piece(lanes):
         return (len(lanes), R, BS)
 
-    own_blocks = [(vmem(OWN_BLOCKS, jnp.bfloat16), VMEM)]
-    nxt, edge_in, edge_out, coefs, mask, own = run(
+    nxt, edge_in, edge_out, mask = run(
         prep_kernel,
         "prep",
-        [(ice_mask, HBM), (start, HBM), (couple.transpose(0, 1, 3, 2, 4), HBM), (inverse, HBM)],
-        made(FIRST, EDGE, EDGE, COEFS, WEIGHTS) + own_blocks,
-        [pltpu.SMEM(ice_mask.shape, jnp.int32), dma((6,))],
+        [(ice_mask, HBM), (start, HBM)],
+        made(FIRST, EDGE, EDGE, WEIGHTS),
+        [pltpu.SMEM(ice_mask.shape, jnp.int32), dma((4,))],
+        cost=6,
     )
     nxt = lax.ppermute(nxt, "strip", to_back)
     halo_out = swapped(edge_out, pairs_out)
     halo_in = swapped(edge_in, pairs_in)
 
     sents = {}
-    rest = inside(rs, start, coefs, mask)
     ends = [piece(FORWARD[0]), piece(FORWARD[2])]
-    source, field, sent, sent_last, own_last, own_outer = run(
+    inverse, coefs, source, field, sent, sent_last = run(
         first_kernel,
         "first",
-        inside(own) + [(inverse, HBM)] + rest,
-        made(FIELD, FIELD_MORE, *ends) + own_blocks * 2,
-        [dma((COLS,)), dma((2,))],
+        [(inverse, HBM), (couple.transpose(0, 1, 3, 2, 4), HBM)] + inside(rs, start, mask),
+        [(vmem(BLOCKS, jnp.bfloat16), VMEM)] + made(COEFS, FIELD, FIELD_MORE, *ends),
+        [dma((3, COLS)), dma((1,))],
         cost=-10,
     )
+    rest = inside(rs, start, coefs, mask)
     source, field, sents[0, 0] = run(
         functools.partial(tail_kernel, 0),
         "tail_0",
-        inside(nxt, own) + rest + inside(source, field, sent),
+        inside(nxt, inverse) + rest + inside(source, field, sent),
         made(FIELD, FIELD_MORE, ends[0]),
         [],
         {6: 0, 7: 1, 8: 2},
@@ -476,7 +510,7 @@
     source, field, edge_in, edge_out, sents[0, 1] = run(
         outer_kernel,
         "outer",
-        inside(nxt, halo_in, halo_out, own_outer) + rest + inside(source, field),
+        inside(nxt, halo_in, halo_out, inverse) + rest + inside(source, field),
         made(FIELD, FIELD_MORE, EDGE, EDGE, piece(FORWARD[OUTER])),
         [],
         {8: 0, 9: 1},
@@ -484,7 +518,7 @@
     source, field, sents[0, 2] = run(
         functools.partial(tail_kernel, 2),
         "tail_2",
-        inside(nxt, own_last) + rest + inside(source, field, sent_last),
+        inside(nxt, inverse) + rest + inside(source, field, sent_last),
         made(FIELD, FIELD_MORE, ends[1]),
         [],
         {6: 0, 7: 1, 8: 2},
@@ -525,14 +559,17 @@
     out_shape = [(jax.ShapeDtypeStruct(FIELD, jnp.float32), HBM)]
     sems = [dma((COLS,)), dma((COLS,))]
     result = out = None
-    for chunk, lanes in enumerate(BACKWARD):
-        sides = inside(halo_in, halo_out) if chunk == len(BACKWARD) - 1 else []
-        operands = inside(inverse, rs, field, coefs, mask) + sides + inside(source)
-        base = len(operands) - 1
+    pieces = [piece(FORWARD[0]), piece(FORWARD[2]), piece(LEFT), piece(RIGHT)]
+    for chunk, shape in enumerate(pieces):
+        operands = inside(inverse, rs, field, coefs, mask)
+        kernel = functools.partial(last_kernel, chunk)
+        if chunk < NEAR:
+            kernel = functools.partial(without_halo, kernel)
+        else:
+            operands += inside(halo_in if chunk == NEAR else halo_out)
+        base = len(operands)
+        operands += inside(source)
         aliases = {base: 0}
-        kernel = functools.partial(last_kernel, chunk)
-        if not sides:
-            kernel = functools.partial(without_halos, kernel)
         if chunk > 0:
             operands += inside(result) + [(out, HBM)]
             aliases |= {base + 1: 1, base + 2: 2}
@@ -540,23 +577,24 @@
             kernel,
             f"last_{chunk}",
             operands,
-            made(FIELD, FIELD) + out_shape + made(piece(lanes)),
+            made(FIELD, FIELD) + out_shape + made(shape),
             sems,
             aliases,
-            cost=COST_LAST,
+            cost=COST_LAST[chunk],
         )
 
     for stage in range(STRIP - 2, -1, -1):
-        for chunk, lanes in enumerate(BACKWARD):
+        for chunk, shape in enumerate(pieces):
             came = lax.ppermute(sents[stage + 1, chunk], "strip", [(stage + 1, stage)])
             sending = stage > 0
             got = run(
                 functools.partial(backward_kernel, chunk, stage),
                 f"backward_{stage}_{chunk}",
                 inside(came, inverse, source, coefs, mask, result) + [(out, HBM)],
-                made(FIELD) + out_shape + (made(piece(lanes)) if sending else []),
-                ([] if sending else [vmem(piece(lanes))]) + sems,
+                made(FIELD) + out_shape + (made(shape) if sending else []),
+                ([] if sending else [vmem(shape)]) + sems,
                 {5: 0, 6: 1},
+                cost=COST_BACK[chunk],
             )
             result, out = got[:2]
             if sending:
@@ -564,8 +602,8 @@
     return out.reshape(right_side.shape)
 
 
-def without_halos(kernel, inverse, rs, field, couple, mask, *refs):
-    kernel(inverse, rs, field, couple, mask, None, None, *refs)
+def without_halo(kernel, inverse, rs, field, couple, mask, *refs):
+    kernel(inverse, rs, field, couple, mask, None, *refs)
 
 
 def solution(mesh):

time: 79.9 us -> 79.3 us (level)
  waiting for transfers between devices: 31.4 us -> 27.5 us
  Pallas kernels: 17 us -> 19.2 us
    ppermute x9 -> x12, waiting for transfers between devices: 22.6 us -> 19.7 us  [on_device(): came = lax.ppermute(sents[stage + 1, chunk], 'strip', [(stage + 1, stage)])]
    ppermute x9 -> x12, starting transfers between devices: 7.89 us -> 10.5 us  [on_device(): came = lax.ppermute(sents[stage + 1, chunk], 'strip', [(stage + 1, stage)])]
    pallas_call x27 -> x31, Pallas kernels: 17 us -> 19.2 us  [run(): pl.pallas_call(kernel, name=name, out_shape=[o for o, _ in outs], in_spec...]
    ppermute x1, waiting for transfers between devices: 2.86 us -> 0.8 us  [on_device(): nxt = lax.ppermute(nxt, 'strip', to_back)]
    ppermute x4, starting transfers between devices: 10.4 us -> 8.88 us  [swapped(): return lax.ppermute(value, 'tile', pairs + [(b, a) for a, b in pairs])]
    ppermute x9, waiting for transfers between devices: 1.51 us -> 2.34 us  [on_device(): came = lax.ppermute(sents[stage - 1, chunk], 'strip', [(stage - 1, stage)])]
  transfers between devices with their start and end apart: 23 -> 26, of which waited for: 7 -> 7; matrix products, arithmetic and copies ran while one was open for 0% -> 0% of each run, Pallas kernels for 15% -> 20%
where the time goes in v6:
time: 79.3 us; the launch traced here: 78.1 us
  starting transfers between devices  30.7 us (39%)
  waiting for transfers between devices  27.5 us (35%)
  Pallas kernels  19.2 us (24%)
    ppermute x12, waiting for transfers between devices, on_device(): came = lax.ppermute(sents[stage + 1, chunk], 'strip', [(stage + 1, stage)])  19.7 us
    pallas_call x31, Pallas kernels, run(): pl.pallas_call(kernel, name=name, out_shape=[o for o, _ in outs], in_spec...  19.2 us
    ppermute x12, starting transfers between devices, on_device(): came = lax.ppermute(sents[stage + 1, chunk], 'strip', [(stage + 1, stage)])  10.5 us
    ppermute x9, starting transfers between devices, on_device(): came = lax.ppermute(sents[stage - 1, chunk], 'strip', [(stage - 1, stage)])  9.86 us
    ppermute x4, starting transfers between devices, swapped(): return lax.ppermute(value, 'tile', pairs + [(b, a) for a, b in pairs])  8.88 us
    ppermute x4, waiting for transfers between devices, swapped(): return lax.ppermute(value, 'tile', pairs + [(b, a) for a, b in pairs])  4.7 us
    ppermute x9, waiting for transfers between devices, on_device(): came = lax.ppermute(sents[stage - 1, chunk], 'strip', [(stage - 1, stage)])  2.34 us
  transfers between devices with their start and end apart: 26, of which 7 were waited for; matrix products, arithmetic and copies ran while one was open for 0% of the time, Pallas kernels for 20%

profile of v6, /device:TPU:96, one launch (start us, length us, event | category | flops | bytes accessed | tf_op | source)
XLA Modules:
  0.0 78.1 jit_solution(15974003871078258841)
XLA Ops:
  0.0 1.6 %prep.1 = (f32[12,32,256]{2,1,0:T(8,128)S(1)}, f32[8,2,32,256]{3,2,1,0:T(8,128)S(1)}, f32[8,2,32,256]{3,2,1,0:T(8,128)S(1)}, f32[9,12,256]{2,1,0:T(8,128)S(1)}) custom-call(s32[2,4,12]{2,1,0:T(4,128)} %ice_hbm.1, f32[8,12,32,256]{3,2,1,0:T(8,128)} %bitcast.13), custom_call_target="tpu_custom_call" | custom-call | flops 4294967296 | bytes 134217728 | tf_op jit(solution)/shard_map/prep/pallas_call | solution.py:441
  1.6 1.4 %collective-permute-start = (f32[12,32,256]{2,1,0:T(8,128)S(1)}, f32[12,32,256]{2,1,0:T(8,128)S(1)}, u32[]{:S(2)}, u32[]{:S(2)}) collective-permute-start(f32[12,32,256]{2,1,0:T(8,128)S(1)} %get-tuple-element.94), channel_id=1, source_target_pairs={{32,0},{64,32},{96,64},{33,1},{65,33},{97,65},{34,2},{66,34},{98,6... | collective-permute-start | bytes 1179656 | tf_op jit(solution)/shard_map/ppermute | solution.py:486
  3.0 0.1 collective-permute-start.1
  3.1 4.9 %collective-permute-start.2 = (f32[8,2,32,256]{3,2,1,0:T(8,128)S(1)}, f32[8,2,32,256]{3,2,1,0:T(8,128)S(1)}, u32[]{:S(2)}, u32[]{:S(2)}) collective-permute-start(f32[8,2,32,256]{3,2,1,0:T(8,128)S(1)} %get-tuple-element.97), channel_id=1, source_target_pairs={{1,2},{3,4},{5,6},{7,8},{9,10},{11,12},{13,14},{15,16},{17,18},{19... | collective-permute-start | bytes 1572872 | tf_op jit(solution)/shard_map/ppermute | solution.py:467
  8.0 5.7 %first.1 = (bf16[8,12,256,256]{3,2,1,0:T(8,128)(2,1)S(1)}, f32[6,2,12,4,256]{4,3,2,1,0:T(4,128)S(1)}, f32[8,12,32,256]{3,2,1,0:T(8,128)S(1)}, f32[9,12,32,256]{3...) custom-call(bf16[8,12,256,256]{3,2,1,0:T(8,128)(2,1)} %bitcast.18, ...), custom_call_target="tpu_custom_call" | custom-call | flops 65536 | bytes 2048 | tf_op jit(solution)/shard_map/first/pallas_call | solution.py:441
  13.7 0.8 %collective-permute-done.nxt = f32[12,32,256]{2,1,0:T(8,128)S(1)} collective-permute-done((f32[12,32,256]{2,1,0:T(8,128)S(1)}, f32[12,32,256]{2,1,0:T(8,128)S(1)}, u32[]{:S(2)}, u32[]{:S(2)}) %collective-permute-start) | collective-permute-done | bytes 393248 | tf_op jit(solution)/shard_map/ppermute | solution.py:486
  14.5 0.3 tail_0.1
  14.8 3.3 %collective-permute-start.5 = (f32[4,32,256]{2,1,0:T(8,128)S(1)}, f32[4,32,256]{2,1,0:T(8,128)S(1)}, u32[]{:S(2)}, u32[]{:S(2)}) collective-permute-start(f32[4,32,256]{2,1,0:T(8,128)S(1)} %get-tuple-element.109), channel_id=1, source_target_pairs={{0,32},{1,33},{2,34},{3,35},{4,36},{5,37},{6,38},{7,39},{8,40},{9,... | collective-permute-start | bytes 393224 | tf_op jit(solution)/shard_map/ppermute | solution.py:532
  18.1 0.0 collective-permute-done.2.halo_out
  18.1 1.4 %outer.1 = (f32[8,12,32,256]{3,2,1,0:T(8,128)S(1)}, f32[9,12,32,256]{3,2,1,0:T(8,128)S(1)}, f32[8,2,32,256]{3,2,1,0:T(8,128)S(1)}, f32[8,2,32,256]{3,2,1,0:T(8,128)S(1)}, f32[4,32,256]{2,1,0:T(8,128)S(1)}) custom-call(f32[12,32,256]{2,1,0:T(8,128)S(1)} %collective-permute-done.nxt, ...), custom_call_target="tpu_custom_call", output_to_operand_aliasing={{0}: (8, {}), {1}: (9, {})} | custom-call | flops 67108864 | bytes 2097152 | tf_op jit(solution)/shard_map/outer/pallas_call | solution.py:441
  19.5 1.3 %collective-permute-start.4 = (f32[4,32,256]{2,1,0:T(8,128)S(1)}, f32[4,32,256]{2,1,0:T(8,128)S(1)}, u32[]{:S(2)}, u32[]{:S(2)}) collective-permute-start(f32[4,32,256]{2,1,0:T(8,128)S(1)} %get-tuple-element.108), channel_id=1, source_target_pairs={{0,32},{1,33},{2,34},{3,35},{4,36},{5,37},{6,38},{7,39},{8,40},{9,... | collective-permute-start | bytes 393224 | tf_op jit(solution)/shard_map/ppermute | solution.py:532
  20.8 0.3 tail_2.1
  21.1 1.3 %collective-permute-start.3 = (f32[4,32,256]{2,1,0:T(8,128)S(1)}, f32[4,32,256]{2,1,0:T(8,128)S(1)}, u32[]{:S(2)}, u32[]{:S(2)}) collective-permute-start(f32[4,32,256]{2,1,0:T(8,128)S(1)} %get-tuple-element.106), channel_id=1, source_target_pairs={{0,32},{1,33},{2,34},{3,35},{4,36},{5,37},{6,38},{7,39},{8,40},{9,... | collective-permute-start | bytes 393224 | tf_op jit(solution)/shard_map/ppermute | solution.py:532
  22.4 0.0 collective-permute-done.5.came
  22.5 0.7 collective-permute-start.8
  23.1 1.6 %collective-permute-done.4.came = f32[4,32,256]{2,1,0:T(8,128)S(1)} collective-permute-done((f32[4,32,256]{2,1,0:T(8,128)S(1)}, f32[4,32,256]{2,1,0:T(8,128)S(1)}, u32[]{:S(2)}, u32[]{:S(2)}) %collective-permute-start.4) | collective-permute-done | bytes 131104 | tf_op jit(solution)/shard_map/ppermute | solution.py:532
  24.7 0.7 collective-permute-start.7
  25.4 0.7 collective-permute-done.3.came
  26.1 0.7 collective-permute-start.6
  26.8 0.7 collective-permute-start.11
  27.5 0.0 collective-permute-done.7.came
  27.5 0.7 collective-permute-start.10
  28.3 0.7 collective-permute-start.9
  28.9 0.0 collective-permute-done.11.came
  29.0 3.9 %collective-permute-start.12 = (f32[8,2,32,256]{3,2,1,0:T(8,128)S(1)}, f32[8,2,32,256]{3,2,1,0:T(8,128)S(1)}, u32[]{:S(2)}, u32[]{:S(2)}) collective-permute-start(f32[8,2,32,256]{3,2,1,0:T(8,128)S(1)} %get-tuple-element.130), channel_id=1, source_target_pairs={{1,2},{3,4},{5,6},{7,8},{9,10},{11,12},{13,14},{15,16},{17,18},{19... | collective-permute-start | bytes 1572872 | tf_op jit(solution)/shard_map/ppermute | solution.py:467
  32.9 0.1 collective-permute-start.13
  33.0 0.0 collective-permute-done.9.came
  33.0 0.2 forward_3_2.1.field
  33.2 0.6 last_0.1
  33.8 0.7 collective-permute-start.17
  34.5 0.6 last_1.1
  35.1 0.7 collective-permute-start.16
  35.8 0.0 collective-permute-done.13.halo
  35.8 0.5 last_2.1
  36.2 0.7 collective-permute-start.15
  36.9 4.7 %collective-permute-done.12.halo = f32[8,2,32,256]{3,2,1,0:T(8,128)S(1)} collective-permute-done((f32[8,2,32,256]{3,2,1,0:T(8,128)S(1)}, f32[8,2,32,256]{3,2,1,0:T(8,128)S(1)}, u32[]{:S(2)}, u32[]{:S(2)}) %collective-permute-start.12) | collective-permute-done | bytes 524320 | tf_op jit(solution)/shard_map/ppermute | solution.py:467
  41.6 0.4 last_3.1
  42.0 0.7 collective-permute-start.14
  42.7 0.2 backward_2_0.1
  42.9 0.7 collective-permute-start.21
  43.6 0.0 collective-permute-done.16.came
  43.6 0.2 backward_2_1.1
  43.8 0.7 collective-permute-start.20
  44.5 0.2 backward_2_2.1
  44.6 0.7 collective-permute-start.19
  45.3 0.2 backward_2_3.1
  45.5 0.7 collective-permute-start.18
  46.2 0.0 collective-permute-done.21.came
  46.2 0.2 backward_1_0.1
  46.4 1.3 %collective-permute-start.25 = (f32[4,32,256]{2,1,0:T(8,128)S(1)}, f32[4,32,256]{2,1,0:T(8,128)S(1)}, u32[]{:S(2)}, u32[]{:S(2)}) collective-permute-start(f32[4,32,256]{2,1,0:T(8,128)S(1)} %get-tuple-element.169), channel_id=1, source_target_pairs={{32,0},{33,1},{34,2},{35,3},{36,4},{37,5},{38,6},{39,7},{40,8},{41... | collective-permute-start | bytes 393224 | tf_op jit(solution)/shard_map/ppermute | solution.py:588
  47.7 0.0 collective-permute-done.20.came
  47.7 0.2 backward_1_1.1
  47.8 1.3 %collective-permute-start.24 = (f32[4,32,256]{2,1,0:T(8,128)S(1)}, f32[4,32,256]{2,1,0:T(8,128)S(1)}, u32[]{:S(2)}, u32[]{:S(2)}) collective-permute-start(f32[4,32,256]{2,1,0:T(8,128)S(1)} %get-tuple-element.168), channel_id=1, source_target_pairs={{32,0},{33,1},{34,2},{35,3},{36,4},{37,5},{38,6},{39,7},{40,8},{41... | collective-permute-start | bytes 393224 | tf_op jit(solution)/shard_map/ppermute | solution.py:588
  49.2 0.2 backward_1_2.1
  49.3 1.3 %collective-permute-start.23 = (f32[2,32,256]{2,1,0:T(8,128)S(1)}, f32[2,32,256]{2,1,0:T(8,128)S(1)}, u32[]{:S(2)}, u32[]{:S(2)}) collective-permute-start(f32[2,32,256]{2,1,0:T(8,128)S(1)} %get-tuple-element.167), channel_id=1, source_target_pairs={{32,0},{33,1},{34,2},{35,3},{36,4},{37,5},{38,6},{39,7},{40,8},{41... | collective-permute-start | bytes 196616 | tf_op jit(solution)/shard_map/ppermute | solution.py:588
  50.6 0.2 backward_1_3.1
  50.8 1.3 %collective-permute-start.22 = (f32[2,32,256]{2,1,0:T(8,128)S(1)}, f32[2,32,256]{2,1,0:T(8,128)S(1)}, u32[]{:S(2)}, u32[]{:S(2)}) collective-permute-start(f32[2,32,256]{2,1,0:T(8,128)S(1)} %get-tuple-element.166), channel_id=1, source_target_pairs={{32,0},{33,1},{34,2},{35,3},{36,4},{37,5},{38,6},{39,7},{40,8},{41... | collective-permute-start | bytes 196616 | tf_op jit(solution)/shard_map/ppermute | solution.py:588
  52.1 16.3 %collective-permute-done.25.came = f32[4,32,256]{2,1,0:T(8,128)S(1)} collective-permute-done((f32[4,32,256]{2,1,0:T(8,128)S(1)}, f32[4,32,256]{2,1,0:T(8,128)S(1)}, u32[]{:S(2)}, u32[]{:S(2)}) %collective-permute-start.25) | collective-permute-done | bytes 131104 | tf_op jit(solution)/shard_map/ppermute | solution.py:588
  68.4 1.5 %backward_0_0.1 = (f32[8,12,32,256]{3,2,1,0:T(8,128)S(1)}, f32[8,12,32,256]{3,2,1,0:T(8,128)}) custom-call(f32[4,32,256]{2,1,0:T(8,128)S(1)} %collective-permute-done.25.came, bf16[8,12,256,256]{3,2,1,0:T(8,128)(2,1)S(1)} %get-tuple-element.93.own.inverse, ...), custom_call_target="tpu_custom_call", output_to_operand_aliasing={{0}: (5, {}), {1}: (6, {})} | custom-call | flops 67108864 | bytes 2097152 | tf_op jit(solution)/shard_map/backward_0_0/pallas_call | solution.py:441
  69.9 2.4 %collective-permute-done.24.came = f32[4,32,256]{2,1,0:T(8,128)S(1)} collective-permute-done((f32[4,32,256]{2,1,0:T(8,128)S(1)}, f32[4,32,256]{2,1,0:T(8,128)S(1)}, u32[]{:S(2)}, u32[]{:S(2)}) %collective-permute-start.24) | collective-permute-done | bytes 131104 | tf_op jit(solution)/shard_map/ppermute | solution.py:588
  72.3 1.6 %backward_0_1.1 = (f32[8,12,32,256]{3,2,1,0:T(8,128)S(1)}, f32[8,12,32,256]{3,2,1,0:T(8,128)}) custom-call(f32[4,32,256]{2,1,0:T(8,128)S(1)} %collective-permute-done.24.came, bf16[8,12,256,256]{3,2,1,0:T(8,128)(2,1)S(1)} %get-tuple-element.93.own.inverse, ...), custom_call_target="tpu_custom_call", output_to_operand_aliasing={{0}: (5, {}), {1}: (6, {})} | custom-call | flops 67108864 | bytes 2097152 | tf_op jit(solution)/shard_map/backward_0_1/pallas_call | solution.py:441
  73.9 1.3 %backward_0_2.1 = (f32[8,12,32,256]{3,2,1,0:T(8,128)S(1)}, f32[8,12,32,256]{3,2,1,0:T(8,128)}) custom-call(f32[2,32,256]{2,1,0:T(8,128)S(1)} %collective-permute-done.23.came, bf16[8,12,256,256]{3,2,1,0:T(8,128)(2,1)S(1)} %get-tuple-element.93.own.inverse, ...), custom_call_target="tpu_custom_call", output_to_operand_aliasing={{0}: (5, {}), {1}: (6, {})} | custom-call | flops 67108864 | bytes 2097152 | tf_op jit(solution)/shard_map/backward_0_2/pallas_call | solution.py:441
  75.2 0.9 %collective-permute-done.22.came = f32[2,32,256]{2,1,0:T(8,128)S(1)} collective-permute-done((f32[2,32,256]{2,1,0:T(8,128)S(1)}, f32[2,32,256]{2,1,0:T(8,128)S(1)}, u32[]{:S(2)}, u32[]{:S(2)}) %collective-permute-start.22) | collective-permute-done | bytes 65568 | tf_op jit(solution)/shard_map/ppermute | solution.py:588
  76.2 1.8 %backward_0_3.1 = (f32[8,12,32,256]{3,2,1,0:T(8,128)S(1)}, f32[8,12,32,256]{3,2,1,0:T(8,128)}) custom-call(f32[2,32,256]{2,1,0:T(8,128)S(1)} %collective-permute-done.22.came, bf16[8,12,256,256]{3,2,1,0:T(8,128)(2,1)S(1)} %get-tuple-element.93.own.inverse, ...), custom_call_target="tpu_custom_call", output_to_operand_aliasing={{0}: (5, {}), {1}: (6, {})} | custom-call | flops 536870912 | bytes 16777216 | tf_op jit(solution)/shard_map/backward_0_3/pallas_call | solution.py:441
  (23 shorter events, 0.2 us)
Async XLA Ops:
  0.0 8.0 %copy-start = (f32[2,4,12,32,256]{4,3,2,1,0:T(8,128)S(1)}, f32[2,4,12,32,256]{4,3,2,1,0:T(8,128)}, u32[]{:S(2)}) copy-start(f32[2,4,12,32,256]{4,3,2,1,0:T(8,128)} %param.5) | copy-start | bytes 9437188
  0.0 8.0 %copy-start.1 = (f32[2,4,12,32,256]{4,3,2,1,0:T(8,128)S(1)}, f32[2,4,12,32,256]{4,3,2,1,0:T(8,128)}, u32[]{:S(2)}) copy-start(f32[2,4,12,32,256]{4,3,2,1,0:T(8,128)} %param.6) | copy-start | bytes 9437188
  1.6 12.9 %collective-permute-start = (f32[12,32,256]{2,1,0:T(8,128)S(1)}, f32[12,32,256]{2,1,0:T(8,128)S(1)}, u32[]{:S(2)}, u32[]{:S(2)}) collective-permute-start(f32[12,32,256]{2,1,0:T(8,128)S(1)} %get-tuple-element.94), channel_id=1, source_target_pairs={{32,0},{64,32},{96,64},{33,1},{65,33},{97,65},{34,2},{66,34},{98,6... | collective-permute-start | bytes 1179656 | tf_op jit(solution)/shard_map/ppermute | solution.py:486
  3.0 15.0 %collective-permute-start.1 = (f32[8,2,32,256]{3,2,1,0:T(8,128)S(1)}, f32[8,2,32,256]{3,2,1,0:T(8,128)S(1)}, u32[]{:S(2)}, u32[]{:S(2)}) collective-permute-start(f32[8,2,32,256]{3,2,1,0:T(8,128)S(1)} %get-tuple-element.96), channel_id=1, source_target_pairs={{0,1},{2,3},{4,5},{6,7},{8,9},{10,11},{12,13},{14,15},{16,17},{18,... | collective-permute-start | bytes 1572872 | tf_op jit(solution)/shard_map/ppermute | solution.py:467
  3.1 14.9 %collective-permute-start.2 = (f32[8,2,32,256]{3,2,1,0:T(8,128)S(1)}, f32[8,2,32,256]{3,2,1,0:T(8,128)S(1)}, u32[]{:S(2)}, u32[]{:S(2)}) collective-permute-start(f32[8,2,32,256]{3,2,1,0:T(8,128)S(1)} %get-tuple-element.97), channel_id=1, source_target_pairs={{1,2},{3,4},{5,6},{7,8},{9,10},{11,12},{13,14},{15,16},{17,18},{19... | collective-permute-start | bytes 1572872 | tf_op jit(solution)/shard_map/ppermute | solution.py:467
  14.8 7.7 %collective-permute-start.5 = (f32[4,32,256]{2,1,0:T(8,128)S(1)}, f32[4,32,256]{2,1,0:T(8,128)S(1)}, u32[]{:S(2)}, u32[]{:S(2)}) collective-permute-start(f32[4,32,256]{2,1,0:T(8,128)S(1)} %get-tuple-element.109), channel_id=1, source_target_pairs={{0,32},{1,33},{2,34},{3,35},{4,36},{5,37},{6,38},{7,39},{8,40},{9,... | collective-permute-start | bytes 393224 | tf_op jit(solution)/shard_map/ppermute | solution.py:532
  19.5 5.2 %collective-permute-start.4 = (f32[4,32,256]{2,1,0:T(8,128)S(1)}, f32[4,32,256]{2,1,0:T(8,128)S(1)}, u32[]{:S(2)}, u32[]{:S(2)}) collective-permute-start(f32[4,32,256]{2,1,0:T(8,128)S(1)} %get-tuple-element.108), channel_id=1, source_target_pairs={{0,32},{1,33},{2,34},{3,35},{4,36},{5,37},{6,38},{7,39},{8,40},{9,... | collective-permute-start | bytes 393224 | tf_op jit(solution)/shard_map/ppermute | solution.py:532
  21.1 5.0 %collective-permute-start.3 = (f32[4,32,256]{2,1,0:T(8,128)S(1)}, f32[4,32,256]{2,1,0:T(8,128)S(1)}, u32[]{:S(2)}, u32[]{:S(2)}) collective-permute-start(f32[4,32,256]{2,1,0:T(8,128)S(1)} %get-tuple-element.106), channel_id=1, source_target_pairs={{0,32},{1,33},{2,34},{3,35},{4,36},{5,37},{6,38},{7,39},{8,40},{9,... | collective-permute-start | bytes 393224 | tf_op jit(solution)/shard_map/ppermute | solution.py:532
  22.5 4.3 %collective-permute-start.8 = (f32[4,32,256]{2,1,0:T(8,128)S(1)}, f32[4,32,256]{2,1,0:T(8,128)S(1)}, u32[]{:S(2)}, u32[]{:S(2)}) collective-permute-start(f32[4,32,256]{2,1,0:T(8,128)S(1)} %get-tuple-element.117), channel_id=1, source_target_pairs={{32,64},{33,65},{34,66},{35,67},{36,68},{37,69},{38,70},{39,71},{4... | collective-permute-start | bytes 393224 | tf_op jit(solution)/shard_map/ppermute | solution.py:532
  24.7 2.8 %collective-permute-start.7 = (f32[4,32,256]{2,1,0:T(8,128)S(1)}, f32[4,32,256]{2,1,0:T(8,128)S(1)}, u32[]{:S(2)}, u32[]{:S(2)}) collective-permute-start(f32[4,32,256]{2,1,0:T(8,128)S(1)} %get-tuple-element.116), channel_id=1, source_target_pairs={{32,64},{33,65},{34,66},{35,67},{36,68},{37,69},{38,70},{39,71},{4... | collective-permute-start | bytes 393224 | tf_op jit(solution)/shard_map/ppermute | solution.py:532
  26.1 2.1 %collective-permute-start.6 = (f32[4,32,256]{2,1,0:T(8,128)S(1)}, f32[4,32,256]{2,1,0:T(8,128)S(1)}, u32[]{:S(2)}, u32[]{:S(2)}) collective-permute-start(f32[4,32,256]{2,1,0:T(8,128)S(1)} %get-tuple-element.115), channel_id=1, source_target_pairs={{32,64},{33,65},{34,66},{35,67},{36,68},{37,69},{38,70},{39,71},{4... | collective-permute-start | bytes 393224 | tf_op jit(solution)/shard_map/ppermute | solution.py:532
  26.8 2.1 %collective-permute-start.11 = (f32[4,32,256]{2,1,0:T(8,128)S(1)}, f32[4,32,256]{2,1,0:T(8,128)S(1)}, u32[]{:S(2)}, u32[]{:S(2)}) collective-permute-start(f32[4,32,256]{2,1,0:T(8,128)S(1)} %get-tuple-element.125), channel_id=1, source_target_pairs={{64,96},{65,97},{66,98},{67,99},{68,100},{69,101},{70,102},{71,103... | collective-permute-start | bytes 393224 | tf_op jit(solution)/shard_map/ppermute | solution.py:532
  27.5 1.4 %collective-permute-start.10 = (f32[4,32,256]{2,1,0:T(8,128)S(1)}, f32[4,32,256]{2,1,0:T(8,128)S(1)}, u32[]{:S(2)}, u32[]{:S(2)}) collective-permute-start(f32[4,32,256]{2,1,0:T(8,128)S(1)} %get-tuple-element.124), channel_id=1, source_target_pairs={{64,96},{65,97},{66,98},{67,99},{68,100},{69,101},{70,102},{71,103... | collective-permute-start | bytes 393224 | tf_op jit(solution)/shard_map/ppermute | solution.py:532
  28.3 4.7 %collective-permute-start.9 = (f32[4,32,256]{2,1,0:T(8,128)S(1)}, f32[4,32,256]{2,1,0:T(8,128)S(1)}, u32[]{:S(2)}, u32[]{:S(2)}) collective-permute-start(f32[4,32,256]{2,1,0:T(8,128)S(1)} %get-tuple-element.123), channel_id=1, source_target_pairs={{64,96},{65,97},{66,98},{67,99},{68,100},{69,101},{70,102},{71,103... | collective-permute-start | bytes 393224 | tf_op jit(solution)/shard_map/ppermute | solution.py:532
  29.0 12.6 %collective-permute-start.12 = (f32[8,2,32,256]{3,2,1,0:T(8,128)S(1)}, f32[8,2,32,256]{3,2,1,0:T(8,128)S(1)}, u32[]{:S(2)}, u32[]{:S(2)}) collective-permute-start(f32[8,2,32,256]{3,2,1,0:T(8,128)S(1)} %get-tuple-element.130), channel_id=1, source_target_pairs={{1,2},{3,4},{5,6},{7,8},{9,10},{11,12},{13,14},{15,16},{17,18},{19... | collective-permute-start | bytes 1572872 | tf_op jit(solution)/shard_map/ppermute | solution.py:467
  32.9 2.9 %collective-permute-start.13 = (f32[8,2,32,256]{3,2,1,0:T(8,128)S(1)}, f32[8,2,32,256]{3,2,1,0:T(8,128)S(1)}, u32[]{:S(2)}, u32[]{:S(2)}) collective-permute-start(f32[8,2,32,256]{3,2,1,0:T(8,128)S(1)} %get-tuple-element.131), channel_id=1, source_target_pairs={{0,1},{2,3},{4,5},{6,7},{8,9},{10,11},{12,13},{14,15},{16,17},{18,... | collective-permute-start | bytes 1572872 | tf_op jit(solution)/shard_map/ppermute | solution.py:467
  33.8 8.9 %collective-permute-start.17 = (f32[4,32,256]{2,1,0:T(8,128)S(1)}, f32[4,32,256]{2,1,0:T(8,128)S(1)}, u32[]{:S(2)}, u32[]{:S(2)}) collective-permute-start(f32[4,32,256]{2,1,0:T(8,128)S(1)} %get-tuple-element.145), channel_id=1, source_target_pairs={{96,64},{97,65},{98,66},{99,67},{100,68},{101,69},{102,70},{103,71... | collective-permute-start | bytes 393224 | tf_op jit(solution)/shard_map/ppermute | solution.py:588
  35.1 8.5 %collective-permute-start.16 = (f32[4,32,256]{2,1,0:T(8,128)S(1)}, f32[4,32,256]{2,1,0:T(8,128)S(1)}, u32[]{:S(2)}, u32[]{:S(2)}) collective-permute-start(f32[4,32,256]{2,1,0:T(8,128)S(1)} %get-tuple-element.144), channel_id=1, source_target_pairs={{96,64},{97,65},{98,66},{99,67},{100,68},{101,69},{102,70},{103,71... | collective-permute-start | bytes 393224 | tf_op jit(solution)/shard_map/ppermute | solution.py:588
  36.2 8.2 %collective-permute-start.15 = (f32[2,32,256]{2,1,0:T(8,128)S(1)}, f32[2,32,256]{2,1,0:T(8,128)S(1)}, u32[]{:S(2)}, u32[]{:S(2)}) collective-permute-start(f32[2,32,256]{2,1,0:T(8,128)S(1)} %get-tuple-element.143), channel_id=1, source_target_pairs={{96,64},{97,65},{98,66},{99,67},{100,68},{101,69},{102,70},{103,71... | collective-permute-start | bytes 196616 | tf_op jit(solution)/shard_map/ppermute | solution.py:588
  42.0 3.3 %collective-permute-start.14 = (f32[2,32,256]{2,1,0:T(8,128)S(1)}, f32[2,32,256]{2,1,0:T(8,128)S(1)}, u32[]{:S(2)}, u32[]{:S(2)}) collective-permute-start(f32[2,32,256]{2,1,0:T(8,128)S(1)} %get-tuple-element.141), channel_id=1, source_target_pairs={{96,64},{97,65},{98,66},{99,67},{100,68},{101,69},{102,70},{103,71... | collective-permute-start | bytes 196616 | tf_op jit(solution)/shard_map/ppermute | solution.py:588
  42.9 3.3 %collective-permute-start.21 = (f32[4,32,256]{2,1,0:T(8,128)S(1)}, f32[4,32,256]{2,1,0:T(8,128)S(1)}, u32[]{:S(2)}, u32[]{:S(2)}) collective-permute-start(f32[4,32,256]{2,1,0:T(8,128)S(1)} %get-tuple-element.157), channel_id=1, source_target_pairs={{64,32},{65,33},{66,34},{67,35},{68,36},{69,37},{70,38},{71,39},{7... | collective-permute-start | bytes 393224 | tf_op jit(solution)/shard_map/ppermute | solution.py:588
  43.8 3.9 %collective-permute-start.20 = (f32[4,32,256]{2,1,0:T(8,128)S(1)}, f32[4,32,256]{2,1,0:T(8,128)S(1)}, u32[]{:S(2)}, u32[]{:S(2)}) collective-permute-start(f32[4,32,256]{2,1,0:T(8,128)S(1)} %get-tuple-element.156), channel_id=1, source_target_pairs={{64,32},{65,33},{66,34},{67,35},{68,36},{69,37},{70,38},{71,39},{7... | collective-permute-start | bytes 393224 | tf_op jit(solution)/shard_map/ppermute | solution.py:588
  44.6 4.5 %collective-permute-start.19 = (f32[2,32,256]{2,1,0:T(8,128)S(1)}, f32[2,32,256]{2,1,0:T(8,128)S(1)}, u32[]{:S(2)}, u32[]{:S(2)}) collective-permute-start(f32[2,32,256]{2,1,0:T(8,128)S(1)} %get-tuple-element.155), channel_id=1, source_target_pairs={{64,32},{65,33},{66,34},{67,35},{68,36},{69,37},{70,38},{71,39},{7... | collective-permute-start | bytes 196616 | tf_op jit(solution)/shard_map/ppermute | solution.py:588
  45.5 5.1 %collective-permute-start.18 = (f32[2,32,256]{2,1,0:T(8,128)S(1)}, f32[2,32,256]{2,1,0:T(8,128)S(1)}, u32[]{:S(2)}, u32[]{:S(2)}) collective-permute-start(f32[2,32,256]{2,1,0:T(8,128)S(1)} %get-tuple-element.154), channel_id=1, source_target_pairs={{64,32},{65,33},{66,34},{67,35},{68,36},{69,37},{70,38},{71,39},{7... | collective-permute-start | bytes 196616 | tf_op jit(solution)/shard_map/ppermute | solution.py:588
  46.4 22.1 %collective-permute-start.25 = (f32[4,32,256]{2,1,0:T(8,128)S(1)}, f32[4,32,256]{2,1,0:T(8,128)S(1)}, u32[]{:S(2)}, u32[]{:S(2)}) collective-permute-start(f32[4,32,256]{2,1,0:T(8,128)S(1)} %get-tuple-element.169), channel_id=1, source_target_pairs={{32,0},{33,1},{34,2},{35,3},{36,4},{37,5},{38,6},{39,7},{40,8},{41... | collective-permute-start | bytes 393224 | tf_op jit(solution)/shard_map/ppermute | solution.py:588
  47.8 24.5 %collective-permute-start.24 = (f32[4,32,256]{2,1,0:T(8,128)S(1)}, f32[4,32,256]{2,1,0:T(8,128)S(1)}, u32[]{:S(2)}, u32[]{:S(2)}) collective-permute-start(f32[4,32,256]{2,1,0:T(8,128)S(1)} %get-tuple-element.168), channel_id=1, source_target_pairs={{32,0},{33,1},{34,2},{35,3},{36,4},{37,5},{38,6},{39,7},{40,8},{41... | collective-permute-start | bytes 393224 | tf_op jit(solution)/shard_map/ppermute | solution.py:588
  49.3 24.6 %collective-permute-start.23 = (f32[2,32,256]{2,1,0:T(8,128)S(1)}, f32[2,32,256]{2,1,0:T(8,128)S(1)}, u32[]{:S(2)}, u32[]{:S(2)}) collective-permute-start(f32[2,32,256]{2,1,0:T(8,128)S(1)} %get-tuple-element.167), channel_id=1, source_target_pairs={{32,0},{33,1},{34,2},{35,3},{36,4},{37,5},{38,6},{39,7},{40,8},{41... | collective-permute-start | bytes 196616 | tf_op jit(solution)/shard_map/ppermute | solution.py:588
  50.8 25.3 %collective-permute-start.22 = (f32[2,32,256]{2,1,0:T(8,128)S(1)}, f32[2,32,256]{2,1,0:T(8,128)S(1)}, u32[]{:S(2)}, u32[]{:S(2)}) collective-permute-start(f32[2,32,256]{2,1,0:T(8,128)S(1)} %get-tuple-element.166), channel_id=1, source_target_pairs={{32,0},{33,1},{34,2},{35,3},{36,4},{37,5},{38,6},{39,7},{40,8},{41... | collective-permute-start | bytes 196616 | tf_op jit(solution)/shard_map/ppermute | solution.py:588

commit v7 on v6

--- a/solution.py
+++ b/solution.py
@@ -363,13 +363,13 @@
                 total = total + coef(couple, k, q, lane) * near(q, lane + step)
             source[q, lane] = total
 
-    def sweep(lanes, before):
+    def sweep(lanes, _):
         for j in range(len(lanes)):
             sent[j] = jnp.zeros((R, BS), jnp.float32)
         source_of(lanes, COLS - 1)
         backward_sweep(
             lanes,
-            before if chunk > 0 else None,
+            None,
             False,
             inverse,
             source,
@@ -403,7 +403,7 @@
         sent[...] = came[...]
         backward_sweep(
             lanes,
-            before if chunk > 0 else None,
+            before if chunk > 0 and stage == 0 else None,
             stage == 0 and chunk == FAR,
             inverse,
             source,
@@ -417,16 +417,14 @@
             None,
         )
 
-    def flush(lanes, _):
-        copy = pltpu.make_async_copy(
-            result.at[:, pl.ds(lanes[0], 2)], out.at[:, pl.ds(lanes[0], 2)], sem_own.at[0]
-        )
-        copy.start()
-        copy.wait()
-
     by_parity(strip == stage, even, chunk, sweep)
     if chunk == 0:
-        by_parity(strip == stage + 1, even, FAR, flush)
+
+        @pl.when(strip == stage + 1)
+        def _():
+            copy = pltpu.make_async_copy(result, out, sem_own.at[0])
+            copy.start()
+            copy.wait()
 
 
 def vmem(shape, dtype=jnp.float32):

time: 79.3 us -> 78.9 us (level)
  no operation moved by 1% of the time
where the time goes in v7:
time: 78.9 us; the launch traced here: 77.8 us
  starting transfers between devices  30.7 us (39%)
  waiting for transfers between devices  27.2 us (34%)
  Pallas kernels  19.2 us (24%)
    ppermute x12, waiting for transfers between devices, on_device(): came = lax.ppermute(sents[stage + 1, chunk], 'strip', [(stage + 1, stage)])  19.3 us
    pallas_call x31, Pallas kernels, run(): pl.pallas_call(kernel, name=name, out_shape=[o for o, _ in outs], in_spec...  19.2 us
    ppermute x12, starting transfers between devices, on_device(): came = lax.ppermute(sents[stage + 1, chunk], 'strip', [(stage + 1, stage)])  10.5 us
    ppermute x9, starting transfers between devices, on_device(): came = lax.ppermute(sents[stage - 1, chunk], 'strip', [(stage - 1, stage)])  9.86 us
    ppermute x4, starting transfers between devices, swapped(): return lax.ppermute(value, 'tile', pairs + [(b, a) for a, b in pairs])  8.88 us
    ppermute x4, waiting for transfers between devices, swapped(): return lax.ppermute(value, 'tile', pairs + [(b, a) for a, b in pairs])  4.71 us
    ppermute x9, waiting for transfers between devices, on_device(): came = lax.ppermute(sents[stage - 1, chunk], 'strip', [(stage - 1, stage)])  2.34 us
  transfers between devices with their start and end apart: 26, of which 7 were waited for; matrix products, arithmetic and copies ran while one was open for 0% of the time, Pallas kernels for 20%

profile of v7, /device:TPU:96, one launch (start us, length us, event | category | flops | bytes accessed | tf_op | source)
XLA Modules:
  0.0 77.8 jit_solution(6005914926508639731)
XLA Ops:
  0.0 1.6 %prep.1 = (f32[12,32,256]{2,1,0:T(8,128)S(1)}, f32[8,2,32,256]{3,2,1,0:T(8,128)S(1)}, f32[8,2,32,256]{3,2,1,0:T(8,128)S(1)}, f32[9,12,256]{2,1,0:T(8,128)S(1)}) custom-call(s32[2,4,12]{2,1,0:T(4,128)} %ice_hbm.1, f32[8,12,32,256]{3,2,1,0:T(8,128)} %bitcast.13), custom_call_target="tpu_custom_call" | custom-call | flops 4294967296 | bytes 134217728 | tf_op jit(solution)/shard_map/prep/pallas_call | solution.py:439
  1.6 1.4 %collective-permute-start = (f32[12,32,256]{2,1,0:T(8,128)S(1)}, f32[12,32,256]{2,1,0:T(8,128)S(1)}, u32[]{:S(2)}, u32[]{:S(2)}) collective-permute-start(f32[12,32,256]{2,1,0:T(8,128)S(1)} %get-tuple-element.94), channel_id=1, source_target_pairs={{32,0},{64,32},{96,64},{33,1},{65,33},{97,65},{34,2},{66,34},{98,6... | collective-permute-start | bytes 1179656 | tf_op jit(solution)/shard_map/ppermute | solution.py:484
  3.0 0.1 collective-permute-start.1
  3.1 4.9 %collective-permute-start.2 = (f32[8,2,32,256]{3,2,1,0:T(8,128)S(1)}, f32[8,2,32,256]{3,2,1,0:T(8,128)S(1)}, u32[]{:S(2)}, u32[]{:S(2)}) collective-permute-start(f32[8,2,32,256]{3,2,1,0:T(8,128)S(1)} %get-tuple-element.97), channel_id=1, source_target_pairs={{1,2},{3,4},{5,6},{7,8},{9,10},{11,12},{13,14},{15,16},{17,18},{19... | collective-permute-start | bytes 1572872 | tf_op jit(solution)/shard_map/ppermute | solution.py:465
  8.0 5.7 %first.1 = (bf16[8,12,256,256]{3,2,1,0:T(8,128)(2,1)S(1)}, f32[6,2,12,4,256]{4,3,2,1,0:T(4,128)S(1)}, f32[8,12,32,256]{3,2,1,0:T(8,128)S(1)}, f32[9,12,32,256]{3...) custom-call(bf16[8,12,256,256]{3,2,1,0:T(8,128)(2,1)} %bitcast.18, ...), custom_call_target="tpu_custom_call" | custom-call | flops 65536 | bytes 2048 | tf_op jit(solution)/shard_map/first/pallas_call | solution.py:439
  13.7 0.8 %collective-permute-done.nxt = f32[12,32,256]{2,1,0:T(8,128)S(1)} collective-permute-done((f32[12,32,256]{2,1,0:T(8,128)S(1)}, f32[12,32,256]{2,1,0:T(8,128)S(1)}, u32[]{:S(2)}, u32[]{:S(2)}) %collective-permute-start) | collective-permute-done | bytes 393248 | tf_op jit(solution)/shard_map/ppermute | solution.py:484
  14.5 0.3 tail_0.1
  14.8 3.3 %collective-permute-start.5 = (f32[4,32,256]{2,1,0:T(8,128)S(1)}, f32[4,32,256]{2,1,0:T(8,128)S(1)}, u32[]{:S(2)}, u32[]{:S(2)}) collective-permute-start(f32[4,32,256]{2,1,0:T(8,128)S(1)} %get-tuple-element.109), channel_id=1, source_target_pairs={{0,32},{1,33},{2,34},{3,35},{4,36},{5,37},{6,38},{7,39},{8,40},{9,... | collective-permute-start | bytes 393224 | tf_op jit(solution)/shard_map/ppermute | solution.py:530
  18.1 0.0 collective-permute-done.2.halo_out
  18.1 1.4 %outer.1 = (f32[8,12,32,256]{3,2,1,0:T(8,128)S(1)}, f32[9,12,32,256]{3,2,1,0:T(8,128)S(1)}, f32[8,2,32,256]{3,2,1,0:T(8,128)S(1)}, f32[8,2,32,256]{3,2,1,0:T(8,128)S(1)}, f32[4,32,256]{2,1,0:T(8,128)S(1)}) custom-call(f32[12,32,256]{2,1,0:T(8,128)S(1)} %collective-permute-done.nxt, ...), custom_call_target="tpu_custom_call", output_to_operand_aliasing={{0}: (8, {}), {1}: (9, {})} | custom-call | flops 67108864 | bytes 2097152 | tf_op jit(solution)/shard_map/outer/pallas_call | solution.py:439
  19.5 1.3 %collective-permute-start.4 = (f32[4,32,256]{2,1,0:T(8,128)S(1)}, f32[4,32,256]{2,1,0:T(8,128)S(1)}, u32[]{:S(2)}, u32[]{:S(2)}) collective-permute-start(f32[4,32,256]{2,1,0:T(8,128)S(1)} %get-tuple-element.108), channel_id=1, source_target_pairs={{0,32},{1,33},{2,34},{3,35},{4,36},{5,37},{6,38},{7,39},{8,40},{9,... | collective-permute-start | bytes 393224 | tf_op jit(solution)/shard_map/ppermute | solution.py:530
  20.8 0.3 tail_2.1
  21.1 1.3 %collective-permute-start.3 = (f32[4,32,256]{2,1,0:T(8,128)S(1)}, f32[4,32,256]{2,1,0:T(8,128)S(1)}, u32[]{:S(2)}, u32[]{:S(2)}) collective-permute-start(f32[4,32,256]{2,1,0:T(8,128)S(1)} %get-tuple-element.106), channel_id=1, source_target_pairs={{0,32},{1,33},{2,34},{3,35},{4,36},{5,37},{6,38},{7,39},{8,40},{9,... | collective-permute-start | bytes 393224 | tf_op jit(solution)/shard_map/ppermute | solution.py:530
  22.4 0.0 collective-permute-done.5.came
  22.5 0.7 collective-permute-start.8
  23.1 1.6 %collective-permute-done.4.came = f32[4,32,256]{2,1,0:T(8,128)S(1)} collective-permute-done((f32[4,32,256]{2,1,0:T(8,128)S(1)}, f32[4,32,256]{2,1,0:T(8,128)S(1)}, u32[]{:S(2)}, u32[]{:S(2)}) %collective-permute-start.4) | collective-permute-done | bytes 131104 | tf_op jit(solution)/shard_map/ppermute | solution.py:530
  24.7 0.7 collective-permute-start.7
  25.4 0.7 collective-permute-done.3.came
  26.1 0.7 collective-permute-start.6
  26.8 0.7 collective-permute-start.11
  27.5 0.0 collective-permute-done.7.came
  27.5 0.7 collective-permute-start.10
  28.3 0.7 collective-permute-start.9
  28.9 0.0 collective-permute-done.11.came
  29.0 3.9 %collective-permute-start.12 = (f32[8,2,32,256]{3,2,1,0:T(8,128)S(1)}, f32[8,2,32,256]{3,2,1,0:T(8,128)S(1)}, u32[]{:S(2)}, u32[]{:S(2)}) collective-permute-start(f32[8,2,32,256]{3,2,1,0:T(8,128)S(1)} %get-tuple-element.130), channel_id=1, source_target_pairs={{1,2},{3,4},{5,6},{7,8},{9,10},{11,12},{13,14},{15,16},{17,18},{19... | collective-permute-start | bytes 1572872 | tf_op jit(solution)/shard_map/ppermute | solution.py:465
  32.9 0.1 collective-permute-start.13
  33.0 0.0 collective-permute-done.9.came
  33.0 0.2 forward_3_2.1.field
  33.2 0.6 last_0.1
  33.8 0.7 collective-permute-start.17
  34.5 0.6 last_1.1
  35.1 0.7 collective-permute-start.16
  35.8 0.0 collective-permute-done.13.halo
  35.8 0.5 last_2.1
  36.2 0.7 collective-permute-start.15
  36.9 4.7 %collective-permute-done.12.halo = f32[8,2,32,256]{3,2,1,0:T(8,128)S(1)} collective-permute-done((f32[8,2,32,256]{3,2,1,0:T(8,128)S(1)}, f32[8,2,32,256]{3,2,1,0:T(8,128)S(1)}, u32[]{:S(2)}, u32[]{:S(2)}) %collective-permute-start.12) | collective-permute-done | bytes 524320 | tf_op jit(solution)/shard_map/ppermute | solution.py:465
  41.6 0.4 last_3.1
  42.0 0.7 collective-permute-start.14
  42.7 0.2 backward_2_0.1
  42.9 0.7 collective-permute-start.21
  43.6 0.0 collective-permute-done.16.came
  43.6 0.2 backward_2_1.1
  43.8 0.7 collective-permute-start.20
  44.5 0.2 backward_2_2.1
  44.6 0.7 collective-permute-start.19
  45.3 0.0 collective-permute-done.14.came
  45.3 0.2 backward_2_3.1
  45.5 0.7 collective-permute-start.18
  46.2 0.2 backward_1_0.1
  46.4 1.3 %collective-permute-start.25 = (f32[4,32,256]{2,1,0:T(8,128)S(1)}, f32[4,32,256]{2,1,0:T(8,128)S(1)}, u32[]{:S(2)}, u32[]{:S(2)}) collective-permute-start(f32[4,32,256]{2,1,0:T(8,128)S(1)} %get-tuple-element.169), channel_id=1, source_target_pairs={{32,0},{33,1},{34,2},{35,3},{36,4},{37,5},{38,6},{39,7},{40,8},{41... | collective-permute-start | bytes 393224 | tf_op jit(solution)/shard_map/ppermute | solution.py:586
  47.6 0.0 collective-permute-done.20.came
  47.7 0.2 backward_1_1.1
  47.8 1.3 %collective-permute-start.24 = (f32[4,32,256]{2,1,0:T(8,128)S(1)}, f32[4,32,256]{2,1,0:T(8,128)S(1)}, u32[]{:S(2)}, u32[]{:S(2)}) collective-permute-start(f32[4,32,256]{2,1,0:T(8,128)S(1)} %get-tuple-element.168), channel_id=1, source_target_pairs={{32,0},{33,1},{34,2},{35,3},{36,4},{37,5},{38,6},{39,7},{40,8},{41... | collective-permute-start | bytes 393224 | tf_op jit(solution)/shard_map/ppermute | solution.py:586
  49.1 0.2 backward_1_2.1
  49.3 1.3 %collective-permute-start.23 = (f32[2,32,256]{2,1,0:T(8,128)S(1)}, f32[2,32,256]{2,1,0:T(8,128)S(1)}, u32[]{:S(2)}, u32[]{:S(2)}) collective-permute-start(f32[2,32,256]{2,1,0:T(8,128)S(1)} %get-tuple-element.167), channel_id=1, source_target_pairs={{32,0},{33,1},{34,2},{35,3},{36,4},{37,5},{38,6},{39,7},{40,8},{41... | collective-permute-start | bytes 196616 | tf_op jit(solution)/shard_map/ppermute | solution.py:586
  50.6 0.2 backward_1_3.1
  50.8 1.3 %collective-permute-start.22 = (f32[2,32,256]{2,1,0:T(8,128)S(1)}, f32[2,32,256]{2,1,0:T(8,128)S(1)}, u32[]{:S(2)}, u32[]{:S(2)}) collective-permute-start(f32[2,32,256]{2,1,0:T(8,128)S(1)} %get-tuple-element.166), channel_id=1, source_target_pairs={{32,0},{33,1},{34,2},{35,3},{36,4},{37,5},{38,6},{39,7},{40,8},{41... | collective-permute-start | bytes 196616 | tf_op jit(solution)/shard_map/ppermute | solution.py:586
  52.1 16.6 %collective-permute-done.25.came = f32[4,32,256]{2,1,0:T(8,128)S(1)} collective-permute-done((f32[4,32,256]{2,1,0:T(8,128)S(1)}, f32[4,32,256]{2,1,0:T(8,128)S(1)}, u32[]{:S(2)}, u32[]{:S(2)}) %collective-permute-start.25) | collective-permute-done | bytes 131104 | tf_op jit(solution)/shard_map/ppermute | solution.py:586
  68.7 1.5 %backward_0_0.1 = (f32[8,12,32,256]{3,2,1,0:T(8,128)S(1)}, f32[8,12,32,256]{3,2,1,0:T(8,128)}) custom-call(f32[4,32,256]{2,1,0:T(8,128)S(1)} %collective-permute-done.25.came, bf16[8,12,256,256]{3,2,1,0:T(8,128)(2,1)S(1)} %get-tuple-element.93.own.inverse, ...), custom_call_target="tpu_custom_call", output_to_operand_aliasing={{0}: (5, {}), {1}: (6, {})} | custom-call | flops 67108864 | bytes 2097152 | tf_op jit(solution)/shard_map/backward_0_0/pallas_call | solution.py:439
  70.2 2.0 %collective-permute-done.24.came = f32[4,32,256]{2,1,0:T(8,128)S(1)} collective-permute-done((f32[4,32,256]{2,1,0:T(8,128)S(1)}, f32[4,32,256]{2,1,0:T(8,128)S(1)}, u32[]{:S(2)}, u32[]{:S(2)}) %collective-permute-start.24) | collective-permute-done | bytes 131104 | tf_op jit(solution)/shard_map/ppermute | solution.py:586
  72.2 1.6 %backward_0_1.1 = (f32[8,12,32,256]{3,2,1,0:T(8,128)S(1)}, f32[8,12,32,256]{3,2,1,0:T(8,128)}) custom-call(f32[4,32,256]{2,1,0:T(8,128)S(1)} %collective-permute-done.24.came, bf16[8,12,256,256]{3,2,1,0:T(8,128)(2,1)S(1)} %get-tuple-element.93.own.inverse, ...), custom_call_target="tpu_custom_call", output_to_operand_aliasing={{0}: (5, {}), {1}: (6, {})} | custom-call | flops 67108864 | bytes 2097152 | tf_op jit(solution)/shard_map/backward_0_1/pallas_call | solution.py:439
  73.7 1.3 %backward_0_2.1 = (f32[8,12,32,256]{3,2,1,0:T(8,128)S(1)}, f32[8,12,32,256]{3,2,1,0:T(8,128)}) custom-call(f32[2,32,256]{2,1,0:T(8,128)S(1)} %collective-permute-done.23.came, bf16[8,12,256,256]{3,2,1,0:T(8,128)(2,1)S(1)} %get-tuple-element.93.own.inverse, ...), custom_call_target="tpu_custom_call", output_to_operand_aliasing={{0}: (5, {}), {1}: (6, {})} | custom-call | flops 67108864 | bytes 2097152 | tf_op jit(solution)/shard_map/backward_0_2/pallas_call | solution.py:439
  75.0 0.7 collective-permute-done.22.came
  75.8 1.8 %backward_0_3.1 = (f32[8,12,32,256]{3,2,1,0:T(8,128)S(1)}, f32[8,12,32,256]{3,2,1,0:T(8,128)}) custom-call(f32[2,32,256]{2,1,0:T(8,128)S(1)} %collective-permute-done.22.came, bf16[8,12,256,256]{3,2,1,0:T(8,128)(2,1)S(1)} %get-tuple-element.93.own.inverse, ...), custom_call_target="tpu_custom_call", output_to_operand_aliasing={{0}: (5, {}), {1}: (6, {})} | custom-call | flops 536870912 | bytes 16777216 | tf_op jit(solution)/shard_map/backward_0_3/pallas_call | solution.py:439
  (23 shorter events, 0.2 us)
Async XLA Ops:
  0.0 8.0 %copy-start = (f32[2,4,12,32,256]{4,3,2,1,0:T(8,128)S(1)}, f32[2,4,12,32,256]{4,3,2,1,0:T(8,128)}, u32[]{:S(2)}) copy-start(f32[2,4,12,32,256]{4,3,2,1,0:T(8,128)} %param.5) | copy-start | bytes 9437188
  0.0 8.0 %copy-start.1 = (f32[2,4,12,32,256]{4,3,2,1,0:T(8,128)S(1)}, f32[2,4,12,32,256]{4,3,2,1,0:T(8,128)}, u32[]{:S(2)}) copy-start(f32[2,4,12,32,256]{4,3,2,1,0:T(8,128)} %param.6) | copy-start | bytes 9437188
  1.6 12.9 %collective-permute-start = (f32[12,32,256]{2,1,0:T(8,128)S(1)}, f32[12,32,256]{2,1,0:T(8,128)S(1)}, u32[]{:S(2)}, u32[]{:S(2)}) collective-permute-start(f32[12,32,256]{2,1,0:T(8,128)S(1)} %get-tuple-element.94), channel_id=1, source_target_pairs={{32,0},{64,32},{96,64},{33,1},{65,33},{97,65},{34,2},{66,34},{98,6... | collective-permute-start | bytes 1179656 | tf_op jit(solution)/shard_map/ppermute | solution.py:484
  3.0 15.0 %collective-permute-start.1 = (f32[8,2,32,256]{3,2,1,0:T(8,128)S(1)}, f32[8,2,32,256]{3,2,1,0:T(8,128)S(1)}, u32[]{:S(2)}, u32[]{:S(2)}) collective-permute-start(f32[8,2,32,256]{3,2,1,0:T(8,128)S(1)} %get-tuple-element.96), channel_id=1, source_target_pairs={{0,1},{2,3},{4,5},{6,7},{8,9},{10,11},{12,13},{14,15},{16,17},{18,... | collective-permute-start | bytes 1572872 | tf_op jit(solution)/shard_map/ppermute | solution.py:465
  3.1 14.9 %collective-permute-start.2 = (f32[8,2,32,256]{3,2,1,0:T(8,128)S(1)}, f32[8,2,32,256]{3,2,1,0:T(8,128)S(1)}, u32[]{:S(2)}, u32[]{:S(2)}) collective-permute-start(f32[8,2,32,256]{3,2,1,0:T(8,128)S(1)} %get-tuple-element.97), channel_id=1, source_target_pairs={{1,2},{3,4},{5,6},{7,8},{9,10},{11,12},{13,14},{15,16},{17,18},{19... | collective-permute-start | bytes 1572872 | tf_op jit(solution)/shard_map/ppermute | solution.py:465
  14.8 7.7 %collective-permute-start.5 = (f32[4,32,256]{2,1,0:T(8,128)S(1)}, f32[4,32,256]{2,1,0:T(8,128)S(1)}, u32[]{:S(2)}, u32[]{:S(2)}) collective-permute-start(f32[4,32,256]{2,1,0:T(8,128)S(1)} %get-tuple-element.109), channel_id=1, source_target_pairs={{0,32},{1,33},{2,34},{3,35},{4,36},{5,37},{6,38},{7,39},{8,40},{9,... | collective-permute-start | bytes 393224 | tf_op jit(solution)/shard_map/ppermute | solution.py:530
  19.5 5.2 %collective-permute-start.4 = (f32[4,32,256]{2,1,0:T(8,128)S(1)}, f32[4,32,256]{2,1,0:T(8,128)S(1)}, u32[]{:S(2)}, u32[]{:S(2)}) collective-permute-start(f32[4,32,256]{2,1,0:T(8,128)S(1)} %get-tuple-element.108), channel_id=1, source_target_pairs={{0,32},{1,33},{2,34},{3,35},{4,36},{5,37},{6,38},{7,39},{8,40},{9,... | collective-permute-start | bytes 393224 | tf_op jit(solution)/shard_map/ppermute | solution.py:530
  21.1 5.0 %collective-permute-start.3 = (f32[4,32,256]{2,1,0:T(8,128)S(1)}, f32[4,32,256]{2,1,0:T(8,128)S(1)}, u32[]{:S(2)}, u32[]{:S(2)}) collective-permute-start(f32[4,32,256]{2,1,0:T(8,128)S(1)} %get-tuple-element.106), channel_id=1, source_target_pairs={{0,32},{1,33},{2,34},{3,35},{4,36},{5,37},{6,38},{7,39},{8,40},{9,... | collective-permute-start | bytes 393224 | tf_op jit(solution)/shard_map/ppermute | solution.py:530
  22.5 4.3 %collective-permute-start.8 = (f32[4,32,256]{2,1,0:T(8,128)S(1)}, f32[4,32,256]{2,1,0:T(8,128)S(1)}, u32[]{:S(2)}, u32[]{:S(2)}) collective-permute-start(f32[4,32,256]{2,1,0:T(8,128)S(1)} %get-tuple-element.117), channel_id=1, source_target_pairs={{32,64},{33,65},{34,66},{35,67},{36,68},{37,69},{38,70},{39,71},{4... | collective-permute-start | bytes 393224 | tf_op jit(solution)/shard_map/ppermute | solution.py:530
  24.7 2.8 %collective-permute-start.7 = (f32[4,32,256]{2,1,0:T(8,128)S(1)}, f32[4,32,256]{2,1,0:T(8,128)S(1)}, u32[]{:S(2)}, u32[]{:S(2)}) collective-permute-start(f32[4,32,256]{2,1,0:T(8,128)S(1)} %get-tuple-element.116), channel_id=1, source_target_pairs={{32,64},{33,65},{34,66},{35,67},{36,68},{37,69},{38,70},{39,71},{4... | collective-permute-start | bytes 393224 | tf_op jit(solution)/shard_map/ppermute | solution.py:530
  26.1 2.1 %collective-permute-start.6 = (f32[4,32,256]{2,1,0:T(8,128)S(1)}, f32[4,32,256]{2,1,0:T(8,128)S(1)}, u32[]{:S(2)}, u32[]{:S(2)}) collective-permute-start(f32[4,32,256]{2,1,0:T(8,128)S(1)} %get-tuple-element.115), channel_id=1, source_target_pairs={{32,64},{33,65},{34,66},{35,67},{36,68},{37,69},{38,70},{39,71},{4... | collective-permute-start | bytes 393224 | tf_op jit(solution)/shard_map/ppermute | solution.py:530
  26.8 2.1 %collective-permute-start.11 = (f32[4,32,256]{2,1,0:T(8,128)S(1)}, f32[4,32,256]{2,1,0:T(8,128)S(1)}, u32[]{:S(2)}, u32[]{:S(2)}) collective-permute-start(f32[4,32,256]{2,1,0:T(8,128)S(1)} %get-tuple-element.125), channel_id=1, source_target_pairs={{64,96},{65,97},{66,98},{67,99},{68,100},{69,101},{70,102},{71,103... | collective-permute-start | bytes 393224 | tf_op jit(solution)/shard_map/ppermute | solution.py:530
  27.5 1.4 %collective-permute-start.10 = (f32[4,32,256]{2,1,0:T(8,128)S(1)}, f32[4,32,256]{2,1,0:T(8,128)S(1)}, u32[]{:S(2)}, u32[]{:S(2)}) collective-permute-start(f32[4,32,256]{2,1,0:T(8,128)S(1)} %get-tuple-element.124), channel_id=1, source_target_pairs={{64,96},{65,97},{66,98},{67,99},{68,100},{69,101},{70,102},{71,103... | collective-permute-start | bytes 393224 | tf_op jit(solution)/shard_map/ppermute | solution.py:530
  28.3 4.7 %collective-permute-start.9 = (f32[4,32,256]{2,1,0:T(8,128)S(1)}, f32[4,32,256]{2,1,0:T(8,128)S(1)}, u32[]{:S(2)}, u32[]{:S(2)}) collective-permute-start(f32[4,32,256]{2,1,0:T(8,128)S(1)} %get-tuple-element.123), channel_id=1, source_target_pairs={{64,96},{65,97},{66,98},{67,99},{68,100},{69,101},{70,102},{71,103... | collective-permute-start | bytes 393224 | tf_op jit(solution)/shard_map/ppermute | solution.py:530
  29.0 12.6 %collective-permute-start.12 = (f32[8,2,32,256]{3,2,1,0:T(8,128)S(1)}, f32[8,2,32,256]{3,2,1,0:T(8,128)S(1)}, u32[]{:S(2)}, u32[]{:S(2)}) collective-permute-start(f32[8,2,32,256]{3,2,1,0:T(8,128)S(1)} %get-tuple-element.130), channel_id=1, source_target_pairs={{1,2},{3,4},{5,6},{7,8},{9,10},{11,12},{13,14},{15,16},{17,18},{19... | collective-permute-start | bytes 1572872 | tf_op jit(solution)/shard_map/ppermute | solution.py:465
  32.9 2.9 %collective-permute-start.13 = (f32[8,2,32,256]{3,2,1,0:T(8,128)S(1)}, f32[8,2,32,256]{3,2,1,0:T(8,128)S(1)}, u32[]{:S(2)}, u32[]{:S(2)}) collective-permute-start(f32[8,2,32,256]{3,2,1,0:T(8,128)S(1)} %get-tuple-element.131), channel_id=1, source_target_pairs={{0,1},{2,3},{4,5},{6,7},{8,9},{10,11},{12,13},{14,15},{16,17},{18,... | collective-permute-start | bytes 1572872 | tf_op jit(solution)/shard_map/ppermute | solution.py:465
  33.8 8.9 %collective-permute-start.17 = (f32[4,32,256]{2,1,0:T(8,128)S(1)}, f32[4,32,256]{2,1,0:T(8,128)S(1)}, u32[]{:S(2)}, u32[]{:S(2)}) collective-permute-start(f32[4,32,256]{2,1,0:T(8,128)S(1)} %get-tuple-element.145), channel_id=1, source_target_pairs={{96,64},{97,65},{98,66},{99,67},{100,68},{101,69},{102,70},{103,71... | collective-permute-start | bytes 393224 | tf_op jit(solution)/shard_map/ppermute | solution.py:586
  35.1 8.5 %collective-permute-start.16 = (f32[4,32,256]{2,1,0:T(8,128)S(1)}, f32[4,32,256]{2,1,0:T(8,128)S(1)}, u32[]{:S(2)}, u32[]{:S(2)}) collective-permute-start(f32[4,32,256]{2,1,0:T(8,128)S(1)} %get-tuple-element.144), channel_id=1, source_target_pairs={{96,64},{97,65},{98,66},{99,67},{100,68},{101,69},{102,70},{103,71... | collective-permute-start | bytes 393224 | tf_op jit(solution)/shard_map/ppermute | solution.py:586
  36.2 8.2 %collective-permute-start.15 = (f32[2,32,256]{2,1,0:T(8,128)S(1)}, f32[2,32,256]{2,1,0:T(8,128)S(1)}, u32[]{:S(2)}, u32[]{:S(2)}) collective-permute-start(f32[2,32,256]{2,1,0:T(8,128)S(1)} %get-tuple-element.143), channel_id=1, source_target_pairs={{96,64},{97,65},{98,66},{99,67},{100,68},{101,69},{102,70},{103,71... | collective-permute-start | bytes 196616 | tf_op jit(solution)/shard_map/ppermute | solution.py:586
  42.0 3.3 %collective-permute-start.14 = (f32[2,32,256]{2,1,0:T(8,128)S(1)}, f32[2,32,256]{2,1,0:T(8,128)S(1)}, u32[]{:S(2)}, u32[]{:S(2)}) collective-permute-start(f32[2,32,256]{2,1,0:T(8,128)S(1)} %get-tuple-element.141), channel_id=1, source_target_pairs={{96,64},{97,65},{98,66},{99,67},{100,68},{101,69},{102,70},{103,71... | collective-permute-start | bytes 196616 | tf_op jit(solution)/shard_map/ppermute | solution.py:586
  42.9 3.3 %collective-permute-start.21 = (f32[4,32,256]{2,1,0:T(8,128)S(1)}, f32[4,32,256]{2,1,0:T(8,128)S(1)}, u32[]{:S(2)}, u32[]{:S(2)}) collective-permute-start(f32[4,32,256]{2,1,0:T(8,128)S(1)} %get-tuple-element.157), channel_id=1, source_target_pairs={{64,32},{65,33},{66,34},{67,35},{68,36},{69,37},{70,38},{71,39},{7... | collective-permute-start | bytes 393224 | tf_op jit(solution)/shard_map/ppermute | solution.py:586
  43.8 3.9 %collective-permute-start.20 = (f32[4,32,256]{2,1,0:T(8,128)S(1)}, f32[4,32,256]{2,1,0:T(8,128)S(1)}, u32[]{:S(2)}, u32[]{:S(2)}) collective-permute-start(f32[4,32,256]{2,1,0:T(8,128)S(1)} %get-tuple-element.156), channel_id=1, source_target_pairs={{64,32},{65,33},{66,34},{67,35},{68,36},{69,37},{70,38},{71,39},{7... | collective-permute-start | bytes 393224 | tf_op jit(solution)/shard_map/ppermute | solution.py:586
  44.6 4.5 %collective-permute-start.19 = (f32[2,32,256]{2,1,0:T(8,128)S(1)}, f32[2,32,256]{2,1,0:T(8,128)S(1)}, u32[]{:S(2)}, u32[]{:S(2)}) collective-permute-start(f32[2,32,256]{2,1,0:T(8,128)S(1)} %get-tuple-element.155), channel_id=1, source_target_pairs={{64,32},{65,33},{66,34},{67,35},{68,36},{69,37},{70,38},{71,39},{7... | collective-permute-start | bytes 196616 | tf_op jit(solution)/shard_map/ppermute | solution.py:586
  45.5 5.1 %collective-permute-start.18 = (f32[2,32,256]{2,1,0:T(8,128)S(1)}, f32[2,32,256]{2,1,0:T(8,128)S(1)}, u32[]{:S(2)}, u32[]{:S(2)}) collective-permute-start(f32[2,32,256]{2,1,0:T(8,128)S(1)} %get-tuple-element.154), channel_id=1, source_target_pairs={{64,32},{65,33},{66,34},{67,35},{68,36},{69,37},{70,38},{71,39},{7... | collective-permute-start | bytes 196616 | tf_op jit(solution)/shard_map/ppermute | solution.py:586
  46.4 22.3 %collective-permute-start.25 = (f32[4,32,256]{2,1,0:T(8,128)S(1)}, f32[4,32,256]{2,1,0:T(8,128)S(1)}, u32[]{:S(2)}, u32[]{:S(2)}) collective-permute-start(f32[4,32,256]{2,1,0:T(8,128)S(1)} %get-tuple-element.169), channel_id=1, source_target_pairs={{32,0},{33,1},{34,2},{35,3},{36,4},{37,5},{38,6},{39,7},{40,8},{41... | collective-permute-start | bytes 393224 | tf_op jit(solution)/shard_map/ppermute | solution.py:586
  47.8 24.3 %collective-permute-start.24 = (f32[4,32,256]{2,1,0:T(8,128)S(1)}, f32[4,32,256]{2,1,0:T(8,128)S(1)}, u32[]{:S(2)}, u32[]{:S(2)}) collective-permute-start(f32[4,32,256]{2,1,0:T(8,128)S(1)} %get-tuple-element.168), channel_id=1, source_target_pairs={{32,0},{33,1},{34,2},{35,3},{36,4},{37,5},{38,6},{39,7},{40,8},{41... | collective-permute-start | bytes 393224 | tf_op jit(solution)/shard_map/ppermute | solution.py:586
  49.3 24.4 %collective-permute-start.23 = (f32[2,32,256]{2,1,0:T(8,128)S(1)}, f32[2,32,256]{2,1,0:T(8,128)S(1)}, u32[]{:S(2)}, u32[]{:S(2)}) collective-permute-start(f32[2,32,256]{2,1,0:T(8,128)S(1)} %get-tuple-element.167), channel_id=1, source_target_pairs={{32,0},{33,1},{34,2},{35,3},{36,4},{37,5},{38,6},{39,7},{40,8},{41... | collective-permute-start | bytes 196616 | tf_op jit(solution)/shard_map/ppermute | solution.py:586
  50.8 25.0 %collective-permute-start.22 = (f32[2,32,256]{2,1,0:T(8,128)S(1)}, f32[2,32,256]{2,1,0:T(8,128)S(1)}, u32[]{:S(2)}, u32[]{:S(2)}) collective-permute-start(f32[2,32,256]{2,1,0:T(8,128)S(1)} %get-tuple-element.166), channel_id=1, source_target_pairs={{32,0},{33,1},{34,2},{35,3},{36,4},{37,5},{38,6},{39,7},{40,8},{41... | collective-permute-start | bytes 196616 | tf_op jit(solution)/shard_map/ppermute | solution.py:586

commit v8 on v7

--- a/solution.py
+++ b/solution.py
@@ -136,8 +136,9 @@
         source[q, lane] = total
 
 
-def forward_chain(lanes, q, source, inverse, couple, mask, field, sent, edges=None):
-    xs = [source[q, lane] + coef(couple, 0, q, lane) * sent[j] for j, lane in enumerate(lanes)]
+def forward_chain(lanes, q, source, inverse, couple, mask, field, sent, edges=None, came=None):
+    prior = sent if came is None else came
+    xs = [source[q, lane] + coef(couple, 0, q, lane) * prior[j] for j, lane in enumerate(lanes)]
     ys = solve(xs, inverse, q, lanes)
     values = [weight(mask, q, lane) * y for y, lane in zip(ys, lanes)]
     for j, lane in enumerate(lanes):
@@ -285,15 +286,16 @@
     @pl.when(lax.axis_index("strip") == stage)
     def _():
         for j, lane in enumerate(lanes):
-            sent[j] = came[j]
             field[0, lane] = came[j]
 
         for q in range(COLS):
-            forward_chain(lanes, q, source, inverse, couple, mask, field, sent, edges)
-
-
-def backward_chain(lanes, q, source, inverse, couple, mask, result, sent):
-    xs = [source[q, lane] + coef(couple, 1, q, lane) * sent[j] for j, lane in enumerate(lanes)]
+            prior = came if q == 0 else None
+            forward_chain(lanes, q, source, inverse, couple, mask, field, sent, edges, prior)
+
+
+def backward_chain(lanes, q, source, inverse, couple, mask, result, sent, came=None):
+    prior = sent if came is None else came
+    xs = [source[q, lane] + coef(couple, 1, q, lane) * prior[j] for j, lane in enumerate(lanes)]
     ys = solve(xs, inverse, q, lanes)
     for j, lane in enumerate(lanes):
         value = weight(mask, q, lane) * ys[j]
@@ -324,7 +326,7 @@
 
 
 def backward_sweep(
-    lanes, before, last, inverse, source, couple, mask, result, out, sent, sem, sem_own, beside
+    lanes, before, last, inverse, source, couple, mask, result, out, sent, sem, sem_own, beside, came=None
 ):
     def earlier(q):
         return lane_copies(result, out, q, before, sem)
@@ -335,7 +337,8 @@
     if before:
         start_all(earlier)
     for q in DOWN:
-        backward_chain(lanes, q, source, inverse, couple, mask, result, sent)
+        prior = came if q == DOWN[0] else None
+        backward_chain(lanes, q, source, inverse, couple, mask, result, sent, prior)
         for copy in own(q):
             copy.start()
         if beside is not None and q > 0:
@@ -400,7 +403,6 @@
     even = is_even()
 
     def sweep(lanes, before):
-        sent[...] = came[...]
         backward_sweep(
             lanes,
             before if chunk > 0 and stage == 0 else None,
@@ -415,6 +417,7 @@
             sem,
             sem_own,
             None,
+            came,
         )
 
     by_parity(strip == stage, even, chunk, sweep)

time: 78.9 us -> 79.1 us (level)
  no operation moved by 1% of the time
where the time goes in v8:
time: 79.1 us; the launch traced here: 78 us
  starting transfers between devices  30.7 us (39%)
  waiting for transfers between devices  27.4 us (35%)
  Pallas kernels  19.1 us (24%)
    ppermute x12, waiting for transfers between devices, on_device(): came = lax.ppermute(sents[stage + 1, chunk], 'strip', [(stage + 1, stage)])  19.6 us
    pallas_call x31, Pallas kernels, run(): pl.pallas_call(kernel, name=name, out_shape=[o for o, _ in outs], in_spec...  19.1 us
    ppermute x12, starting transfers between devices, on_device(): came = lax.ppermute(sents[stage + 1, chunk], 'strip', [(stage + 1, stage)])  10.5 us
    ppermute x9, starting transfers between devices, on_device(): came = lax.ppermute(sents[stage - 1, chunk], 'strip', [(stage - 1, stage)])  9.86 us
    ppermute x4, starting transfers between devices, swapped(): return lax.ppermute(value, 'tile', pairs + [(b, a) for a, b in pairs])  8.88 us
    ppermute x4, waiting for transfers between devices, swapped(): return lax.ppermute(value, 'tile', pairs + [(b, a) for a, b in pairs])  4.71 us
    ppermute x9, waiting for transfers between devices, on_device(): came = lax.ppermute(sents[stage - 1, chunk], 'strip', [(stage - 1, stage)])  2.34 us
  transfers between devices with their start and end apart: 26, of which 7 were waited for; matrix products, arithmetic and copies ran while one was open for 0% of the time, Pallas kernels for 20%

profile of v8, /device:TPU:96, one launch (start us, length us, event | category | flops | bytes accessed | tf_op | source)
XLA Modules:
  0.0 78.0 jit_solution(1350055821658617466)
XLA Ops:
  0.0 1.6 %prep.1 = (f32[12,32,256]{2,1,0:T(8,128)S(1)}, f32[8,2,32,256]{3,2,1,0:T(8,128)S(1)}, f32[8,2,32,256]{3,2,1,0:T(8,128)S(1)}, f32[9,12,256]{2,1,0:T(8,128)S(1)}) custom-call(s32[2,4,12]{2,1,0:T(4,128)} %ice_hbm.1, f32[8,12,32,256]{3,2,1,0:T(8,128)} %bitcast.13), custom_call_target="tpu_custom_call" | custom-call | flops 4294967296 | bytes 134217728 | tf_op jit(solution)/shard_map/prep/pallas_call | solution.py:442
  1.6 1.4 %collective-permute-start = (f32[12,32,256]{2,1,0:T(8,128)S(1)}, f32[12,32,256]{2,1,0:T(8,128)S(1)}, u32[]{:S(2)}, u32[]{:S(2)}) collective-permute-start(f32[12,32,256]{2,1,0:T(8,128)S(1)} %get-tuple-element.94), channel_id=1, source_target_pairs={{32,0},{64,32},{96,64},{33,1},{65,33},{97,65},{34,2},{66,34},{98,6... | collective-permute-start | bytes 1179656 | tf_op jit(solution)/shard_map/ppermute | solution.py:487
  3.0 0.1 collective-permute-start.1
  3.1 4.9 %collective-permute-start.2 = (f32[8,2,32,256]{3,2,1,0:T(8,128)S(1)}, f32[8,2,32,256]{3,2,1,0:T(8,128)S(1)}, u32[]{:S(2)}, u32[]{:S(2)}) collective-permute-start(f32[8,2,32,256]{3,2,1,0:T(8,128)S(1)} %get-tuple-element.97), channel_id=1, source_target_pairs={{1,2},{3,4},{5,6},{7,8},{9,10},{11,12},{13,14},{15,16},{17,18},{19... | collective-permute-start | bytes 1572872 | tf_op jit(solution)/shard_map/ppermute | solution.py:468
  8.0 5.7 %first.1 = (bf16[8,12,256,256]{3,2,1,0:T(8,128)(2,1)S(1)}, f32[6,2,12,4,256]{4,3,2,1,0:T(4,128)S(1)}, f32[8,12,32,256]{3,2,1,0:T(8,128)S(1)}, f32[9,12,32,256]{3...) custom-call(bf16[8,12,256,256]{3,2,1,0:T(8,128)(2,1)} %bitcast.18, ...), custom_call_target="tpu_custom_call" | custom-call | flops 65536 | bytes 2048 | tf_op jit(solution)/shard_map/first/pallas_call | solution.py:442
  13.7 0.8 %collective-permute-done.nxt = f32[12,32,256]{2,1,0:T(8,128)S(1)} collective-permute-done((f32[12,32,256]{2,1,0:T(8,128)S(1)}, f32[12,32,256]{2,1,0:T(8,128)S(1)}, u32[]{:S(2)}, u32[]{:S(2)}) %collective-permute-start) | collective-permute-done | bytes 393248 | tf_op jit(solution)/shard_map/ppermute | solution.py:487
  14.5 0.3 tail_0.1
  14.8 3.3 %collective-permute-start.5 = (f32[4,32,256]{2,1,0:T(8,128)S(1)}, f32[4,32,256]{2,1,0:T(8,128)S(1)}, u32[]{:S(2)}, u32[]{:S(2)}) collective-permute-start(f32[4,32,256]{2,1,0:T(8,128)S(1)} %get-tuple-element.109), channel_id=1, source_target_pairs={{0,32},{1,33},{2,34},{3,35},{4,36},{5,37},{6,38},{7,39},{8,40},{9,... | collective-permute-start | bytes 393224 | tf_op jit(solution)/shard_map/ppermute | solution.py:533
  18.1 0.0 collective-permute-done.2.halo_out
  18.1 1.4 %outer.1 = (f32[8,12,32,256]{3,2,1,0:T(8,128)S(1)}, f32[9,12,32,256]{3,2,1,0:T(8,128)S(1)}, f32[8,2,32,256]{3,2,1,0:T(8,128)S(1)}, f32[8,2,32,256]{3,2,1,0:T(8,128)S(1)}, f32[4,32,256]{2,1,0:T(8,128)S(1)}) custom-call(f32[12,32,256]{2,1,0:T(8,128)S(1)} %collective-permute-done.nxt, ...), custom_call_target="tpu_custom_call", output_to_operand_aliasing={{0}: (8, {}), {1}: (9, {})} | custom-call | flops 67108864 | bytes 2097152 | tf_op jit(solution)/shard_map/outer/pallas_call | solution.py:442
  19.5 1.3 %collective-permute-start.4 = (f32[4,32,256]{2,1,0:T(8,128)S(1)}, f32[4,32,256]{2,1,0:T(8,128)S(1)}, u32[]{:S(2)}, u32[]{:S(2)}) collective-permute-start(f32[4,32,256]{2,1,0:T(8,128)S(1)} %get-tuple-element.108), channel_id=1, source_target_pairs={{0,32},{1,33},{2,34},{3,35},{4,36},{5,37},{6,38},{7,39},{8,40},{9,... | collective-permute-start | bytes 393224 | tf_op jit(solution)/shard_map/ppermute | solution.py:533
  20.8 0.3 tail_2.1
  21.1 1.3 %collective-permute-start.3 = (f32[4,32,256]{2,1,0:T(8,128)S(1)}, f32[4,32,256]{2,1,0:T(8,128)S(1)}, u32[]{:S(2)}, u32[]{:S(2)}) collective-permute-start(f32[4,32,256]{2,1,0:T(8,128)S(1)} %get-tuple-element.106), channel_id=1, source_target_pairs={{0,32},{1,33},{2,34},{3,35},{4,36},{5,37},{6,38},{7,39},{8,40},{9,... | collective-permute-start | bytes 393224 | tf_op jit(solution)/shard_map/ppermute | solution.py:533
  22.4 0.0 collective-permute-done.5.came
  22.5 0.7 collective-permute-start.8
  23.1 1.6 %collective-permute-done.4.came = f32[4,32,256]{2,1,0:T(8,128)S(1)} collective-permute-done((f32[4,32,256]{2,1,0:T(8,128)S(1)}, f32[4,32,256]{2,1,0:T(8,128)S(1)}, u32[]{:S(2)}, u32[]{:S(2)}) %collective-permute-start.4) | collective-permute-done | bytes 131104 | tf_op jit(solution)/shard_map/ppermute | solution.py:533
  24.7 0.7 collective-permute-start.7
  25.4 0.7 collective-permute-done.3.came
  26.1 0.7 collective-permute-start.6
  26.8 0.0 collective-permute-done.8.came
  26.8 0.7 collective-permute-start.11
  27.5 0.7 collective-permute-start.10
  28.3 0.7 collective-permute-start.9
  28.9 0.0 collective-permute-done.11.came
  29.0 3.9 %collective-permute-start.12 = (f32[8,2,32,256]{3,2,1,0:T(8,128)S(1)}, f32[8,2,32,256]{3,2,1,0:T(8,128)S(1)}, u32[]{:S(2)}, u32[]{:S(2)}) collective-permute-start(f32[8,2,32,256]{3,2,1,0:T(8,128)S(1)} %get-tuple-element.130), channel_id=1, source_target_pairs={{1,2},{3,4},{5,6},{7,8},{9,10},{11,12},{13,14},{15,16},{17,18},{19... | collective-permute-start | bytes 1572872 | tf_op jit(solution)/shard_map/ppermute | solution.py:468
  32.9 0.1 collective-permute-start.13
  33.0 0.2 forward_3_2.1.field
  33.2 0.6 last_0.1
  33.8 0.7 collective-permute-start.17
  34.5 0.6 last_1.1
  35.1 0.7 collective-permute-start.16
  35.8 0.0 collective-permute-done.13.halo
  35.8 0.5 last_2.1
  36.2 0.7 collective-permute-start.15
  36.9 4.7 %collective-permute-done.12.halo = f32[8,2,32,256]{3,2,1,0:T(8,128)S(1)} collective-permute-done((f32[8,2,32,256]{3,2,1,0:T(8,128)S(1)}, f32[8,2,32,256]{3,2,1,0:T(8,128)S(1)}, u32[]{:S(2)}, u32[]{:S(2)}) %collective-permute-start.12) | collective-permute-done | bytes 524320 | tf_op jit(solution)/shard_map/ppermute | solution.py:468
  41.6 0.4 last_3.1
  42.0 0.7 collective-permute-start.14
  42.7 0.0 collective-permute-done.17.came
  42.7 0.2 backward_2_0.1
  42.9 0.7 collective-permute-start.21
  43.6 0.2 backward_2_1.1
  43.8 0.7 collective-permute-start.20
  44.5 0.2 backward_2_2.1
  44.6 0.7 collective-permute-start.19
  45.3 0.0 collective-permute-done.14.came
  45.3 0.2 backward_2_3.1
  45.5 0.7 collective-permute-start.18
  46.2 0.2 backward_1_0.1
  46.4 1.3 %collective-permute-start.25 = (f32[4,32,256]{2,1,0:T(8,128)S(1)}, f32[4,32,256]{2,1,0:T(8,128)S(1)}, u32[]{:S(2)}, u32[]{:S(2)}) collective-permute-start(f32[4,32,256]{2,1,0:T(8,128)S(1)} %get-tuple-element.169), channel_id=1, source_target_pairs={{32,0},{33,1},{34,2},{35,3},{36,4},{37,5},{38,6},{39,7},{40,8},{41... | collective-permute-start | bytes 393224 | tf_op jit(solution)/shard_map/ppermute | solution.py:589
  47.6 0.0 collective-permute-done.20.came
  47.7 0.2 backward_1_1.1
  47.8 1.3 %collective-permute-start.24 = (f32[4,32,256]{2,1,0:T(8,128)S(1)}, f32[4,32,256]{2,1,0:T(8,128)S(1)}, u32[]{:S(2)}, u32[]{:S(2)}) collective-permute-start(f32[4,32,256]{2,1,0:T(8,128)S(1)} %get-tuple-element.168), channel_id=1, source_target_pairs={{32,0},{33,1},{34,2},{35,3},{36,4},{37,5},{38,6},{39,7},{40,8},{41... | collective-permute-start | bytes 393224 | tf_op jit(solution)/shard_map/ppermute | solution.py:589
  49.1 0.0 collective-permute-done.19.came
  49.1 0.2 backward_1_2.1
  49.3 1.3 %collective-permute-start.23 = (f32[2,32,256]{2,1,0:T(8,128)S(1)}, f32[2,32,256]{2,1,0:T(8,128)S(1)}, u32[]{:S(2)}, u32[]{:S(2)}) collective-permute-start(f32[2,32,256]{2,1,0:T(8,128)S(1)} %get-tuple-element.167), channel_id=1, source_target_pairs={{32,0},{33,1},{34,2},{35,3},{36,4},{37,5},{38,6},{39,7},{40,8},{41... | collective-permute-start | bytes 196616 | tf_op jit(solution)/shard_map/ppermute | solution.py:589
  50.6 0.2 backward_1_3.1
  50.8 1.3 %collective-permute-start.22 = (f32[2,32,256]{2,1,0:T(8,128)S(1)}, f32[2,32,256]{2,1,0:T(8,128)S(1)}, u32[]{:S(2)}, u32[]{:S(2)}) collective-permute-start(f32[2,32,256]{2,1,0:T(8,128)S(1)} %get-tuple-element.166), channel_id=1, source_target_pairs={{32,0},{33,1},{34,2},{35,3},{36,4},{37,5},{38,6},{39,7},{40,8},{41... | collective-permute-start | bytes 196616 | tf_op jit(solution)/shard_map/ppermute | solution.py:589
  52.1 16.6 %collective-permute-done.25.came = f32[4,32,256]{2,1,0:T(8,128)S(1)} collective-permute-done((f32[4,32,256]{2,1,0:T(8,128)S(1)}, f32[4,32,256]{2,1,0:T(8,128)S(1)}, u32[]{:S(2)}, u32[]{:S(2)}) %collective-permute-start.25) | collective-permute-done | bytes 131104 | tf_op jit(solution)/shard_map/ppermute | solution.py:589
  68.7 1.5 %backward_0_0.1 = (f32[8,12,32,256]{3,2,1,0:T(8,128)S(1)}, f32[8,12,32,256]{3,2,1,0:T(8,128)}) custom-call(f32[4,32,256]{2,1,0:T(8,128)S(1)} %collective-permute-done.25.came, bf16[8,12,256,256]{3,2,1,0:T(8,128)(2,1)S(1)} %get-tuple-element.93.own.inverse, ...), custom_call_target="tpu_custom_call", output_to_operand_aliasing={{0}: (5, {}), {1}: (6, {})} | custom-call | flops 67108864 | bytes 2097152 | tf_op jit(solution)/shard_map/backward_0_0/pallas_call | solution.py:442
  70.2 2.2 %collective-permute-done.24.came = f32[4,32,256]{2,1,0:T(8,128)S(1)} collective-permute-done((f32[4,32,256]{2,1,0:T(8,128)S(1)}, f32[4,32,256]{2,1,0:T(8,128)S(1)}, u32[]{:S(2)}, u32[]{:S(2)}) %collective-permute-start.24) | collective-permute-done | bytes 131104 | tf_op jit(solution)/shard_map/ppermute | solution.py:589
  72.4 1.5 %backward_0_1.1 = (f32[8,12,32,256]{3,2,1,0:T(8,128)S(1)}, f32[8,12,32,256]{3,2,1,0:T(8,128)}) custom-call(f32[4,32,256]{2,1,0:T(8,128)S(1)} %collective-permute-done.24.came, bf16[8,12,256,256]{3,2,1,0:T(8,128)(2,1)S(1)} %get-tuple-element.93.own.inverse, ...), custom_call_target="tpu_custom_call", output_to_operand_aliasing={{0}: (5, {}), {1}: (6, {})} | custom-call | flops 67108864 | bytes 2097152 | tf_op jit(solution)/shard_map/backward_0_1/pallas_call | solution.py:442
  73.9 1.3 %backward_0_2.1 = (f32[8,12,32,256]{3,2,1,0:T(8,128)S(1)}, f32[8,12,32,256]{3,2,1,0:T(8,128)}) custom-call(f32[2,32,256]{2,1,0:T(8,128)S(1)} %collective-permute-done.23.came, bf16[8,12,256,256]{3,2,1,0:T(8,128)(2,1)S(1)} %get-tuple-element.93.own.inverse, ...), custom_call_target="tpu_custom_call", output_to_operand_aliasing={{0}: (5, {}), {1}: (6, {})} | custom-call | flops 67108864 | bytes 2097152 | tf_op jit(solution)/shard_map/backward_0_2/pallas_call | solution.py:442
  75.2 0.8 %collective-permute-done.22.came = f32[2,32,256]{2,1,0:T(8,128)S(1)} collective-permute-done((f32[2,32,256]{2,1,0:T(8,128)S(1)}, f32[2,32,256]{2,1,0:T(8,128)S(1)}, u32[]{:S(2)}, u32[]{:S(2)}) %collective-permute-start.22) | collective-permute-done | bytes 65568 | tf_op jit(solution)/shard_map/ppermute | solution.py:589
  76.0 1.8 %backward_0_3.1 = (f32[8,12,32,256]{3,2,1,0:T(8,128)S(1)}, f32[8,12,32,256]{3,2,1,0:T(8,128)}) custom-call(f32[2,32,256]{2,1,0:T(8,128)S(1)} %collective-permute-done.22.came, bf16[8,12,256,256]{3,2,1,0:T(8,128)(2,1)S(1)} %get-tuple-element.93.own.inverse, ...), custom_call_target="tpu_custom_call", output_to_operand_aliasing={{0}: (5, {}), {1}: (6, {})} | custom-call | flops 536870912 | bytes 16777216 | tf_op jit(solution)/shard_map/backward_0_3/pallas_call | solution.py:442
  (23 shorter events, 0.2 us)
Async XLA Ops:
  0.0 8.0 %copy-start = (f32[2,4,12,32,256]{4,3,2,1,0:T(8,128)S(1)}, f32[2,4,12,32,256]{4,3,2,1,0:T(8,128)}, u32[]{:S(2)}) copy-start(f32[2,4,12,32,256]{4,3,2,1,0:T(8,128)} %param.5) | copy-start | bytes 9437188
  0.0 8.0 %copy-start.1 = (f32[2,4,12,32,256]{4,3,2,1,0:T(8,128)S(1)}, f32[2,4,12,32,256]{4,3,2,1,0:T(8,128)}, u32[]{:S(2)}) copy-start(f32[2,4,12,32,256]{4,3,2,1,0:T(8,128)} %param.6) | copy-start | bytes 9437188
  1.6 12.9 %collective-permute-start = (f32[12,32,256]{2,1,0:T(8,128)S(1)}, f32[12,32,256]{2,1,0:T(8,128)S(1)}, u32[]{:S(2)}, u32[]{:S(2)}) collective-permute-start(f32[12,32,256]{2,1,0:T(8,128)S(1)} %get-tuple-element.94), channel_id=1, source_target_pairs={{32,0},{64,32},{96,64},{33,1},{65,33},{97,65},{34,2},{66,34},{98,6... | collective-permute-start | bytes 1179656 | tf_op jit(solution)/shard_map/ppermute | solution.py:487
  3.0 15.0 %collective-permute-start.1 = (f32[8,2,32,256]{3,2,1,0:T(8,128)S(1)}, f32[8,2,32,256]{3,2,1,0:T(8,128)S(1)}, u32[]{:S(2)}, u32[]{:S(2)}) collective-permute-start(f32[8,2,32,256]{3,2,1,0:T(8,128)S(1)} %get-tuple-element.96), channel_id=1, source_target_pairs={{0,1},{2,3},{4,5},{6,7},{8,9},{10,11},{12,13},{14,15},{16,17},{18,... | collective-permute-start | bytes 1572872 | tf_op jit(solution)/shard_map/ppermute | solution.py:468
  3.1 14.9 %collective-permute-start.2 = (f32[8,2,32,256]{3,2,1,0:T(8,128)S(1)}, f32[8,2,32,256]{3,2,1,0:T(8,128)S(1)}, u32[]{:S(2)}, u32[]{:S(2)}) collective-permute-start(f32[8,2,32,256]{3,2,1,0:T(8,128)S(1)} %get-tuple-element.97), channel_id=1, source_target_pairs={{1,2},{3,4},{5,6},{7,8},{9,10},{11,12},{13,14},{15,16},{17,18},{19... | collective-permute-start | bytes 1572872 | tf_op jit(solution)/shard_map/ppermute | solution.py:468
  14.8 7.7 %collective-permute-start.5 = (f32[4,32,256]{2,1,0:T(8,128)S(1)}, f32[4,32,256]{2,1,0:T(8,128)S(1)}, u32[]{:S(2)}, u32[]{:S(2)}) collective-permute-start(f32[4,32,256]{2,1,0:T(8,128)S(1)} %get-tuple-element.109), channel_id=1, source_target_pairs={{0,32},{1,33},{2,34},{3,35},{4,36},{5,37},{6,38},{7,39},{8,40},{9,... | collective-permute-start | bytes 393224 | tf_op jit(solution)/shard_map/ppermute | solution.py:533
  19.5 5.2 %collective-permute-start.4 = (f32[4,32,256]{2,1,0:T(8,128)S(1)}, f32[4,32,256]{2,1,0:T(8,128)S(1)}, u32[]{:S(2)}, u32[]{:S(2)}) collective-permute-start(f32[4,32,256]{2,1,0:T(8,128)S(1)} %get-tuple-element.108), channel_id=1, source_target_pairs={{0,32},{1,33},{2,34},{3,35},{4,36},{5,37},{6,38},{7,39},{8,40},{9,... | collective-permute-start | bytes 393224 | tf_op jit(solution)/shard_map/ppermute | solution.py:533
  21.1 5.0 %collective-permute-start.3 = (f32[4,32,256]{2,1,0:T(8,128)S(1)}, f32[4,32,256]{2,1,0:T(8,128)S(1)}, u32[]{:S(2)}, u32[]{:S(2)}) collective-permute-start(f32[4,32,256]{2,1,0:T(8,128)S(1)} %get-tuple-element.106), channel_id=1, source_target_pairs={{0,32},{1,33},{2,34},{3,35},{4,36},{5,37},{6,38},{7,39},{8,40},{9,... | collective-permute-start | bytes 393224 | tf_op jit(solution)/shard_map/ppermute | solution.py:533
  22.5 4.3 %collective-permute-start.8 = (f32[4,32,256]{2,1,0:T(8,128)S(1)}, f32[4,32,256]{2,1,0:T(8,128)S(1)}, u32[]{:S(2)}, u32[]{:S(2)}) collective-permute-start(f32[4,32,256]{2,1,0:T(8,128)S(1)} %get-tuple-element.117), channel_id=1, source_target_pairs={{32,64},{33,65},{34,66},{35,67},{36,68},{37,69},{38,70},{39,71},{4... | collective-permute-start | bytes 393224 | tf_op jit(solution)/shard_map/ppermute | solution.py:533
  24.7 2.8 %collective-permute-start.7 = (f32[4,32,256]{2,1,0:T(8,128)S(1)}, f32[4,32,256]{2,1,0:T(8,128)S(1)}, u32[]{:S(2)}, u32[]{:S(2)}) collective-permute-start(f32[4,32,256]{2,1,0:T(8,128)S(1)} %get-tuple-element.116), channel_id=1, source_target_pairs={{32,64},{33,65},{34,66},{35,67},{36,68},{37,69},{38,70},{39,71},{4... | collective-permute-start | bytes 393224 | tf_op jit(solution)/shard_map/ppermute | solution.py:533
  26.1 2.1 %collective-permute-start.6 = (f32[4,32,256]{2,1,0:T(8,128)S(1)}, f32[4,32,256]{2,1,0:T(8,128)S(1)}, u32[]{:S(2)}, u32[]{:S(2)}) collective-permute-start(f32[4,32,256]{2,1,0:T(8,128)S(1)} %get-tuple-element.115), channel_id=1, source_target_pairs={{32,64},{33,65},{34,66},{35,67},{36,68},{37,69},{38,70},{39,71},{4... | collective-permute-start | bytes 393224 | tf_op jit(solution)/shard_map/ppermute | solution.py:533
  26.8 2.1 %collective-permute-start.11 = (f32[4,32,256]{2,1,0:T(8,128)S(1)}, f32[4,32,256]{2,1,0:T(8,128)S(1)}, u32[]{:S(2)}, u32[]{:S(2)}) collective-permute-start(f32[4,32,256]{2,1,0:T(8,128)S(1)} %get-tuple-element.125), channel_id=1, source_target_pairs={{64,96},{65,97},{66,98},{67,99},{68,100},{69,101},{70,102},{71,103... | collective-permute-start | bytes 393224 | tf_op jit(solution)/shard_map/ppermute | solution.py:533
  27.5 1.4 %collective-permute-start.10 = (f32[4,32,256]{2,1,0:T(8,128)S(1)}, f32[4,32,256]{2,1,0:T(8,128)S(1)}, u32[]{:S(2)}, u32[]{:S(2)}) collective-permute-start(f32[4,32,256]{2,1,0:T(8,128)S(1)} %get-tuple-element.124), channel_id=1, source_target_pairs={{64,96},{65,97},{66,98},{67,99},{68,100},{69,101},{70,102},{71,103... | collective-permute-start | bytes 393224 | tf_op jit(solution)/shard_map/ppermute | solution.py:533
  28.3 4.7 %collective-permute-start.9 = (f32[4,32,256]{2,1,0:T(8,128)S(1)}, f32[4,32,256]{2,1,0:T(8,128)S(1)}, u32[]{:S(2)}, u32[]{:S(2)}) collective-permute-start(f32[4,32,256]{2,1,0:T(8,128)S(1)} %get-tuple-element.123), channel_id=1, source_target_pairs={{64,96},{65,97},{66,98},{67,99},{68,100},{69,101},{70,102},{71,103... | collective-permute-start | bytes 393224 | tf_op jit(solution)/shard_map/ppermute | solution.py:533
  29.0 12.6 %collective-permute-start.12 = (f32[8,2,32,256]{3,2,1,0:T(8,128)S(1)}, f32[8,2,32,256]{3,2,1,0:T(8,128)S(1)}, u32[]{:S(2)}, u32[]{:S(2)}) collective-permute-start(f32[8,2,32,256]{3,2,1,0:T(8,128)S(1)} %get-tuple-element.130), channel_id=1, source_target_pairs={{1,2},{3,4},{5,6},{7,8},{9,10},{11,12},{13,14},{15,16},{17,18},{19... | collective-permute-start | bytes 1572872 | tf_op jit(solution)/shard_map/ppermute | solution.py:468
  32.9 2.9 %collective-permute-start.13 = (f32[8,2,32,256]{3,2,1,0:T(8,128)S(1)}, f32[8,2,32,256]{3,2,1,0:T(8,128)S(1)}, u32[]{:S(2)}, u32[]{:S(2)}) collective-permute-start(f32[8,2,32,256]{3,2,1,0:T(8,128)S(1)} %get-tuple-element.131), channel_id=1, source_target_pairs={{0,1},{2,3},{4,5},{6,7},{8,9},{10,11},{12,13},{14,15},{16,17},{18,... | collective-permute-start | bytes 1572872 | tf_op jit(solution)/shard_map/ppermute | solution.py:468
  33.8 8.9 %collective-permute-start.17 = (f32[4,32,256]{2,1,0:T(8,128)S(1)}, f32[4,32,256]{2,1,0:T(8,128)S(1)}, u32[]{:S(2)}, u32[]{:S(2)}) collective-permute-start(f32[4,32,256]{2,1,0:T(8,128)S(1)} %get-tuple-element.145), channel_id=1, source_target_pairs={{96,64},{97,65},{98,66},{99,67},{100,68},{101,69},{102,70},{103,71... | collective-permute-start | bytes 393224 | tf_op jit(solution)/shard_map/ppermute | solution.py:589
  35.1 8.5 %collective-permute-start.16 = (f32[4,32,256]{2,1,0:T(8,128)S(1)}, f32[4,32,256]{2,1,0:T(8,128)S(1)}, u32[]{:S(2)}, u32[]{:S(2)}) collective-permute-start(f32[4,32,256]{2,1,0:T(8,128)S(1)} %get-tuple-element.144), channel_id=1, source_target_pairs={{96,64},{97,65},{98,66},{99,67},{100,68},{101,69},{102,70},{103,71... | collective-permute-start | bytes 393224 | tf_op jit(solution)/shard_map/ppermute | solution.py:589
  36.2 8.2 %collective-permute-start.15 = (f32[2,32,256]{2,1,0:T(8,128)S(1)}, f32[2,32,256]{2,1,0:T(8,128)S(1)}, u32[]{:S(2)}, u32[]{:S(2)}) collective-permute-start(f32[2,32,256]{2,1,0:T(8,128)S(1)} %get-tuple-element.143), channel_id=1, source_target_pairs={{96,64},{97,65},{98,66},{99,67},{100,68},{101,69},{102,70},{103,71... | collective-permute-start | bytes 196616 | tf_op jit(solution)/shard_map/ppermute | solution.py:589
  42.0 3.3 %collective-permute-start.14 = (f32[2,32,256]{2,1,0:T(8,128)S(1)}, f32[2,32,256]{2,1,0:T(8,128)S(1)}, u32[]{:S(2)}, u32[]{:S(2)}) collective-permute-start(f32[2,32,256]{2,1,0:T(8,128)S(1)} %get-tuple-element.141), channel_id=1, source_target_pairs={{96,64},{97,65},{98,66},{99,67},{100,68},{101,69},{102,70},{103,71... | collective-permute-start | bytes 196616 | tf_op jit(solution)/shard_map/ppermute | solution.py:589
  42.9 3.3 %collective-permute-start.21 = (f32[4,32,256]{2,1,0:T(8,128)S(1)}, f32[4,32,256]{2,1,0:T(8,128)S(1)}, u32[]{:S(2)}, u32[]{:S(2)}) collective-permute-start(f32[4,32,256]{2,1,0:T(8,128)S(1)} %get-tuple-element.157), channel_id=1, source_target_pairs={{64,32},{65,33},{66,34},{67,35},{68,36},{69,37},{70,38},{71,39},{7... | collective-permute-start | bytes 393224 | tf_op jit(solution)/shard_map/ppermute | solution.py:589
  43.8 3.9 %collective-permute-start.20 = (f32[4,32,256]{2,1,0:T(8,128)S(1)}, f32[4,32,256]{2,1,0:T(8,128)S(1)}, u32[]{:S(2)}, u32[]{:S(2)}) collective-permute-start(f32[4,32,256]{2,1,0:T(8,128)S(1)} %get-tuple-element.156), channel_id=1, source_target_pairs={{64,32},{65,33},{66,34},{67,35},{68,36},{69,37},{70,38},{71,39},{7... | collective-permute-start | bytes 393224 | tf_op jit(solution)/shard_map/ppermute | solution.py:589
  44.6 4.5 %collective-permute-start.19 = (f32[2,32,256]{2,1,0:T(8,128)S(1)}, f32[2,32,256]{2,1,0:T(8,128)S(1)}, u32[]{:S(2)}, u32[]{:S(2)}) collective-permute-start(f32[2,32,256]{2,1,0:T(8,128)S(1)} %get-tuple-element.155), channel_id=1, source_target_pairs={{64,32},{65,33},{66,34},{67,35},{68,36},{69,37},{70,38},{71,39},{7... | collective-permute-start | bytes 196616 | tf_op jit(solution)/shard_map/ppermute | solution.py:589
  45.5 5.1 %collective-permute-start.18 = (f32[2,32,256]{2,1,0:T(8,128)S(1)}, f32[2,32,256]{2,1,0:T(8,128)S(1)}, u32[]{:S(2)}, u32[]{:S(2)}) collective-permute-start(f32[2,32,256]{2,1,0:T(8,128)S(1)} %get-tuple-element.154), channel_id=1, source_target_pairs={{64,32},{65,33},{66,34},{67,35},{68,36},{69,37},{70,38},{71,39},{7... | collective-permute-start | bytes 196616 | tf_op jit(solution)/shard_map/ppermute | solution.py:589
  46.4 22.3 %collective-permute-start.25 = (f32[4,32,256]{2,1,0:T(8,128)S(1)}, f32[4,32,256]{2,1,0:T(8,128)S(1)}, u32[]{:S(2)}, u32[]{:S(2)}) collective-permute-start(f32[4,32,256]{2,1,0:T(8,128)S(1)} %get-tuple-element.169), channel_id=1, source_target_pairs={{32,0},{33,1},{34,2},{35,3},{36,4},{37,5},{38,6},{39,7},{40,8},{41... | collective-permute-start | bytes 393224 | tf_op jit(solution)/shard_map/ppermute | solution.py:589
  47.8 24.5 %collective-permute-start.24 = (f32[4,32,256]{2,1,0:T(8,128)S(1)}, f32[4,32,256]{2,1,0:T(8,128)S(1)}, u32[]{:S(2)}, u32[]{:S(2)}) collective-permute-start(f32[4,32,256]{2,1,0:T(8,128)S(1)} %get-tuple-element.168), channel_id=1, source_target_pairs={{32,0},{33,1},{34,2},{35,3},{36,4},{37,5},{38,6},{39,7},{40,8},{41... | collective-permute-start | bytes 393224 | tf_op jit(solution)/shard_map/ppermute | solution.py:589
  49.3 24.6 %collective-permute-start.23 = (f32[2,32,256]{2,1,0:T(8,128)S(1)}, f32[2,32,256]{2,1,0:T(8,128)S(1)}, u32[]{:S(2)}, u32[]{:S(2)}) collective-permute-start(f32[2,32,256]{2,1,0:T(8,128)S(1)} %get-tuple-element.167), channel_id=1, source_target_pairs={{32,0},{33,1},{34,2},{35,3},{36,4},{37,5},{38,6},{39,7},{40,8},{41... | collective-permute-start | bytes 196616 | tf_op jit(solution)/shard_map/ppermute | solution.py:589
  50.8 25.2 %collective-permute-start.22 = (f32[2,32,256]{2,1,0:T(8,128)S(1)}, f32[2,32,256]{2,1,0:T(8,128)S(1)}, u32[]{:S(2)}, u32[]{:S(2)}) collective-permute-start(f32[2,32,256]{2,1,0:T(8,128)S(1)} %get-tuple-element.166), channel_id=1, source_target_pairs={{32,0},{33,1},{34,2},{35,3},{36,4},{37,5},{38,6},{39,7},{40,8},{41... | collective-permute-start | bytes 196616 | tf_op jit(solution)/shard_map/ppermute | solution.py:589
